TPU v7x, 128 devices: a whole 4x4x4 slice. The times are simulated.
128 devices in a mesh: gx: 16 (over x, y), gy: 8 (over z, core).
Axes of the slice: x: 4, y: 4, z: 4, core: 2. Of those that a mesh axis runs over, the one named last changes fastest.
Arguments:
- pressure_old: float32 [64, 256, 2048], P(None, 'gx', 'gy'), may hold values from -2.5 to 0.5
- conductivity: float32 [64, 256, 2048], P(None, 'gx', 'gy'), may hold values from 0.2 to 12
- forcing: float32 [8, 256, 2048], P(None, 'gx', 'gy'), may hold values from -5 to 5
- vegetated: int32 [256, 2048], P('gx', 'gy'), may hold values from 0 to 1, as said below
- cover_type: int32 [256, 2048], P('gx', 'gy'), may hold values from 0 to 15
- canopy_table: float32 [16, 8], replicated, may hold values from -2 to 2
- root_table: float32 [16, 8], replicated, may hold values from 0.2 to 2
- pair_counts: int32 [16, 16, 8], P('gx', None, 'gy'), may hold values from 0 to 256, as said below
- send_cols: int32 [16, 16, 8, 256], P('gx', None, 'gy'), may hold values from 0 to 4095, as said below
- canopy_state: float32 [16, 16, 8, 16, 256], P('gx', None, 'gy'), may hold values from -6 to 6
Outputs:
- pressure: float32 [64, 256, 2048], P(None, 'gx', 'gy')
- new_state: float32 [16, 16, 8, 16, 256], P('gx', None, 'gy')
Inputs may be any that keep to these rules, and one draw needn't show every extreme that they name: `pair_counts`: in each column j of tiles one owner o receives exactly 256 columns from every tile (i, j). `send_cols`: for tile (i, j) and owner o the first pair_counts[i, o, j] entries are distinct local column numbers; over all o they are exactly the tile's vegetated columns, each once. The remaining entries are arbitrary local column numbers. `vegetated`: 1 exactly at the columns named by live entries of send_cols.
All inputs are finite; a program needn't handle non-finite values.
Results may differ from a plain program's by a relative error of at most 0.00022.
Values sent between devices are 32-bit elements; how exact they have to be, the bound alone decides.
No kernel may reach another device: no remote copies, remote signals or barrier semaphores. Data moves between devices by JAX's collectives and lax.ppermute only.
A program may use at most 128 MiB of HBM per device.

v0:
```python
import jax
import jax.numpy as jnp
from jax import lax
from jax.sharding import PartitionSpec as P

FORC = 8
ROOT = 8
NEWTON = 2
ITERS = 3


specific_storage = 0.05
gravity_step = 0.5


def padded_2(block, sides, width):
    for axis, dim in sides:
        count = lax.axis_size(axis)
        forward = [(i, i + 1) for i in range(count - 1)]
        backward = [(target, source) for source, target in forward]
        low = lax.ppermute(
            lax.slice_in_dim(block, block.shape[dim] - width, None, axis=dim), axis, forward
        )
        high = lax.ppermute(lax.slice_in_dim(block, 0, width, axis=dim), axis, backward)
        block = jnp.concatenate([low, block, high], axis=dim)
    return block


def canopy_physics(payload, state_in):
    forcing_part = payload[0:FORC]
    weights_part = payload[FORC : 2 * FORC]
    root_part = payload[2 * FORC : 2 * FORC + ROOT]
    soil_head = payload[2 * FORC + ROOT : 2 * FORC + 2 * ROOT]
    conductance = 2.0 * jax.nn.sigmoid(jnp.sum(weights_part * forcing_part, axis=0))
    start_temp = state_in[1]
    leaf_temp = start_temp
    for repeat in range(3):
        leaf_temp = 0.5 * (start_temp + forcing_part[0]) + 0.5 * jnp.tanh(
            forcing_part[1] - conductance * (leaf_temp - forcing_part[2])
        )
    demand = (
        conductance
        * jax.nn.softplus(leaf_temp - forcing_part[3])
        / (1.0 + state_in[0] * state_in[0])
    )
    uptake = demand[None] * root_part * jax.nn.sigmoid(2.0 * (soil_head + 1.5))
    canopy_water = 0.8 * state_in[0] + 0.2 * jnp.tanh(forcing_part[4])
    soil_temp = state_in[2:]
    temp_above = jnp.concatenate([leaf_temp[None], soil_temp[:-1]], axis=0)
    temp_below = jnp.concatenate([soil_temp[1:], soil_temp[-1:]], axis=0)
    soil_next = 0.6 * soil_temp + 0.2 * temp_above + 0.2 * temp_below
    return (uptake, jnp.concatenate([canopy_water[None], leaf_temp[None], soil_next], axis=0))


def vertical(field):
    padded = jnp.pad(field, ((1, 1), (0, 0), (0, 0)))
    return [padded[:-2], padded[2:]]


def beside_all(rim_field):
    return [
        rim_field[..., :-2, 1:-1],
        rim_field[..., 2:, 1:-1],
        rim_field[..., 1:-1, :-2],
        rim_field[..., 1:-1, 2:],
    ]


def apply_jacobian(field, capacity, coupling):
    rim_field = padded_2(field, (("gx", 1), ("gy", 2)), 1)
    result = capacity * field
    for weight, other in zip(coupling, vertical(field) + beside_all(rim_field)):
        result = result + weight * (field - other)
    return (result, rim_field)


def squares(residual):
    return lax.psum(jnp.sum(residual * residual), ("gx", "gy"))


def body(
    pressure_old,
    conductivity,
    forcing,
    vegetated,
    cover_type,
    canopy_table,
    root_table,
    pair_counts,
    send_cols,
    canopy_state,
):
    levels, tile_rows, tile_cols = pressure_old.shape
    columns = tile_rows * tile_cols
    owners = send_cols.shape[1]
    slot_count = send_cols.shape[3]
    state_count = canopy_state.shape[3]
    kind_count = canopy_table.shape[0]
    index_list = send_cols.reshape(owners * slot_count)
    counts = pair_counts.reshape(owners, 1)
    slot_live = jnp.arange(slot_count)[None, :] < counts
    onehot = (cover_type.reshape(1, columns) == jnp.arange(kind_count)[:, None]).astype(jnp.float32)
    param_table = jnp.concatenate([canopy_table, root_table], axis=1).T
    params = jnp.dot(param_table, onehot, precision=lax.Precision.HIGHEST)
    local_data = jnp.concatenate(
        [forcing.reshape(FORC, columns), params, pressure_old[:ROOT].reshape(ROOT, columns)], axis=0
    )
    picked = jnp.take(local_data, index_list, axis=1).reshape(
        local_data.shape[0], owners, slot_count
    )
    held_state = canopy_state.reshape(owners, state_count, slot_count).transpose(1, 0, 2)
    counts_row = counts.astype(jnp.float32).reshape(1, owners)
    arrived, arrived_counts = (
        lax.all_to_all(picked, "gx", split_axis=1, concat_axis=1, tiled=True),
        lax.all_to_all(counts_row, "gx", split_axis=1, concat_axis=1, tiled=True),
    )
    uptake, updated = canopy_physics(arrived, held_state)
    owner_live = jnp.arange(slot_count).astype(jnp.float32)[None, :] < arrived_counts.reshape(
        owners, 1
    )
    new_held = jnp.where(owner_live[None], updated, held_state)
    returned = lax.all_to_all(uptake, "gx", split_axis=1, concat_axis=1, tiled=True)
    new_state = new_held.transpose(1, 0, 2).reshape(canopy_state.shape)
    values = jnp.where(slot_live[None], returned, jnp.float32(0.0)).reshape(
        ROOT, owners * slot_count
    )
    root_sink = (
        jnp.zeros((ROOT, columns), jnp.float32)
        .at[:, index_list]
        .add(values)
        .reshape(ROOT, tile_rows, tile_cols)
    )
    veg_float = vegetated.astype(jnp.float32)
    evaporation = (
        (1.0 - veg_float)
        * 0.5
        * jax.nn.softplus(forcing[3] - forcing[2])
        * jax.nn.sigmoid(2.0 * (pressure_old[0] + 1.5))
    )
    rainfall = 0.3 * jax.nn.softplus(forcing[4])
    source_field = jnp.concatenate(
        [-root_sink, jnp.zeros((levels - ROOT, tile_rows, tile_cols), jnp.float32)], axis=0
    )
    source_field = source_field.at[0].add(rainfall - evaporation)
    layer_depth = jnp.arange(levels).astype(jnp.float32)[:, None, None]
    stored_old = 0.3 + 0.7 * jax.nn.sigmoid(2.0 * pressure_old) + specific_storage * pressure_old
    head = pressure_old
    for newton_index in range(NEWTON):
        squash = jax.nn.sigmoid(2.0 * head)
        mobility = conductivity * (0.1 + 0.9 * squash)
        potential = head - gravity_step * layer_depth
        rim_field = padded_2(jnp.stack([mobility, potential]), (("gx", 2), ("gy", 3)), 1)
        mob_near = vertical(mobility) + beside_all(rim_field[0])
        pot_near = vertical(potential) + beside_all(rim_field[1])
        coupling = [2.0 * mobility * other / (mobility + other) for other in mob_near]
        outflow = jnp.zeros_like(head)
        for weight, other in zip(coupling, pot_near):
            outflow = outflow + weight * (potential - other)
        stored = 0.3 + 0.7 * squash + specific_storage * head
        imbalance = stored - stored_old + outflow - source_field
        capacity = 1.4 * squash * (1.0 - squash) + specific_storage
        right_side = -imbalance
        update = jnp.zeros_like(head)
        update_wide = jnp.zeros((levels, tile_rows + 2, tile_cols + 2), jnp.float32)
        residual = right_side
        direction = right_side
        norm_now = squares(residual)
        for sweep_index in range(ITERS):
            image, direction_wide = apply_jacobian(direction, capacity, coupling)
            step_size = norm_now / lax.psum(jnp.sum(direction * image), ("gx", "gy"))
            update = update + step_size * direction
            update_wide = update_wide + step_size * direction_wide
            residual = residual - step_size * image
            norm_after = squares(residual)
            direction = residual + norm_after / norm_now * direction
            norm_now = norm_after
        head = head + update
    return (head, new_state)


def solution(mesh):
    placed = (
        P(None, "gx", "gy"),
        P(None, "gx", "gy"),
        P(None, "gx", "gy"),
        P("gx", "gy"),
        P("gx", "gy"),
        P(),
        P(),
        P("gx", None, "gy"),
        P("gx", None, "gy", None),
        P("gx", None, "gy", None, None),
    )
    return jax.shard_map(
        body,
        mesh=mesh,
        in_specs=placed,
        out_specs=(P(None, "gx", "gy"), P("gx", None, "gy", None, None)),
        check_vma=False,
    )
```

profile of v0, /device:TPU:1, one launch (start us, length us, event | category | flops | bytes accessed | tf_op | source)
XLA Modules:
  0.0 1062.5 jit_solution(5020702187113620313)
XLA Ops:
  7.0 14.2 %gather_fusion = f32[4096,32]{1,0:T(8,128)} fusion(f32[32,4096]{0,1:T(8,128)S(1)} %copy.80, s32[4096]{0:T(1024)S(1)} %broadcast_clamp_fusion), kind=kCustom, calls=%fused_computation | custom fusion | bytes 1064960 | tf_op jit(solution)/shard_map/jit(_take)/gather | solution.py:108
  24.3 7.6 all-to-all-start
  74.7 8.0 all-to-all-start.1
  91.8 24.1 %scatter_custom_fusion = f32[8,4096]{0,1:T(8,128)} fusion(s32[4096]{0:T(1024)} %bitcast.144, f32[4096,8]{1,0:T(8,128)} %copy.87, f32[]{:T(128)} %constant.77.clone.1), kind=kCustom, calls=%fused_computation.263 | custom fusion | flops 32768 | bytes 131584 | tf_op jit(solution)/shard_map/scatter-add | solution.py:130
  124.4 10.5 fusion.198
  144.9 6.3 collective-permute-start.6
  160.3 10.7 %multiply_reduce_fusion.8 = (f32[]{:T(128)}, f32[]{:T(128)}, f32[64,16,256]{2,0,1:T(8,128)}) fusion(f32[64,16,256]{2,0,1:T(8,128)S(1)} %get-tuple-element.49, f32[64,16,256]{2,0,1:T(8,128)} %get-tuple-element.53, f32[64,16,256]{2,0,1:T(8,128)} %copy-done.15, f32[64,18,1]{2,0,1:T(8,128)} %copy.93, f32[64,1,256]{2,0,1:T(8,128)S(1)} %collective-permute-done.5, ...), kind=kLoop, calls=%fused_computation.260 | loop fusion | flops 10485758 | bytes 10626056 | tf_op jit(solution)/shard_map/reduce_sum | solution.py:170
  171.0 67.0 %all-reduce.12 = (f32[]{:T(128)}, f32[]{:T(128)}) all-reduce(f32[]{:T(128)} %get-tuple-element.23, f32[]{:T(128)} %get-tuple-element.22), channel_id=1, replica_groups=mesh['gx'=16,'gy'=8] {'gx','gy'}, use_global_device_ids=true, to_apply=%region_3.4 | all-reduce | flops 2 | bytes 16 | tf_op jit(solution)/shard_map/psum | solution.py:78
  242.4 62.8 %psum.86 = f32[]{:T(128)} all-reduce(f32[]{:T(128)} %get-tuple-element.45), channel_id=1, replica_groups=mesh['gx'=16,'gy'=8] {'gx','gy'}, use_global_device_ids=true, to_apply=%region_7.8 | all-reduce | flops 1 | bytes 8 | tf_op jit(solution)/shard_map/psum | solution.py:78
  327.7 6.9 multiply_reduce_fusion.6
  334.6 66.1 %psum.87 = f32[]{:T(128)} all-reduce(f32[]{:T(128)} %get-tuple-element.43), channel_id=1, replica_groups=mesh['gx'=16,'gy'=8] {'gx','gy'}, use_global_device_ids=true, to_apply=%region_9.10 | all-reduce | flops 1 | bytes 8 | tf_op jit(solution)/shard_map/psum | solution.py:170
  404.1 63.8 %psum.88 = f32[]{:T(128)} all-reduce(f32[]{:T(128)} %multiply_reduce_fusion.5), channel_id=1, replica_groups=mesh['gx'=16,'gy'=8] {'gx','gy'}, use_global_device_ids=true, to_apply=%region_11.12 | all-reduce | flops 1 | bytes 8 | tf_op jit(solution)/shard_map/psum | solution.py:78
  493.9 8.8 fusion.143
  502.6 66.4 %psum.89 = f32[]{:T(128)} all-reduce(f32[]{:T(128)} %fusion.143), channel_id=1, replica_groups=mesh['gx'=16,'gy'=8] {'gx','gy'}, use_global_device_ids=true, to_apply=%region_13.14 | all-reduce | flops 1 | bytes 8 | tf_op jit(solution)/shard_map/psum | solution.py:170
  605.2 5.6 fusion.194
  632.1 8.9 all-to-all-start.2
  644.7 9.4 multiply_reduce_fusion.3
  654.1 65.9 %all-reduce.11 = (f32[]{:T(128)}, f32[]{:T(128)}) all-reduce(f32[]{:T(128)} %get-tuple-element.21, f32[]{:T(128)} %get-tuple-element.20), channel_id=1, replica_groups=mesh['gx'=16,'gy'=8] {'gx','gy'}, use_global_device_ids=true, to_apply=%region_15.16 | all-reduce | flops 2 | bytes 16 | tf_op jit(solution)/shard_map/psum | solution.py:78
  723.3 62.9 %psum.92 = f32[]{:T(128)} all-reduce(f32[]{:T(128)} %get-tuple-element.30), channel_id=1, replica_groups=mesh['gx'=16,'gy'=8] {'gx','gy'}, use_global_device_ids=true, to_apply=%region_19.20 | all-reduce | flops 1 | bytes 8 | tf_op jit(solution)/shard_map/psum | solution.py:78
  813.0 5.8 multiply_reduce_fusion.1
  818.9 67.0 %psum.93 = f32[]{:T(128)} all-reduce(f32[]{:T(128)} %get-tuple-element.28), channel_id=1, replica_groups=mesh['gx'=16,'gy'=8] {'gx','gy'}, use_global_device_ids=true, to_apply=%region_21.22 | all-reduce | flops 1 | bytes 8 | tf_op jit(solution)/shard_map/psum | solution.py:170
  889.8 62.6 %psum.94 = f32[]{:T(128)} all-reduce(f32[]{:T(128)} %multiply_reduce_fusion), channel_id=1, replica_groups=mesh['gx'=16,'gy'=8] {'gx','gy'}, use_global_device_ids=true, to_apply=%region_23.24 | all-reduce | flops 1 | bytes 8 | tf_op jit(solution)/shard_map/psum | solution.py:78
  980.4 9.2 fusion.142
  990.5 66.8 %psum.95 = f32[]{:T(128)} all-reduce(f32[]{:T(128)} %fusion.142), channel_id=1, replica_groups=mesh['gx'=16,'gy'=8] {'gx','gy'}, use_global_device_ids=true, to_apply=%region_25.26 | all-reduce | flops 1 | bytes 8 | tf_op jit(solution)/shard_map/psum | solution.py:170
  (258 shorter events, 261.2 us)
Async XLA Ops:
  24.3 45.5 %all-to-all-start = ((f32[32,16,256]{2,0,1:T(8,128)}), f32[32,16,256]{2,0,1:T(8,128)}, u32[]{:S(2)}, u32[]{:S(2)}) async-start(f32[32,16,256]{2,0,1:T(8,128)} %broadcast_select_fusion), calls=%async_computation | async-start | bytes 1048576 | tf_op jit(solution)/shard_map/all_to_all | solution.py:114
  34.8 7.0 collective-permute-start
  38.0 6.1 collective-permute-start.1
  51.2 11.7 %collective-permute-start.3 = (f32[2,64,18,1]{1,0,3,2:T(2,128)}, f32[2,64,18,1]{1,0,3,2:T(2,128)}, u32[]{:S(2)}, u32[]{:S(2)}) collective-permute-start(f32[2,64,18,1]{1,0,3,2:T(2,128)} %copy.77), channel_id=1, source_target_pairs={{1,0},{2,1},{3,2},{4,3},{5,4},{6,5},{7,6},{9,8},{10,9},{11,10},{12... | collective-permute-start | bytes 27656 | tf_op jit(solution)/shard_map/ppermute | solution.py:24
  55.4 5.2 collective-permute-start.2
  74.7 15.2 %all-to-all-start.1 = ((f32[8,16,256]{2,0,1:T(8,128)}), f32[8,16,256]{2,0,1:T(8,128)S(1)}, u32[]{:S(2)}, u32[]{:S(2)}) async-start(f32[8,16,256]{2,0,1:T(8,128)} %fusion.153), calls=%async_computation.1 | async-start | bytes 262144 | tf_op jit(solution)/shard_map/all_to_all | solution.py:122
  136.6 5.0 collective-permute-start.5
  144.9 10.2 collective-permute-start.6
  153.2 5.3 collective-permute-start.7
  310.2 5.0 collective-permute-start.9
  317.7 5.9 collective-permute-start.10
  472.1 5.0 collective-permute-start.13
  480.4 8.3 collective-permute-start.14
  486.8 5.3 collective-permute-start.15
  575.6 5.7 collective-permute-start.17
  584.7 10.2 collective-permute-start.18
  592.5 5.4 collective-permute-start.19
  612.8 5.1 collective-permute-start.21
  621.3 19.8 %collective-permute-start.22 = (f32[64,18,1]{0,1,2:T(8,128)}, f32[64,18,1]{0,1,2:T(8,128)}, u32[]{:S(2)}, u32[]{:S(2)}) collective-permute-start(f32[64,18,1]{0,1,2:T(8,128)} %copy.108), channel_id=1, source_target_pairs={{0,1},{1,2},{2,3},{3,4},{4,5},{5,6},{6,7},{8,9},{9,10},{10,11},{11... | collective-permute-start | bytes 13832 | tf_op jit(solution)/shard_map/ppermute | solution.py:21
  627.8 15.1 %collective-permute-start.23 = (f32[64,18,1]{0,1,2:T(8,128)}, f32[64,18,1]{0,1,2:T(8,128)}, u32[]{:S(2)}, u32[]{:S(2)}) collective-permute-start(f32[64,18,1]{0,1,2:T(8,128)} %copy.110), channel_id=1, source_target_pairs={{1,0},{2,1},{3,2},{4,3},{5,4},{6,5},{7,6},{9,8},{10,9},{11,10},{12... | collective-permute-start | bytes 13832 | tf_op jit(solution)/shard_map/ppermute | solution.py:24
  632.1 175.8 %all-to-all-start.2 = ((f32[1,16,1]{2,0,1:T(1,128)}), f32[1,16,1]{2,0,1:T(1,128)}, u32[]{:S(2)}, u32[]{:S(2)}) async-start(f32[1,16,1]{2,0,1:T(1,128)} %copy.120), calls=%async_computation.2 | async-start | bytes 16384 | tf_op jit(solution)/shard_map/all_to_all | solution.py:115
  791.1 5.0 collective-permute-start.25
  801.3 9.8 collective-permute-start.27
  968.7 9.9 collective-permute-start.31
  (52 other events, 822.6 us)
where the time goes:
time: 1070 us; the launch traced here: 1060 us
  blocking collectives  651 us (61%)
  other arithmetic  140 us (13%)
  local copies, waits for them, and re-layouts  112 us (10%)
  starting transfers between devices  107 us (10%)
  waiting for transfers between devices  37.4 us (3%)
  between operations  14.2 us (1%)
    psum x6, blocking collectives, squares(): return lax.psum(jnp.sum(residual * residual), ('gx', 'gy'))  385 us
    psum x4, blocking collectives, body(): step_size = norm_now / lax.psum(jnp.sum(direction * image), ('gx', 'gy'))  266 us
    reduce_sum x6, other arithmetic, body(): step_size = norm_now / lax.psum(jnp.sum(direction * image), ('gx', 'gy'))  50.7 us
    ppermute x16, starting transfers between devices, padded_2(): lax.ppermute(lax.slice_in_dim(block, block.shape[dim] - width, None, axis...  49.2 us
    ppermute x16, starting transfers between devices, padded_2(): lax.ppermute(lax.slice_in_dim(block, 0, width, axis=dim), axis, backward)  33 us
    ppermute x16, waiting for transfers between devices, padded_2(): lax.ppermute(lax.slice_in_dim(block, 0, width, axis=dim), axis, backward)  32.7 us
    slice x22, local copies, waits for them, and re-layouts, padded_2(): lax.slice_in_dim(block, block.shape[dim] - width, None, axis=dim)  25 us
    scatter-add x1, other arithmetic, body(): root_sink = jnp.zeros((ROOT, columns), jnp.float32).at[:, index_list].add...  24.1 us
  transfers between devices with their start and end apart: 35, of which 15 were waited for; matrix products, arithmetic and copies ran while one was open for 7% of the time, Pallas kernels for 0%

commit v1 on v0

v1 whole, which is shorter than its diff:
```python
import jax
import jax.numpy as jnp
from jax import lax
from jax.experimental import pallas as pl
from jax.experimental.pallas import tpu as pltpu
from jax.sharding import PartitionSpec as P

FORC = 8
ROOT = 8
LEV = 64
ROWS = 16
COLS = 256
XR = 24
XC = 384
STORE = 0.05
GRAV = 0.5
F32 = jnp.float32
BF16 = jnp.bfloat16
VMEM_LIMIT = 56 * 1024 * 1024


def vmem(n=1):
    return [pl.BlockSpec(memory_space=pltpu.VMEM)] * n


def params():
    return pltpu.CompilerParams(vmem_limit_bytes=VMEM_LIMIT)


def shaped(*shape):
    return jax.ShapeDtypeStruct(shape, F32)


def iota(shape, dim):
    return lax.broadcasted_iota(jnp.int32, shape, dim)


def right(v):
    return pltpu.roll(v, v.shape[1] - 1, 1)


def left(v):
    return pltpu.roll(v, 1, 1)


def below(v):
    return pltpu.roll(v, v.shape[0] - 1, 0)


def above(v):
    return pltpu.roll(v, 1, 0)


def lanes(v, shift):
    return v if shift % 128 == 0 else pltpu.roll(v, shift % 128, v.ndim - 1)


def pieces(v):
    high = v.astype(BF16)
    rest = v - high.astype(F32)
    mid = rest.astype(BF16)
    low = (rest - mid.astype(F32)).astype(BF16)
    return high, mid, low


def canopy_send_kernel(
    forcing, cover, canopy_table, counts, cols, state, payload, split, gathered
):
    weights = [jnp.zeros((ROWS, COLS), F32) for _ in range(FORC)]
    kinds = cover[...]
    for kind in range(canopy_table.shape[0]):
        hit = kinds == kind
        for m in range(FORC):
            weights[m] = jnp.where(hit, canopy_table[kind, m], weights[m])
    total = weights[0] * forcing[0]
    for m in range(1, FORC):
        total = total + weights[m] * forcing[m]
    conductance = 2.0 * jax.nn.sigmoid(total)
    channels = [forcing[0], forcing[1], forcing[2], jnp.tanh(forcing[4]), conductance]
    used = len(channels)
    for c, channel in enumerate(channels):
        for p, piece in enumerate(pieces(channel)):
            split[pl.ds((p * used + c) * ROWS, ROWS), :] = piece

    def owner(o, carry):
        index = cols[pl.ds(o, 1), :]
        row_hit = iota((ROWS, COLS), 0) == (index // COLS)
        col_hit = iota((COLS, COLS), 0) == (index % COLS)
        onehot = jnp.where(col_hit, 1.0, 0.0).astype(BF16)
        picked = jnp.dot(split[...], onehot, preferred_element_type=F32)
        span = used * ROWS
        picked = picked[:span] + picked[span : 2 * span] + picked[2 * span :]
        sub = iota((8, COLS), 0)
        out = pltpu.roll(state[o, 0:8, :], 6, 0)
        for c in range(used):
            chosen = jnp.where(row_hit, picked[c * ROWS : (c + 1) * ROWS], 0.0)
            chosen = jnp.sum(chosen, axis=0, keepdims=True)
            out = jnp.where(sub == c, chosen, out)
        live = jnp.where(iota((8, COLS), 1) < counts[o], 1.0, 0.0)
        payload[o] = jnp.where(sub == used, live, out)
        return carry

    lax.fori_loop(0, cols.shape[0], owner, 0)


def canopy_send(forcing, cover, canopy_table, counts, cols, state):
    owners = cols.shape[0]
    return pl.pallas_call(
        canopy_send_kernel,
        out_shape=shaped(owners, 8, COLS),
        in_specs=vmem(2)
        + [pl.BlockSpec(memory_space=pltpu.SMEM)] * 2
        + vmem(2),
        out_specs=vmem()[0],
        scratch_shapes=[
            pltpu.VMEM((15 * ROWS, COLS), BF16),
            pltpu.VMEM((8, COLS), F32),
        ],
        compiler_params=params(),
        name="canopy_send",
    )(forcing, cover, canopy_table, counts, cols, state)


def softplus(v):
    return jnp.maximum(v, 0.0) + jnp.log1p(jnp.exp(-jnp.abs(v)))


def leaf(start, f0, f1, f2, g):
    temp = start
    for _ in range(3):
        temp = 0.5 * (start + f0) + 0.5 * jnp.tanh(f1 - g * (temp - f2))
    return temp


def source_kernel(
    arrived, cols, counts, forcing, cover, vegetated, canopy_table, root_table, pressure, source, edge, total
):
    total[...] = jnp.zeros_like(total)

    def owner(o, carry):
        index = cols[pl.ds(o, 1), :]
        row_hit = iota((ROWS, COLS), 0) == (index // COLS)
        col_hit = iota((COLS, COLS), 0) == (index % COLS)
        onehot = jnp.where(col_hit, 1.0, 0.0).astype(BF16)
        wanted = jnp.logical_and(row_hit, iota((ROWS, COLS), 1) < counts[o])
        block = arrived[o]
        parts = []
        for c in (6, 7):
            value = jnp.where(wanted, block[c : c + 1, :], 0.0)
            parts.extend(pieces(value))
        stacked = jnp.concatenate(parts, axis=0)
        placed = lax.dot_general(
            stacked, onehot, (((1,), (1,)), ((), ())), preferred_element_type=F32
        )
        total[...] += placed
        return carry

    lax.fori_loop(0, cols.shape[0], owner, 0)

    def piece(k):
        return total[k * ROWS : (k + 1) * ROWS, :]

    water = piece(0) + piece(1) + piece(2)
    start = piece(3) + piece(4) + piece(5)
    kinds = cover[...]
    weights = [jnp.zeros((ROWS, COLS), F32) for _ in range(FORC)]
    roots = [jnp.zeros((ROWS, COLS), F32) for _ in range(ROOT)]
    for kind in range(canopy_table.shape[0]):
        hit = kinds == kind
        for m in range(FORC):
            weights[m] = jnp.where(hit, canopy_table[kind, m], weights[m])
        for m in range(ROOT):
            roots[m] = jnp.where(hit, root_table[kind, m], roots[m])
    mixed = weights[0] * forcing[0]
    for m in range(1, FORC):
        mixed = mixed + weights[m] * forcing[m]
    conductance = 2.0 * jax.nn.sigmoid(mixed)
    temp = leaf(start, forcing[0], forcing[1], forcing[2], conductance)
    demand = conductance * softplus(temp - forcing[3]) / (1.0 + water * water)
    planted = vegetated[...] == 1
    demand = jnp.where(planted, demand, 0.0)
    dry = jnp.where(planted, 0.0, 0.5)
    lane = iota((ROWS, 128), 1)
    packed = jnp.zeros((ROWS, 128), F32)
    for m in range(ROOT):
        moist = jax.nn.sigmoid(2.0 * (pressure[m] + 1.5))
        value = -(demand * roots[m] * moist)
        if m == 0:
            evaporation = dry * softplus(forcing[3] - forcing[2]) * moist
            value = value + (0.3 * softplus(forcing[4]) - evaporation)
        source[m] = value
        first = jnp.logical_and(lane >= 8 * m, lane < 8 * m + 8)
        last = jnp.logical_and(lane >= 64 + 8 * m, lane < 72 + 8 * m)
        packed = jnp.where(first, lanes(value[:, :128], 8 * m), packed)
        packed = jnp.where(last, lanes(value[:, 128:], 64 + 8 * m - 120), packed)
    edge[...] = packed


def canopy_source(arrived, cols, counts, forcing, cover, vegetated, canopy_table, root_table, pressure):
    smem = pl.BlockSpec(memory_space=pltpu.SMEM)
    v = vmem()[0]
    return pl.pallas_call(
        source_kernel,
        out_shape=(shaped(ROOT, ROWS, COLS), shaped(ROWS, 128)),
        in_specs=[v, v, smem, v, v, v, smem, smem, v],
        out_specs=(v, v),
        scratch_shapes=[pltpu.VMEM((6 * ROWS, COLS), F32)],
        compiler_params=params(),
        name="canopy_source",
    )(arrived, cols, counts, forcing, cover, vegetated, canopy_table, root_table, pressure)


def owner_kernel(arrived, state, updated):
    def slot(i, carry):
        block = arrived[i]
        old = state[i]
        temp = leaf(old[1:2], block[0:1], block[1:2], block[2:3], block[4:5])
        sub = iota(old.shape, 0)
        base = jnp.where(sub == 1, temp, old)
        upper = pltpu.roll(base, 1, 0)
        lower = pltpu.roll(base, base.shape[0] - 1, 0)
        lower = jnp.where(sub == base.shape[0] - 1, base, lower)
        fresh = 0.6 * base + 0.2 * upper + 0.2 * lower
        fresh = jnp.where(sub == 1, temp, fresh)
        fresh = jnp.where(sub == 0, 0.8 * old + 0.2 * block[3:4], fresh)
        updated[i] = jnp.where(block[5:6] > 0.5, fresh, old)
        return carry

    lax.fori_loop(0, arrived.shape[0], slot, 0)


def owner_update(arrived, state):
    return pl.pallas_call(
        owner_kernel,
        out_shape=shaped(*state.shape),
        in_specs=vmem(2),
        out_specs=vmem()[0],
        compiler_params=params(),
        name="owner_update",
    )(arrived, state)


def edge_pack_kernel(pressure, conductivity, to_right, to_left):
    lane = iota((ROWS, 128), 1)
    for f, field in enumerate((pressure, conductivity)):

        def group(g, carry):
            low = jnp.zeros((ROWS, 128), F32)
            high = jnp.zeros((ROWS, 128), F32)
            for k in range(16):
                here = jnp.logical_and(lane >= 8 * k, lane < 8 * k + 8)
                low = jnp.where(here, lanes(field[g * 16 + k, :, :128], 8 * k), low)
                high = jnp.where(here, lanes(field[g * 16 + k, :, 128:], 8 * k - 120), high)
            to_left[f, g] = low
            to_right[f, g] = high
            return carry

        lax.fori_loop(0, LEV // 16, group, 0)


def edge_pack(pressure, conductivity):
    return pl.pallas_call(
        edge_pack_kernel,
        out_shape=(shaped(2, 4, ROWS, 128), shaped(2, 4, ROWS, 128)),
        in_specs=vmem(2),
        out_specs=tuple(vmem(2)),
        compiler_params=params(),
        name="edge_pack",
    )(pressure, conductivity)


RIM = LEV * 2 + 8


def rim_pack_kernel(pressure, conductivity, from_left, from_right, to_next, to_prev):
    low = iota((8, COLS), 0) < 4
    low_one = iota((8, 128), 0) < 4

    def level(z, carry):
        q = pressure[z]
        k = conductivity[z]
        ahead = jnp.where(low, pltpu.roll(q[8:], 4, 0), k[8:])
        behind = jnp.where(low, q[:8], pltpu.roll(k[:8], 4, 0))
        to_next[2 * z] = ahead[:, :128]
        to_next[2 * z + 1] = ahead[:, 128:]
        to_prev[2 * z] = behind[:, :128]
        to_prev[2 * z + 1] = behind[:, 128:]
        return carry

    lax.fori_loop(0, LEV, level, 0, unroll=4)
    for s, side in enumerate((from_left, from_right)):
        for g in range(4):
            q = side[0, g]
            k = side[1, g]
            to_next[2 * LEV + 4 * s + g] = jnp.where(low_one, pltpu.roll(q[8:], 4, 0), k[8:])
            to_prev[2 * LEV + 4 * s + g] = jnp.where(low_one, q[:8], pltpu.roll(k[:8], 4, 0))


def rim_pack(pressure, conductivity, from_left, from_right):
    return pl.pallas_call(
        rim_pack_kernel,
        out_shape=(shaped(RIM, 8, 128), shaped(RIM, 8, 128)),
        in_specs=vmem(4),
        out_specs=tuple(vmem(2)),
        compiler_params=params(),
        name="rim_pack",
    )(pressure, conductivity, from_left, from_right)


def source_rim_kernel(source, edge, from_left, from_right, wide, to_both):
    lane = iota((ROWS, 128), 1)
    low = iota((8, XC), 0) < 4
    wide[...] = jnp.zeros_like(wide)
    for m in range(ROOT):
        halo = jnp.where(lane < 8, lanes(from_right[...], -8 * m), 0.0)
        halo = jnp.where(lane >= 120, lanes(from_left[...], 120 - 64 - 8 * m), halo)
        row = jnp.concatenate([source[m], halo], axis=1)
        wide[m, 0:ROWS, :] = row
        to_both[m] = jnp.where(low, row[:8], row[8:])


def source_rim(source, edge, from_left, from_right):
    return pl.pallas_call(
        source_rim_kernel,
        out_shape=(shaped(ROOT, XR, XC), shaped(ROOT, 8, XC)),
        in_specs=vmem(4),
        out_specs=tuple(vmem(2)),
        compiler_params=params(),
        name="source_rim",
    )(source, edge, from_left, from_right)


def harmonic(m, n):
    return 2.0 * m * n / jnp.maximum(m + n, 1e-30)


def own(v):
    return v[:ROWS, :COLS]


def couplings(q_ref, k_ref, right_hand, cx, cy, cz, cap, v0):
    def parts(z):
        q = q_ref[z]
        s = 0.5 + 0.5 * jnp.tanh(q)
        return q, s, k_ref[z] * (0.1 + 0.9 * s)

    def level(z, carry):
        q, s, m, flux_z = carry
        after = jnp.minimum(z + 1, LEV - 1)
        q_n, s_n, m_n = parts(after)
        y = harmonic(m, right(m))
        x = harmonic(m, below(m))
        deep = jnp.where(z < LEV - 1, harmonic(m, m_n), 0.0)
        cy[z] = y
        cx[z] = x
        cz[z] = deep
        cap[z] = 1.4 * s * (1.0 - s) + STORE
        flow_y = y * (q - right(q))
        flow_x = x * (q - below(q))
        flow_z = deep * (q - q_n + GRAV)
        out = (flow_y - left(flow_y)) + (flow_x - above(flow_x)) + (flow_z - flux_z)
        v0[z] = right_hand(z, q, s) - out
        return q_n, s_n, m_n, flow_z

    lax.fori_loop(0, LEV, level, (*parts(0), jnp.zeros((XR, XC), F32)))


def apply(v_in, cx, cy, cz, cap, visit, sums):
    def level(z, carry):
        v, flux_z, held = carry
        v_n = v_in[jnp.minimum(z + 1, LEV - 1)]
        flow_y = cy[z] * (v - right(v))
        flow_x = cx[z] * (v - below(v))
        flow_z = cz[z] * (v - v_n)
        image = (
            cap[z] * v
            + (flow_y - left(flow_y))
            + (flow_x - above(flow_x))
            + (flow_z - flux_z)
        )
        held = visit(z, v, image, held)
        return v_n, flow_z, held

    start = (v_in[0], jnp.zeros((XR, XC), F32), sums)
    return lax.fori_loop(0, LEV, level, start)[2]


def chain(cx, cy, cz, cap, v0, v1, v2, moments):
    zero = jnp.zeros((ROWS, COLS), F32)

    def store(target):
        def visit(z, v, image, held):
            target[z] = image
            a, b = own(v), own(image)
            return held[0] + a * a, held[1] + a * b

        return visit

    def last(z, v, image, held):
        a, b = own(v), own(image)
        return held[0] + a * a, held[1] + a * b

    sums = []
    sums += apply(v0, cx, cy, cz, cap, store(v1), (zero, zero))
    sums += apply(v1, cx, cy, cz, cap, store(v2), (zero, zero))
    sums += apply(v2, cx, cy, cz, cap, last, (zero, zero))
    row = jnp.zeros((1, 128), F32)
    lane = iota((1, 128), 1)
    for k, held in enumerate(sums):
        value = jnp.sum(jnp.sum(held, axis=0, keepdims=True), axis=1, keepdims=True)
        row = jnp.where(lane == k, value, row)
    moments[...] = jnp.broadcast_to(row, moments.shape)


def coefficients(gathered):
    row = jnp.sum(gathered[...], axis=0, keepdims=True)
    lane = iota((1, 128), 1)
    m = [
        jnp.sum(jnp.where(lane == k, row, 0.0), axis=1, keepdims=True) for k in range(6)
    ]

    def dot(a, b, shift):
        total = jnp.zeros((1, 1), F32)
        for i, p in enumerate(a):
            for j, q in enumerate(b):
                total = total + p * q * m[i + j + shift]
        return total

    one = jnp.ones((1, 1), F32)
    a0 = m[0] / m[1]
    r1 = [one, -a0]
    n1 = dot(r1, r1, 0)
    b0 = n1 / m[0]
    p1 = [one + b0, -a0]
    a1 = n1 / dot(p1, p1, 1)
    r2 = [one, -a0 - a1 * p1[0], -a1 * p1[1]]
    n2 = dot(r2, r2, 0)
    b1 = n2 / n1
    p2 = [r2[0] + b1 * p1[0], r2[1] + b1 * p1[1], r2[2]]
    a2 = n2 / dot(p2, p2, 1)
    return (
        a0 + a1 * p1[0] + a2 * p2[0],
        a1 * p1[1] + a2 * p2[1],
        a2 * p2[2],
    )


def spread(part, lane, k, width, half):
    moved = lanes(part, -half - width * k) if half < width else lanes(part, -width * k)
    return moved


def first_kernel(
    pressure, conductivity, from_left, from_right, from_prev, from_next, source, source_prev, source_next,
    q, k, b, v0, v1, v2, to_next, to_prev, moments,
    cx, cy, cz, cap,
):
    lane = iota((ROWS, 128), 1)
    lane8 = iota((8, 128), 1)
    low = iota((8, COLS), 0) < 4
    low_one = iota((8, 128), 0) < 4

    def fill(g, carry):
        for j in range(16):
            z = g * 16 + j
            q[z, 0:ROWS, 0:COLS] = pressure[z]
            k[z, 0:ROWS, 0:COLS] = conductivity[z]
            for f, target in enumerate((q, k)):
                halo = jnp.where(lane < 8, lanes(from_right[f, g], -8 * j), 0.0)
                halo = jnp.where(lane >= 120, lanes(from_left[f, g], 120 - 8 * j), halo)
                target[z, 0:ROWS, COLS:] = halo
            ahead = jnp.concatenate([from_next[2 * z], from_next[2 * z + 1]], axis=1)
            behind = jnp.concatenate([from_prev[2 * z], from_prev[2 * z + 1]], axis=1)
            q[z, ROWS:, 0:COLS] = jnp.where(low, ahead, pltpu.roll(behind, 4, 0))
            k[z, ROWS:, 0:COLS] = jnp.where(low, pltpu.roll(ahead, 4, 0), behind)
            corner = []
            for side in (from_next, from_prev):
                halo = jnp.where(lane8 < 8, lanes(side[2 * LEV + 4 + g], -8 * j), 0.0)
                halo = jnp.where(lane8 >= 120, lanes(side[2 * LEV + g], 120 - 8 * j), halo)
                corner.append(halo)
            q[z, ROWS:, COLS:] = jnp.where(low_one, corner[0], pltpu.roll(corner[1], 4, 0))
            k[z, ROWS:, COLS:] = jnp.where(low_one, pltpu.roll(corner[0], 4, 0), corner[1])
        return carry

    lax.fori_loop(0, LEV // 16, fill, 0)

    low_wide = iota((8, XC), 0) < 4
    for m in range(ROOT):
        b[m, 0:ROWS, :] = source[m, 0:ROWS, :]
        b[m, ROWS:, :] = jnp.where(low_wide, source_next[m], source_prev[m])

    def right_hand(z, q_z, s_z):
        level = b[jnp.minimum(z, ROOT - 1)]
        return jnp.where(z < ROOT, level, 0.0)

    couplings(q, k, right_hand, cx, cy, cz, cap, v0)
    chain(cx, cy, cz, cap, v0, v1, v2, moments)

    sub = iota((8, XC), 0)

    def rims(g, carry):
        corner_next = jnp.zeros((8, 128), F32)
        corner_prev = jnp.zeros((8, 128), F32)
        for j in range(16):
            z = g * 16 + j
            t0, t1, t2 = v0[z, 0:8, :], v1[z, 0:8, :], v2[z, 0:8, :]
            prev = jnp.where(sub >= 6, pltpu.roll(t1, 4, 0), t2)
            prev = jnp.where(sub == 4, pltpu.roll(t0, 1, 0), prev)
            t0, t1, t2 = v0[z, 8:16, :], v1[z, 8:16, :], v2[z, 8:16, :]
            nxt = jnp.where(sub < 2, pltpu.roll(t1, 4, 0), t2)
            nxt = jnp.where(sub == 3, pltpu.roll(t0, 7, 0), nxt)
            to_next[2 * z] = nxt[:, 0:128]
            to_next[2 * z + 1] = nxt[:, 128:256]
            to_prev[2 * z] = prev[:, 0:128]
            to_prev[2 * z + 1] = prev[:, 128:256]
            here = jnp.logical_and(lane8 >= 8 * j, lane8 < 8 * j + 8)
            corner_next = jnp.where(here, lanes(nxt[:, 256:], 4 + 8 * j), corner_next)
            corner_prev = jnp.where(here, lanes(prev[:, 256:], 4 + 8 * j), corner_prev)
        to_next[2 * LEV + g] = corner_next
        to_prev[2 * LEV + g] = corner_prev
        return carry

    lax.fori_loop(0, LEV // 16, rims, 0)


RIM2 = 2 * LEV + 4


def wide_shape():
    return shaped(LEV, XR, XC)


def scratch(n):
    return [pltpu.VMEM((LEV, XR, XC), F32)] * n


def first_newton(*arrays):
    w = wide_shape()
    outs = (w, w, shaped(ROOT, XR, XC), w, w, w, shaped(RIM2, 8, 128), shaped(RIM2, 8, 128), shaped(128, 128))
    return pl.pallas_call(
        first_kernel,
        out_shape=outs,
        in_specs=vmem(len(arrays)),
        out_specs=tuple(vmem(len(outs))),
        scratch_shapes=scratch(4),
        compiler_params=params(),
        name="first_newton",
    )(*arrays)


def second_kernel(
    q, k, b, u0, u1, u2, from_prev, from_next, gathered,
    q_own, w0, w1, w2, moments,
    q1, cx, cy, cz, cap, v0, v1, v2,
):
    c0, c1, c2 = coefficients(gathered)
    sub = iota((8, XC), 0)
    lane8 = iota((8, 128), 1)
    row_in = jnp.logical_or(lane8 < 4, lane8 >= 124)

    def update(g, carry):
        for j in range(16):
            z = g * 16 + j
            q1[z, 0:ROWS, :] = (
                q[z, 0:ROWS, :] + c0 * u0[z, 0:ROWS, :] + c1 * u1[z, 0:ROWS, :] + c2 * u2[z, 0:ROWS, :]
            )
            sides = []
            for side in (from_next, from_prev):
                halo = jnp.where(row_in, lanes(side[2 * LEV + g], -4 - 8 * j), 0.0)
                sides.append(jnp.concatenate([side[2 * z], side[2 * z + 1], halo], axis=1))
            ahead, behind = sides
            t0, t1, t2 = u0[z, ROWS:, :], u1[z, ROWS:, :], u2[z, ROWS:, :]
            t0 = jnp.where(sub == 3, pltpu.roll(ahead, 7, 0), t0)
            t0 = jnp.where(sub == 4, pltpu.roll(behind, 1, 0), t0)
            t1 = jnp.where(jnp.logical_or(sub == 2, sub == 3), pltpu.roll(ahead, 4, 0), t1)
            t1 = jnp.where(jnp.logical_or(sub == 4, sub == 5), pltpu.roll(behind, 4, 0), t1)
            t2 = jnp.where(jnp.logical_and(sub >= 1, sub <= 3), ahead, t2)
            t2 = jnp.where(jnp.logical_and(sub >= 4, sub <= 6), behind, t2)
            q1[z, ROWS:, :] = q[z, ROWS:, :] + c0 * t0 + c1 * t1 + c2 * t2
        return carry

    lax.fori_loop(0, LEV // 16, update, 0)

    def right_hand(z, q_z, s_z):
        before = q[z]
        s_b = 0.5 + 0.5 * jnp.tanh(before)
        stored = 0.7 * (s_z - s_b) + STORE * (q_z - before)
        level = b[jnp.minimum(z, ROOT - 1)]
        return jnp.where(z < ROOT, level, 0.0) - stored

    couplings(q1, k, right_hand, cx, cy, cz, cap, v0)
    chain(cx, cy, cz, cap, v0, v1, v2, moments)
    for source, target in ((q1, q_own), (v0, w0), (v1, w1), (v2, w2)):
        target[...] = source[:, 0:ROWS, 0:COLS]


def second_newton(*arrays):
    o = shaped(LEV, ROWS, COLS)
    outs = (o, o, o, o, shaped(128, 128))
    return pl.pallas_call(
        second_kernel,
        out_shape=outs,
        in_specs=vmem(len(arrays)),
        out_specs=tuple(vmem(len(outs))),
        scratch_shapes=scratch(8),
        compiler_params=params(),
        name="second_newton",
    )(*arrays)


def final_kernel(q, v0, v1, v2, gathered, out):
    c0, c1, c2 = coefficients(gathered)

    def level(z, carry):
        out[z] = q[z] + c0 * v0[z] + c1 * v1[z] + c2 * v2[z]
        return carry

    lax.fori_loop(0, LEV, level, 0, unroll=4)


def final_update(*arrays):
    return pl.pallas_call(
        final_kernel,
        out_shape=shaped(LEV, ROWS, COLS),
        in_specs=vmem(len(arrays)),
        out_specs=vmem()[0],
        compiler_params=params(),
        name="final_update",
    )(*arrays)


def exchange(to_high, to_low, axis):
    count = lax.axis_size(axis)
    up = [(i, i + 1) for i in range(count - 1)]
    down = [(i + 1, i) for i in range(count - 1)]
    return lax.ppermute(to_high, axis, up), lax.ppermute(to_low, axis, down)


def share(moments):
    return lax.all_to_all(moments, ("gx", "gy"), split_axis=0, concat_axis=0, tiled=True)


def body(
    pressure_old,
    conductivity,
    forcing,
    vegetated,
    cover_type,
    canopy_table,
    root_table,
    pair_counts,
    send_cols,
    canopy_state,
):
    owners = send_cols.shape[1]
    cols = send_cols.reshape(owners, COLS)
    counts = pair_counts.reshape(owners)
    state = canopy_state.reshape(owners, 16, COLS)

    to_right, to_left = edge_pack(pressure_old, conductivity)
    from_left, from_right = exchange(to_right, to_left, "gy")
    payload = canopy_send(forcing, cover_type, canopy_table, counts, cols, state)
    to_next, to_prev = rim_pack(pressure_old, conductivity, from_left, from_right)
    from_prev, from_next = exchange(to_next, to_prev, "gx")
    arrived = lax.all_to_all(payload, "gx", split_axis=0, concat_axis=0, tiled=True)

    source, edge = canopy_source(
        arrived, cols, counts, forcing, cover_type, vegetated, canopy_table, root_table, pressure_old[:ROOT]
    )
    source_left, source_right = exchange(edge, edge, "gy")
    source_wide, both = source_rim(source, edge, source_left, source_right)
    source_prev, source_next = exchange(both, both, "gx")
    new_state = owner_update(arrived, state).reshape(canopy_state.shape)

    q, k, b, v0, v1, v2, to_next, to_prev, moments = first_newton(
        pressure_old, conductivity, from_left, from_right, from_prev, from_next,
        source_wide, source_prev, source_next,
    )
    from_prev, from_next = exchange(to_next, to_prev, "gx")
    gathered = share(moments)
    q1, w0, w1, w2, moments = second_newton(q, k, b, v0, v1, v2, from_prev, from_next, gathered)
    pressure = final_update(q1, w0, w1, w2, share(moments))
    return pressure, new_state


def solution(mesh):
    placed = (
        P(None, "gx", "gy"),
        P(None, "gx", "gy"),
        P(None, "gx", "gy"),
        P("gx", "gy"),
        P("gx", "gy"),
        P(),
        P(),
        P("gx", None, "gy"),
        P("gx", None, "gy", None),
        P("gx", None, "gy", None, None),
    )
    return jax.shard_map(
        body,
        mesh=mesh,
        in_specs=placed,
        out_specs=(P(None, "gx", "gy"), P("gx", None, "gy", None, None)),
        check_vma=False,
    )
```

time: 1070 us -> 216 us (0.20)
  blocking collectives: 651 us -> 23.2 us
  other arithmetic: 140 us -> 0 us
  Pallas kernels: 0 us -> 121 us
  local copies, waits for them, and re-layouts: 112 us -> 7.99 us
  starting transfers between devices: 107 us -> 39.2 us
  waiting for transfers between devices: 37.4 us -> 22.6 us
  between operations: 14.2 us -> 0.84 us
    psum x10 -> x0, blocking collectives: 651 us -> none  [the longest x6 385 us: squares(): return lax.psum(jnp.sum(residual * residual), ('gx', 'gy'))]
    pallas_call x0 -> x9, Pallas kernels: none -> 121 us  [the longest x1 48.6 us: first_newton(): pl.pallas_call(first_kernel, out_shape=outs, in_specs=vmem(len(arrays)),...]
    reduce_sum x11 -> x0, other arithmetic: 61.2 us -> none  [the longest x6 50.7 us: body(): step_size = norm_now / lax.psum(jnp.sum(direction * image), ('gx', 'gy'))]
    ppermute x32 -> x10, starting transfers between devices: 82.2 us -> 25 us  [exchange(): return (lax.ppermute(to_high, axis, up), lax.ppermute(to_low, axis, down))]
    slice x32 -> x1, local copies, waits for them, and re-layouts: 41.9 us -> 1.56 us  [body(): pressure_old[:ROOT]]
    ppermute x16 -> x0, local copies, waits for them, and re-layouts: 29 us -> none  [the longest x8 14.5 us: padded_2(): lax.ppermute(lax.slice_in_dim(block, block.shape[dim] - width, None, axis...]
    scatter-add x1 -> x0, other arithmetic: 24.1 us -> none  [body(): root_sink = jnp.zeros((ROOT, columns), jnp.float32).at[:, index_list].add...]
    all_to_all x0 -> x1, blocking collectives: none -> 23.2 us  [share(): lax.all_to_all(moments, ('gx', 'gy'), split_axis=0, concat_axis=0, tiled=...]
  transfers between devices with their start and end apart: 35 -> 12, of which waited for: 15 -> 6; matrix products, arithmetic and copies ran while one was open for 7% -> 2% of each run, Pallas kernels for 0% -> 7%
where the time goes in v1:
time: 216 us; the launch traced here: 215 us
  Pallas kernels  121 us (56%)
  starting transfers between devices  39.2 us (18%)
  blocking collectives  23.2 us (11%)
  waiting for transfers between devices  22.6 us (10%)
  local copies, waits for them, and re-layouts  7.99 us (4%)
    pallas_call x1, Pallas kernels, first_newton(): pl.pallas_call(first_kernel, out_shape=outs, in_specs=vmem(len(arrays)),...  48.6 us
    pallas_call x1, Pallas kernels, second_newton(): pl.pallas_call(second_kernel, out_shape=outs, in_specs=vmem(len(arrays)),...  48.3 us
    ppermute x10, starting transfers between devices, exchange(): return (lax.ppermute(to_high, axis, up), lax.ppermute(to_low, axis, down))  25 us
    all_to_all x1, blocking collectives, share(): lax.all_to_all(moments, ('gx', 'gy'), split_axis=0, concat_axis=0, tiled=...  23.2 us
    ppermute x10, waiting for transfers between devices, exchange(): return (lax.ppermute(to_high, axis, up), lax.ppermute(to_low, axis, down))  11.4 us
    all_to_all x1, starting transfers between devices, body(): lax.all_to_all(payload, 'gx', split_axis=0, concat_axis=0, tiled=True)  7.51 us
    all_to_all x1, waiting for transfers between devices, share(): lax.all_to_all(moments, ('gx', 'gy'), split_axis=0, concat_axis=0, tiled=...  6.8 us
    all_to_all x1, starting transfers between devices, share(): lax.all_to_all(moments, ('gx', 'gy'), split_axis=0, concat_axis=0, tiled=...  6.69 us
  transfers between devices with their start and end apart: 12, of which 6 were waited for; matrix products, arithmetic and copies ran while one was open for 2% of the time, Pallas kernels for 7%

profile of v1, /device:TPU:1, one launch (start us, length us, event | category | flops | bytes accessed | tf_op | source)
XLA Modules:
  0.0 215.4 jit_solution(12059201869368483888)
XLA Ops:
  0.7 3.3 %edge_pack.1 = (f32[2,4,16,128]{3,2,1,0:T(8,128)}, f32[2,4,16,128]{3,2,1,0:T(8,128)}) custom-call(f32[64,16,256]{2,1,0:T(8,128)} %pressure.5, f32[64,16,256]{2,1,0:T(8,128)} %conductivity.5), custom_call_target="tpu_custom_call" | custom-call | tf_op jit(solution)/shard_map/edge_pack/pallas_call | solution.py:262
  3.9 4.9 %collective-permute-start = (f32[2,4,16,128]{3,2,1,0:T(8,128)}, f32[2,4,16,128]{3,2,1,0:T(8,128)S(1)}, u32[]{:S(2)}, u32[]{:S(2)}) collective-permute-start(f32[2,4,16,128]{3,2,1,0:T(8,128)} %get-tuple-element.24), channel_id=1, source_target_pairs={{0,1},{1,2},{2,3},{3,4},{4,5},{5,6},{6,7},{8,9},{9,10},{10,11},{11... | collective-permute-start | bytes 196616 | tf_op jit(solution)/shard_map/ppermute | solution.py:636
  8.8 1.9 collective-permute-start.1
  10.8 3.8 %collective-permute-done.1.from_right = f32[2,4,16,128]{3,2,1,0:T(8,128)S(1)} collective-permute-done((f32[2,4,16,128]{3,2,1,0:T(8,128)}, f32[2,4,16,128]{3,2,1,0:T(8,128)S(1)}, u32[]{:S(2)}, u32[]{:S(2)}) %collective-permute-start.1) | collective-permute-done | bytes 65568 | tf_op jit(solution)/shard_map/ppermute | solution.py:636
  15.3 2.7 %rim_pack.1 = (f32[136,8,128]{2,1,0:T(8,128)}, f32[136,8,128]{2,1,0:T(8,128)}) custom-call(f32[64,16,256]{2,1,0:T(8,128)} %pressure.5, f32[64,16,256]{2,1,0:T(8,128)} %conductivity.5, f32[2,4,16,128]{3,2,1,0:T(8,128)} %copy-done.5, f32[2,4,16,128]{3,2,1,0:T(8,128)} %copy-done.6), custom_call_target="tpu_custom_call" | custom-call | tf_op jit(solution)/shard_map/rim_pack/pallas_call | solution.py:300
  18.0 3.2 %collective-permute-start.2 = (f32[136,8,128]{2,1,0:T(8,128)}, f32[136,8,128]{2,1,0:T(8,128)S(1)}, u32[]{:S(2)}, u32[]{:S(2)}) collective-permute-start(f32[136,8,128]{2,1,0:T(8,128)} %get-tuple-element.26), channel_id=1, source_target_pairs={{0,8},{8,16},{16,24},{24,32},{32,40},{40,48},{48,56},{56,64},{64,7... | collective-permute-start | bytes 1671176 | tf_op jit(solution)/shard_map/ppermute | solution.py:636
  23.8 5.3 %canopy_send.1 = f32[16,8,256]{2,1,0:T(8,128)} custom-call(f32[8,16,256]{2,1,0:T(8,128)} %forcing.3, s32[16,256]{1,0:T(8,128)} %cover.3, f32[16,8]{1,0:T(8,128)} %copy.16.canopy_table, s32[16]{0:T(128)} %bitcast.25, s32[16,256]{1,0:T(8,128)} %bitcast.21, f32[16,16,256]{2,1,0:T(8,128)} %bitcast.16), custom_call_target="tpu_custom_call" | custom-call | tf_op jit(solution)/shard_map/canopy_send/pallas_call | solution.py:108
  29.1 7.5 %all-to-all-start = ((f32[16,8,256]{2,1,0:T(8,128)}), f32[16,8,256]{2,1,0:T(8,128)S(1)}, u32[]{:S(2)}, u32[]{:S(2)}) async-start(f32[16,8,256]{2,1,0:T(8,128)} %canopy_send.1), calls=%async_computation | async-start | bytes 262144 | tf_op jit(solution)/shard_map/all_to_all | solution.py:665
  38.8 4.5 %all-to-all-done.arrived = f32[16,8,256]{2,1,0:T(8,128)S(1)} async-done(((f32[16,8,256]{2,1,0:T(8,128)}), f32[16,8,256]{2,1,0:T(8,128)S(1)}, u32[]{:S(2)}, u32[]{:S(2)}) %all-to-all-start) | async-done | bytes 131104 | tf_op jit(solution)/shard_map/all_to_all | solution.py:665
  43.9 5.4 %canopy_source.1 = (f32[8,16,256]{2,1,0:T(8,128)}, f32[16,128]{1,0:T(8,128)}) custom-call(f32[16,8,256]{2,1,0:T(8,128)} %copy-done, s32[16,256]{1,0:T(8,128)} %bitcast.22, s32[16]{0:T(128)} %bitcast.26, f32[8,16,256]{2,1,0:T(8,128)} %forcing.3, s32[16,256]{1,0:T(8,128)} %cover.3, s32[16,256]{1,0:T(8,128)} %vegetated.1, f32[16,8]{1,0:T(8,128)} %copy.16.canopy_table, ...), custom_call_target="tpu_custom_call" | custom-call | tf_op jit(solution)/shard_map/canopy_source/pallas_call | solution.py:202
  49.3 4.3 %collective-permute-start.4 = (f32[16,128]{1,0:T(8,128)}, f32[16,128]{1,0:T(8,128)S(1)}, u32[]{:S(2)}, u32[]{:S(2)}) collective-permute-start(f32[16,128]{1,0:T(8,128)} %get-tuple-element.29.edge), channel_id=1, source_target_pairs={{0,1},{1,2},{2,3},{3,4},{4,5},{5,6},{6,7},{8,9},{9,10},{10,11},{11... | collective-permute-start | bytes 24584 | tf_op jit(solution)/shard_map/ppermute | solution.py:636
  53.6 1.9 collective-permute-start.5
  55.5 3.2 %collective-permute-done.5.from_right = f32[16,128]{1,0:T(8,128)S(1)} collective-permute-done((f32[16,128]{1,0:T(8,128)}, f32[16,128]{1,0:T(8,128)S(1)}, u32[]{:S(2)}, u32[]{:S(2)}) %collective-permute-start.5) | collective-permute-done | bytes 8224 | tf_op jit(solution)/shard_map/ppermute | solution.py:636
  59.4 1.8 source_rim.1
  61.2 2.1 collective-permute-start.6
  65.2 3.6 %collective-permute-done.7.source_next = f32[8,8,384]{2,1,0:T(8,128)S(1)} collective-permute-done((f32[8,8,384]{2,1,0:T(8,128)}, f32[8,8,384]{2,1,0:T(8,128)S(1)}, u32[]{:S(2)}, u32[]{:S(2)}) %collective-permute-start.7) | collective-permute-done | bytes 98336 | tf_op jit(solution)/shard_map/ppermute | solution.py:636
  69.9 48.6 %first_newton.1 = (f32[64,24,384]{2,1,0:T(8,128)}, f32[64,24,384]{2,1,0:T(8,128)}, f32[8,24,384]{2,1,0:T(8,128)}, f32[64,24,384]{2,1,0:T(8,128)}, f32[64,24,384]...) custom-call(f32[64,16,256]{2,1,0:T(8,128)} %pressure.5, ...), custom_call_target="tpu_custom_call" | custom-call | tf_op jit(solution)/shard_map/first_newton/pallas_call | solution.py:540
  118.5 2.7 %collective-permute-start.8 = (f32[132,8,128]{2,1,0:T(8,128)}, f32[132,8,128]{2,1,0:T(8,128)S(1)}, u32[]{:S(2)}, u32[]{:S(2)}) collective-permute-start(f32[132,8,128]{2,1,0:T(8,128)} %get-tuple-element.38), channel_id=1, source_target_pairs={{0,8},{8,16},{16,24},{24,32},{32,40},{40,48},{48,56},{56,64},{64,7... | collective-permute-start | bytes 1622024 | tf_op jit(solution)/shard_map/ppermute | solution.py:636
  122.6 23.2 %all_to_all.27 = f32[128,1,128]{2,1,0:T(1,128)} all-to-all(f32[128,1,128]{2,1,0:T(1,128)} %bitcast.23), channel_id=1, replica_groups=mesh['gx'=16,'gy'=8] {'gx','gy'}, dimensions={0} | all-to-all | bytes 131072 | tf_op jit(solution)/shard_map/all_to_all | solution.py:640
  146.8 48.3 %second_newton.1 = (f32[64,16,256]{2,1,0:T(8,128)}, f32[64,16,256]{2,1,0:T(8,128)}, f32[64,16,256]{2,1,0:T(8,128)}, f32[64,16,256]{2,1,0:T(8,128)}, f32[128,128]{1,0:T(8,128)}) custom-call(f32[64,24,384]{2,1,0:T(8,128)} %get-tuple-element.32.q, f32[64,24,384]{2,1,0:T(8,128)} %get-tuple-element.33.k, f32[8,24,384]{2,1,0:T(8,128)} %get-tuple-element.34.b, ...), custom_call_target="tpu_custom_call" | custom-call | tf_op jit(solution)/shard_map/second_newton/pallas_call | solution.py:600
  195.1 6.7 %all-to-all-start.2 = ((f32[128,1,128]{2,1,0:T(1,128)}), f32[128,1,128]{2,1,0:T(1,128)S(1)}, u32[]{:S(2)}, u32[]{:S(2)}) async-start(f32[128,1,128]{2,1,0:T(1,128)} %bitcast.24), calls=%async_computation.2 | async-start | bytes 131072 | tf_op jit(solution)/shard_map/all_to_all | solution.py:640
  201.8 2.5 %owner_update.1 = f32[16,16,256]{2,1,0:T(8,128)} custom-call(f32[16,8,256]{2,1,0:T(8,128)} %copy-done, f32[16,16,256]{2,1,0:T(8,128)} %bitcast.17), custom_call_target="tpu_custom_call" | custom-call | tf_op jit(solution)/shard_map/owner_update/pallas_call | solution.py:233
  204.3 6.8 %all-to-all-done.2 = f32[128,1,128]{2,1,0:T(1,128)S(1)} async-done(((f32[128,1,128]{2,1,0:T(1,128)}), f32[128,1,128]{2,1,0:T(1,128)S(1)}, u32[]{:S(2)}, u32[]{:S(2)}) %all-to-all-start.2) | async-done | bytes 65568 | tf_op jit(solution)/shard_map/all_to_all | solution.py:640
  211.8 3.6 %final_update.1 = f32[64,16,256]{2,1,0:T(8,128)} custom-call(f32[64,16,256]{2,1,0:T(8,128)} %get-tuple-element.41.q, f32[64,16,256]{2,1,0:T(8,128)} %get-tuple-element.42.v0, f32[64,16,256]{2,1,0:T(8,128)} %get-tuple-element.43.v1, f32[64,16,256]{2,1,0:T(8,128)} %get-tuple-element.44.v2, f32[128,128]{1,0:T(8,128)} %bitcast.20), custom_call_target="tpu_custom_call" | custom-call | tf_op jit(solution)/shard_map/final_update/pallas_call | solution.py:622
  (44 shorter events, 12.5 us)
Async XLA Ops:
  0.6 21.9 %copy-start.10 = (s32[1,16,1,256]{3,2,1,0:T(1,128)S(1)}, s32[1,16,1,256]{3,2,1,0:T(1,128)}, u32[]{:S(2)}) copy-start(s32[1,16,1,256]{3,2,1,0:T(1,128)} %param.18) | copy-start | bytes 49156
  0.6 22.5 %copy-start.13 = (f32[16,8]{0,1:T(8,128)S(1)}, f32[16,8]{0,1:T(8,128)}, u32[]{:S(2)}) copy-start(f32[16,8]{0,1:T(8,128)} %param.15) | copy-start | bytes 1540
  0.7 37.5 %copy-start.14 = (f32[16,8]{0,1:T(8,128)S(1)}, f32[16,8]{0,1:T(8,128)}, u32[]{:S(2)}) copy-start(f32[16,8]{0,1:T(8,128)} %param.16) | copy-start | bytes 1540
  3.9 6.9 %collective-permute-start = (f32[2,4,16,128]{3,2,1,0:T(8,128)}, f32[2,4,16,128]{3,2,1,0:T(8,128)S(1)}, u32[]{:S(2)}, u32[]{:S(2)}) collective-permute-start(f32[2,4,16,128]{3,2,1,0:T(8,128)} %get-tuple-element.24), channel_id=1, source_target_pairs={{0,1},{1,2},{2,3},{3,4},{4,5},{5,6},{6,7},{8,9},{9,10},{10,11},{11... | collective-permute-start | bytes 196616 | tf_op jit(solution)/shard_map/ppermute | solution.py:636
  8.8 5.8 %collective-permute-start.1 = (f32[2,4,16,128]{3,2,1,0:T(8,128)}, f32[2,4,16,128]{3,2,1,0:T(8,128)S(1)}, u32[]{:S(2)}, u32[]{:S(2)}) collective-permute-start(f32[2,4,16,128]{3,2,1,0:T(8,128)} %get-tuple-element.25), channel_id=1, source_target_pairs={{1,0},{2,1},{3,2},{4,3},{5,4},{6,5},{7,6},{9,8},{10,9},{11,10},{12... | collective-permute-start | bytes 196616 | tf_op jit(solution)/shard_map/ppermute | solution.py:636
  10.8 3.9 %copy-start.5 = (f32[2,4,16,128]{3,2,1,0:T(8,128)}, f32[2,4,16,128]{3,2,1,0:T(8,128)S(1)}, u32[]{:S(2)}) copy-start(f32[2,4,16,128]{3,2,1,0:T(8,128)S(1)} %collective-permute-done.from_left) | copy-start | bytes 196612
  18.0 50.9 %collective-permute-start.2 = (f32[136,8,128]{2,1,0:T(8,128)}, f32[136,8,128]{2,1,0:T(8,128)S(1)}, u32[]{:S(2)}, u32[]{:S(2)}) collective-permute-start(f32[136,8,128]{2,1,0:T(8,128)} %get-tuple-element.26), channel_id=1, source_target_pairs={{0,8},{8,16},{16,24},{24,32},{32,40},{40,48},{48,56},{56,64},{64,7... | collective-permute-start | bytes 1671176 | tf_op jit(solution)/shard_map/ppermute | solution.py:636
  21.2 47.6 %collective-permute-start.3 = (f32[136,8,128]{2,1,0:T(8,128)}, f32[136,8,128]{2,1,0:T(8,128)S(1)}, u32[]{:S(2)}, u32[]{:S(2)}) collective-permute-start(f32[136,8,128]{2,1,0:T(8,128)} %get-tuple-element.27), channel_id=1, source_target_pairs={{8,0},{16,8},{24,16},{32,24},{40,32},{48,40},{56,48},{64,56},{72,6... | collective-permute-start | bytes 1671176 | tf_op jit(solution)/shard_map/ppermute | solution.py:636
  29.1 14.2 %all-to-all-start = ((f32[16,8,256]{2,1,0:T(8,128)}), f32[16,8,256]{2,1,0:T(8,128)S(1)}, u32[]{:S(2)}, u32[]{:S(2)}) async-start(f32[16,8,256]{2,1,0:T(8,128)} %canopy_send.1), calls=%async_computation | async-start | bytes 262144 | tf_op jit(solution)/shard_map/all_to_all | solution.py:665
  43.3 0.6 copy-start
  49.3 6.2 %collective-permute-start.4 = (f32[16,128]{1,0:T(8,128)}, f32[16,128]{1,0:T(8,128)S(1)}, u32[]{:S(2)}, u32[]{:S(2)}) collective-permute-start(f32[16,128]{1,0:T(8,128)} %get-tuple-element.29.edge), channel_id=1, source_target_pairs={{0,1},{1,2},{2,3},{3,4},{4,5},{5,6},{6,7},{8,9},{9,10},{10,11},{11... | collective-permute-start | bytes 24584 | tf_op jit(solution)/shard_map/ppermute | solution.py:636
  53.6 5.2 %collective-permute-start.5 = (f32[16,128]{1,0:T(8,128)}, f32[16,128]{1,0:T(8,128)S(1)}, u32[]{:S(2)}, u32[]{:S(2)}) collective-permute-start(f32[16,128]{1,0:T(8,128)} %get-tuple-element.29.edge), channel_id=1, source_target_pairs={{1,0},{2,1},{3,2},{4,3},{5,4},{6,5},{7,6},{9,8},{10,9},{11,10},{12... | collective-permute-start | bytes 24584 | tf_op jit(solution)/shard_map/ppermute | solution.py:636
  55.5 3.2 %copy-start.11 = (f32[16,128]{1,0:T(8,128)}, f32[16,128]{1,0:T(8,128)S(1)}, u32[]{:S(2)}) copy-start(f32[16,128]{1,0:T(8,128)S(1)} %collective-permute-done.4.from_left) | copy-start | bytes 24580
  61.2 4.1 %collective-permute-start.6 = (f32[8,8,384]{2,1,0:T(8,128)}, f32[8,8,384]{2,1,0:T(8,128)S(1)}, u32[]{:S(2)}, u32[]{:S(2)}) collective-permute-start(f32[8,8,384]{2,1,0:T(8,128)} %get-tuple-element.31), channel_id=1, source_target_pairs={{0,8},{8,16},{16,24},{24,32},{32,40},{40,48},{48,56},{56,64},{64,7... | collective-permute-start | bytes 294920 | tf_op jit(solution)/shard_map/ppermute | solution.py:636
  63.3 5.6 %collective-permute-start.7 = (f32[8,8,384]{2,1,0:T(8,128)}, f32[8,8,384]{2,1,0:T(8,128)S(1)}, u32[]{:S(2)}, u32[]{:S(2)}) collective-permute-start(f32[8,8,384]{2,1,0:T(8,128)} %get-tuple-element.31), channel_id=1, source_target_pairs={{8,0},{16,8},{24,16},{32,24},{40,32},{48,40},{56,48},{64,56},{72,6... | collective-permute-start | bytes 294920 | tf_op jit(solution)/shard_map/ppermute | solution.py:636
  65.2 3.7 %copy-start.8 = (f32[8,8,384]{2,1,0:T(8,128)}, f32[8,8,384]{2,1,0:T(8,128)S(1)}, u32[]{:S(2)}) copy-start(f32[8,8,384]{2,1,0:T(8,128)S(1)} %collective-permute-done.6.source_prev) | copy-start | bytes 294916
  68.9 0.6 copy-start.9
  68.9 0.8 copy-start.1
  68.9 1.0 copy-start.2
  118.5 27.2 %collective-permute-start.8 = (f32[132,8,128]{2,1,0:T(8,128)}, f32[132,8,128]{2,1,0:T(8,128)S(1)}, u32[]{:S(2)}, u32[]{:S(2)}) collective-permute-start(f32[132,8,128]{2,1,0:T(8,128)} %get-tuple-element.38), channel_id=1, source_target_pairs={{0,8},{8,16},{16,24},{24,32},{32,40},{40,48},{48,56},{56,64},{64,7... | collective-permute-start | bytes 1622024 | tf_op jit(solution)/shard_map/ppermute | solution.py:636
  121.3 24.5 %collective-permute-start.9 = (f32[132,8,128]{2,1,0:T(8,128)}, f32[132,8,128]{2,1,0:T(8,128)S(1)}, u32[]{:S(2)}, u32[]{:S(2)}) collective-permute-start(f32[132,8,128]{2,1,0:T(8,128)} %get-tuple-element.39), channel_id=1, source_target_pairs={{8,0},{16,8},{24,16},{32,24},{40,32},{48,40},{56,48},{64,56},{72,6... | collective-permute-start | bytes 1622024 | tf_op jit(solution)/shard_map/ppermute | solution.py:636
  145.8 0.8 copy-start.3
  145.8 1.0 copy-start.4
  195.1 16.0 %all-to-all-start.2 = ((f32[128,1,128]{2,1,0:T(1,128)}), f32[128,1,128]{2,1,0:T(1,128)S(1)}, u32[]{:S(2)}, u32[]{:S(2)}) async-start(f32[128,1,128]{2,1,0:T(1,128)} %bitcast.24), calls=%async_computation.2 | async-start | bytes 131072 | tf_op jit(solution)/shard_map/all_to_all | solution.py:640
  (3 other events, 1.8 us)

commit v2 on v1

v2 whole, which is shorter than its diff:
```python
import jax
import jax.numpy as jnp
from jax import lax
from jax.experimental import pallas as pl
from jax.experimental.pallas import tpu as pltpu
from jax.sharding import PartitionSpec as P

FORC = 8
ROOT = 8
LEV = 64
ROWS = 16
COLS = 256
L = 8
HALO = 7
XR = ROWS + 2 * HALO
XC = 384
OUTSIDE = 1e37
STORE = 0.05
GRAV = 0.5
F32 = jnp.float32
BF16 = jnp.bfloat16


def vmem(n=1):
    return [pl.BlockSpec(memory_space=pltpu.VMEM)] * n


def params(mib):
    return pltpu.CompilerParams(vmem_limit_bytes=mib * 1024 * 1024)


def shaped(*shape):
    return jax.ShapeDtypeStruct(shape, F32)


def iota(shape, dim):
    return lax.broadcasted_iota(jnp.int32, shape, dim)


def right(v):
    return pltpu.roll(v, v.shape[1] - 1, 1)


def left(v):
    return pltpu.roll(v, 1, 1)


def deeper(v):
    return pltpu.roll(v, v.shape[0] - 1, 0)


def higher(v):
    return pltpu.roll(v, 1, 0)


def lanes(v, shift):
    return v if shift % 128 == 0 else pltpu.roll(v, shift % 128, v.ndim - 1)


def pieces(v):
    high = v.astype(BF16)
    rest = v - high.astype(F32)
    mid = rest.astype(BF16)
    low = (rest - mid.astype(F32)).astype(BF16)
    return high, mid, low


def canopy_send_kernel(
    forcing, cover, canopy_table, counts, cols, state, payload, split, gathered
):
    weights = [jnp.zeros((ROWS, COLS), F32) for _ in range(FORC)]
    kinds = cover[...]
    for kind in range(canopy_table.shape[0]):
        hit = kinds == kind
        for m in range(FORC):
            weights[m] = jnp.where(hit, canopy_table[kind, m], weights[m])
    total = weights[0] * forcing[0]
    for m in range(1, FORC):
        total = total + weights[m] * forcing[m]
    conductance = 2.0 * jax.nn.sigmoid(total)
    channels = [forcing[0], forcing[1], forcing[2], jnp.tanh(forcing[4]), conductance]
    used = len(channels)
    for c, channel in enumerate(channels):
        for p, piece in enumerate(pieces(channel)):
            split[pl.ds((p * used + c) * ROWS, ROWS), :] = piece

    def owner(o, carry):
        index = cols[pl.ds(o, 1), :]
        row_hit = iota((ROWS, COLS), 0) == (index // COLS)
        col_hit = iota((COLS, COLS), 0) == (index % COLS)
        onehot = jnp.where(col_hit, 1.0, 0.0).astype(BF16)
        picked = jnp.dot(split[...], onehot, preferred_element_type=F32)
        span = used * ROWS
        picked = picked[:span] + picked[span : 2 * span] + picked[2 * span :]
        sub = iota((8, COLS), 0)
        out = pltpu.roll(state[o, 0:8, :], 6, 0)
        for c in range(used):
            chosen = jnp.where(row_hit, picked[c * ROWS : (c + 1) * ROWS], 0.0)
            chosen = jnp.sum(chosen, axis=0, keepdims=True)
            out = jnp.where(sub == c, chosen, out)
        live = jnp.where(iota((8, COLS), 1) < counts[o], 1.0, 0.0)
        payload[o] = jnp.where(sub == used, live, out)
        return carry

    lax.fori_loop(0, cols.shape[0], owner, 0)


def canopy_send(forcing, cover, canopy_table, counts, cols, state):
    owners = cols.shape[0]
    return pl.pallas_call(
        canopy_send_kernel,
        out_shape=shaped(owners, 8, COLS),
        in_specs=vmem(2)
        + [pl.BlockSpec(memory_space=pltpu.SMEM)] * 2
        + vmem(2),
        out_specs=vmem()[0],
        scratch_shapes=[
            pltpu.VMEM((15 * ROWS, COLS), BF16),
            pltpu.VMEM((8, COLS), F32),
        ],
        compiler_params=params(8),
        name="canopy_send",
    )(forcing, cover, canopy_table, counts, cols, state)


def softplus(v):
    return jnp.maximum(v, 0.0) + jnp.log1p(jnp.exp(-jnp.abs(v)))


def leaf(start, f0, f1, f2, g):
    temp = start
    for _ in range(3):
        temp = 0.5 * (start + f0) + 0.5 * jnp.tanh(f1 - g * (temp - f2))
    return temp


def source_kernel(
    arrived, cols, counts, forcing, cover, vegetated, canopy_table, root_table, pressure,
    source, to_right, to_left, total, turned,
):
    total[...] = jnp.zeros_like(total)

    def owner(o, carry):
        index = cols[pl.ds(o, 1), :]
        row_hit = iota((ROWS, COLS), 0) == (index // COLS)
        col_hit = iota((COLS, COLS), 0) == (index % COLS)
        onehot = jnp.where(col_hit, 1.0, 0.0).astype(BF16)
        wanted = jnp.logical_and(row_hit, iota((ROWS, COLS), 1) < counts[o])
        block = arrived[o]
        parts = []
        for c in (6, 7):
            value = jnp.where(wanted, block[c : c + 1, :], 0.0)
            parts.extend(pieces(value))
        stacked = jnp.concatenate(parts, axis=0)
        placed = lax.dot_general(
            stacked, onehot, (((1,), (1,)), ((), ())), preferred_element_type=F32
        )
        total[...] += placed
        return carry

    lax.fori_loop(0, cols.shape[0], owner, 0)

    def piece(k):
        return total[k * ROWS : (k + 1) * ROWS, :]

    water = piece(0) + piece(1) + piece(2)
    start = piece(3) + piece(4) + piece(5)
    kinds = cover[...]
    weights = [jnp.zeros((ROWS, COLS), F32) for _ in range(FORC)]
    roots = [jnp.zeros((ROWS, COLS), F32) for _ in range(ROOT)]
    for kind in range(canopy_table.shape[0]):
        hit = kinds == kind
        for m in range(FORC):
            weights[m] = jnp.where(hit, canopy_table[kind, m], weights[m])
        for m in range(ROOT):
            roots[m] = jnp.where(hit, root_table[kind, m], roots[m])
    mixed = weights[0] * forcing[0]
    for m in range(1, FORC):
        mixed = mixed + weights[m] * forcing[m]
    conductance = 2.0 * jax.nn.sigmoid(mixed)
    temp = leaf(start, forcing[0], forcing[1], forcing[2], conductance)
    demand = conductance * softplus(temp - forcing[3]) / (1.0 + water * water)
    planted = vegetated[...] == 1
    demand = jnp.where(planted, demand, 0.0)
    dry = jnp.where(planted, 0.0, 0.5)
    for m in range(ROOT):
        moist = jax.nn.sigmoid(2.0 * (pressure[m] + 1.5))
        value = -(demand * roots[m] * moist)
        if m == 0:
            evaporation = dry * softplus(forcing[3] - forcing[2]) * moist
            value = value + (0.3 * softplus(forcing[4]) - evaporation)
        for t in range(2):
            turned[pl.ds(t * 128 + m * ROWS, ROWS), :] = value[:, t * 128 : t * 128 + 128]
    lane = iota((L, 128), 1)
    first = jnp.zeros((L, 128), F32)
    last = jnp.zeros((L, 128), F32)
    for x in range(ROWS):
        low = turned[pl.ds(x, L, stride=ROWS), :]
        high = turned[pl.ds(128 + x, L, stride=ROWS), :]
        source[x, :, :128] = low
        source[x, :, 128:] = high
        here = jnp.logical_and(lane >= 8 * x, lane < 8 * x + 8)
        first = jnp.where(here, lanes(low, 8 * x), first)
        last = jnp.where(here, lanes(high, 8 * x - 120), last)
    to_left[...] = first
    to_right[...] = last


def canopy_source(arrived, cols, counts, forcing, cover, vegetated, canopy_table, root_table, pressure):
    smem = pl.BlockSpec(memory_space=pltpu.SMEM)
    v = vmem()[0]
    return pl.pallas_call(
        source_kernel,
        out_shape=(shaped(ROWS, ROOT, COLS), shaped(L, 128), shaped(L, 128)),
        in_specs=[v, v, smem, v, v, v, smem, smem, v],
        out_specs=(v, v, v),
        scratch_shapes=[pltpu.VMEM((6 * ROWS, COLS), F32), pltpu.VMEM((2 * 128, 128), F32)],
        compiler_params=params(8),
        name="canopy_source",
    )(arrived, cols, counts, forcing, cover, vegetated, canopy_table, root_table, pressure)


def owner_kernel(arrived, state, updated):
    def slot(i, carry):
        block = arrived[i]
        old = state[i]
        temp = leaf(old[1:2], block[0:1], block[1:2], block[2:3], block[4:5])
        sub = iota(old.shape, 0)
        base = jnp.where(sub == 1, temp, old)
        upper = pltpu.roll(base, 1, 0)
        lower = pltpu.roll(base, base.shape[0] - 1, 0)
        lower = jnp.where(sub == base.shape[0] - 1, base, lower)
        fresh = 0.6 * base + 0.2 * upper + 0.2 * lower
        fresh = jnp.where(sub == 1, temp, fresh)
        fresh = jnp.where(sub == 0, 0.8 * old + 0.2 * block[3:4], fresh)
        updated[i] = jnp.where(block[5:6] > 0.5, fresh, old)
        return carry

    lax.fori_loop(0, arrived.shape[0], slot, 0)


def owner_update(arrived, state):
    return pl.pallas_call(
        owner_kernel,
        out_shape=shaped(*state.shape),
        in_specs=vmem(2),
        out_specs=vmem()[0],
        compiler_params=params(8),
        name="owner_update",
    )(arrived, state)


def flat(v):
    return v.reshape(LEV, 2, 8, 2, 128).transpose(0, 1, 3, 2, 4).reshape(32 * LEV, 128)


def unflat(v):
    return v.reshape(LEV, 2, 2, 8, 128).transpose(0, 1, 3, 2, 4).reshape(LEV, ROWS, COLS)


def chunk(x, l, t):
    return pl.ds(32 * l + 16 * (x // 8) + 8 * t + x % 8, 8, stride=32 * L)


def turn_kernel(pressure, conductivity, q, k, to_right, to_left):
    lane = iota((8, 128), 1)

    def layer(l, carry):
        for f, (field, target) in enumerate(((pressure, q), (conductivity, k))):
            first = jnp.zeros((8, 128), F32)
            last = jnp.zeros((8, 128), F32)
            for x in range(ROWS):
                low = field[chunk(x, l, 0), :]
                high = field[chunk(x, l, 1), :]
                target[x, l, :, :128] = low
                target[x, l, :, 128:] = high
                here = jnp.logical_and(lane >= 8 * x, lane < 8 * x + 8)
                first = jnp.where(here, lanes(low, 8 * x), first)
                last = jnp.where(here, lanes(high, 8 * x - 120), last)
            to_left[f, l] = first
            to_right[f, l] = last
        return carry

    lax.fori_loop(0, L, layer, 0)


def turn(pressure, conductivity):
    own_shape = shaped(ROWS, L, 8, COLS)
    return pl.pallas_call(
        turn_kernel,
        out_shape=(own_shape, own_shape, shaped(2, L, 8, 128), shaped(2, L, 8, 128)),
        in_specs=vmem(2),
        out_specs=tuple(vmem(4)),
        compiler_params=params(16),
        name="turn",
    )(pressure, conductivity)


RIM = 2 * HALO * 2 + 2


def rim_kernel(q, k, from_left, from_right, to_next, to_prev):
    low = iota((8, 128), 1) < 64

    def layer(l, carry):
        for f, field in enumerate((q, k)):
            for i in range(HALO):
                for t in range(2):
                    part = pl.ds(128 * t, 128)
                    to_next[2 * (f * HALO + i) + t, l] = field[ROWS - HALO + i, l, :, part]
                    to_prev[2 * (f * HALO + i) + t, l] = field[i, l, :, part]
            a, b = from_left[f, l], from_right[f, l]
            to_next[4 * HALO + f, l] = jnp.where(low, lanes(a, 64), b)
            to_prev[4 * HALO + f, l] = jnp.where(low, a, lanes(b, 64))
        return carry

    lax.fori_loop(0, L, layer, 0)


def rim(*arrays):
    outs = (shaped(RIM, L, 8, 128), shaped(RIM, L, 8, 128))
    return pl.pallas_call(
        rim_kernel,
        out_shape=outs,
        in_specs=vmem(4),
        out_specs=tuple(vmem(2)),
        compiler_params=params(16),
        name="rim",
    )(*arrays)


BHALO = 6
SRIM = 2 * BHALO + 1


def source_rim_kernel(source, from_left, from_right, to_next, to_prev):
    low = iota((L, 128), 1) < 64
    for i in range(BHALO):
        for t in range(2):
            part = pl.ds(128 * t, 128)
            to_next[2 * i + t] = source[ROWS - BHALO + i, :, part]
            to_prev[2 * i + t] = source[i, :, part]
    a, b = from_left[...], from_right[...]
    to_next[2 * BHALO] = jnp.where(low, lanes(a, 64), b)
    to_prev[2 * BHALO] = jnp.where(low, a, lanes(b, 64))


def source_rim(*arrays):
    outs = (shaped(SRIM, L, 128), shaped(SRIM, L, 128))
    return pl.pallas_call(
        source_rim_kernel,
        out_shape=outs,
        in_specs=vmem(3),
        out_specs=tuple(vmem(2)),
        compiler_params=params(8),
        name="source_rim",
    )(*arrays)


def halo_tile(from_left, from_right, lane, at_left, at_right):
    tile = jnp.where(lane < 8, lanes(from_right, -at_right), 0.0)
    return jnp.where(lane >= 120, lanes(from_left, 120 - at_left), tile)


def own(v):
    return v[:, :COLS]


def mobilities(q, k, resist, diag, rows, block):
    def step(i, carry):
        for j in range(block):
            r = rows[0] + i * block + j
            for l in range(L):
                s = 0.5 + 0.5 * jnp.tanh(q[r, l])
                m = k[r, l] * (0.1 + 0.9 * s)
                resist[r, l] = jnp.where(m > 0.0, 0.5 / m, OUTSIDE)
                diag[r, l] = 1.4 * s * (1.0 - s) + STORE
        return carry

    lax.fori_loop(0, (rows[1] - rows[0]) // block, step, 0)


def couplings(q, resist, right_hand, cx, cy, cyl, cz, diag, v0, rows, block):
    last = iota((8, XC), 0) == 7

    def row(r):
        q_0, m_0, q_7, m_7 = q[r, 0], resist[r, 0], q[r, 7], resist[r, 7]
        c_7 = jnp.where(last, 0.0, 1.0 / (m_7 + deeper(m_0)))
        f_7 = c_7 * (q_7 - deeper(q_0) + GRAV)
        cz[r, 7] = c_7
        c_up, f_up = higher(c_7), higher(f_7)
        v, m = q_0, m_0
        for l in range(L):
            if l < L - 1:
                m_n, v_n = resist[r, l + 1], q[r, l + 1]
                c = 1.0 / (m + m_n)
                f = c * (v - v_n + GRAV)
                cz[r, l] = c
            else:
                c, f = c_7, f_7
            y = 1.0 / (m + right(m))
            yl = 1.0 / (m + left(m))
            x = 1.0 / (m + resist[r + 1, l])
            xp = cx[r - 1, l]
            cy[r, l] = y
            cyl[r, l] = yl
            cx[r, l] = x
            out = y * (v - right(v)) + yl * (v - left(v))
            out = out + (x * (v - q[r + 1, l]) + xp * (v - q[r - 1, l])) + (f - f_up)
            diag[r, l] = diag[r, l] + ((y + yl) + (x + xp) + (c + c_up))
            v0[r, l] = right_hand(r, l, v) - out
            c_up, f_up = c, f
            if l < L - 1:
                v, m = v_n, m_n

    def step(i, carry):
        for j in range(block):
            row(rows[0] + i * block + j)
        return carry

    for l in range(L):
        cx[rows[0] - 1, l] = 1.0 / (resist[rows[0] - 1, l] + resist[rows[0], l])
    lax.fori_loop(0, (rows[1] - rows[0]) // block, step, 0)


def apply(v_in, v_out, cx, cy, cyl, cz, diag, rows, block, first):
    zero = jnp.zeros((8, COLS), F32)

    def row(r, held):
        c_up, v_up = higher(cz[r, 7]), higher(v_in[r, 7])
        v_0 = v_in[r, 0]
        v = v_0
        here = jnp.logical_and(r >= HALO, r < HALO + ROWS)
        square, cross = zero, zero
        for l in range(L):
            v_n = v_in[r, l + 1] if l < L - 1 else deeper(v_0)
            c = cz[r, l]
            image = diag[r, l] * v - cy[r, l] * right(v) - cyl[r, l] * left(v)
            image = image - cx[r, l] * v_in[r + 1, l] - cx[r - 1, l] * v_in[r - 1, l]
            image = image - c * v_n - c_up * v_up
            if v_out is not None:
                v_out[r, l] = image
            a, b = own(v), own(image)
            square = square + a * a
            cross = cross + a * b
            v_up, c_up, v = v, c, v_n
        if not first:
            square = jnp.where(here, square, 0.0)
            cross = jnp.where(here, cross, 0.0)
        return held[0] + square, held[1] + cross

    def step(i, held):
        for j in range(block):
            held = row(rows[0] + i * block + j, held)
        return held

    return lax.fori_loop(0, (rows[1] - rows[0]) // block, step, (zero, zero))


def chain(cx, cy, cyl, cz, diag, v0, v1, v2, moments, spans, blocks):
    coefs = (cx, cy, cyl, cz, diag)
    sums = []
    sums += apply(v0, v1, *coefs, spans[0], blocks[0], False)
    sums += apply(v1, v2, *coefs, spans[1], blocks[1], False)
    sums += apply(v2, None, *coefs, spans[2], blocks[2], True)
    row = jnp.zeros((1, 128), F32)
    lane = iota((1, 128), 1)
    for k, held in enumerate(sums):
        value = jnp.sum(jnp.sum(held, axis=0, keepdims=True), axis=1, keepdims=True)
        row = jnp.where(lane == k, value, row)
    moments[...] = jnp.broadcast_to(row, moments.shape)


def coefficients(gathered):
    row = jnp.sum(gathered[...], axis=0, keepdims=True)
    lane = iota((1, 128), 1)
    m = [jnp.sum(jnp.where(lane == k, row, 0.0), axis=1, keepdims=True) for k in range(6)]

    def dot(a, b, shift):
        total = jnp.zeros((1, 1), F32)
        for i, p in enumerate(a):
            for j, q in enumerate(b):
                total = total + p * q * m[i + j + shift]
        return total

    one = jnp.ones((1, 1), F32)
    a0 = m[0] / m[1]
    r1 = [one, -a0]
    n1 = dot(r1, r1, 0)
    b0 = n1 / m[0]
    p1 = [one + b0, -a0]
    a1 = n1 / dot(p1, p1, 1)
    r2 = [one, -a0 - a1 * p1[0], -a1 * p1[1]]
    n2 = dot(r2, r2, 0)
    b1 = n2 / n1
    p2 = [r2[0] + b1 * p1[0], r2[1] + b1 * p1[1], r2[2]]
    a2 = n2 / dot(p2, p2, 1)
    return (
        a0 + a1 * p1[0] + a2 * p2[0],
        a1 * p1[1] + a2 * p2[1],
        a2 * p2[2],
    )


def source_at(b, r, l, sub):
    return jnp.where(sub == 0, pltpu.roll(b[r], (8 - l) % 8, 0), 0.0)


def first_kernel(
    q_own, k_own, from_left, from_right, from_prev, from_next,
    source, source_left, source_right, source_prev, source_next,
    q, k, b, v0, v1, v2, moments,
    resist, cx, cy, cyl, cz, diag,
):
    lane = iota((8, 128), 1)

    def fill(l, carry):
        for f, (field, target) in enumerate(((q_own, q), (k_own, k))):
            for x in range(ROWS):
                target[HALO + x, l, :, :COLS] = field[x, l]
                target[HALO + x, l, :, COLS:] = halo_tile(
                    from_left[f, l], from_right[f, l], lane, 8 * x, 8 * x
                )
            for i in range(HALO):
                for side, r, at in (
                    (from_prev, i, 8 * (8 - HALO + i)),
                    (from_next, HALO + ROWS + i, 8 * i),
                ):
                    for t in range(2):
                        target[r, l, :, 128 * t : 128 * t + 128] = side[2 * (f * HALO + i) + t, l]
                    corner = side[4 * HALO + f, l]
                    target[r, l, :, COLS:] = halo_tile(corner, corner, lane, at, 64 + at)
        return carry

    lax.fori_loop(0, L, fill, 0)

    for x in range(ROWS):
        b[HALO + x, :, :COLS] = source[x]
        b[HALO + x, :, COLS:] = halo_tile(source_left[...], source_right[...], lane, 8 * x, 8 * x)
    gap = HALO - BHALO
    for i in range(BHALO):
        for side, r, at in (
            (source_prev, gap + i, 8 * (8 - BHALO + i)),
            (source_next, HALO + ROWS + i, 8 * i),
        ):
            for t in range(2):
                b[r, :, 128 * t : 128 * t + 128] = side[2 * i + t]
            corner = side[2 * BHALO]
            b[r, :, COLS:] = halo_tile(corner, corner, lane, at, 64 + at)

    sub = iota((8, XC), 0)

    def right_hand(r, l, v):
        return source_at(b, r, l, sub)

    mobilities(q, k, resist, diag, (0, XR), 2)
    couplings(q, resist, right_hand, cx, cy, cyl, cz, diag, v0, (1, XR - 1), 4)
    chain(
        cx, cy, cyl, cz, diag, v0, v1, v2, moments,
        ((2, XR - 2), (3, XR - 3), (HALO, HALO + ROWS)), (13, 8, 8),
    )


def wide():
    return shaped(XR, L, 8, XC)


def scratch(n):
    return [pltpu.VMEM((XR, L, 8, XC), F32)] * n


def first_newton(*arrays):
    w = wide()
    outs = (w, w, shaped(XR, L, XC), w, w, w, shaped(128, 128))
    return pl.pallas_call(
        first_kernel,
        out_shape=outs,
        in_specs=vmem(len(arrays)),
        out_specs=tuple(vmem(len(outs))),
        scratch_shapes=scratch(6),
        compiler_params=params(44),
        name="first_newton",
    )(*arrays)


def second_kernel(
    q, k, b, u0, u1, u2, gathered,
    q_own, w0, w1, w2, moments,
    q1, resist, cx, cy, cyl, cz, diag, v0, v1, v2,
):
    c0, c1, c2 = coefficients(gathered)

    def update(r, carry):
        for l in range(L):
            q1[r, l] = q[r, l] + c0 * u0[r, l] + c1 * u1[r, l] + c2 * u2[r, l]
        return carry

    lax.fori_loop(3, XR - 3, update, 0, unroll=2)
    sub = iota((8, XC), 0)

    def right_hand(r, l, v):
        before = q[r, l]
        stored = 0.35 * (jnp.tanh(v) - jnp.tanh(before)) + STORE * (v - before)
        return source_at(b, r, l, sub) - stored

    mobilities(q1, k, resist, diag, (3, XR - 3), 2)
    couplings(q1, resist, right_hand, cx, cy, cyl, cz, diag, v0, (4, XR - 4), 2)
    chain(
        cx, cy, cyl, cz, diag, v0, v1, v2, moments,
        ((5, XR - 5), (6, XR - 6), (HALO, HALO + ROWS)), (10, 9, 8),
    )

    def keep(x, carry):
        for l in range(L):
            for source, target in ((q1, q_own), (v0, w0), (v1, w1), (v2, w2)):
                target[x, l] = source[HALO + x, l, :, :COLS]
        return carry

    lax.fori_loop(0, ROWS, keep, 0)


def second_newton(*arrays):
    o = shaped(ROWS, L, 8, COLS)
    outs = (o, o, o, o, shaped(128, 128))
    return pl.pallas_call(
        second_kernel,
        out_shape=outs,
        in_specs=vmem(len(arrays)),
        out_specs=tuple(vmem(len(outs))),
        scratch_shapes=scratch(10),
        compiler_params=params(54),
        name="second_newton",
    )(*arrays)


def final_kernel(q, v0, v1, v2, gathered, out):
    c0, c1, c2 = coefficients(gathered)

    def row(x, carry):
        for l in range(L):
            value = q[x, l] + c0 * v0[x, l] + c1 * v1[x, l] + c2 * v2[x, l]
            out[chunk(x, l, 0), :] = value[:, :128]
            out[chunk(x, l, 1), :] = value[:, 128:]
        return carry

    lax.fori_loop(0, ROWS, row, 0)


def final_update(*arrays):
    return pl.pallas_call(
        final_kernel,
        out_shape=shaped(32 * LEV, 128),
        in_specs=vmem(len(arrays)),
        out_specs=vmem()[0],
        compiler_params=params(16),
        name="final_update",
    )(*arrays)


def exchange(to_high, to_low, axis):
    count = lax.axis_size(axis)
    up = [(i, i + 1) for i in range(count - 1)]
    down = [(i + 1, i) for i in range(count - 1)]
    return lax.ppermute(to_high, axis, up), lax.ppermute(to_low, axis, down)


def share(moments):
    return lax.all_to_all(moments, ("gx", "gy"), split_axis=0, concat_axis=0, tiled=True)


def body(
    pressure_old,
    conductivity,
    forcing,
    vegetated,
    cover_type,
    canopy_table,
    root_table,
    pair_counts,
    send_cols,
    canopy_state,
):
    owners = send_cols.shape[1]
    cols = send_cols.reshape(owners, COLS)
    counts = pair_counts.reshape(owners)
    state = canopy_state.reshape(owners, 16, COLS)

    q_own, k_own, to_right, to_left = turn(flat(pressure_old), flat(conductivity))
    from_left, from_right = exchange(to_right, to_left, "gy")
    payload = canopy_send(forcing, cover_type, canopy_table, counts, cols, state)
    to_next, to_prev = rim(q_own, k_own, from_left, from_right)
    from_prev, from_next = exchange(to_next, to_prev, "gx")
    arrived = lax.all_to_all(payload, "gx", split_axis=0, concat_axis=0, tiled=True)

    source, to_right, to_left = canopy_source(
        arrived, cols, counts, forcing, cover_type, vegetated, canopy_table, root_table, pressure_old[:ROOT]
    )
    source_left, source_right = exchange(to_right, to_left, "gy")
    to_next, to_prev = source_rim(source, source_left, source_right)
    source_prev, source_next = exchange(to_next, to_prev, "gx")
    new_state = owner_update(arrived, state).reshape(canopy_state.shape)

    q, k, b, v0, v1, v2, moments = first_newton(
        q_own, k_own, from_left, from_right, from_prev, from_next,
        source, source_left, source_right, source_prev, source_next,
    )
    q1, w0, w1, w2, moments = second_newton(q, k, b, v0, v1, v2, share(moments))
    pressure = unflat(final_update(q1, w0, w1, w2, share(moments)))
    return pressure, new_state


def solution(mesh):
    placed = (
        P(None, "gx", "gy"),
        P(None, "gx", "gy"),
        P(None, "gx", "gy"),
        P("gx", "gy"),
        P("gx", "gy"),
        P(),
        P(),
        P("gx", None, "gy"),
        P("gx", None, "gy", None),
        P("gx", None, "gy", None, None),
    )
    return jax.shard_map(
        body,
        mesh=mesh,
        in_specs=placed,
        out_specs=(P(None, "gx", "gy"), P("gx", None, "gy", None, None)),
        check_vma=False,
    )
```

time: 216 us -> 155 us (0.72)
  Pallas kernels: 121 us -> 50.1 us
  local copies, waits for them, and re-layouts: 7.99 us -> 22.8 us
  starting transfers between devices: 39.2 us -> 34.8 us
  blocking collectives: 23.2 us -> 20 us
  waiting for transfers between devices: 22.6 us -> 25.3 us
    pallas_call x1, Pallas kernels: 48.6 us -> 16.8 us  [first_newton(): pl.pallas_call(first_kernel, out_shape=outs, in_specs=vmem(len(arrays)),...]
    pallas_call x1, Pallas kernels: 48.3 us -> 17.1 us  [second_newton(): pl.pallas_call(second_kernel, out_shape=outs, in_specs=vmem(len(arrays)),...]
    unnamed x33 -> x51, local copies, waits for them, and re-layouts: 6.43 us -> 21.2 us
    pallas_call x5, Pallas kernels: 16.7 us -> 10.4 us  [the longest x1 4.53 us: canopy_source(): pl.pallas_call(source_kernel, out_shape=(shaped(ROWS, ROOT, COLS), shaped...]
    all_to_all x1, blocking collectives: 23.2 us -> 20 us  [share(): lax.all_to_all(moments, ('gx', 'gy'), split_axis=0, concat_axis=0, tiled=...]
    ppermute x10 -> x8, starting transfers between devices: 25 us -> 22.1 us  [exchange(): return (lax.ppermute(to_high, axis, up), lax.ppermute(to_low, axis, down))]
    all_to_all x1, waiting for transfers between devices: 4.46 us -> 7.25 us  [body(): lax.all_to_all(payload, 'gx', split_axis=0, concat_axis=0, tiled=True)]
    ppermute x10 -> x8, waiting for transfers between devices: 11.4 us -> 10.2 us  [exchange(): return (lax.ppermute(to_high, axis, up), lax.ppermute(to_low, axis, down))]
  transfers between devices with their start and end apart: 12 -> 10, of which waited for: 6 -> 5; matrix products, arithmetic and copies ran while one was open for 2% -> 3% of each run, Pallas kernels for 7% -> 7%
where the time goes in v2:
time: 155 us; the launch traced here: 154 us
  Pallas kernels  50.1 us (32%)
  starting transfers between devices  34.8 us (22%)
  waiting for transfers between devices  25.3 us (16%)
  local copies, waits for them, and re-layouts  22.8 us (15%)
  blocking collectives  20 us (13%)
    ppermute x8, starting transfers between devices, exchange(): return (lax.ppermute(to_high, axis, up), lax.ppermute(to_low, axis, down))  22.1 us
    unnamed x51, local copies, waits for them, and re-layouts  21.2 us
    all_to_all x1, blocking collectives, share(): lax.all_to_all(moments, ('gx', 'gy'), split_axis=0, concat_axis=0, tiled=...  20 us
    pallas_call x1, Pallas kernels, second_newton(): pl.pallas_call(second_kernel, out_shape=outs, in_specs=vmem(len(arrays)),...  17.1 us
    pallas_call x1, Pallas kernels, first_newton(): pl.pallas_call(first_kernel, out_shape=outs, in_specs=vmem(len(arrays)),...  16.8 us
    ppermute x8, waiting for transfers between devices, exchange(): return (lax.ppermute(to_high, axis, up), lax.ppermute(to_low, axis, down))  10.2 us
    all_to_all x1, starting transfers between devices, body(): lax.all_to_all(payload, 'gx', split_axis=0, concat_axis=0, tiled=True)  8.03 us
    all_to_all x1, waiting for transfers between devices, share(): lax.all_to_all(moments, ('gx', 'gy'), split_axis=0, concat_axis=0, tiled=...  7.83 us
  transfers between devices with their start and end apart: 10, of which 5 were waited for; matrix products, arithmetic and copies ran while one was open for 3% of the time, Pallas kernels for 7%

profile of v2, /device:TPU:1, one launch (start us, length us, event | category | flops | bytes accessed | tf_op | source)
XLA Modules:
  0.0 153.8 jit_solution(3031256840875076900)
XLA Ops:
  3.1 1.7 %turn.1 = (f32[16,8,8,256]{3,2,1,0:T(8,128)S(1)}, f32[16,8,8,256]{3,2,1,0:T(8,128)S(1)}, f32[2,8,8,128]{3,2,1,0:T(8,128)S(1)}, f32[2,8,8,128]{3,2,1,0:T(8,128)S(1)}) custom-call(f32[2048,128]{1,0:T(8,128)S(1)} %bitcast.31, f32[2048,128]{1,0:T(8,128)S(1)} %bitcast.34), custom_call_target="tpu_custom_call" | custom-call | tf_op jit(solution)/shard_map/turn/pallas_call | solution.py:289
  4.8 4.9 %collective-permute-start = (f32[2,8,8,128]{3,2,1,0:T(8,128)S(1)}, f32[2,8,8,128]{3,2,1,0:T(8,128)S(1)}, u32[]{:S(2)}, u32[]{:S(2)}) collective-permute-start(f32[2,8,8,128]{3,2,1,0:T(8,128)S(1)} %get-tuple-element.27), channel_id=1, source_target_pairs={{0,1},{1,2},{2,3},{3,4},{4,5},{5,6},{6,7},{8,9},{9,10},{10,11},{11... | collective-permute-start | bytes 196616 | tf_op jit(solution)/shard_map/ppermute | solution.py:664
  9.8 1.9 %collective-permute-start.1 = (f32[2,8,8,128]{3,2,1,0:T(8,128)S(1)}, f32[2,8,8,128]{3,2,1,0:T(8,128)S(1)}, u32[]{:S(2)}, u32[]{:S(2)}) collective-permute-start(f32[2,8,8,128]{3,2,1,0:T(8,128)S(1)} %get-tuple-element.28), channel_id=1, source_target_pairs={{1,0},{2,1},{3,2},{4,3},{5,4},{6,5},{7,6},{9,8},{10,9},{11,10},{12... | collective-permute-start | bytes 196616 | tf_op jit(solution)/shard_map/ppermute | solution.py:664
  11.7 3.6 %collective-permute-done.1.from_right = f32[2,8,8,128]{3,2,1,0:T(8,128)S(1)} collective-permute-done((f32[2,8,8,128]{3,2,1,0:T(8,128)S(1)}, f32[2,8,8,128]{3,2,1,0:T(8,128)S(1)}, u32[]{:S(2)}, u32[]{:S(2)}) %collective-permute-start.1) | collective-permute-done | bytes 65568 | tf_op jit(solution)/shard_map/ppermute | solution.py:664
  15.4 2.1 %rim.1 = (f32[30,8,8,128]{3,2,1,0:T(8,128)}, f32[30,8,8,128]{3,2,1,0:T(8,128)}) custom-call(f32[16,8,8,256]{3,2,1,0:T(8,128)S(1)} %get-tuple-element.25.q.q_own, f32[16,8,8,256]{3,2,1,0:T(8,128)S(1)} %get-tuple-element.26.k.k_own, f32[2,8,8,128]{3,2,1,0:T(8,128)S(1)} %collective-permute-done.from_left, f32[2,8,8,128]{3,2,1,0:T(8,128)S(1)} %collective-permute-done.1.from_right), custom_call_target="tpu_custom_call" | custom-call | tf_op jit(solution)/shard_map/rim/pallas_call | solution.py:322
  17.5 3.3 %collective-permute-start.2 = (f32[30,8,8,128]{3,2,1,0:T(8,128)}, f32[30,8,8,128]{3,2,1,0:T(8,128)S(1)}, u32[]{:S(2)}, u32[]{:S(2)}) collective-permute-start(f32[30,8,8,128]{3,2,1,0:T(8,128)} %get-tuple-element.29), channel_id=1, source_target_pairs={{0,8},{8,16},{16,24},{24,32},{32,40},{40,48},{48,56},{56,64},{64,7... | collective-permute-start | bytes 2949128 | tf_op jit(solution)/shard_map/ppermute | solution.py:664
  25.5 4.2 %canopy_send.1 = f32[16,8,256]{2,1,0:T(8,128)S(1)} custom-call(f32[8,16,256]{2,1,0:T(8,128)S(1)} %copy-done.9, s32[16,256]{1,0:T(8,128)S(1)} %copy-done.17, f32[16,8]{1,0:T(8,128)S(1)} %copy-done.15, s32[16]{0:T(128)S(1)} %bitcast.39, s32[16,256]{1,0:T(8,128)S(1)} %bitcast.36, f32[16,16,256]{2,1,0:T(8,128)S(1)} %bitcast.32), custom_call_target="tpu_custom_call" | custom-call | tf_op jit(solution)/shard_map/canopy_send/pallas_call | solution.py:110
  30.3 8.0 %all-to-all-start = ((f32[16,8,256]{2,1,0:T(8,128)}), f32[16,8,256]{2,1,0:T(8,128)S(1)}, u32[]{:S(2)}, u32[]{:S(2)}) async-start(f32[16,8,256]{2,1,0:T(8,128)} %copy-done.8), calls=%async_computation | async-start | bytes 262144 | tf_op jit(solution)/shard_map/all_to_all | solution.py:693
  38.4 1.6 %slice.3.pressure = f32[8,16,256]{2,1,0:T(8,128)} slice(f32[64,16,256]{2,1,0:T(8,128)} %param.10), slice={[0:8], [0:16], [0:256]} | slice | bytes 262144 | tf_op jit(solution)/shard_map/slice | solution.py:696
  41.3 7.3 %all-to-all-done.arrived = f32[16,8,256]{2,1,0:T(8,128)S(1)} async-done(((f32[16,8,256]{2,1,0:T(8,128)}), f32[16,8,256]{2,1,0:T(8,128)S(1)}, u32[]{:S(2)}, u32[]{:S(2)}) %all-to-all-start) | async-done | bytes 131104 | tf_op jit(solution)/shard_map/all_to_all | solution.py:693
  53.8 4.5 %canopy_source.1 = (f32[16,8,256]{2,1,0:T(8,128)S(1)}, f32[8,128]{1,0:T(8,128)S(1)}, f32[8,128]{1,0:T(8,128)S(1)}) custom-call(f32[16,8,256]{2,1,0:T(8,128)S(1)} %all-to-all-done.arrived, s32[16,256]{1,0:T(8,128)S(1)} %bitcast.37, s32[16]{0:T(128)S(1)} %bitcast.40, f32[8,16,256]{2,1,0:T(8,128)S(1)} %copy-done.10, s32[16,256]{1,0:T(8,128)S(1)} %copy-done.18, ...), custom_call_target="tpu_custom_call" | custom-call | tf_op jit(solution)/shard_map/canopy_source/pallas_call | solution.py:212
  58.4 3.7 %collective-permute-start.4 = (f32[8,128]{1,0:T(8,128)S(1)}, f32[8,128]{1,0:T(8,128)S(1)}, u32[]{:S(2)}, u32[]{:S(2)}) collective-permute-start(f32[8,128]{1,0:T(8,128)S(1)} %get-tuple-element.32), channel_id=1, source_target_pairs={{0,1},{1,2},{2,3},{3,4},{4,5},{5,6},{6,7},{8,9},{9,10},{10,11},{11... | collective-permute-start | bytes 12296 | tf_op jit(solution)/shard_map/ppermute | solution.py:664
  62.1 1.9 %collective-permute-start.5 = (f32[8,128]{1,0:T(8,128)S(1)}, f32[8,128]{1,0:T(8,128)S(1)}, u32[]{:S(2)}, u32[]{:S(2)}) collective-permute-start(f32[8,128]{1,0:T(8,128)S(1)} %get-tuple-element.33), channel_id=1, source_target_pairs={{1,0},{2,1},{3,2},{4,3},{5,4},{6,5},{7,6},{9,8},{10,9},{11,10},{12... | collective-permute-start | bytes 12296 | tf_op jit(solution)/shard_map/ppermute | solution.py:664
  64.1 3.0 %collective-permute-done.5.from_right.source_right = f32[8,128]{1,0:T(8,128)S(1)} collective-permute-done((f32[8,128]{1,0:T(8,128)S(1)}, f32[8,128]{1,0:T(8,128)S(1)}, u32[]{:S(2)}, u32[]{:S(2)}) %collective-permute-start.5) | collective-permute-done | bytes 4128 | tf_op jit(solution)/shard_map/ppermute | solution.py:664
  67.1 3.8 %collective-permute-start.6 = (f32[13,8,128]{2,1,0:T(8,128)S(1)}, f32[13,8,128]{2,1,0:T(8,128)S(1)}, u32[]{:S(2)}, u32[]{:S(2)}) collective-permute-start(f32[13,8,128]{2,1,0:T(8,128)S(1)} %get-tuple-element.34), channel_id=1, source_target_pairs={{0,8},{8,16},{16,24},{24,32},{32,40},{40,48},{48,56},{56,64},{64,7... | collective-permute-start | bytes 159752 | tf_op jit(solution)/shard_map/ppermute | solution.py:664
  72.2 3.6 %collective-permute-done.7.source_next = f32[13,8,128]{2,1,0:T(8,128)S(1)} collective-permute-done((f32[13,8,128]{2,1,0:T(8,128)S(1)}, f32[13,8,128]{2,1,0:T(8,128)S(1)}, u32[]{:S(2)}, u32[]{:S(2)}) %collective-permute-start.7) | collective-permute-done | bytes 53280 | tf_op jit(solution)/shard_map/ppermute | solution.py:664
  76.6 16.8 %first_newton.1 = (f32[30,8,8,384]{3,2,1,0:T(8,128)S(1)}, f32[30,8,8,384]{3,2,1,0:T(8,128)}, f32[30,8,384]{2,1,0:T(8,128)S(1)}, f32[30,8,8,384]{3,2,1,0:T(8,128)...) custom-call(f32[16,8,8,256]{3,2,1,0:T(8,128)S(1)} %get-tuple-element.25.q.q_own, ...), custom_call_target="tpu_custom_call" | custom-call | tf_op jit(solution)/shard_map/first_newton/pallas_call | solution.py:575
  93.5 1.6 %copy-done = f32[30,8,8,384]{3,2,1,0:T(8,128)} copy-done((f32[30,8,8,384]{3,2,1,0:T(8,128)}, f32[30,8,8,384]{3,2,1,0:T(8,128)S(1)}, u32[]{:S(2)}) %copy-start) | copy-done | bytes 2949144
  95.8 20.0 %all_to_all.27 = f32[128,1,128]{2,1,0:T(1,128)} all-to-all(f32[128,1,128]{2,1,0:T(1,128)S(1)} %bitcast.38), channel_id=1, replica_groups=mesh['gx'=16,'gy'=8] {'gx','gy'}, dimensions={0} | all-to-all | bytes 131072 | tf_op jit(solution)/shard_map/all_to_all | solution.py:668
  115.8 17.1 %second_newton.1 = (f32[16,8,8,256]{3,2,1,0:T(8,128)}, f32[16,8,8,256]{3,2,1,0:T(8,128)}, f32[16,8,8,256]{3,2,1,0:T(8,128)}, f32[16,8,8,256]{3,2,1,0:T(8,128)}, f32[128,128]{1,0:T(8,128)}) custom-call(f32[30,8,8,384]{3,2,1,0:T(8,128)} %copy-done, f32[30,8,8,384]{3,2,1,0:T(8,128)} %get-tuple-element.37.k, f32[30,8,384]{2,1,0:T(8,128)} %copy-done.12, ...), custom_call_target="tpu_custom_call" | custom-call | tf_op jit(solution)/shard_map/second_newton/pallas_call | solution.py:625
  132.9 4.7 %all-to-all-start.2 = ((f32[128,1,128]{2,1,0:T(1,128)}), f32[128,1,128]{2,1,0:T(1,128)S(1)}, u32[]{:S(2)}, u32[]{:S(2)}) async-start(f32[128,1,128]{2,1,0:T(1,128)} %bitcast.44), calls=%async_computation.2 | async-start | bytes 131072 | tf_op jit(solution)/shard_map/all_to_all | solution.py:668
  137.6 1.5 owner_update.1
  139.1 7.8 %all-to-all-done.2 = f32[128,1,128]{2,1,0:T(1,128)S(1)} async-done(((f32[128,1,128]{2,1,0:T(1,128)}), f32[128,1,128]{2,1,0:T(1,128)S(1)}, u32[]{:S(2)}, u32[]{:S(2)}) %all-to-all-start.2) | async-done | bytes 65568 | tf_op jit(solution)/shard_map/all_to_all | solution.py:668
  151.9 2.0 %final_update.1 = f32[2048,128]{1,0:T(8,128)} custom-call(f32[16,8,8,256]{3,2,1,0:T(8,128)S(1)} %copy-done.4, f32[16,8,8,256]{3,2,1,0:T(8,128)S(1)} %copy-done.5, f32[16,8,8,256]{3,2,1,0:T(8,128)S(1)} %copy-done.6, f32[16,8,8,256]{3,2,1,0:T(8,128)S(1)} %copy-done.7, f32[128,128]{1,0:T(8,128)S(1)} %bitcast.35), custom_call_target="tpu_custom_call" | custom-call | tf_op jit(solution)/shard_map/final_update/pallas_call | solution.py:650
  (58 shorter events, 22.3 us)
Async XLA Ops:
  0.6 1.2 copy-start.1
  1.9 1.2 copy-start.3
  3.1 18.9 %copy-start.23 = (s32[1,16,1,256]{3,2,1,0:T(1,128)S(1)}, s32[1,16,1,256]{3,2,1,0:T(1,128)}, u32[]{:S(2)}) copy-start(s32[1,16,1,256]{3,2,1,0:T(1,128)} %param.18) | copy-start | bytes 49156
  3.1 20.3 %copy-start.2 = (f32[1,16,1,16,256]{4,3,2,1,0:T(8,128)S(1)}, f32[1,16,1,16,256]{4,3,2,1,0:T(8,128)}, u32[]{:S(2)}) copy-start(f32[1,16,1,16,256]{4,3,2,1,0:T(8,128)} %param.19) | copy-start | bytes 786436
  3.1 20.3 %copy-start.9 = (f32[8,16,256]{2,1,0:T(8,128)S(1)}, f32[8,16,256]{2,1,0:T(8,128)}, u32[]{:S(2)}) copy-start(f32[8,16,256]{2,1,0:T(8,128)} %forcing.3) | copy-start | bytes 393220
  4.8 6.9 %collective-permute-start = (f32[2,8,8,128]{3,2,1,0:T(8,128)S(1)}, f32[2,8,8,128]{3,2,1,0:T(8,128)S(1)}, u32[]{:S(2)}, u32[]{:S(2)}) collective-permute-start(f32[2,8,8,128]{3,2,1,0:T(8,128)S(1)} %get-tuple-element.27), channel_id=1, source_target_pairs={{0,1},{1,2},{2,3},{3,4},{4,5},{5,6},{6,7},{8,9},{9,10},{10,11},{11... | collective-permute-start | bytes 196616 | tf_op jit(solution)/shard_map/ppermute | solution.py:664
  9.8 5.6 %collective-permute-start.1 = (f32[2,8,8,128]{3,2,1,0:T(8,128)S(1)}, f32[2,8,8,128]{3,2,1,0:T(8,128)S(1)}, u32[]{:S(2)}, u32[]{:S(2)}) collective-permute-start(f32[2,8,8,128]{3,2,1,0:T(8,128)S(1)} %get-tuple-element.28), channel_id=1, source_target_pairs={{1,0},{2,1},{3,2},{4,3},{5,4},{6,5},{7,6},{9,8},{10,9},{11,10},{12... | collective-permute-start | bytes 196616 | tf_op jit(solution)/shard_map/ppermute | solution.py:664
  15.3 2.1 %copy-start.13 = (f32[2,8,8,128]{3,2,1,0:T(8,128)}, f32[2,8,8,128]{3,2,1,0:T(8,128)S(1)}, u32[]{:S(2)}) copy-start(f32[2,8,8,128]{3,2,1,0:T(8,128)S(1)} %collective-permute-done.1.from_right) | copy-start | bytes 196612
  17.5 58.3 %collective-permute-start.2 = (f32[30,8,8,128]{3,2,1,0:T(8,128)}, f32[30,8,8,128]{3,2,1,0:T(8,128)S(1)}, u32[]{:S(2)}, u32[]{:S(2)}) collective-permute-start(f32[30,8,8,128]{3,2,1,0:T(8,128)} %get-tuple-element.29), channel_id=1, source_target_pairs={{0,8},{8,16},{16,24},{24,32},{32,40},{40,48},{48,56},{56,64},{64,7... | collective-permute-start | bytes 2949128 | tf_op jit(solution)/shard_map/ppermute | solution.py:664
  20.7 55.1 %collective-permute-start.3 = (f32[30,8,8,128]{3,2,1,0:T(8,128)}, f32[30,8,8,128]{3,2,1,0:T(8,128)}, u32[]{:S(2)}, u32[]{:S(2)}) collective-permute-start(f32[30,8,8,128]{3,2,1,0:T(8,128)} %get-tuple-element.30), channel_id=1, source_target_pairs={{8,0},{16,8},{24,16},{32,24},{40,32},{48,40},{56,48},{64,56},{72,6... | collective-permute-start | bytes 2949128 | tf_op jit(solution)/shard_map/ppermute | solution.py:664
  30.3 18.2 %all-to-all-start = ((f32[16,8,256]{2,1,0:T(8,128)}), f32[16,8,256]{2,1,0:T(8,128)S(1)}, u32[]{:S(2)}, u32[]{:S(2)}) async-start(f32[16,8,256]{2,1,0:T(8,128)} %copy-done.8), calls=%async_computation | async-start | bytes 262144 | tf_op jit(solution)/shard_map/all_to_all | solution.py:693
  48.6 0.9 copy-start.10
  49.5 0.9 copy-start.11
  58.4 5.7 %collective-permute-start.4 = (f32[8,128]{1,0:T(8,128)S(1)}, f32[8,128]{1,0:T(8,128)S(1)}, u32[]{:S(2)}, u32[]{:S(2)}) collective-permute-start(f32[8,128]{1,0:T(8,128)S(1)} %get-tuple-element.32), channel_id=1, source_target_pairs={{0,1},{1,2},{2,3},{3,4},{4,5},{5,6},{6,7},{8,9},{9,10},{10,11},{11... | collective-permute-start | bytes 12296 | tf_op jit(solution)/shard_map/ppermute | solution.py:664
  62.1 4.9 %collective-permute-start.5 = (f32[8,128]{1,0:T(8,128)S(1)}, f32[8,128]{1,0:T(8,128)S(1)}, u32[]{:S(2)}, u32[]{:S(2)}) collective-permute-start(f32[8,128]{1,0:T(8,128)S(1)} %get-tuple-element.33), channel_id=1, source_target_pairs={{1,0},{2,1},{3,2},{4,3},{5,4},{6,5},{7,6},{9,8},{10,9},{11,10},{12... | collective-permute-start | bytes 12296 | tf_op jit(solution)/shard_map/ppermute | solution.py:664
  67.1 5.1 %collective-permute-start.6 = (f32[13,8,128]{2,1,0:T(8,128)S(1)}, f32[13,8,128]{2,1,0:T(8,128)S(1)}, u32[]{:S(2)}, u32[]{:S(2)}) collective-permute-start(f32[13,8,128]{2,1,0:T(8,128)S(1)} %get-tuple-element.34), channel_id=1, source_target_pairs={{0,8},{8,16},{16,24},{24,32},{32,40},{40,48},{48,56},{56,64},{64,7... | collective-permute-start | bytes 159752 | tf_op jit(solution)/shard_map/ppermute | solution.py:664
  70.9 4.9 %collective-permute-start.7 = (f32[13,8,128]{2,1,0:T(8,128)S(1)}, f32[13,8,128]{2,1,0:T(8,128)S(1)}, u32[]{:S(2)}, u32[]{:S(2)}) collective-permute-start(f32[13,8,128]{2,1,0:T(8,128)S(1)} %get-tuple-element.35), channel_id=1, source_target_pairs={{8,0},{16,8},{24,16},{32,24},{40,32},{48,40},{56,48},{64,56},{72,6... | collective-permute-start | bytes 159752 | tf_op jit(solution)/shard_map/ppermute | solution.py:664
  75.8 0.8 copy-start.14
  93.5 1.6 %copy-start = (f32[30,8,8,384]{3,2,1,0:T(8,128)}, f32[30,8,8,384]{3,2,1,0:T(8,128)S(1)}, u32[]{:S(2)}) copy-start(f32[30,8,8,384]{3,2,1,0:T(8,128)S(1)} %get-tuple-element.36.q) | copy-start | bytes 8847364
  132.9 14.0 %all-to-all-start.2 = ((f32[128,1,128]{2,1,0:T(1,128)}), f32[128,1,128]{2,1,0:T(1,128)S(1)}, u32[]{:S(2)}, u32[]{:S(2)}) async-start(f32[128,1,128]{2,1,0:T(1,128)} %bitcast.44), calls=%async_computation.2 | async-start | bytes 131072 | tf_op jit(solution)/shard_map/all_to_all | solution.py:668
  147.0 1.2 copy-start.4
  148.2 1.2 copy-start.5
  149.4 1.2 copy-start.6
  150.6 1.2 copy-start.7
  (10 other events, 6.9 us)

commit v3 on v2

--- a/solution.py
+++ b/solution.py
@@ -15,6 +15,8 @@
 XR = ROWS + 2 * HALO
 XC = 384
 OUTSIDE = 1e37
+BHALO = 6
+SRIM = 2 * BHALO
 STORE = 0.05
 GRAV = 0.5
 F32 = jnp.float32
@@ -65,30 +67,48 @@
     return high, mid, low
 
 
+def in_hbm(v):
+    return pltpu.with_memory_space_constraint(v, pltpu.HBM)
+
+
+def smem():
+    return pl.BlockSpec(memory_space=pltpu.SMEM)
+
+
+def looked_up(kinds, table):
+    found = [jnp.zeros(kinds.shape, F32) for _ in range(table.shape[0])]
+    for kind in range(table.shape[1]):
+        hit = kinds == kind
+        for m in range(table.shape[0]):
+            found[m] = jnp.where(hit, table[m, kind], found[m])
+    return found
+
+
+def hits(index):
+    row = lax.shift_right_logical(index, 8)
+    col = jnp.bitwise_and(index, COLS - 1)
+    row_hit = iota((ROWS, COLS), 0) == row
+    col_hit = iota((COLS, COLS), 0) == col
+    return row_hit, jnp.where(col_hit, 1.0, 0.0).astype(BF16)
+
+
 def canopy_send_kernel(
-    forcing, cover, canopy_table, counts, cols, state, payload, split, gathered
+    forcing, cover, canopy_table, counts, cols, state, payload, conductance, split
 ):
-    weights = [jnp.zeros((ROWS, COLS), F32) for _ in range(FORC)]
-    kinds = cover[...]
-    for kind in range(canopy_table.shape[0]):
-        hit = kinds == kind
-        for m in range(FORC):
-            weights[m] = jnp.where(hit, canopy_table[kind, m], weights[m])
+    weights = looked_up(cover[...], canopy_table)
     total = weights[0] * forcing[0]
     for m in range(1, FORC):
         total = total + weights[m] * forcing[m]
-    conductance = 2.0 * jax.nn.sigmoid(total)
-    channels = [forcing[0], forcing[1], forcing[2], jnp.tanh(forcing[4]), conductance]
+    g = 2.0 * jax.nn.sigmoid(total)
+    conductance[...] = g
+    channels = [forcing[0], forcing[1], forcing[2], jnp.tanh(forcing[4]), g]
     used = len(channels)
     for c, channel in enumerate(channels):
         for p, piece in enumerate(pieces(channel)):
             split[pl.ds((p * used + c) * ROWS, ROWS), :] = piece
 
     def owner(o, carry):
-        index = cols[pl.ds(o, 1), :]
-        row_hit = iota((ROWS, COLS), 0) == (index // COLS)
-        col_hit = iota((COLS, COLS), 0) == (index % COLS)
-        onehot = jnp.where(col_hit, 1.0, 0.0).astype(BF16)
+        row_hit, onehot = hits(cols[o])
         picked = jnp.dot(split[...], onehot, preferred_element_type=F32)
         span = used * ROWS
         picked = picked[:span] + picked[span : 2 * span] + picked[2 * span :]
@@ -102,23 +122,18 @@
         payload[o] = jnp.where(sub == used, live, out)
         return carry
 
-    lax.fori_loop(0, cols.shape[0], owner, 0)
+    lax.fori_loop(0, cols.shape[0], owner, 0, unroll=4)
 
 
 def canopy_send(forcing, cover, canopy_table, counts, cols, state):
     owners = cols.shape[0]
     return pl.pallas_call(
         canopy_send_kernel,
-        out_shape=shaped(owners, 8, COLS),
-        in_specs=vmem(2)
-        + [pl.BlockSpec(memory_space=pltpu.SMEM)] * 2
-        + vmem(2),
-        out_specs=vmem()[0],
-        scratch_shapes=[
-            pltpu.VMEM((15 * ROWS, COLS), BF16),
-            pltpu.VMEM((8, COLS), F32),
-        ],
-        compiler_params=params(8),
+        out_shape=(shaped(owners, 8, COLS), shaped(ROWS, COLS)),
+        in_specs=vmem(2) + [smem(), smem()] + vmem(2),
+        out_specs=tuple(vmem(2)),
+        scratch_shapes=[pltpu.VMEM((15 * ROWS, COLS), BF16)],
+        compiler_params=params(16),
         name="canopy_send",
     )(forcing, cover, canopy_table, counts, cols, state)
 
@@ -135,16 +150,13 @@
 
 
 def source_kernel(
-    arrived, cols, counts, forcing, cover, vegetated, canopy_table, root_table, pressure,
-    source, to_right, to_left, total, turned,
+    arrived, cols, counts, forcing, conductance, uptake, surface,
+    source, to_next, to_prev, total, turned,
 ):
     total[...] = jnp.zeros_like(total)
 
     def owner(o, carry):
-        index = cols[pl.ds(o, 1), :]
-        row_hit = iota((ROWS, COLS), 0) == (index // COLS)
-        col_hit = iota((COLS, COLS), 0) == (index % COLS)
-        onehot = jnp.where(col_hit, 1.0, 0.0).astype(BF16)
+        row_hit, onehot = hits(cols[o])
         wanted = jnp.logical_and(row_hit, iota((ROWS, COLS), 1) < counts[o])
         block = arrived[o]
         parts = []
@@ -152,72 +164,48 @@
             value = jnp.where(wanted, block[c : c + 1, :], 0.0)
             parts.extend(pieces(value))
         stacked = jnp.concatenate(parts, axis=0)
-        placed = lax.dot_general(
+        total[...] += lax.dot_general(
             stacked, onehot, (((1,), (1,)), ((), ())), preferred_element_type=F32
         )
-        total[...] += placed
-        return carry
-
-    lax.fori_loop(0, cols.shape[0], owner, 0)
+        return carry
+
+    lax.fori_loop(0, cols.shape[0], owner, 0, unroll=4)
 
     def piece(k):
         return total[k * ROWS : (k + 1) * ROWS, :]
 
     water = piece(0) + piece(1) + piece(2)
     start = piece(3) + piece(4) + piece(5)
-    kinds = cover[...]
-    weights = [jnp.zeros((ROWS, COLS), F32) for _ in range(FORC)]
-    roots = [jnp.zeros((ROWS, COLS), F32) for _ in range(ROOT)]
-    for kind in range(canopy_table.shape[0]):
-        hit = kinds == kind
-        for m in range(FORC):
-            weights[m] = jnp.where(hit, canopy_table[kind, m], weights[m])
-        for m in range(ROOT):
-            roots[m] = jnp.where(hit, root_table[kind, m], roots[m])
-    mixed = weights[0] * forcing[0]
-    for m in range(1, FORC):
-        mixed = mixed + weights[m] * forcing[m]
-    conductance = 2.0 * jax.nn.sigmoid(mixed)
-    temp = leaf(start, forcing[0], forcing[1], forcing[2], conductance)
-    demand = conductance * softplus(temp - forcing[3]) / (1.0 + water * water)
-    planted = vegetated[...] == 1
-    demand = jnp.where(planted, demand, 0.0)
-    dry = jnp.where(planted, 0.0, 0.5)
+    g = conductance[...]
+    temp = leaf(start, forcing[0], forcing[1], forcing[2], g)
+    demand = g * softplus(temp - forcing[3]) / (1.0 + water * water)
     for m in range(ROOT):
-        moist = jax.nn.sigmoid(2.0 * (pressure[m] + 1.5))
-        value = -(demand * roots[m] * moist)
+        value = -(demand * uptake[m])
         if m == 0:
-            evaporation = dry * softplus(forcing[3] - forcing[2]) * moist
-            value = value + (0.3 * softplus(forcing[4]) - evaporation)
+            value = value + surface[...]
         for t in range(2):
             turned[pl.ds(t * 128 + m * ROWS, ROWS), :] = value[:, t * 128 : t * 128 + 128]
-    lane = iota((L, 128), 1)
-    first = jnp.zeros((L, 128), F32)
-    last = jnp.zeros((L, 128), F32)
     for x in range(ROWS):
-        low = turned[pl.ds(x, L, stride=ROWS), :]
-        high = turned[pl.ds(128 + x, L, stride=ROWS), :]
-        source[x, :, :128] = low
-        source[x, :, 128:] = high
-        here = jnp.logical_and(lane >= 8 * x, lane < 8 * x + 8)
-        first = jnp.where(here, lanes(low, 8 * x), first)
-        last = jnp.where(here, lanes(high, 8 * x - 120), last)
-    to_left[...] = first
-    to_right[...] = last
-
-
-def canopy_source(arrived, cols, counts, forcing, cover, vegetated, canopy_table, root_table, pressure):
-    smem = pl.BlockSpec(memory_space=pltpu.SMEM)
+        for t in range(2):
+            part = turned[pl.ds(128 * t + x, L, stride=ROWS), :]
+            source[x, :, 128 * t : 128 * t + 128] = part
+            if x < BHALO:
+                to_prev[2 * x + t] = part
+            if x >= ROWS - BHALO:
+                to_next[2 * (x - ROWS + BHALO) + t] = part
+
+
+def canopy_source(*arrays):
     v = vmem()[0]
     return pl.pallas_call(
         source_kernel,
-        out_shape=(shaped(ROWS, ROOT, COLS), shaped(L, 128), shaped(L, 128)),
-        in_specs=[v, v, smem, v, v, v, smem, smem, v],
+        out_shape=(shaped(ROWS, ROOT, COLS), shaped(SRIM, L, 128), shaped(SRIM, L, 128)),
+        in_specs=[v, v, smem(), v, v, v, v],
         out_specs=(v, v, v),
         scratch_shapes=[pltpu.VMEM((6 * ROWS, COLS), F32), pltpu.VMEM((2 * 128, 128), F32)],
-        compiler_params=params(8),
+        compiler_params=params(16),
         name="canopy_source",
-    )(arrived, cols, counts, forcing, cover, vegetated, canopy_table, root_table, pressure)
+    )(*arrays)
 
 
 def owner_kernel(arrived, state, updated):
@@ -262,7 +250,13 @@
     return pl.ds(32 * l + 16 * (x // 8) + 8 * t + x % 8, 8, stride=32 * L)
 
 
-def turn_kernel(pressure, conductivity, q, k, to_right, to_left):
+RIM = 2 * HALO * 2
+
+
+def turn_kernel(
+    pressure, conductivity, forcing, cover, vegetated, root_table, after,
+    q, k, to_next, to_prev, edge_left, edge_right, uptake, surface,
+):
     lane = iota((8, 128), 1)
 
     def layer(l, carry):
@@ -270,96 +264,107 @@
             first = jnp.zeros((8, 128), F32)
             last = jnp.zeros((8, 128), F32)
             for x in range(ROWS):
-                low = field[chunk(x, l, 0), :]
-                high = field[chunk(x, l, 1), :]
-                target[x, l, :, :128] = low
-                target[x, l, :, 128:] = high
-                here = jnp.logical_and(lane >= 8 * x, lane < 8 * x + 8)
-                first = jnp.where(here, lanes(low, 8 * x), first)
-                last = jnp.where(here, lanes(high, 8 * x - 120), last)
-            to_left[f, l] = first
-            to_right[f, l] = last
+                for t in range(2):
+                    part = field[chunk(x, l, t), :]
+                    target[x, l, :, 128 * t : 128 * t + 128] = part
+                    if x < HALO:
+                        to_prev[2 * (f * HALO + x) + t, l] = part
+                    if x >= ROWS - HALO:
+                        to_next[2 * (f * HALO + x - ROWS + HALO) + t, l] = part
+                    here = jnp.logical_and(lane >= 8 * x, lane < 8 * x + 8)
+                    if t == 0:
+                        first = jnp.where(here, lanes(part, 8 * x), first)
+                    else:
+                        last = jnp.where(here, lanes(part, 8 * x - 120), last)
+            edge_left[f, l] = first
+            edge_right[f, l] = last
         return carry
 
     lax.fori_loop(0, L, layer, 0)
-
-
-def turn(pressure, conductivity):
+    roots = looked_up(cover[...], root_table)
+    planted = vegetated[...] == 1
+    for m in range(ROOT):
+        top = jnp.concatenate(
+            [
+                jnp.concatenate([pressure[pl.ds(32 * m + 16 * xt + 8 * t, 8), :] for t in range(2)], axis=1)
+                for xt in range(2)
+            ],
+            axis=0,
+        )
+        moist = jax.nn.sigmoid(2.0 * (top + 1.5))
+        uptake[m] = jnp.where(planted, roots[m] * moist, 0.0)
+        if m == 0:
+            evaporation = jnp.where(planted, 0.0, 0.5) * softplus(forcing[3] - forcing[2]) * moist
+            surface[...] = 0.3 * softplus(forcing[4]) - evaporation
+
+
+def turn(*arrays):
     own_shape = shaped(ROWS, L, 8, COLS)
+    rim = shaped(RIM, L, 8, 128)
+    edge = shaped(2, L, 8, 128)
+    outs = (own_shape, own_shape, rim, rim, edge, edge, shaped(ROOT, ROWS, COLS), shaped(ROWS, COLS))
     return pl.pallas_call(
         turn_kernel,
-        out_shape=(own_shape, own_shape, shaped(2, L, 8, 128), shaped(2, L, 8, 128)),
-        in_specs=vmem(2),
-        out_specs=tuple(vmem(4)),
-        compiler_params=params(16),
+        out_shape=outs,
+        in_specs=vmem(5) + [smem(), pl.BlockSpec(memory_space=pl.ANY)],
+        out_specs=tuple(vmem(len(outs))),
+        compiler_params=params(24),
         name="turn",
-    )(pressure, conductivity)
-
-
-RIM = 2 * HALO * 2 + 2
-
-
-def rim_kernel(q, k, from_left, from_right, to_next, to_prev):
-    low = iota((8, 128), 1) < 64
+    )(*arrays)
+
+
+EDGE = 4 * L + 2
+
+
+def edge_kernel(edge_left, edge_right, from_prev, from_next, source, source_prev, source_next, to_right, to_left):
+    lane = iota((8, 128), 1)
+
+    def packed(parts, shift):
+        tile = jnp.zeros((8, 128), F32)
+        for at, part in parts:
+            here = jnp.logical_and(lane >= at, lane < at + 8)
+            tile = jnp.where(here, lanes(part, at - shift), tile)
+        return tile
 
     def layer(l, carry):
-        for f, field in enumerate((q, k)):
-            for i in range(HALO):
-                for t in range(2):
-                    part = pl.ds(128 * t, 128)
-                    to_next[2 * (f * HALO + i) + t, l] = field[ROWS - HALO + i, l, :, part]
-                    to_prev[2 * (f * HALO + i) + t, l] = field[i, l, :, part]
-            a, b = from_left[f, l], from_right[f, l]
-            to_next[4 * HALO + f, l] = jnp.where(low, lanes(a, 64), b)
-            to_prev[4 * HALO + f, l] = jnp.where(low, a, lanes(b, 64))
+        for f in range(2):
+            at = 2 * (8 * f + l)
+            to_left[at] = edge_left[f, l]
+            to_right[at] = edge_right[f, l]
+            for t, target, shift in ((0, to_left, 0), (1, to_right, 120)):
+                parts = []
+                for i in range(HALO):
+                    parts.append((8 * i, from_prev[2 * (f * HALO + i) + t, l]))
+                    parts.append((64 + 8 * i, from_next[2 * (f * HALO + i) + t, l]))
+                target[at + 1] = packed(parts, shift)
         return carry
 
     lax.fori_loop(0, L, layer, 0)
-
-
-def rim(*arrays):
-    outs = (shaped(RIM, L, 8, 128), shaped(RIM, L, 8, 128))
+    for t, target, shift in ((0, to_left, 0), (1, to_right, 120)):
+        part = pl.ds(128 * t, 128)
+        target[4 * L] = packed([(8 * x, source[x, :, part]) for x in range(ROWS)], shift)
+        parts = []
+        for i in range(BHALO):
+            parts.append((8 * i, source_prev[2 * i + t]))
+            parts.append((64 + 8 * i, source_next[2 * i + t]))
+        target[4 * L + 1] = packed(parts, shift)
+
+
+def edges(*arrays):
+    outs = (shaped(EDGE, 8, 128), shaped(EDGE, 8, 128))
     return pl.pallas_call(
-        rim_kernel,
+        edge_kernel,
         out_shape=outs,
-        in_specs=vmem(4),
+        in_specs=vmem(len(arrays)),
         out_specs=tuple(vmem(2)),
         compiler_params=params(16),
-        name="rim",
+        name="edges",
     )(*arrays)
 
 
-BHALO = 6
-SRIM = 2 * BHALO + 1
-
-
-def source_rim_kernel(source, from_left, from_right, to_next, to_prev):
-    low = iota((L, 128), 1) < 64
-    for i in range(BHALO):
-        for t in range(2):
-            part = pl.ds(128 * t, 128)
-            to_next[2 * i + t] = source[ROWS - BHALO + i, :, part]
-            to_prev[2 * i + t] = source[i, :, part]
-    a, b = from_left[...], from_right[...]
-    to_next[2 * BHALO] = jnp.where(low, lanes(a, 64), b)
-    to_prev[2 * BHALO] = jnp.where(low, a, lanes(b, 64))
-
-
-def source_rim(*arrays):
-    outs = (shaped(SRIM, L, 128), shaped(SRIM, L, 128))
-    return pl.pallas_call(
-        source_rim_kernel,
-        out_shape=outs,
-        in_specs=vmem(3),
-        out_specs=tuple(vmem(2)),
-        compiler_params=params(8),
-        name="source_rim",
-    )(*arrays)
-
-
-def halo_tile(from_left, from_right, lane, at_left, at_right):
-    tile = jnp.where(lane < 8, lanes(from_right, -at_right), 0.0)
-    return jnp.where(lane >= 120, lanes(from_left, 120 - at_left), tile)
+def halo_tile(from_left, from_right, lane, at):
+    tile = jnp.where(lane < 8, lanes(from_right, -at), 0.0)
+    return jnp.where(lane >= 120, lanes(from_left, 120 - at), tile)
 
 
 def own(v):
@@ -507,8 +512,7 @@
 
 
 def first_kernel(
-    q_own, k_own, from_left, from_right, from_prev, from_next,
-    source, source_left, source_right, source_prev, source_next,
+    q_own, k_own, from_prev, from_next, source, source_prev, source_next, from_left, from_right,
     q, k, b, v0, v1, v2, moments,
     resist, cx, cy, cyl, cz, diag,
 ):
@@ -516,37 +520,34 @@
 
     def fill(l, carry):
         for f, (field, target) in enumerate(((q_own, q), (k_own, k))):
+            at = 2 * (8 * f + l)
+            a, c = from_left[at], from_right[at]
             for x in range(ROWS):
                 target[HALO + x, l, :, :COLS] = field[x, l]
-                target[HALO + x, l, :, COLS:] = halo_tile(
-                    from_left[f, l], from_right[f, l], lane, 8 * x, 8 * x
-                )
+                target[HALO + x, l, :, COLS:] = halo_tile(a, c, lane, 8 * x)
+            a, c = from_left[at + 1], from_right[at + 1]
             for i in range(HALO):
-                for side, r, at in (
-                    (from_prev, i, 8 * (8 - HALO + i)),
-                    (from_next, HALO + ROWS + i, 8 * i),
-                ):
+                for side, r, spot in ((from_prev, i, 8 * i), (from_next, HALO + ROWS + i, 64 + 8 * i)):
                     for t in range(2):
                         target[r, l, :, 128 * t : 128 * t + 128] = side[2 * (f * HALO + i) + t, l]
-                    corner = side[4 * HALO + f, l]
-                    target[r, l, :, COLS:] = halo_tile(corner, corner, lane, at, 64 + at)
+                    target[r, l, :, COLS:] = halo_tile(a, c, lane, spot)
         return carry
 
     lax.fori_loop(0, L, fill, 0)
 
+    a, c = from_left[4 * L], from_right[4 * L]
     for x in range(ROWS):
         b[HALO + x, :, :COLS] = source[x]
-        b[HALO + x, :, COLS:] = halo_tile(source_left[...], source_right[...], lane, 8 * x, 8 * x)
-    gap = HALO - BHALO
+        b[HALO + x, :, COLS:] = halo_tile(a, c, lane, 8 * x)
+    a, c = from_left[4 * L + 1], from_right[4 * L + 1]
     for i in range(BHALO):
-        for side, r, at in (
-            (source_prev, gap + i, 8 * (8 - BHALO + i)),
-            (source_next, HALO + ROWS + i, 8 * i),
+        for side, r, spot in (
+            (source_prev, HALO - BHALO + i, 8 * i),
+            (source_next, HALO + ROWS + i, 64 + 8 * i),
         ):
             for t in range(2):
                 b[r, :, 128 * t : 128 * t + 128] = side[2 * i + t]
-            corner = side[2 * BHALO]
-            b[r, :, COLS:] = halo_tile(corner, corner, lane, at, 64 + at)
+            b[r, :, COLS:] = halo_tile(a, c, lane, spot)
 
     sub = iota((8, XC), 0)
 
@@ -578,7 +579,7 @@
         in_specs=vmem(len(arrays)),
         out_specs=tuple(vmem(len(outs))),
         scratch_shapes=scratch(6),
-        compiler_params=params(44),
+        compiler_params=params(22),
         name="first_newton",
     )(*arrays)
 
@@ -586,8 +587,9 @@
 def second_kernel(
     q, k, b, u0, u1, u2, gathered,
     q_own, w0, w1, w2, moments,
-    q1, resist, cx, cy, cyl, cz, diag, v0, v1, v2,
+    q1, resist, cx, cy, cyl, cz, diag, v0, v2,
 ):
+    v1 = resist
     c0, c1, c2 = coefficients(gathered)
 
     def update(r, carry):
@@ -627,8 +629,8 @@
         out_shape=outs,
         in_specs=vmem(len(arrays)),
         out_specs=tuple(vmem(len(outs))),
-        scratch_shapes=scratch(10),
-        compiler_params=params(54),
+        scratch_shapes=scratch(9),
+        compiler_params=params(28),
         name="second_newton",
     )(*arrays)
 
@@ -681,28 +683,32 @@
     canopy_state,
 ):
     owners = send_cols.shape[1]
-    cols = send_cols.reshape(owners, COLS)
-    counts = pair_counts.reshape(owners)
-    state = canopy_state.reshape(owners, 16, COLS)
-
-    q_own, k_own, to_right, to_left = turn(flat(pressure_old), flat(conductivity))
+    cols = in_hbm(send_cols.reshape(owners, 1, COLS))
+    counts = in_hbm(pair_counts.reshape(owners))
+    state = in_hbm(canopy_state.reshape(owners, 16, COLS))
+    forcing, cover_type, vegetated = in_hbm(forcing), in_hbm(cover_type), in_hbm(vegetated)
+    old, conductivity = in_hbm(flat(pressure_old)), in_hbm(flat(conductivity))
+    canopy_table, root_table = in_hbm(canopy_table.T), in_hbm(root_table.T)
+
+    payload, conductance = canopy_send(forcing, cover_type, canopy_table, counts, cols, state)
+    arrived = lax.all_to_all(payload, "gx", split_axis=0, concat_axis=0, tiled=True)
+    q_own, k_own, to_next, to_prev, edge_left, edge_right, uptake, surface = turn(
+        old, conductivity, forcing, cover_type, vegetated, root_table, payload
+    )
+    to_next, to_prev, arrived = lax.optimization_barrier((to_next, to_prev, arrived))
+    from_prev, from_next = exchange(to_next, to_prev, "gx")
+    source, to_next, to_prev = canopy_source(
+        arrived, cols, counts, forcing, conductance, uptake, surface
+    )
+    source_prev, source_next = exchange(to_next, to_prev, "gx")
+    to_right, to_left = edges(
+        edge_left, edge_right, from_prev, from_next, source, source_prev, source_next
+    )
     from_left, from_right = exchange(to_right, to_left, "gy")
-    payload = canopy_send(forcing, cover_type, canopy_table, counts, cols, state)
-    to_next, to_prev = rim(q_own, k_own, from_left, from_right)
-    from_prev, from_next = exchange(to_next, to_prev, "gx")
-    arrived = lax.all_to_all(payload, "gx", split_axis=0, concat_axis=0, tiled=True)
-
-    source, to_right, to_left = canopy_source(
-        arrived, cols, counts, forcing, cover_type, vegetated, canopy_table, root_table, pressure_old[:ROOT]
-    )
-    source_left, source_right = exchange(to_right, to_left, "gy")
-    to_next, to_prev = source_rim(source, source_left, source_right)
-    source_prev, source_next = exchange(to_next, to_prev, "gx")
     new_state = owner_update(arrived, state).reshape(canopy_state.shape)
 
     q, k, b, v0, v1, v2, moments = first_newton(
-        q_own, k_own, from_left, from_right, from_prev, from_next,
-        source, source_left, source_right, source_prev, source_next,
+        q_own, k_own, from_prev, from_next, source, source_prev, source_next, from_left, from_right
     )
     q1, w0, w1, w2, moments = second_newton(q, k, b, v0, v1, v2, share(moments))
     pressure = unflat(final_update(q1, w0, w1, w2, share(moments)))

time: 155 us -> 118 us (0.76)
  local copies, waits for them, and re-layouts: 22.8 us -> 3.11 us
  Pallas kernels: 50.1 us -> 37.8 us
  starting transfers between devices: 34.8 us -> 29.5 us
  waiting for transfers between devices: 25.3 us -> 27.1 us
    unnamed x51 -> x6, local copies, waits for them, and re-layouts: 21.2 us -> 3.11 us
    ppermute x8 -> x6, waiting for transfers between devices: 10.2 us -> 17.9 us  [exchange(): return (lax.ppermute(to_high, axis, up), lax.ppermute(to_low, axis, down))]
    pallas_call x1, Pallas kernels: 17.1 us -> 10.3 us  [second_newton(): pl.pallas_call(second_kernel, out_shape=outs, in_specs=vmem(len(arrays)),...]
    ppermute x8 -> x6, starting transfers between devices: 22.1 us -> 17.2 us  [exchange(): return (lax.ppermute(to_high, axis, up), lax.ppermute(to_low, axis, down))]
    all_to_all x1, waiting for transfers between devices: 7.25 us -> 2.34 us  [body(): lax.all_to_all(payload, 'gx', split_axis=0, concat_axis=0, tiled=True)]
    pallas_call x1, Pallas kernels: 16.8 us -> 12.8 us  [first_newton(): pl.pallas_call(first_kernel, out_shape=outs, in_specs=vmem(len(arrays)),...]
    pallas_call x1, Pallas kernels: 4.53 us -> 2.49 us  [canopy_source(): pl.pallas_call(source_kernel, out_shape=(shaped(ROWS, ROOT, COLS), shaped...]
    slice x1 -> x0, local copies, waits for them, and re-layouts: 1.56 us -> none  [body(): pressure_old[:ROOT]]
  transfers between devices with their start and end apart: 10 -> 8, of which waited for: 5 -> 6; matrix products, arithmetic and copies ran while one was open for 3% -> 0% of each run, Pallas kernels for 7% -> 7%
where the time goes in v3:
time: 118 us
  Pallas kernels  37.8 us (32%)
  starting transfers between devices  29.5 us (25%)
  waiting for transfers between devices  27.1 us (23%)
  blocking collectives  19.5 us (17%)
  local copies, waits for them, and re-layouts  3.11 us (3%)
    all_to_all x1, blocking collectives, share(): lax.all_to_all(moments, ('gx', 'gy'), split_axis=0, concat_axis=0, tiled=...  19.5 us
    ppermute x6, waiting for transfers between devices, exchange(): return (lax.ppermute(to_high, axis, up), lax.ppermute(to_low, axis, down))  17.9 us
    ppermute x6, starting transfers between devices, exchange(): return (lax.ppermute(to_high, axis, up), lax.ppermute(to_low, axis, down))  17.2 us
    pallas_call x1, Pallas kernels, first_newton(): pl.pallas_call(first_kernel, out_shape=outs, in_specs=vmem(len(arrays)),...  12.8 us
    pallas_call x1, Pallas kernels, second_newton(): pl.pallas_call(second_kernel, out_shape=outs, in_specs=vmem(len(arrays)),...  10.3 us
    all_to_all x1, starting transfers between devices, body(): lax.all_to_all(payload, 'gx', split_axis=0, concat_axis=0, tiled=True)  7.58 us
    all_to_all x1, waiting for transfers between devices, share(): lax.all_to_all(moments, ('gx', 'gy'), split_axis=0, concat_axis=0, tiled=...  6.89 us
    all_to_all x1, starting transfers between devices, share(): lax.all_to_all(moments, ('gx', 'gy'), split_axis=0, concat_axis=0, tiled=...  4.75 us
  transfers between devices with their start and end apart: 8, of which 6 were waited for; matrix products, arithmetic and copies ran while one was open for 0% of the time, Pallas kernels for 7%

profile of v3, /device:TPU:1, one launch (start us, length us, event | category | flops | bytes accessed | tf_op | source)
XLA Modules:
  0.0 117.8 jit_solution(15558342328841807752)
XLA Ops:
  0.6 3.1 %canopy_send.1 = (f32[16,8,256]{2,1,0:T(8,128)}, f32[16,256]{1,0:T(8,128)S(1)}) custom-call(f32[8,16,256]{2,1,0:T(8,128)} %forcing.5, s32[16,256]{1,0:T(8,128)} %cover.3, f32[8,16]{1,0:T(8,128)} %bitcast.42, s32[16]{0:T(128)} %bitcast.44, s32[16,1,256]{2,1,0:T(1,128)} %bitcast.40, f32[16,16,256]{2,1,0:T(8,128)} %bitcast.36), custom_call_target="tpu_custom_call" | custom-call | tf_op jit(solution)/shard_map/canopy_send/pallas_call | solution.py:130
  3.7 7.6 %all-to-all-start = ((f32[16,8,256]{2,1,0:T(8,128)}), f32[16,8,256]{2,1,0:T(8,128)S(1)}, u32[]{:S(2)}, u32[]{:S(2)}) async-start(f32[16,8,256]{2,1,0:T(8,128)} %get-tuple-element.32.after), calls=%async_computation | async-start | bytes 262144 | tf_op jit(solution)/shard_map/all_to_all | solution.py:694
  11.3 3.6 %turn.1 = (f32[16,8,8,256]{3,2,1,0:T(8,128)S(1)}, f32[16,8,8,256]{3,2,1,0:T(8,128)S(1)}, f32[28,8,8,128]{3,2,1,0:T(8,128)S(1)}, f32[28,8,8,128]{3,2,1,0:T(8,128)...) custom-call(f32[2048,128]{1,0:T(8,128)} %bitcast.34, ...), custom_call_target="tpu_custom_call" | custom-call | tf_op jit(solution)/shard_map/turn/pallas_call | solution.py:306
  15.8 2.3 %all-to-all-done.arrived = f32[16,8,256]{2,1,0:T(8,128)S(1)} async-done(((f32[16,8,256]{2,1,0:T(8,128)}), f32[16,8,256]{2,1,0:T(8,128)S(1)}, u32[]{:S(2)}, u32[]{:S(2)}) %all-to-all-start) | async-done | bytes 131104 | tf_op jit(solution)/shard_map/all_to_all | solution.py:694
  18.2 2.1 %collective-permute-start = (f32[28,8,8,128]{3,2,1,0:T(8,128)}, f32[28,8,8,128]{3,2,1,0:T(8,128)S(1)}, u32[]{:S(2)}, u32[]{:S(2)}) collective-permute-start(f32[28,8,8,128]{3,2,1,0:T(8,128)} %copy-done.2), channel_id=1, source_target_pairs={{0,8},{8,16},{16,24},{24,32},{32,40},{40,48},{48,56},{56,64},{64,7... | collective-permute-start | bytes 2752520 | tf_op jit(solution)/shard_map/ppermute | solution.py:666
  20.3 1.3 %collective-permute-start.1 = (f32[28,8,8,128]{3,2,1,0:T(8,128)S(1)}, f32[28,8,8,128]{3,2,1,0:T(8,128)S(1)}, u32[]{:S(2)}, u32[]{:S(2)}) collective-permute-start(f32[28,8,8,128]{3,2,1,0:T(8,128)S(1)} %get-tuple-element.38), channel_id=1, source_target_pairs={{8,0},{16,8},{24,16},{32,24},{40,32},{48,40},{56,48},{64,56},{72,6... | collective-permute-start | bytes 2752520 | tf_op jit(solution)/shard_map/ppermute | solution.py:666
  21.6 2.5 %canopy_source.1 = (f32[16,8,256]{2,1,0:T(8,128)S(1)}, f32[12,8,128]{2,1,0:T(8,128)S(1)}, f32[12,8,128]{2,1,0:T(8,128)S(1)}) custom-call(f32[16,8,256]{2,1,0:T(8,128)S(1)} %all-to-all-done.arrived, s32[16,1,256]{2,1,0:T(1,128)} %bitcast.41, s32[16]{0:T(128)} %bitcast.45, f32[8,16,256]{2,1,0:T(8,128)} %forcing.5, ...), custom_call_target="tpu_custom_call" | custom-call | tf_op jit(solution)/shard_map/canopy_source/pallas_call | solution.py:200
  24.1 4.0 %collective-permute-start.2 = (f32[12,8,128]{2,1,0:T(8,128)S(1)}, f32[12,8,128]{2,1,0:T(8,128)S(1)}, u32[]{:S(2)}, u32[]{:S(2)}) collective-permute-start(f32[12,8,128]{2,1,0:T(8,128)S(1)} %get-tuple-element.44), channel_id=1, source_target_pairs={{0,8},{8,16},{16,24},{24,32},{32,40},{40,48},{48,56},{56,64},{64,7... | collective-permute-start | bytes 147464 | tf_op jit(solution)/shard_map/ppermute | solution.py:666
  28.1 1.3 %collective-permute-start.3 = (f32[12,8,128]{2,1,0:T(8,128)S(1)}, f32[12,8,128]{2,1,0:T(8,128)S(1)}, u32[]{:S(2)}, u32[]{:S(2)}) collective-permute-start(f32[12,8,128]{2,1,0:T(8,128)S(1)} %get-tuple-element.45), channel_id=1, source_target_pairs={{8,0},{16,8},{24,16},{32,24},{40,32},{48,40},{56,48},{64,56},{72,6... | collective-permute-start | bytes 147464 | tf_op jit(solution)/shard_map/ppermute | solution.py:666
  29.4 9.7 %collective-permute-done.2.source_prev = f32[12,8,128]{2,1,0:T(8,128)S(1)} collective-permute-done((f32[12,8,128]{2,1,0:T(8,128)S(1)}, f32[12,8,128]{2,1,0:T(8,128)S(1)}, u32[]{:S(2)}, u32[]{:S(2)}) %collective-permute-start.2) | collective-permute-done | bytes 49184 | tf_op jit(solution)/shard_map/ppermute | solution.py:666
  39.1 3.7 %collective-permute-done.3.source_next = f32[12,8,128]{2,1,0:T(8,128)S(1)} collective-permute-done((f32[12,8,128]{2,1,0:T(8,128)S(1)}, f32[12,8,128]{2,1,0:T(8,128)S(1)}, u32[]{:S(2)}, u32[]{:S(2)}) %collective-permute-start.3) | collective-permute-done | bytes 49184 | tf_op jit(solution)/shard_map/ppermute | solution.py:666
  42.8 1.1 edges.1
  43.9 6.6 %collective-permute-start.4 = (f32[34,8,128]{2,1,0:T(8,128)S(1)}, f32[34,8,128]{2,1,0:T(8,128)S(1)}, u32[]{:S(2)}, u32[]{:S(2)}) collective-permute-start(f32[34,8,128]{2,1,0:T(8,128)S(1)} %get-tuple-element.48), channel_id=1, source_target_pairs={{0,1},{1,2},{2,3},{3,4},{4,5},{5,6},{6,7},{8,9},{9,10},{10,11},{11... | collective-permute-start | bytes 417800 | tf_op jit(solution)/shard_map/ppermute | solution.py:666
  50.5 1.9 %collective-permute-start.5 = (f32[34,8,128]{2,1,0:T(8,128)S(1)}, f32[34,8,128]{2,1,0:T(8,128)S(1)}, u32[]{:S(2)}, u32[]{:S(2)}) collective-permute-start(f32[34,8,128]{2,1,0:T(8,128)S(1)} %get-tuple-element.49), channel_id=1, source_target_pairs={{1,0},{2,1},{3,2},{4,3},{5,4},{6,5},{7,6},{9,8},{10,9},{11,10},{12... | collective-permute-start | bytes 417800 | tf_op jit(solution)/shard_map/ppermute | solution.py:666
  52.5 4.4 %collective-permute-done.5.from_right = f32[34,8,128]{2,1,0:T(8,128)S(1)} collective-permute-done((f32[34,8,128]{2,1,0:T(8,128)S(1)}, f32[34,8,128]{2,1,0:T(8,128)S(1)}, u32[]{:S(2)}, u32[]{:S(2)}) %collective-permute-start.5) | collective-permute-done | bytes 139296 | tf_op jit(solution)/shard_map/ppermute | solution.py:666
  56.9 12.8 %first_newton.1 = (f32[30,8,8,384]{3,2,1,0:T(8,128)S(1)}, f32[30,8,8,384]{3,2,1,0:T(8,128)S(1)}, f32[30,8,384]{2,1,0:T(8,128)S(1)}, f32[30,8,8,384]{3,2,1,0:T(8,...) custom-call(f32[16,8,8,256]{3,2,1,0:T(8,128)S(1)} %get-tuple-element.33.q_own, ...), custom_call_target="tpu_custom_call" | custom-call | tf_op jit(solution)/shard_map/first_newton/pallas_call | solution.py:576
  69.7 19.5 %all_to_all.27 = f32[128,1,128]{2,1,0:T(1,128)S(1)} all-to-all(f32[128,1,128]{2,1,0:T(1,128)S(1)} %bitcast.33), channel_id=1, replica_groups=mesh['gx'=16,'gy'=8] {'gx','gy'}, dimensions={0} | all-to-all | bytes 131072 | tf_op jit(solution)/shard_map/all_to_all | solution.py:670
  89.2 10.3 %second_newton.1 = (f32[16,8,8,256]{3,2,1,0:T(8,128)S(1)}, f32[16,8,8,256]{3,2,1,0:T(8,128)S(1)}, f32[16,8,8,256]{3,2,1,0:T(8,128)S(1)}, f32[16,8,8,256]{3,2,1,0:T(8,128)S(1)}, f32[128,128]{1,0:T(8,128)}) custom-call(f32[30,8,8,384]{3,2,1,0:T(8,128)S(1)} %get-tuple-element.50.q, f32[30,8,8,384]{3,2,1,0:T(8,128)S(1)} %get-tuple-element.51.k, ...), custom_call_target="tpu_custom_call" | custom-call | tf_op jit(solution)/shard_map/second_newton/pallas_call | solution.py:627
  99.5 1.0 copy-done
  100.5 4.8 %all-to-all-start.2 = ((f32[128,1,128]{2,1,0:T(1,128)}), f32[128,1,128]{2,1,0:T(1,128)S(1)}, u32[]{:S(2)}, u32[]{:S(2)}) async-start(f32[128,1,128]{2,1,0:T(1,128)} %bitcast.15), calls=%async_computation.2 | async-start | bytes 131072 | tf_op jit(solution)/shard_map/all_to_all | solution.py:670
  105.2 2.5 %owner_update.1 = f32[16,16,256]{2,1,0:T(8,128)} custom-call(f32[16,8,256]{2,1,0:T(8,128)S(1)} %all-to-all-done.arrived, f32[16,16,256]{2,1,0:T(8,128)} %bitcast.37), custom_call_target="tpu_custom_call" | custom-call | tf_op jit(solution)/shard_map/owner_update/pallas_call | solution.py:231
  107.7 6.9 %all-to-all-done.2 = f32[128,1,128]{2,1,0:T(1,128)S(1)} async-done(((f32[128,1,128]{2,1,0:T(1,128)}), f32[128,1,128]{2,1,0:T(1,128)S(1)}, u32[]{:S(2)}, u32[]{:S(2)}) %all-to-all-start.2) | async-done | bytes 65568 | tf_op jit(solution)/shard_map/all_to_all | solution.py:670
  114.6 1.2 %copy-done.1 = f32[16,8,8,256]{3,2,1,0:T(8,128)S(1)} copy-done((f32[16,8,8,256]{3,2,1,0:T(8,128)S(1)}, f32[16,8,8,256]{3,2,1,0:T(8,128)}, u32[]{:S(2)}) %copy-start.1) | copy-done | bytes 1048600
  115.8 2.0 %final_update.1 = f32[2048,128]{1,0:T(8,128)} custom-call(f32[16,8,8,256]{3,2,1,0:T(8,128)S(1)} %get-tuple-element.57.q, f32[16,8,8,256]{3,2,1,0:T(8,128)S(1)} %get-tuple-element.58.v0, f32[16,8,8,256]{3,2,1,0:T(8,128)S(1)} %get-tuple-element.59.v1, f32[16,8,8,256]{3,2,1,0:T(8,128)S(1)} %copy-done.1, f32[128,128]{1,0:T(8,128)S(1)} %bitcast.32), custom_call_target="tpu_custom_call" | custom-call | tf_op jit(solution)/shard_map/final_update/pallas_call | solution.py:652
  (7 shorter events, 1.0 us)
Async XLA Ops:
  3.7 14.5 %all-to-all-start = ((f32[16,8,256]{2,1,0:T(8,128)}), f32[16,8,256]{2,1,0:T(8,128)S(1)}, u32[]{:S(2)}, u32[]{:S(2)}) async-start(f32[16,8,256]{2,1,0:T(8,128)} %get-tuple-element.32.after), calls=%async_computation | async-start | bytes 262144 | tf_op jit(solution)/shard_map/all_to_all | solution.py:694
  14.9 0.9 copy-start.2
  18.2 24.6 %collective-permute-start = (f32[28,8,8,128]{3,2,1,0:T(8,128)}, f32[28,8,8,128]{3,2,1,0:T(8,128)S(1)}, u32[]{:S(2)}, u32[]{:S(2)}) collective-permute-start(f32[28,8,8,128]{3,2,1,0:T(8,128)} %copy-done.2), channel_id=1, source_target_pairs={{0,8},{8,16},{16,24},{24,32},{32,40},{40,48},{48,56},{56,64},{64,7... | collective-permute-start | bytes 2752520 | tf_op jit(solution)/shard_map/ppermute | solution.py:666
  20.3 22.5 %collective-permute-start.1 = (f32[28,8,8,128]{3,2,1,0:T(8,128)S(1)}, f32[28,8,8,128]{3,2,1,0:T(8,128)S(1)}, u32[]{:S(2)}, u32[]{:S(2)}) collective-permute-start(f32[28,8,8,128]{3,2,1,0:T(8,128)S(1)} %get-tuple-element.38), channel_id=1, source_target_pairs={{8,0},{16,8},{24,16},{32,24},{40,32},{48,40},{56,48},{64,56},{72,6... | collective-permute-start | bytes 2752520 | tf_op jit(solution)/shard_map/ppermute | solution.py:666
  24.1 15.0 %collective-permute-start.2 = (f32[12,8,128]{2,1,0:T(8,128)S(1)}, f32[12,8,128]{2,1,0:T(8,128)S(1)}, u32[]{:S(2)}, u32[]{:S(2)}) collective-permute-start(f32[12,8,128]{2,1,0:T(8,128)S(1)} %get-tuple-element.44), channel_id=1, source_target_pairs={{0,8},{8,16},{16,24},{24,32},{32,40},{40,48},{48,56},{56,64},{64,7... | collective-permute-start | bytes 147464 | tf_op jit(solution)/shard_map/ppermute | solution.py:666
  28.1 14.7 %collective-permute-start.3 = (f32[12,8,128]{2,1,0:T(8,128)S(1)}, f32[12,8,128]{2,1,0:T(8,128)S(1)}, u32[]{:S(2)}, u32[]{:S(2)}) collective-permute-start(f32[12,8,128]{2,1,0:T(8,128)S(1)} %get-tuple-element.45), channel_id=1, source_target_pairs={{8,0},{16,8},{24,16},{32,24},{40,32},{48,40},{56,48},{64,56},{72,6... | collective-permute-start | bytes 147464 | tf_op jit(solution)/shard_map/ppermute | solution.py:666
  43.9 8.7 %collective-permute-start.4 = (f32[34,8,128]{2,1,0:T(8,128)S(1)}, f32[34,8,128]{2,1,0:T(8,128)S(1)}, u32[]{:S(2)}, u32[]{:S(2)}) collective-permute-start(f32[34,8,128]{2,1,0:T(8,128)S(1)} %get-tuple-element.48), channel_id=1, source_target_pairs={{0,1},{1,2},{2,3},{3,4},{4,5},{5,6},{6,7},{8,9},{9,10},{10,11},{11... | collective-permute-start | bytes 417800 | tf_op jit(solution)/shard_map/ppermute | solution.py:666
  50.5 6.4 %collective-permute-start.5 = (f32[34,8,128]{2,1,0:T(8,128)S(1)}, f32[34,8,128]{2,1,0:T(8,128)S(1)}, u32[]{:S(2)}, u32[]{:S(2)}) collective-permute-start(f32[34,8,128]{2,1,0:T(8,128)S(1)} %get-tuple-element.49), channel_id=1, source_target_pairs={{1,0},{2,1},{3,2},{4,3},{5,4},{6,5},{7,6},{9,8},{10,9},{11,10},{12... | collective-permute-start | bytes 417800 | tf_op jit(solution)/shard_map/ppermute | solution.py:666
  99.5 1.0 copy-start
  100.5 14.1 %all-to-all-start.2 = ((f32[128,1,128]{2,1,0:T(1,128)}), f32[128,1,128]{2,1,0:T(1,128)S(1)}, u32[]{:S(2)}, u32[]{:S(2)}) async-start(f32[128,1,128]{2,1,0:T(1,128)} %bitcast.15), calls=%async_computation.2 | async-start | bytes 131072 | tf_op jit(solution)/shard_map/all_to_all | solution.py:670
  114.6 1.2 %copy-start.1 = (f32[16,8,8,256]{3,2,1,0:T(8,128)S(1)}, f32[16,8,8,256]{3,2,1,0:T(8,128)}, u32[]{:S(2)}) copy-start(f32[16,8,8,256]{3,2,1,0:T(8,128)} %copy-done) | copy-start | bytes 3145732

commit v4 on v3

--- a/solution.py
+++ b/solution.py
@@ -16,7 +16,8 @@
 XC = 384
 OUTSIDE = 1e37
 BHALO = 6
-SRIM = 2 * BHALO
+SIDE = 2 * L + 1
+CORNER = 2 * BHALO + SIDE
 STORE = 0.05
 GRAV = 0.5
 F32 = jnp.float32
@@ -150,8 +151,8 @@
 
 
 def source_kernel(
-    arrived, cols, counts, forcing, conductance, uptake, surface,
-    source, to_next, to_prev, total, turned,
+    arrived, cols, counts, forcing, conductance, uptake, surface, edge_left, edge_right,
+    source, to_right, to_left, total, turned,
 ):
     total[...] = jnp.zeros_like(total)
 
@@ -185,22 +186,28 @@
             value = value + surface[...]
         for t in range(2):
             turned[pl.ds(t * 128 + m * ROWS, ROWS), :] = value[:, t * 128 : t * 128 + 128]
+    lane = iota((L, 128), 1)
+    first = jnp.zeros((L, 128), F32)
+    last = jnp.zeros((L, 128), F32)
     for x in range(ROWS):
-        for t in range(2):
-            part = turned[pl.ds(128 * t + x, L, stride=ROWS), :]
-            source[x, :, 128 * t : 128 * t + 128] = part
-            if x < BHALO:
-                to_prev[2 * x + t] = part
-            if x >= ROWS - BHALO:
-                to_next[2 * (x - ROWS + BHALO) + t] = part
+        low = turned[pl.ds(x, L, stride=ROWS), :]
+        high = turned[pl.ds(128 + x, L, stride=ROWS), :]
+        source[x, :, :128] = low
+        source[x, :, 128:] = high
+        here = jnp.logical_and(lane >= 8 * x, lane < 8 * x + 8)
+        first = jnp.where(here, lanes(low, 8 * x), first)
+        last = jnp.where(here, lanes(high, 8 * x - 120), last)
+    for target, edge, own_edge in ((to_left, edge_left, first), (to_right, edge_right, last)):
+        target[0 : 2 * L] = edge[...]
+        target[2 * L] = own_edge
 
 
 def canopy_source(*arrays):
     v = vmem()[0]
     return pl.pallas_call(
         source_kernel,
-        out_shape=(shaped(ROWS, ROOT, COLS), shaped(SRIM, L, 128), shaped(SRIM, L, 128)),
-        in_specs=[v, v, smem(), v, v, v, v],
+        out_shape=(shaped(ROWS, ROOT, COLS), shaped(SIDE, L, 128), shaped(SIDE, L, 128)),
+        in_specs=[v, v, smem(), v, v, v, v, v, v],
         out_specs=(v, v, v),
         scratch_shapes=[pltpu.VMEM((6 * ROWS, COLS), F32), pltpu.VMEM((2 * 128, 128), F32)],
         compiler_params=params(16),
@@ -276,8 +283,8 @@
                         first = jnp.where(here, lanes(part, 8 * x), first)
                     else:
                         last = jnp.where(here, lanes(part, 8 * x - 120), last)
-            edge_left[f, l] = first
-            edge_right[f, l] = last
+            edge_left[f * L + l] = first
+            edge_right[f * L + l] = last
         return carry
 
     lax.fori_loop(0, L, layer, 0)
@@ -301,7 +308,7 @@
 def turn(*arrays):
     own_shape = shaped(ROWS, L, 8, COLS)
     rim = shaped(RIM, L, 8, 128)
-    edge = shaped(2, L, 8, 128)
+    edge = shaped(2 * L, 8, 128)
     outs = (own_shape, own_shape, rim, rim, edge, edge, shaped(ROOT, ROWS, COLS), shaped(ROWS, COLS))
     return pl.pallas_call(
         turn_kernel,
@@ -313,82 +320,60 @@
     )(*arrays)
 
 
-EDGE = 4 * L + 2
-
-
-def edge_kernel(edge_left, edge_right, from_prev, from_next, source, source_prev, source_next, to_right, to_left):
-    lane = iota((8, 128), 1)
-
-    def packed(parts, shift):
-        tile = jnp.zeros((8, 128), F32)
-        for at, part in parts:
-            here = jnp.logical_and(lane >= at, lane < at + 8)
-            tile = jnp.where(here, lanes(part, at - shift), tile)
-        return tile
-
-    def layer(l, carry):
-        for f in range(2):
-            at = 2 * (8 * f + l)
-            to_left[at] = edge_left[f, l]
-            to_right[at] = edge_right[f, l]
-            for t, target, shift in ((0, to_left, 0), (1, to_right, 120)):
-                parts = []
-                for i in range(HALO):
-                    parts.append((8 * i, from_prev[2 * (f * HALO + i) + t, l]))
-                    parts.append((64 + 8 * i, from_next[2 * (f * HALO + i) + t, l]))
-                target[at + 1] = packed(parts, shift)
-        return carry
-
-    lax.fori_loop(0, L, layer, 0)
-    for t, target, shift in ((0, to_left, 0), (1, to_right, 120)):
-        part = pl.ds(128 * t, 128)
-        target[4 * L] = packed([(8 * x, source[x, :, part]) for x in range(ROWS)], shift)
-        parts = []
-        for i in range(BHALO):
-            parts.append((8 * i, source_prev[2 * i + t]))
-            parts.append((64 + 8 * i, source_next[2 * i + t]))
-        target[4 * L + 1] = packed(parts, shift)
-
-
-def edges(*arrays):
-    outs = (shaped(EDGE, 8, 128), shaped(EDGE, 8, 128))
-    return pl.pallas_call(
-        edge_kernel,
+def corner_kernel(source, from_left, from_right, after, to_next, to_prev):
+    low = iota((8, 128), 1) < 64
+    for i in range(BHALO):
+        for t in range(2):
+            part = pl.ds(128 * t, 128)
+            to_next[2 * i + t] = source[ROWS - BHALO + i, :, part]
+            to_prev[2 * i + t] = source[i, :, part]
+    for j in range(SIDE):
+        a, b = from_left[j], from_right[j]
+        to_next[2 * BHALO + j] = jnp.where(low, lanes(a, 64), b)
+        to_prev[2 * BHALO + j] = jnp.where(low, a, lanes(b, 64))
+
+
+def corners(*arrays):
+    outs = (shaped(CORNER, 8, 128), shaped(CORNER, 8, 128))
+    return pl.pallas_call(
+        corner_kernel,
         out_shape=outs,
-        in_specs=vmem(len(arrays)),
+        in_specs=vmem(3) + [pl.BlockSpec(memory_space=pl.ANY)],
         out_specs=tuple(vmem(2)),
         compiler_params=params(16),
-        name="edges",
+        name="corners",
     )(*arrays)
 
 
-def halo_tile(from_left, from_right, lane, at):
-    tile = jnp.where(lane < 8, lanes(from_right, -at), 0.0)
-    return jnp.where(lane >= 120, lanes(from_left, 120 - at), tile)
+def halo_tile(from_left, from_right, lane, at_left, at_right):
+    tile = jnp.where(lane < 8, lanes(from_right, -at_right), 0.0)
+    return jnp.where(lane >= 120, lanes(from_left, 120 - at_left), tile)
 
 
 def own(v):
     return v[:, :COLS]
 
 
-def mobilities(q, k, resist, diag, rows, block):
-    def step(i, carry):
+def local_terms(q, k):
+    bend = jnp.tanh(q)
+    s = 0.5 + 0.5 * bend
+    m = k * (0.1 + 0.9 * s)
+    return bend, jnp.where(m > 0.0, 0.5 / m, OUTSIDE), 1.4 * s * (1.0 - s) + STORE
+
+
+def blocks(rows, block, row, carry=None):
+    def step(i, held):
         for j in range(block):
-            r = rows[0] + i * block + j
-            for l in range(L):
-                s = 0.5 + 0.5 * jnp.tanh(q[r, l])
-                m = k[r, l] * (0.1 + 0.9 * s)
-                resist[r, l] = jnp.where(m > 0.0, 0.5 / m, OUTSIDE)
-                diag[r, l] = 1.4 * s * (1.0 - s) + STORE
-        return carry
-
-    lax.fori_loop(0, (rows[1] - rows[0]) // block, step, 0)
-
-
-def couplings(q, resist, right_hand, cx, cy, cyl, cz, diag, v0, rows, block):
+            held = row(rows[0] + i * block + j, held)
+        return held
+
+    return lax.fori_loop(0, (rows[1] - rows[0]) // block, step, carry)
+
+
+def couplings(q, resist, cx, cy, cyl, cz, diag, rows, block, emit):
     last = iota((8, XC), 0) == 7
 
-    def row(r):
+    def row(r, carry):
         q_0, m_0, q_7, m_7 = q[r, 0], resist[r, 0], q[r, 7], resist[r, 7]
         c_7 = jnp.where(last, 0.0, 1.0 / (m_7 + deeper(m_0)))
         f_7 = c_7 * (q_7 - deeper(q_0) + GRAV)
@@ -413,67 +398,56 @@
             out = y * (v - right(v)) + yl * (v - left(v))
             out = out + (x * (v - q[r + 1, l]) + xp * (v - q[r - 1, l])) + (f - f_up)
             diag[r, l] = diag[r, l] + ((y + yl) + (x + xp) + (c + c_up))
-            v0[r, l] = right_hand(r, l, v) - out
+            emit(r, l, out)
             c_up, f_up = c, f
             if l < L - 1:
                 v, m = v_n, m_n
-
-    def step(i, carry):
-        for j in range(block):
-            row(rows[0] + i * block + j)
         return carry
 
     for l in range(L):
         cx[rows[0] - 1, l] = 1.0 / (resist[rows[0] - 1, l] + resist[rows[0], l])
-    lax.fori_loop(0, (rows[1] - rows[0]) // block, step, 0)
-
-
-def apply(v_in, v_out, cx, cy, cyl, cz, diag, rows, block, first):
-    zero = jnp.zeros((8, COLS), F32)
+    blocks(rows, block, row, 0)
+
+
+def apply(v_in, v_out, coefs, shift, rows, block, held, counted):
+    cx, cy, cyl, cz, diag = coefs
 
     def row(r, held):
-        c_up, v_up = higher(cz[r, 7]), higher(v_in[r, 7])
+        at = r - shift
+        c_up, v_up = higher(cz[at, 7]), higher(v_in[r, 7])
         v_0 = v_in[r, 0]
         v = v_0
-        here = jnp.logical_and(r >= HALO, r < HALO + ROWS)
-        square, cross = zero, zero
+        square, cross = held
         for l in range(L):
             v_n = v_in[r, l + 1] if l < L - 1 else deeper(v_0)
-            c = cz[r, l]
-            image = diag[r, l] * v - cy[r, l] * right(v) - cyl[r, l] * left(v)
-            image = image - cx[r, l] * v_in[r + 1, l] - cx[r - 1, l] * v_in[r - 1, l]
+            c = cz[at, l]
+            image = diag[at, l] * v - cy[at, l] * right(v) - cyl[at, l] * left(v)
+            image = image - cx[at, l] * v_in[r + 1, l] - cx[at - 1, l] * v_in[r - 1, l]
             image = image - c * v_n - c_up * v_up
             if v_out is not None:
                 v_out[r, l] = image
-            a, b = own(v), own(image)
-            square = square + a * a
-            cross = cross + a * b
+            if counted:
+                a, b = own(v), own(image)
+                square = square + a * a
+                cross = cross + a * b
             v_up, c_up, v = v, c, v_n
-        if not first:
-            square = jnp.where(here, square, 0.0)
-            cross = jnp.where(here, cross, 0.0)
-        return held[0] + square, held[1] + cross
-
-    def step(i, held):
-        for j in range(block):
-            held = row(rows[0] + i * block + j, held)
-        return held
-
-    return lax.fori_loop(0, (rows[1] - rows[0]) // block, step, (zero, zero))
-
-
-def chain(cx, cy, cyl, cz, diag, v0, v1, v2, moments, spans, blocks):
-    coefs = (cx, cy, cyl, cz, diag)
-    sums = []
-    sums += apply(v0, v1, *coefs, spans[0], blocks[0], False)
-    sums += apply(v1, v2, *coefs, spans[1], blocks[1], False)
-    sums += apply(v2, None, *coefs, spans[2], blocks[2], True)
+        return square, cross
+
+    return blocks(rows, block, row, held)
+
+
+def write_moments(sums, moments):
     row = jnp.zeros((1, 128), F32)
     lane = iota((1, 128), 1)
     for k, held in enumerate(sums):
         value = jnp.sum(jnp.sum(held, axis=0, keepdims=True), axis=1, keepdims=True)
         row = jnp.where(lane == k, value, row)
     moments[...] = jnp.broadcast_to(row, moments.shape)
+
+
+def no_sums():
+    zero = jnp.zeros((8, COLS), F32)
+    return zero, zero
 
 
 def coefficients(gathered):
@@ -511,106 +485,179 @@
     return jnp.where(sub == 0, pltpu.roll(b[r], (8 - l) % 8, 0), 0.0)
 
 
+def prepare_kernel(
+    q_own, k_own, from_left, from_right,
+    q, k, resist, cx, cy, cyl, cz, diag, base,
+):
+    lane = iota((8, 128), 1)
+
+    def fill(l, carry):
+        for f, (field, target) in enumerate(((q_own, q), (k_own, k))):
+            a, c = from_left[f * L + l], from_right[f * L + l]
+            for x in range(ROWS):
+                target[x, l, :, :COLS] = field[x, l]
+                target[x, l, :, COLS:] = halo_tile(a, c, lane, 8 * x, 8 * x)
+        for x in range(ROWS):
+            _, resist[x, l], diag[x, l] = local_terms(q[x, l], k[x, l])
+        return carry
+
+    lax.fori_loop(0, L, fill, 0)
+
+    def emit(r, l, out):
+        base[r, l] = -out
+
+    couplings(q, resist, cx, cy, cyl, cz, diag, (1, ROWS - 1), 2, emit)
+
+
+def prepare(*arrays):
+    outs = (shaped(ROWS, L, 8, XC),) * 9
+    return pl.pallas_call(
+        prepare_kernel,
+        out_shape=outs,
+        in_specs=vmem(4),
+        out_specs=tuple(vmem(9)),
+        compiler_params=params(4),
+        name="prepare",
+    )(*arrays)
+
+
+RSHIFT = 12
+RROWS = 18
+
+
 def first_kernel(
-    q_own, k_own, from_prev, from_next, source, source_prev, source_next, from_left, from_right,
+    q_mid, k_mid, resist_mid, cx_mid, cy_mid, cyl_mid, cz_mid, diag_mid, base,
+    from_prev, from_next, source, corner_prev, corner_next, from_left, from_right,
     q, k, b, v0, v1, v2, moments,
     resist, cx, cy, cyl, cz, diag,
 ):
     lane = iota((8, 128), 1)
 
     def fill(l, carry):
-        for f, (field, target) in enumerate(((q_own, q), (k_own, k))):
-            at = 2 * (8 * f + l)
-            a, c = from_left[at], from_right[at]
-            for x in range(ROWS):
-                target[HALO + x, l, :, :COLS] = field[x, l]
-                target[HALO + x, l, :, COLS:] = halo_tile(a, c, lane, 8 * x)
-            a, c = from_left[at + 1], from_right[at + 1]
-            for i in range(HALO):
-                for side, r, spot in ((from_prev, i, 8 * i), (from_next, HALO + ROWS + i, 64 + 8 * i)):
+        for f, target in enumerate((q, k)):
+            at = 2 * BHALO + f * L + l
+            for side, corner, r, spot in (
+                (from_prev, corner_prev, 0, 8 * (8 - HALO)),
+                (from_next, corner_next, HALO + ROWS - RSHIFT, 0),
+            ):
+                tile = corner[at]
+                for i in range(HALO):
                     for t in range(2):
-                        target[r, l, :, 128 * t : 128 * t + 128] = side[2 * (f * HALO + i) + t, l]
-                    target[r, l, :, COLS:] = halo_tile(a, c, lane, spot)
+                        target[r + i, l, :, 128 * t : 128 * t + 128] = side[2 * (f * HALO + i) + t, l]
+                    left_at = spot + 8 * i
+                    target[r + i, l, :, COLS:] = halo_tile(tile, tile, lane, left_at, 64 + left_at)
+        for r in (*range(HALO), *range(RROWS - HALO, RROWS)):
+            _, resist[r, l], diag[r, l] = local_terms(q[r, l], k[r, l])
+        for r, x in ((7, 0), (8, 1), (9, ROWS - 2), (10, ROWS - 1)):
+            q[r, l] = q_mid[x, l]
+            resist[r, l] = resist_mid[x, l]
+            diag[r, l] = diag_mid[x, l]
         return carry
 
     lax.fori_loop(0, L, fill, 0)
 
-    a, c = from_left[4 * L], from_right[4 * L]
+    a, c = from_left[2 * L], from_right[2 * L]
     for x in range(ROWS):
         b[HALO + x, :, :COLS] = source[x]
-        b[HALO + x, :, COLS:] = halo_tile(a, c, lane, 8 * x)
-    a, c = from_left[4 * L + 1], from_right[4 * L + 1]
-    for i in range(BHALO):
-        for side, r, spot in (
-            (source_prev, HALO - BHALO + i, 8 * i),
-            (source_next, HALO + ROWS + i, 64 + 8 * i),
-        ):
+        b[HALO + x, :, COLS:] = halo_tile(a, c, lane, 8 * x, 8 * x)
+    for side, r, spot in (
+        (corner_prev, HALO - BHALO, 8 * (8 - BHALO)),
+        (corner_next, HALO + ROWS, 0),
+    ):
+        tile = side[CORNER - 1]
+        for i in range(BHALO):
             for t in range(2):
-                b[r, :, 128 * t : 128 * t + 128] = side[2 * i + t]
-            b[r, :, COLS:] = halo_tile(a, c, lane, spot)
+                b[r + i, :, 128 * t : 128 * t + 128] = side[2 * i + t]
+            left_at = spot + 8 * i
+            b[r + i, :, COLS:] = halo_tile(tile, tile, lane, left_at, 64 + left_at)
 
     sub = iota((8, XC), 0)
-
-    def right_hand(r, l, v):
-        return source_at(b, r, l, sub)
-
-    mobilities(q, k, resist, diag, (0, XR), 2)
-    couplings(q, resist, right_hand, cx, cy, cyl, cz, diag, v0, (1, XR - 1), 4)
-    chain(
-        cx, cy, cyl, cz, diag, v0, v1, v2, moments,
-        ((2, XR - 2), (3, XR - 3), (HALO, HALO + ROWS)), (13, 8, 8),
-    )
-
-
-def wide():
-    return shaped(XR, L, 8, XC)
-
-
-def scratch(n):
-    return [pltpu.VMEM((XR, L, 8, XC), F32)] * n
+    coefs = (cx, cy, cyl, cz, diag)
+    mids = (cx_mid, cy_mid, cyl_mid, cz_mid, diag_mid)
+
+    for shift, rows in ((0, (1, HALO + 1)), (RSHIFT, (RROWS - HALO - 1, RROWS - 1))):
+
+        def emit(r, l, out, shift=shift):
+            v0[r + shift, l] = source_at(b, r + shift, l, sub) - out
+
+        couplings(q, resist, *coefs, rows, 1, emit)
+
+    def inner(r, carry):
+        for l in range(L):
+            v0[r, l] = source_at(b, r, l, sub) + base[r - HALO, l]
+        return carry
+
+    low, high = HALO, HALO + ROWS - 1
+    blocks((low + 1, high), 2, inner, 0)
+
+    sums = []
+    for v_in, v_out, deep in ((v0, v1, 5), (v1, v2, 4), (v2, None, 0)):
+        held = apply(v_in, v_out, mids, HALO, (low + 1, high), 7, no_sums(), True)
+        held = apply(v_in, v_out, coefs, 0, (low, low + 1), 1, held, True)
+        held = apply(v_in, v_out, coefs, RSHIFT, (high, high + 1), 1, held, True)
+        if deep:
+            apply(v_in, v_out, coefs, 0, (low - deep, low), deep, no_sums(), False)
+            apply(v_in, v_out, coefs, RSHIFT, (high + 1, high + 1 + deep), deep, no_sums(), False)
+        sums += held
+    write_moments(sums, moments)
 
 
 def first_newton(*arrays):
-    w = wide()
-    outs = (w, w, shaped(XR, L, XC), w, w, w, shaped(128, 128))
+    w = shaped(XR, L, 8, XC)
+    rim = shaped(RROWS, L, 8, XC)
+    outs = (rim, rim, shaped(XR, L, XC), w, w, w, shaped(128, 128))
     return pl.pallas_call(
         first_kernel,
         out_shape=outs,
         in_specs=vmem(len(arrays)),
         out_specs=tuple(vmem(len(outs))),
-        scratch_shapes=scratch(6),
-        compiler_params=params(22),
+        scratch_shapes=[pltpu.VMEM((RROWS, L, 8, XC), F32)] * 6,
+        compiler_params=params(14),
         name="first_newton",
     )(*arrays)
 
 
 def second_kernel(
-    q, k, b, u0, u1, u2, gathered,
+    q_mid, k_mid, q_rim, k_rim, b, u0, u1, u2, gathered,
     q_own, w0, w1, w2, moments,
     q1, resist, cx, cy, cyl, cz, diag, v0, v2,
 ):
     v1 = resist
     c0, c1, c2 = coefficients(gathered)
-
-    def update(r, carry):
-        for l in range(L):
-            q1[r, l] = q[r, l] + c0 * u0[r, l] + c1 * u1[r, l] + c2 * u2[r, l]
-        return carry
-
-    lax.fori_loop(3, XR - 3, update, 0, unroll=2)
     sub = iota((8, XC), 0)
 
-    def right_hand(r, l, v):
-        before = q[r, l]
-        stored = 0.35 * (jnp.tanh(v) - jnp.tanh(before)) + STORE * (v - before)
-        return source_at(b, r, l, sub) - stored
-
-    mobilities(q1, k, resist, diag, (3, XR - 3), 2)
-    couplings(q1, resist, right_hand, cx, cy, cyl, cz, diag, v0, (4, XR - 4), 2)
-    chain(
-        cx, cy, cyl, cz, diag, v0, v1, v2, moments,
-        ((5, XR - 5), (6, XR - 6), (HALO, HALO + ROWS)), (10, 9, 8),
-    )
+    for q, k, shift, rows in (
+        (q_rim, k_rim, 0, (3, HALO)),
+        (q_mid, k_mid, HALO, (HALO, HALO + ROWS)),
+        (q_rim, k_rim, RSHIFT, (HALO + ROWS, XR - 3)),
+    ):
+
+        def update(r, carry, q=q, k=k, shift=shift):
+            for l in range(L):
+                old = q[r - shift, l]
+                step = c0 * u0[r, l] + c1 * u1[r, l] + c2 * u2[r, l]
+                new = old + step
+                q1[r, l] = new
+                bend, resist[r, l], diag[r, l] = local_terms(new, k[r - shift, l])
+                stored = 0.35 * (bend - jnp.tanh(old)) + STORE * step
+                v0[r, l] = source_at(b, r, l, sub) - stored
+            return carry
+
+        blocks(rows, 2, update, 0)
+
+    def emit(r, l, out):
+        v0[r, l] = v0[r, l] - out
+
+    coefs = (cx, cy, cyl, cz, diag)
+    couplings(q1, resist, *coefs, (4, XR - 4), 2, emit)
+    low, high = HALO, HALO + ROWS
+    sums = []
+    for v_in, v_out, deep in ((v0, v1, 2), (v1, v2, 1), (v2, None, 0)):
+        sums += apply(v_in, v_out, coefs, 0, (low, high), 8, no_sums(), True)
+        if deep:
+            apply(v_in, v_out, coefs, 0, (low - deep, low), deep, no_sums(), False)
+            apply(v_in, v_out, coefs, 0, (high, high + deep), deep, no_sums(), False)
+    write_moments(sums, moments)
 
     def keep(x, carry):
         for l in range(L):
@@ -629,7 +676,7 @@
         out_shape=outs,
         in_specs=vmem(len(arrays)),
         out_specs=tuple(vmem(len(outs))),
-        scratch_shapes=scratch(9),
+        scratch_shapes=[pltpu.VMEM((XR, L, 8, XC), F32)] * 9,
         compiler_params=params(28),
         name="second_newton",
     )(*arrays)
@@ -695,24 +742,22 @@
     q_own, k_own, to_next, to_prev, edge_left, edge_right, uptake, surface = turn(
         old, conductivity, forcing, cover_type, vegetated, root_table, payload
     )
-    to_next, to_prev, arrived = lax.optimization_barrier((to_next, to_prev, arrived))
     from_prev, from_next = exchange(to_next, to_prev, "gx")
-    source, to_next, to_prev = canopy_source(
-        arrived, cols, counts, forcing, conductance, uptake, surface
-    )
-    source_prev, source_next = exchange(to_next, to_prev, "gx")
-    to_right, to_left = edges(
-        edge_left, edge_right, from_prev, from_next, source, source_prev, source_next
+    source, to_right, to_left = canopy_source(
+        arrived, cols, counts, forcing, conductance, uptake, surface, edge_left, edge_right
     )
     from_left, from_right = exchange(to_right, to_left, "gy")
-    new_state = owner_update(arrived, state).reshape(canopy_state.shape)
-
+    new_state = owner_update(arrived, state)
+    to_next, to_prev = corners(source, from_left, from_right, in_hbm(new_state))
+    corner_prev, corner_next = exchange(to_next, to_prev, "gx")
+
+    mids = prepare(q_own, k_own, from_left, from_right)
     q, k, b, v0, v1, v2, moments = first_newton(
-        q_own, k_own, from_prev, from_next, source, source_prev, source_next, from_left, from_right
+        *mids, from_prev, from_next, source, corner_prev, corner_next, from_left, from_right
     )
-    q1, w0, w1, w2, moments = second_newton(q, k, b, v0, v1, v2, share(moments))
+    q1, w0, w1, w2, moments = second_newton(mids[0], mids[1], q, k, b, v0, v1, v2, share(moments))
     pressure = unflat(final_update(q1, w0, w1, w2, share(moments)))
-    return pressure, new_state
+    return pressure, new_state.reshape(canopy_state.shape)
 
 
 def solution(mesh):

time: 118 us -> 117 us (level)
  blocking collectives: 19.5 us -> 60.3 us
  waiting for transfers between devices: 27.1 us -> 2.15 us
  starting transfers between devices: 29.5 us -> 17.8 us
  local copies, waits for them, and re-layouts: 3.11 us -> 0 us
  Pallas kernels: 37.8 us -> 35.7 us
    all_to_all x0 -> x1, blocking collectives: none -> 25 us  [body(): lax.all_to_all(payload, 'gx', split_axis=0, concat_axis=0, tiled=True)]
    all_to_all x1 -> x2, blocking collectives: 19.5 us -> 35.3 us  [share(): lax.all_to_all(moments, ('gx', 'gy'), split_axis=0, concat_axis=0, tiled=...]
    ppermute x6, waiting for transfers between devices: 17.9 us -> 2.15 us  [exchange(): return (lax.ppermute(to_high, axis, up), lax.ppermute(to_low, axis, down))]
    all_to_all x2 -> x0, starting transfers between devices: 12.3 us -> none  [the longest x1 7.58 us: body(): lax.all_to_all(payload, 'gx', split_axis=0, concat_axis=0, tiled=True)]
    all_to_all x2 -> x0, waiting for transfers between devices: 9.24 us -> none  [the longest x1 6.89 us: share(): lax.all_to_all(moments, ('gx', 'gy'), split_axis=0, concat_axis=0, tiled=...]
    pallas_call x1, Pallas kernels: 12.8 us -> 9.51 us  [first_newton(): pl.pallas_call(first_kernel, out_shape=outs, in_specs=vmem(len(arrays)),...]
    unnamed x6 -> x0, local copies, waits for them, and re-layouts: 3.11 us -> none
    pallas_call x1 -> x2, Pallas kernels: 1.1 us -> 3.44 us  [the longest x1 3.34 us: prepare(): pl.pallas_call(prepare_kernel, out_shape=outs, in_specs=vmem(4), out_spec...]
  transfers between devices with their start and end apart: 8 -> 6, of which waited for: 6 -> 2; matrix products, arithmetic and copies ran while one was open for 0% -> 0% of each run, Pallas kernels for 7% -> 7%
where the time goes in v4:
time: 117 us
  blocking collectives  60.3 us (52%)
  Pallas kernels  35.7 us (31%)
  starting transfers between devices  17.8 us (15%)
  waiting for transfers between devices  2.15 us (2%)
    all_to_all x2, blocking collectives, share(): lax.all_to_all(moments, ('gx', 'gy'), split_axis=0, concat_axis=0, tiled=...  35.3 us
    all_to_all x1, blocking collectives, body(): lax.all_to_all(payload, 'gx', split_axis=0, concat_axis=0, tiled=True)  25 us
    ppermute x6, starting transfers between devices, exchange(): return (lax.ppermute(to_high, axis, up), lax.ppermute(to_low, axis, down))  17.8 us
    pallas_call x1, Pallas kernels, second_newton(): pl.pallas_call(second_kernel, out_shape=outs, in_specs=vmem(len(arrays)),...  9.75 us
    pallas_call x1, Pallas kernels, first_newton(): pl.pallas_call(first_kernel, out_shape=outs, in_specs=vmem(len(arrays)),...  9.51 us
    pallas_call x1, Pallas kernels, turn(): pl.pallas_call(turn_kernel, out_shape=outs, in_specs=vmem(5) + [smem(), p...  3.59 us
    pallas_call x1, Pallas kernels, prepare(): pl.pallas_call(prepare_kernel, out_shape=outs, in_specs=vmem(4), out_spec...  3.34 us
    pallas_call x1, Pallas kernels, canopy_source(): pl.pallas_call(source_kernel, out_shape=(shaped(ROWS, ROOT, COLS), shaped...  2.56 us
  transfers between devices with their start and end apart: 6, of which 2 were waited for; matrix products, arithmetic and copies ran while one was open for 0% of the time, Pallas kernels for 7%

profile of v4, /device:TPU:1, one launch (start us, length us, event | category | flops | bytes accessed | tf_op | source)
XLA Modules:
  0.0 116.7 jit_solution(18214258369523438935)
XLA Ops:
  0.6 2.4 %canopy_send.1 = (f32[16,8,256]{2,1,0:T(8,128)S(1)}, f32[16,256]{1,0:T(8,128)S(1)}) custom-call(f32[8,16,256]{2,1,0:T(8,128)} %forcing.5, s32[16,256]{1,0:T(8,128)} %cover.3, f32[8,16]{1,0:T(8,128)} %bitcast.43, s32[16]{0:T(128)} %bitcast.45, s32[16,1,256]{2,1,0:T(1,128)} %bitcast.41, f32[16,16,256]{2,1,0:T(8,128)} %bitcast.37), custom_call_target="tpu_custom_call" | custom-call | tf_op jit(solution)/shard_map/canopy_send/pallas_call | solution.py:131
  3.1 3.6 %turn.1 = (f32[16,8,8,256]{3,2,1,0:T(8,128)S(1)}, f32[16,8,8,256]{3,2,1,0:T(8,128)S(1)}, f32[28,8,8,128]{3,2,1,0:T(8,128)S(1)}, f32[28,8,8,128]{3,2,1,0:T(8,128)...) custom-call(f32[2048,128]{1,0:T(8,128)} %bitcast.35, ...), custom_call_target="tpu_custom_call" | custom-call | tf_op jit(solution)/shard_map/turn/pallas_call | solution.py:313
  6.7 4.1 %collective-permute-start.2 = (f32[28,8,8,128]{3,2,1,0:T(8,128)S(1)}, f32[28,8,8,128]{3,2,1,0:T(8,128)S(1)}, u32[]{:S(2)}, u32[]{:S(2)}) collective-permute-start(f32[28,8,8,128]{3,2,1,0:T(8,128)S(1)} %get-tuple-element.57), channel_id=1, source_target_pairs={{0,8},{8,16},{16,24},{24,32},{32,40},{40,48},{48,56},{56,64},{64,7... | collective-permute-start | bytes 2752520 | tf_op jit(solution)/shard_map/ppermute | solution.py:713
  10.8 1.3 %collective-permute-start.3 = (f32[28,8,8,128]{3,2,1,0:T(8,128)S(1)}, f32[28,8,8,128]{3,2,1,0:T(8,128)S(1)}, u32[]{:S(2)}, u32[]{:S(2)}) collective-permute-start(f32[28,8,8,128]{3,2,1,0:T(8,128)S(1)} %get-tuple-element.58), channel_id=1, source_target_pairs={{8,0},{16,8},{24,16},{32,24},{40,32},{48,40},{56,48},{64,56},{72,6... | collective-permute-start | bytes 2752520 | tf_op jit(solution)/shard_map/ppermute | solution.py:713
  12.1 25.0 %all_to_all.27.arrived = f32[16,8,256]{2,1,0:T(8,128)S(1)} all-to-all(f32[16,8,256]{2,1,0:T(8,128)S(1)} %get-tuple-element.38.after), channel_id=1, replica_groups=mesh['gx'=16,'gy'=8] {'gx'}, dimensions={0} | all-to-all | bytes 262144 | tf_op jit(solution)/shard_map/all_to_all | solution.py:741
  37.1 2.6 %canopy_source.1 = (f32[16,8,256]{2,1,0:T(8,128)S(1)}, f32[17,8,128]{2,1,0:T(8,128)S(1)}, f32[17,8,128]{2,1,0:T(8,128)S(1)}) custom-call(f32[16,8,256]{2,1,0:T(8,128)S(1)} %all_to_all.27.arrived, s32[16,1,256]{2,1,0:T(1,128)} %bitcast.42, s32[16]{0:T(128)} %bitcast.46, f32[8,16,256]{2,1,0:T(8,128)} %forcing.5, f32[16,256]{1,0:T(8,128)S(1)} %get-tuple-element.41.conductance, ...), custom_call_target="tpu_custom_call" | custom-call | tf_op jit(solution)/shard_map/canopy_source/pallas_call | solution.py:207
  39.6 5.7 %collective-permute-start = (f32[17,8,128]{2,1,0:T(8,128)S(1)}, f32[17,8,128]{2,1,0:T(8,128)S(1)}, u32[]{:S(2)}, u32[]{:S(2)}) collective-permute-start(f32[17,8,128]{2,1,0:T(8,128)S(1)} %get-tuple-element.46), channel_id=1, source_target_pairs={{0,1},{1,2},{2,3},{3,4},{4,5},{5,6},{6,7},{8,9},{9,10},{10,11},{11... | collective-permute-start | bytes 208904 | tf_op jit(solution)/shard_map/ppermute | solution.py:713
  45.4 1.9 %collective-permute-start.1 = (f32[17,8,128]{2,1,0:T(8,128)S(1)}, f32[17,8,128]{2,1,0:T(8,128)S(1)}, u32[]{:S(2)}, u32[]{:S(2)}) collective-permute-start(f32[17,8,128]{2,1,0:T(8,128)S(1)} %get-tuple-element.47), channel_id=1, source_target_pairs={{1,0},{2,1},{3,2},{4,3},{5,4},{6,5},{7,6},{9,8},{10,9},{11,10},{12... | collective-permute-start | bytes 208904 | tf_op jit(solution)/shard_map/ppermute | solution.py:713
  47.3 2.5 %owner_update.1.after = f32[16,16,256]{2,1,0:T(8,128)} custom-call(f32[16,8,256]{2,1,0:T(8,128)S(1)} %all_to_all.27.arrived, f32[16,16,256]{2,1,0:T(8,128)} %bitcast.38), custom_call_target="tpu_custom_call" | custom-call | tf_op jit(solution)/shard_map/owner_update/pallas_call | solution.py:238
  49.8 0.0 collective-permute-done.from_left
  49.8 1.2 %collective-permute-done.1.from_right = f32[17,8,128]{2,1,0:T(8,128)S(1)} collective-permute-done((f32[17,8,128]{2,1,0:T(8,128)S(1)}, f32[17,8,128]{2,1,0:T(8,128)S(1)}, u32[]{:S(2)}, u32[]{:S(2)}) %collective-permute-start.1) | collective-permute-done | bytes 69664 | tf_op jit(solution)/shard_map/ppermute | solution.py:713
  51.0 0.1 corners.1
  51.1 3.4 %collective-permute-start.4 = (f32[29,8,128]{2,1,0:T(8,128)S(1)}, f32[29,8,128]{2,1,0:T(8,128)S(1)}, u32[]{:S(2)}, u32[]{:S(2)}) collective-permute-start(f32[29,8,128]{2,1,0:T(8,128)S(1)} %get-tuple-element.60), channel_id=1, source_target_pairs={{0,8},{8,16},{16,24},{24,32},{32,40},{40,48},{48,56},{56,64},{64,7... | collective-permute-start | bytes 356360 | tf_op jit(solution)/shard_map/ppermute | solution.py:713
  54.6 1.3 %collective-permute-start.5 = (f32[29,8,128]{2,1,0:T(8,128)S(1)}, f32[29,8,128]{2,1,0:T(8,128)S(1)}, u32[]{:S(2)}, u32[]{:S(2)}) collective-permute-start(f32[29,8,128]{2,1,0:T(8,128)S(1)} %get-tuple-element.61), channel_id=1, source_target_pairs={{8,0},{16,8},{24,16},{32,24},{40,32},{48,40},{56,48},{64,56},{72,6... | collective-permute-start | bytes 356360 | tf_op jit(solution)/shard_map/ppermute | solution.py:713
  55.9 3.3 %prepare.1 = (f32[16,8,8,384]{3,2,1,0:T(8,128)S(1)}, f32[16,8,8,384]{3,2,1,0:T(8,128)S(1)}, f32[16,8,8,384]{3,2,1,0:T(8,128)S(1)}, f32[16,8,8,384]{3,2,1,0:T(8,1...) custom-call(f32[16,8,8,256]{3,2,1,0:T(8,128)S(1)} %get-tuple-element, ...), custom_call_target="tpu_custom_call" | custom-call | tf_op jit(solution)/shard_map/prepare/pallas_call | solution.py:514
  59.2 0.0 collective-permute-done.4.corner_prev
  59.2 0.9 collective-permute-done.5.corner_next
  60.1 0.0 collective-permute-done.2.from_prev
  60.2 0.0 collective-permute-done.3.from_next
  60.2 9.5 %first_newton.1 = (f32[18,8,8,384]{3,2,1,0:T(8,128)S(1)}, f32[18,8,8,384]{3,2,1,0:T(8,128)S(1)}, f32[30,8,384]{2,1,0:T(8,128)S(1)}, f32[30,8,8,384]{3,2,1,0:T(8,...) custom-call(f32[16,8,8,384]{3,2,1,0:T(8,128)S(1)} %get-tuple-element.48.q_mid, ...), custom_call_target="tpu_custom_call" | custom-call | tf_op jit(solution)/shard_map/first_newton/pallas_call | solution.py:609
  69.7 21.4 %all_to_all.28 = f32[128,1,128]{2,1,0:T(1,128)S(1)} all-to-all(f32[128,1,128]{2,1,0:T(1,128)S(1)} %bitcast.33), channel_id=1, replica_groups=mesh['gx'=16,'gy'=8] {'gx','gy'}, dimensions={0} | all-to-all | bytes 131072 | tf_op jit(solution)/shard_map/all_to_all | solution.py:717
  91.0 9.8 %second_newton.1 = (f32[16,8,8,256]{3,2,1,0:T(8,128)S(1)}, f32[16,8,8,256]{3,2,1,0:T(8,128)S(1)}, f32[16,8,8,256]{3,2,1,0:T(8,128)S(1)}, f32[16,8,8,256]{3,2,1,0:T(8,128)S(1)}, f32[128,128]{1,0:T(8,128)S(1)}) custom-call(f32[16,8,8,384]{3,2,1,0:T(8,128)S(1)} %get-tuple-element.48.q_mid, f32[16,8,8,384]{3,2,1,0:T(8,128)S(1)} %get-tuple-element.49.k_mid, ...), custom_call_target="tpu_custom_call" | custom-call | tf_op jit(solution)/shard_map/second_newton/pallas_call | solution.py:674
  100.8 13.9 %all_to_all.29 = f32[128,1,128]{2,1,0:T(1,128)S(1)} all-to-all(f32[128,1,128]{2,1,0:T(1,128)S(1)} %bitcast.34), channel_id=1, replica_groups=mesh['gx'=16,'gy'=8] {'gx','gy'}, dimensions={0} | all-to-all | bytes 131072 | tf_op jit(solution)/shard_map/all_to_all | solution.py:717
  114.7 2.0 %final_update.1 = f32[2048,128]{1,0:T(8,128)} custom-call(f32[16,8,8,256]{3,2,1,0:T(8,128)S(1)} %get-tuple-element.69.q, f32[16,8,8,256]{3,2,1,0:T(8,128)S(1)} %get-tuple-element.70.v0, f32[16,8,8,256]{3,2,1,0:T(8,128)S(1)} %get-tuple-element.71.v1, f32[16,8,8,256]{3,2,1,0:T(8,128)S(1)} %get-tuple-element.72.v2, f32[128,128]{1,0:T(8,128)S(1)} %bitcast.32), custom_call_target="tpu_custom_call" | custom-call | tf_op jit(solution)/shard_map/final_update/pallas_call | solution.py:699
Async XLA Ops:
  6.7 53.5 %collective-permute-start.2 = (f32[28,8,8,128]{3,2,1,0:T(8,128)S(1)}, f32[28,8,8,128]{3,2,1,0:T(8,128)S(1)}, u32[]{:S(2)}, u32[]{:S(2)}) collective-permute-start(f32[28,8,8,128]{3,2,1,0:T(8,128)S(1)} %get-tuple-element.57), channel_id=1, source_target_pairs={{0,8},{8,16},{16,24},{24,32},{32,40},{40,48},{48,56},{56,64},{64,7... | collective-permute-start | bytes 2752520 | tf_op jit(solution)/shard_map/ppermute | solution.py:713
  10.8 49.4 %collective-permute-start.3 = (f32[28,8,8,128]{3,2,1,0:T(8,128)S(1)}, f32[28,8,8,128]{3,2,1,0:T(8,128)S(1)}, u32[]{:S(2)}, u32[]{:S(2)}) collective-permute-start(f32[28,8,8,128]{3,2,1,0:T(8,128)S(1)} %get-tuple-element.58), channel_id=1, source_target_pairs={{8,0},{16,8},{24,16},{32,24},{40,32},{48,40},{56,48},{64,56},{72,6... | collective-permute-start | bytes 2752520 | tf_op jit(solution)/shard_map/ppermute | solution.py:713
  39.6 10.2 %collective-permute-start = (f32[17,8,128]{2,1,0:T(8,128)S(1)}, f32[17,8,128]{2,1,0:T(8,128)S(1)}, u32[]{:S(2)}, u32[]{:S(2)}) collective-permute-start(f32[17,8,128]{2,1,0:T(8,128)S(1)} %get-tuple-element.46), channel_id=1, source_target_pairs={{0,1},{1,2},{2,3},{3,4},{4,5},{5,6},{6,7},{8,9},{9,10},{10,11},{11... | collective-permute-start | bytes 208904 | tf_op jit(solution)/shard_map/ppermute | solution.py:713
  45.4 5.6 %collective-permute-start.1 = (f32[17,8,128]{2,1,0:T(8,128)S(1)}, f32[17,8,128]{2,1,0:T(8,128)S(1)}, u32[]{:S(2)}, u32[]{:S(2)}) collective-permute-start(f32[17,8,128]{2,1,0:T(8,128)S(1)} %get-tuple-element.47), channel_id=1, source_target_pairs={{1,0},{2,1},{3,2},{4,3},{5,4},{6,5},{7,6},{9,8},{10,9},{11,10},{12... | collective-permute-start | bytes 208904 | tf_op jit(solution)/shard_map/ppermute | solution.py:713
  51.1 8.1 %collective-permute-start.4 = (f32[29,8,128]{2,1,0:T(8,128)S(1)}, f32[29,8,128]{2,1,0:T(8,128)S(1)}, u32[]{:S(2)}, u32[]{:S(2)}) collective-permute-start(f32[29,8,128]{2,1,0:T(8,128)S(1)} %get-tuple-element.60), channel_id=1, source_target_pairs={{0,8},{8,16},{16,24},{24,32},{32,40},{40,48},{48,56},{56,64},{64,7... | collective-permute-start | bytes 356360 | tf_op jit(solution)/shard_map/ppermute | solution.py:713
  54.6 5.6 %collective-permute-start.5 = (f32[29,8,128]{2,1,0:T(8,128)S(1)}, f32[29,8,128]{2,1,0:T(8,128)S(1)}, u32[]{:S(2)}, u32[]{:S(2)}) collective-permute-start(f32[29,8,128]{2,1,0:T(8,128)S(1)} %get-tuple-element.61), channel_id=1, source_target_pairs={{8,0},{16,8},{24,16},{32,24},{40,32},{48,40},{56,48},{64,56},{72,6... | collective-permute-start | bytes 356360 | tf_op jit(solution)/shard_map/ppermute | solution.py:713

commit v5 on v4

--- a/solution.py
+++ b/solution.py
@@ -320,7 +320,7 @@
     )(*arrays)
 
 
-def corner_kernel(source, from_left, from_right, after, to_next, to_prev):
+def corner_kernel(source, from_left, from_right, to_next, to_prev):
     low = iota((8, 128), 1) < 64
     for i in range(BHALO):
         for t in range(2):
@@ -338,7 +338,7 @@
     return pl.pallas_call(
         corner_kernel,
         out_shape=outs,
-        in_specs=vmem(3) + [pl.BlockSpec(memory_space=pl.ANY)],
+        in_specs=vmem(3),
         out_specs=tuple(vmem(2)),
         compiler_params=params(16),
         name="corners",
@@ -682,26 +682,36 @@
     )(*arrays)
 
 
-def final_kernel(q, v0, v1, v2, gathered, out):
+def final_kernel(q, v0, v1, v2, gathered, out, held, sems):
     c0, c1, c2 = coefficients(gathered)
 
-    def row(x, carry):
-        for l in range(L):
+    def send(l):
+        part = pl.ds(32 * l, 32)
+        return pltpu.make_async_copy(held.at[:, part], out.at[:, part], sems.at[l])
+
+    for l in range(L):
+
+        def row(x, carry, l=l):
             value = q[x, l] + c0 * v0[x, l] + c1 * v1[x, l] + c2 * v2[x, l]
-            out[chunk(x, l, 0), :] = value[:, :128]
-            out[chunk(x, l, 1), :] = value[:, 128:]
-        return carry
-
-    lax.fori_loop(0, ROWS, row, 0)
+            at = 32 * l + 16 * (x // 8) + x % 8
+            held[:, at, :] = value[:, :128]
+            held[:, at + 8, :] = value[:, 128:]
+            return carry
+
+        lax.fori_loop(0, ROWS, row, 0, unroll=4)
+        send(l).start()
+    for l in range(L):
+        send(l).wait()
 
 
 def final_update(*arrays):
     return pl.pallas_call(
         final_kernel,
-        out_shape=shaped(32 * LEV, 128),
+        out_shape=shaped(8, 32 * L, 128),
         in_specs=vmem(len(arrays)),
-        out_specs=vmem()[0],
-        compiler_params=params(16),
+        out_specs=pl.BlockSpec(memory_space=pltpu.HBM),
+        scratch_shapes=[pltpu.VMEM((8, 32 * L, 128), F32), pltpu.SemaphoreType.DMA((L,))],
+        compiler_params=params(4),
         name="final_update",
     )(*arrays)
 
@@ -742,19 +752,21 @@
     q_own, k_own, to_next, to_prev, edge_left, edge_right, uptake, surface = turn(
         old, conductivity, forcing, cover_type, vegetated, root_table, payload
     )
+    to_next, to_prev, arrived = lax.optimization_barrier((to_next, to_prev, arrived))
     from_prev, from_next = exchange(to_next, to_prev, "gx")
     source, to_right, to_left = canopy_source(
         arrived, cols, counts, forcing, conductance, uptake, surface, edge_left, edge_right
     )
     from_left, from_right = exchange(to_right, to_left, "gy")
-    new_state = owner_update(arrived, state)
-    to_next, to_prev = corners(source, from_left, from_right, in_hbm(new_state))
+    to_next, to_prev = corners(source, from_left, from_right)
     corner_prev, corner_next = exchange(to_next, to_prev, "gx")
 
     mids = prepare(q_own, k_own, from_left, from_right)
     q, k, b, v0, v1, v2, moments = first_newton(
         *mids, from_prev, from_next, source, corner_prev, corner_next, from_left, from_right
     )
+    moments, arrived = lax.optimization_barrier((moments, arrived))
+    new_state = owner_update(arrived, state)
     q1, w0, w1, w2, moments = second_newton(mids[0], mids[1], q, k, b, v0, v1, v2, share(moments))
     pressure = unflat(final_update(q1, w0, w1, w2, share(moments)))
     return pressure, new_state.reshape(canopy_state.shape)

time: 117 us -> 107 us (0.915)
  blocking collectives: 60.3 us -> 21 us
  waiting for transfers between devices: 2.15 us -> 15.1 us
  starting transfers between devices: 17.8 us -> 28.9 us
  local copies, waits for them, and re-layouts: 0 us -> 3.11 us
  Pallas kernels: 35.7 us -> 37.2 us
    all_to_all x1 -> x0, blocking collectives: 25 us -> none  [body(): lax.all_to_all(payload, 'gx', split_axis=0, concat_axis=0, tiled=True)]
    all_to_all x2 -> x1, blocking collectives: 35.3 us -> 21 us  [share(): lax.all_to_all(moments, ('gx', 'gy'), split_axis=0, concat_axis=0, tiled=...]
    all_to_all x0 -> x2, starting transfers between devices: none -> 12.3 us  [the longest x1 7.58 us: body(): lax.all_to_all(payload, 'gx', split_axis=0, concat_axis=0, tiled=True)]
    all_to_all x0 -> x2, waiting for transfers between devices: none -> 9.24 us  [the longest x1 6.89 us: share(): lax.all_to_all(moments, ('gx', 'gy'), split_axis=0, concat_axis=0, tiled=...]
    ppermute x6, waiting for transfers between devices: 2.15 us -> 5.88 us  [exchange(): return (lax.ppermute(to_high, axis, up), lax.ppermute(to_low, axis, down))]
    unnamed x0 -> x6, local copies, waits for them, and re-layouts: none -> 3.11 us
    ppermute x6, starting transfers between devices: 17.8 us -> 16.6 us  [exchange(): return (lax.ppermute(to_high, axis, up), lax.ppermute(to_low, axis, down))]
  transfers between devices with their start and end apart: 6 -> 8, of which waited for: 2 -> 4; matrix products, arithmetic and copies ran while one was open for 0% -> 0% of each run, Pallas kernels for 7% -> 11%
where the time goes in v5:
time: 107 us; the launch traced here: 106 us
  Pallas kernels  37.2 us (35%)
  starting transfers between devices  28.9 us (27%)
  blocking collectives  21 us (20%)
  waiting for transfers between devices  15.1 us (14%)
  local copies, waits for them, and re-layouts  3.11 us (3%)
    all_to_all x1, blocking collectives, share(): lax.all_to_all(moments, ('gx', 'gy'), split_axis=0, concat_axis=0, tiled=...  21 us
    ppermute x6, starting transfers between devices, exchange(): return (lax.ppermute(to_high, axis, up), lax.ppermute(to_low, axis, down))  16.6 us
    pallas_call x1, Pallas kernels, second_newton(): pl.pallas_call(second_kernel, out_shape=outs, in_specs=vmem(len(arrays)),...  10.4 us
    pallas_call x1, Pallas kernels, first_newton(): pl.pallas_call(first_kernel, out_shape=outs, in_specs=vmem(len(arrays)),...  9.37 us
    all_to_all x1, starting transfers between devices, body(): lax.all_to_all(payload, 'gx', split_axis=0, concat_axis=0, tiled=True)  7.58 us
    all_to_all x1, waiting for transfers between devices, share(): lax.all_to_all(moments, ('gx', 'gy'), split_axis=0, concat_axis=0, tiled=...  6.89 us
    ppermute x6, waiting for transfers between devices, exchange(): return (lax.ppermute(to_high, axis, up), lax.ppermute(to_low, axis, down))  5.88 us
    all_to_all x1, starting transfers between devices, share(): lax.all_to_all(moments, ('gx', 'gy'), split_axis=0, concat_axis=0, tiled=...  4.75 us
  transfers between devices with their start and end apart: 8, of which 4 were waited for; matrix products, arithmetic and copies ran while one was open for 0% of the time, Pallas kernels for 11%

profile of v5, /device:TPU:1, one launch (start us, length us, event | category | flops | bytes accessed | tf_op | source)
XLA Modules:
  0.0 106.1 jit_solution(6885022325379861822)
XLA Ops:
  0.6 3.1 %canopy_send.1 = (f32[16,8,256]{2,1,0:T(8,128)}, f32[16,256]{1,0:T(8,128)S(1)}) custom-call(f32[8,16,256]{2,1,0:T(8,128)} %forcing.5, s32[16,256]{1,0:T(8,128)} %cover.3, f32[8,16]{1,0:T(8,128)} %bitcast.42, s32[16]{0:T(128)} %bitcast.44, s32[16,1,256]{2,1,0:T(1,128)} %bitcast.40, f32[16,16,256]{2,1,0:T(8,128)} %bitcast.36), custom_call_target="tpu_custom_call" | custom-call | tf_op jit(solution)/shard_map/canopy_send/pallas_call | solution.py:131
  3.7 7.6 %all-to-all-start = ((f32[16,8,256]{2,1,0:T(8,128)}), f32[16,8,256]{2,1,0:T(8,128)S(1)}, u32[]{:S(2)}, u32[]{:S(2)}) async-start(f32[16,8,256]{2,1,0:T(8,128)} %get-tuple-element.43.after), calls=%async_computation | async-start | bytes 262144 | tf_op jit(solution)/shard_map/all_to_all | solution.py:751
  11.3 3.6 %turn.1 = (f32[16,8,8,256]{3,2,1,0:T(8,128)S(1)}, f32[16,8,8,256]{3,2,1,0:T(8,128)S(1)}, f32[28,8,8,128]{3,2,1,0:T(8,128)S(1)}, f32[28,8,8,128]{3,2,1,0:T(8,128)...) custom-call(f32[2048,128]{1,0:T(8,128)} %bitcast.34, ...), custom_call_target="tpu_custom_call" | custom-call | tf_op jit(solution)/shard_map/turn/pallas_call | solution.py:313
  14.9 0.9 copy-done.2
  15.8 2.3 %all-to-all-done.arrived = f32[16,8,256]{2,1,0:T(8,128)S(1)} async-done(((f32[16,8,256]{2,1,0:T(8,128)}), f32[16,8,256]{2,1,0:T(8,128)S(1)}, u32[]{:S(2)}, u32[]{:S(2)}) %all-to-all-start) | async-done | bytes 131104 | tf_op jit(solution)/shard_map/all_to_all | solution.py:751
  18.2 2.1 %collective-permute-start.2 = (f32[28,8,8,128]{3,2,1,0:T(8,128)}, f32[28,8,8,128]{3,2,1,0:T(8,128)S(1)}, u32[]{:S(2)}, u32[]{:S(2)}) collective-permute-start(f32[28,8,8,128]{3,2,1,0:T(8,128)} %copy-done.2), channel_id=1, source_target_pairs={{0,8},{8,16},{16,24},{24,32},{32,40},{40,48},{48,56},{56,64},{64,7... | collective-permute-start | bytes 2752520 | tf_op jit(solution)/shard_map/ppermute | solution.py:723
  20.3 1.3 %collective-permute-start.3 = (f32[28,8,8,128]{3,2,1,0:T(8,128)S(1)}, f32[28,8,8,128]{3,2,1,0:T(8,128)S(1)}, u32[]{:S(2)}, u32[]{:S(2)}) collective-permute-start(f32[28,8,8,128]{3,2,1,0:T(8,128)S(1)} %get-tuple-element.66), channel_id=1, source_target_pairs={{8,0},{16,8},{24,16},{32,24},{40,32},{48,40},{56,48},{64,56},{72,6... | collective-permute-start | bytes 2752520 | tf_op jit(solution)/shard_map/ppermute | solution.py:723
  21.6 2.6 %canopy_source.1 = (f32[16,8,256]{2,1,0:T(8,128)S(1)}, f32[17,8,128]{2,1,0:T(8,128)S(1)}, f32[17,8,128]{2,1,0:T(8,128)S(1)}) custom-call(f32[16,8,256]{2,1,0:T(8,128)S(1)} %all-to-all-done.arrived, s32[16,1,256]{2,1,0:T(1,128)} %bitcast.41, s32[16]{0:T(128)} %bitcast.45, f32[8,16,256]{2,1,0:T(8,128)} %forcing.5, ...), custom_call_target="tpu_custom_call" | custom-call | tf_op jit(solution)/shard_map/canopy_source/pallas_call | solution.py:207
  24.1 5.7 %collective-permute-start = (f32[17,8,128]{2,1,0:T(8,128)S(1)}, f32[17,8,128]{2,1,0:T(8,128)S(1)}, u32[]{:S(2)}, u32[]{:S(2)}) collective-permute-start(f32[17,8,128]{2,1,0:T(8,128)S(1)} %get-tuple-element.54), channel_id=1, source_target_pairs={{0,1},{1,2},{2,3},{3,4},{4,5},{5,6},{6,7},{8,9},{9,10},{10,11},{11... | collective-permute-start | bytes 208904 | tf_op jit(solution)/shard_map/ppermute | solution.py:723
  29.9 1.9 %collective-permute-start.1 = (f32[17,8,128]{2,1,0:T(8,128)S(1)}, f32[17,8,128]{2,1,0:T(8,128)S(1)}, u32[]{:S(2)}, u32[]{:S(2)}) collective-permute-start(f32[17,8,128]{2,1,0:T(8,128)S(1)} %get-tuple-element.55), channel_id=1, source_target_pairs={{1,0},{2,1},{3,2},{4,3},{5,4},{6,5},{7,6},{9,8},{10,9},{11,10},{12... | collective-permute-start | bytes 208904 | tf_op jit(solution)/shard_map/ppermute | solution.py:723
  31.8 4.0 %collective-permute-done.1.from_right = f32[17,8,128]{2,1,0:T(8,128)S(1)} collective-permute-done((f32[17,8,128]{2,1,0:T(8,128)S(1)}, f32[17,8,128]{2,1,0:T(8,128)S(1)}, u32[]{:S(2)}, u32[]{:S(2)}) %collective-permute-start.1) | collective-permute-done | bytes 69664 | tf_op jit(solution)/shard_map/ppermute | solution.py:723
  35.9 4.3 %collective-permute-start.4 = (f32[29,8,128]{2,1,0:T(8,128)S(1)}, f32[29,8,128]{2,1,0:T(8,128)S(1)}, u32[]{:S(2)}, u32[]{:S(2)}) collective-permute-start(f32[29,8,128]{2,1,0:T(8,128)S(1)} %get-tuple-element.68), channel_id=1, source_target_pairs={{0,8},{8,16},{16,24},{24,32},{32,40},{40,48},{48,56},{56,64},{64,7... | collective-permute-start | bytes 356360 | tf_op jit(solution)/shard_map/ppermute | solution.py:723
  40.2 1.3 %collective-permute-start.5 = (f32[29,8,128]{2,1,0:T(8,128)S(1)}, f32[29,8,128]{2,1,0:T(8,128)S(1)}, u32[]{:S(2)}, u32[]{:S(2)}) collective-permute-start(f32[29,8,128]{2,1,0:T(8,128)S(1)} %get-tuple-element.69), channel_id=1, source_target_pairs={{8,0},{16,8},{24,16},{32,24},{40,32},{48,40},{56,48},{64,56},{72,6... | collective-permute-start | bytes 356360 | tf_op jit(solution)/shard_map/ppermute | solution.py:723
  41.5 3.4 %prepare.1 = (f32[16,8,8,384]{3,2,1,0:T(8,128)S(1)}, f32[16,8,8,384]{3,2,1,0:T(8,128)S(1)}, f32[16,8,8,384]{3,2,1,0:T(8,128)S(1)}, f32[16,8,8,384]{3,2,1,0:T(8,1...) custom-call(f32[16,8,8,256]{3,2,1,0:T(8,128)S(1)} %get-tuple-element, ...), custom_call_target="tpu_custom_call" | custom-call | tf_op jit(solution)/shard_map/prepare/pallas_call | solution.py:514
  44.9 1.9 %collective-permute-done.5.corner_next = f32[29,8,128]{2,1,0:T(8,128)S(1)} collective-permute-done((f32[29,8,128]{2,1,0:T(8,128)S(1)}, f32[29,8,128]{2,1,0:T(8,128)S(1)}, u32[]{:S(2)}, u32[]{:S(2)}) %collective-permute-start.5) | collective-permute-done | bytes 118816 | tf_op jit(solution)/shard_map/ppermute | solution.py:723
  46.8 9.4 %first_newton.1 = (f32[18,8,8,384]{3,2,1,0:T(8,128)S(1)}, f32[18,8,8,384]{3,2,1,0:T(8,128)S(1)}, f32[30,8,384]{2,1,0:T(8,128)S(1)}, f32[30,8,8,384]{3,2,1,0:T(8,...) custom-call(f32[16,8,8,384]{3,2,1,0:T(8,128)S(1)} %get-tuple-element.56.q_mid, ...), custom_call_target="tpu_custom_call" | custom-call | tf_op jit(solution)/shard_map/first_newton/pallas_call | solution.py:609
  56.2 21.0 %all_to_all.27 = f32[128,1,128]{2,1,0:T(1,128)S(1)} all-to-all(f32[128,1,128]{2,1,0:T(1,128)S(1)} %bitcast.33), channel_id=1, replica_groups=mesh['gx'=16,'gy'=8] {'gx','gy'}, dimensions={0} | all-to-all | bytes 131072 | tf_op jit(solution)/shard_map/all_to_all | solution.py:727
  77.2 10.4 %second_newton.1 = (f32[16,8,8,256]{3,2,1,0:T(8,128)S(1)}, f32[16,8,8,256]{3,2,1,0:T(8,128)S(1)}, f32[16,8,8,256]{3,2,1,0:T(8,128)S(1)}, f32[16,8,8,256]{3,2,1,0:T(8,128)S(1)}, f32[128,128]{1,0:T(8,128)}) custom-call(f32[16,8,8,384]{3,2,1,0:T(8,128)S(1)} %get-tuple-element.56.q_mid, f32[16,8,8,384]{3,2,1,0:T(8,128)S(1)} %get-tuple-element.57.k_mid, ...), custom_call_target="tpu_custom_call" | custom-call | tf_op jit(solution)/shard_map/second_newton/pallas_call | solution.py:674
  87.5 1.0 copy-done
  88.5 4.8 %all-to-all-start.2 = ((f32[128,1,128]{2,1,0:T(1,128)}), f32[128,1,128]{2,1,0:T(1,128)S(1)}, u32[]{:S(2)}, u32[]{:S(2)}) async-start(f32[128,1,128]{2,1,0:T(1,128)} %bitcast.15), calls=%async_computation.2 | async-start | bytes 131072 | tf_op jit(solution)/shard_map/all_to_all | solution.py:727
  93.3 2.5 %owner_update.1 = f32[16,16,256]{2,1,0:T(8,128)} custom-call(f32[16,8,256]{2,1,0:T(8,128)S(1)} %all-to-all-done.arrived, f32[16,16,256]{2,1,0:T(8,128)} %bitcast.37), custom_call_target="tpu_custom_call" | custom-call | tf_op jit(solution)/shard_map/owner_update/pallas_call | solution.py:238
  95.7 6.9 %all-to-all-done.2 = f32[128,1,128]{2,1,0:T(1,128)S(1)} async-done(((f32[128,1,128]{2,1,0:T(1,128)}), f32[128,1,128]{2,1,0:T(1,128)S(1)}, u32[]{:S(2)}, u32[]{:S(2)}) %all-to-all-start.2) | async-done | bytes 65568 | tf_op jit(solution)/shard_map/all_to_all | solution.py:727
  102.6 1.2 %copy-done.1 = f32[16,8,8,256]{3,2,1,0:T(8,128)S(1)} copy-done((f32[16,8,8,256]{3,2,1,0:T(8,128)S(1)}, f32[16,8,8,256]{3,2,1,0:T(8,128)}, u32[]{:S(2)}) %copy-start.1) | copy-done | bytes 1048600
  103.8 2.2 %final_update.1 = f32[8,256,128]{2,1,0:T(8,128)} custom-call(f32[16,8,8,256]{3,2,1,0:T(8,128)S(1)} %get-tuple-element.78.q, f32[16,8,8,256]{3,2,1,0:T(8,128)S(1)} %get-tuple-element.79.v0, f32[16,8,8,256]{3,2,1,0:T(8,128)S(1)} %get-tuple-element.80.v1, f32[16,8,8,256]{3,2,1,0:T(8,128)S(1)} %copy-done.1, f32[128,128]{1,0:T(8,128)S(1)} %bitcast.32), custom_call_target="tpu_custom_call" | custom-call | tf_op jit(solution)/shard_map/final_update/pallas_call | solution.py:708
  (8 shorter events, 0.1 us)
Async XLA Ops:
  3.7 14.5 %all-to-all-start = ((f32[16,8,256]{2,1,0:T(8,128)}), f32[16,8,256]{2,1,0:T(8,128)S(1)}, u32[]{:S(2)}, u32[]{:S(2)}) async-start(f32[16,8,256]{2,1,0:T(8,128)} %get-tuple-element.43.after), calls=%async_computation | async-start | bytes 262144 | tf_op jit(solution)/shard_map/all_to_all | solution.py:751
  14.9 0.9 copy-start.2
  18.2 28.6 %collective-permute-start.2 = (f32[28,8,8,128]{3,2,1,0:T(8,128)}, f32[28,8,8,128]{3,2,1,0:T(8,128)S(1)}, u32[]{:S(2)}, u32[]{:S(2)}) collective-permute-start(f32[28,8,8,128]{3,2,1,0:T(8,128)} %copy-done.2), channel_id=1, source_target_pairs={{0,8},{8,16},{16,24},{24,32},{32,40},{40,48},{48,56},{56,64},{64,7... | collective-permute-start | bytes 2752520 | tf_op jit(solution)/shard_map/ppermute | solution.py:723
  20.3 26.5 %collective-permute-start.3 = (f32[28,8,8,128]{3,2,1,0:T(8,128)S(1)}, f32[28,8,8,128]{3,2,1,0:T(8,128)S(1)}, u32[]{:S(2)}, u32[]{:S(2)}) collective-permute-start(f32[28,8,8,128]{3,2,1,0:T(8,128)S(1)} %get-tuple-element.66), channel_id=1, source_target_pairs={{8,0},{16,8},{24,16},{32,24},{40,32},{48,40},{56,48},{64,56},{72,6... | collective-permute-start | bytes 2752520 | tf_op jit(solution)/shard_map/ppermute | solution.py:723
  24.1 7.7 %collective-permute-start = (f32[17,8,128]{2,1,0:T(8,128)S(1)}, f32[17,8,128]{2,1,0:T(8,128)S(1)}, u32[]{:S(2)}, u32[]{:S(2)}) collective-permute-start(f32[17,8,128]{2,1,0:T(8,128)S(1)} %get-tuple-element.54), channel_id=1, source_target_pairs={{0,1},{1,2},{2,3},{3,4},{4,5},{5,6},{6,7},{8,9},{9,10},{10,11},{11... | collective-permute-start | bytes 208904 | tf_op jit(solution)/shard_map/ppermute | solution.py:723
  29.9 5.9 %collective-permute-start.1 = (f32[17,8,128]{2,1,0:T(8,128)S(1)}, f32[17,8,128]{2,1,0:T(8,128)S(1)}, u32[]{:S(2)}, u32[]{:S(2)}) collective-permute-start(f32[17,8,128]{2,1,0:T(8,128)S(1)} %get-tuple-element.55), channel_id=1, source_target_pairs={{1,0},{2,1},{3,2},{4,3},{5,4},{6,5},{7,6},{9,8},{10,9},{11,10},{12... | collective-permute-start | bytes 208904 | tf_op jit(solution)/shard_map/ppermute | solution.py:723
  35.9 9.0 %collective-permute-start.4 = (f32[29,8,128]{2,1,0:T(8,128)S(1)}, f32[29,8,128]{2,1,0:T(8,128)S(1)}, u32[]{:S(2)}, u32[]{:S(2)}) collective-permute-start(f32[29,8,128]{2,1,0:T(8,128)S(1)} %get-tuple-element.68), channel_id=1, source_target_pairs={{0,8},{8,16},{16,24},{24,32},{32,40},{40,48},{48,56},{56,64},{64,7... | collective-permute-start | bytes 356360 | tf_op jit(solution)/shard_map/ppermute | solution.py:723
  40.2 6.6 %collective-permute-start.5 = (f32[29,8,128]{2,1,0:T(8,128)S(1)}, f32[29,8,128]{2,1,0:T(8,128)S(1)}, u32[]{:S(2)}, u32[]{:S(2)}) collective-permute-start(f32[29,8,128]{2,1,0:T(8,128)S(1)} %get-tuple-element.69), channel_id=1, source_target_pairs={{8,0},{16,8},{24,16},{32,24},{40,32},{48,40},{56,48},{64,56},{72,6... | collective-permute-start | bytes 356360 | tf_op jit(solution)/shard_map/ppermute | solution.py:723
  87.5 1.0 copy-start
  88.5 14.1 %all-to-all-start.2 = ((f32[128,1,128]{2,1,0:T(1,128)}), f32[128,1,128]{2,1,0:T(1,128)S(1)}, u32[]{:S(2)}, u32[]{:S(2)}) async-start(f32[128,1,128]{2,1,0:T(1,128)} %bitcast.15), calls=%async_computation.2 | async-start | bytes 131072 | tf_op jit(solution)/shard_map/all_to_all | solution.py:727
  102.6 1.2 %copy-start.1 = (f32[16,8,8,256]{3,2,1,0:T(8,128)S(1)}, f32[16,8,8,256]{3,2,1,0:T(8,128)}, u32[]{:S(2)}) copy-start(f32[16,8,8,256]{3,2,1,0:T(8,128)} %copy-done) | copy-start | bytes 3145732

commit v6 on v5

--- a/solution.py
+++ b/solution.py
@@ -263,6 +263,7 @@
 def turn_kernel(
     pressure, conductivity, forcing, cover, vegetated, root_table, after,
     q, k, to_next, to_prev, edge_left, edge_right, uptake, surface,
+    next_rim, prev_rim, sems,
 ):
     lane = iota((8, 128), 1)
 
@@ -275,9 +276,9 @@
                     part = field[chunk(x, l, t), :]
                     target[x, l, :, 128 * t : 128 * t + 128] = part
                     if x < HALO:
-                        to_prev[2 * (f * HALO + x) + t, l] = part
+                        prev_rim[2 * (f * HALO + x) + t, l] = part
                     if x >= ROWS - HALO:
-                        to_next[2 * (f * HALO + x - ROWS + HALO) + t, l] = part
+                        next_rim[2 * (f * HALO + x - ROWS + HALO) + t, l] = part
                     here = jnp.logical_and(lane >= 8 * x, lane < 8 * x + 8)
                     if t == 0:
                         first = jnp.where(here, lanes(part, 8 * x), first)
@@ -288,6 +289,12 @@
         return carry
 
     lax.fori_loop(0, L, layer, 0)
+    sends = [
+        pltpu.make_async_copy(next_rim, to_next, sems.at[0]),
+        pltpu.make_async_copy(prev_rim, to_prev, sems.at[1]),
+    ]
+    for send in sends:
+        send.start()
     roots = looked_up(cover[...], root_table)
     planted = vegetated[...] == 1
     for m in range(ROOT):
@@ -303,6 +310,8 @@
         if m == 0:
             evaporation = jnp.where(planted, 0.0, 0.5) * softplus(forcing[3] - forcing[2]) * moist
             surface[...] = 0.3 * softplus(forcing[4]) - evaporation
+    for send in sends:
+        send.wait()
 
 
 def turn(*arrays):
@@ -314,13 +323,18 @@
         turn_kernel,
         out_shape=outs,
         in_specs=vmem(5) + [smem(), pl.BlockSpec(memory_space=pl.ANY)],
-        out_specs=tuple(vmem(len(outs))),
+        out_specs=(*vmem(2), *[pl.BlockSpec(memory_space=pltpu.HBM)] * 2, *vmem(4)),
+        scratch_shapes=[
+            pltpu.VMEM((RIM, L, 8, 128), F32),
+            pltpu.VMEM((RIM, L, 8, 128), F32),
+            pltpu.SemaphoreType.DMA((2,)),
+        ],
         compiler_params=params(24),
         name="turn",
     )(*arrays)
 
 
-def corner_kernel(source, from_left, from_right, to_next, to_prev):
+def corner_kernel(source, from_left, from_right, after, to_next, to_prev):
     low = iota((8, 128), 1) < 64
     for i in range(BHALO):
         for t in range(2):
@@ -338,11 +352,21 @@
     return pl.pallas_call(
         corner_kernel,
         out_shape=outs,
-        in_specs=vmem(3),
+        in_specs=vmem(3) + [pl.BlockSpec(memory_space=pl.ANY)],
         out_specs=tuple(vmem(2)),
         compiler_params=params(16),
         name="corners",
     )(*arrays)
+
+
+def inside(axis):
+    at, count = lax.axis_index(axis), lax.axis_size(axis)
+    return jnp.where(at > 0, 1.0, 0.0), jnp.where(at < count - 1, 1.0, 0.0)
+
+
+def side_mask(lane):
+    has_left, has_right = inside("gy")
+    return jnp.where(lane < 8, has_right, jnp.where(lane >= 120, has_left, 0.0))
 
 
 def halo_tile(from_left, from_right, lane, at_left, at_right):
@@ -490,13 +514,15 @@
     q, k, resist, cx, cy, cyl, cz, diag, base,
 ):
     lane = iota((8, 128), 1)
+    keep = side_mask(lane)
 
     def fill(l, carry):
         for f, (field, target) in enumerate(((q_own, q), (k_own, k))):
             a, c = from_left[f * L + l], from_right[f * L + l]
             for x in range(ROWS):
                 target[x, l, :, :COLS] = field[x, l]
-                target[x, l, :, COLS:] = halo_tile(a, c, lane, 8 * x, 8 * x)
+                tile = halo_tile(a, c, lane, 8 * x, 8 * x)
+                target[x, l, :, COLS:] = tile * keep if f == 1 else tile
         for x in range(ROWS):
             _, resist[x, l], diag[x, l] = local_terms(q[x, l], k[x, l])
         return carry
@@ -532,20 +558,26 @@
     resist, cx, cy, cyl, cz, diag,
 ):
     lane = iota((8, 128), 1)
+    keep = side_mask(lane)
+    has_prev, has_next = inside("gx")
 
     def fill(l, carry):
         for f, target in enumerate((q, k)):
             at = 2 * BHALO + f * L + l
-            for side, corner, r, spot in (
-                (from_prev, corner_prev, 0, 8 * (8 - HALO)),
-                (from_next, corner_next, HALO + ROWS - RSHIFT, 0),
+            for side, corner, r, spot, here in (
+                (from_prev, corner_prev, 0, 8 * (8 - HALO), has_prev),
+                (from_next, corner_next, HALO + ROWS - RSHIFT, 0, has_next),
             ):
                 tile = corner[at]
                 for i in range(HALO):
-                    for t in range(2):
-                        target[r + i, l, :, 128 * t : 128 * t + 128] = side[2 * (f * HALO + i) + t, l]
                     left_at = spot + 8 * i
-                    target[r + i, l, :, COLS:] = halo_tile(tile, tile, lane, left_at, 64 + left_at)
+                    row = [side[2 * (f * HALO + i) + t, l] for t in range(2)]
+                    row.append(halo_tile(tile, tile, lane, left_at, 64 + left_at))
+                    for t in range(3):
+                        part = row[t]
+                        if f == 1:
+                            part = part * (here * keep if t == 2 else here)
+                        target[r + i, l, :, 128 * t : 128 * t + 128] = part
         for r in (*range(HALO), *range(RROWS - HALO, RROWS)):
             _, resist[r, l], diag[r, l] = local_terms(q[r, l], k[r, l])
         for r, x in ((7, 0), (8, 1), (9, ROWS - 2), (10, ROWS - 1)):
@@ -718,8 +750,8 @@
 
 def exchange(to_high, to_low, axis):
     count = lax.axis_size(axis)
-    up = [(i, i + 1) for i in range(count - 1)]
-    down = [(i + 1, i) for i in range(count - 1)]
+    up = [(i, (i + 1) % count) for i in range(count)]
+    down = [((i + 1) % count, i) for i in range(count)]
     return lax.ppermute(to_high, axis, up), lax.ppermute(to_low, axis, down)
 
 
@@ -758,15 +790,14 @@
         arrived, cols, counts, forcing, conductance, uptake, surface, edge_left, edge_right
     )
     from_left, from_right = exchange(to_right, to_left, "gy")
-    to_next, to_prev = corners(source, from_left, from_right)
+    new_state = owner_update(arrived, state)
+    to_next, to_prev = corners(source, from_left, from_right, in_hbm(new_state))
     corner_prev, corner_next = exchange(to_next, to_prev, "gx")
 
     mids = prepare(q_own, k_own, from_left, from_right)
     q, k, b, v0, v1, v2, moments = first_newton(
         *mids, from_prev, from_next, source, corner_prev, corner_next, from_left, from_right
     )
-    moments, arrived = lax.optimization_barrier((moments, arrived))
-    new_state = owner_update(arrived, state)
     q1, w0, w1, w2, moments = second_newton(mids[0], mids[1], q, k, b, v0, v1, v2, share(moments))
     pressure = unflat(final_update(q1, w0, w1, w2, share(moments)))
     return pressure, new_state.reshape(canopy_state.shape)

time: 107 us -> 101 us (0.944)
  blocking collectives: 21 us -> 35.1 us
  waiting for transfers between devices: 15.1 us -> 5.65 us
  starting transfers between devices: 28.9 us -> 21.2 us
  local copies, waits for them, and re-layouts: 3.11 us -> 0.92 us
    all_to_all x1 -> x2, blocking collectives: 21 us -> 35.1 us  [share(): lax.all_to_all(moments, ('gx', 'gy'), split_axis=0, concat_axis=0, tiled=...]
    all_to_all x1 -> x0, waiting for transfers between devices: 6.89 us -> none  [share(): lax.all_to_all(moments, ('gx', 'gy'), split_axis=0, concat_axis=0, tiled=...]
    all_to_all x1 -> x0, starting transfers between devices: 4.75 us -> none  [share(): lax.all_to_all(moments, ('gx', 'gy'), split_axis=0, concat_axis=0, tiled=...]
    ppermute x6, starting transfers between devices: 16.6 us -> 13.7 us  [exchange(): return (lax.ppermute(to_high, axis, up), lax.ppermute(to_low, axis, down))]
    unnamed x6 -> x2, local copies, waits for them, and re-layouts: 3.11 us -> 0.92 us
    ppermute x6, waiting for transfers between devices: 5.88 us -> 3.76 us  [exchange(): return (lax.ppermute(to_high, axis, up), lax.ppermute(to_low, axis, down))]
  transfers between devices with their start and end apart: 8 -> 7, of which waited for: 4 -> 3; matrix products, arithmetic and copies ran while one was open for 0% -> 0% of each run, Pallas kernels for 11% -> 13%
where the time goes in v6:
time: 101 us
  Pallas kernels  36.9 us (37%)
  blocking collectives  35.1 us (35%)
  starting transfers between devices  21.2 us (21%)
  waiting for transfers between devices  5.65 us (6%)
    all_to_all x2, blocking collectives, share(): lax.all_to_all(moments, ('gx', 'gy'), split_axis=0, concat_axis=0, tiled=...  35.1 us
    ppermute x6, starting transfers between devices, exchange(): return (lax.ppermute(to_high, axis, up), lax.ppermute(to_low, axis, down))  13.7 us
    pallas_call x1, Pallas kernels, second_newton(): pl.pallas_call(second_kernel, out_shape=outs, in_specs=vmem(len(arrays)),...  9.73 us
    pallas_call x1, Pallas kernels, first_newton(): pl.pallas_call(first_kernel, out_shape=outs, in_specs=vmem(len(arrays)),...  9.25 us
    all_to_all x1, starting transfers between devices, body(): lax.all_to_all(payload, 'gx', split_axis=0, concat_axis=0, tiled=True)  7.58 us
    pallas_call x1, Pallas kernels, turn(): pl.pallas_call(turn_kernel, out_shape=outs, in_specs=vmem(5) + [smem(), p...  4.04 us
    ppermute x6, waiting for transfers between devices, exchange(): return (lax.ppermute(to_high, axis, up), lax.ppermute(to_low, axis, down))  3.76 us
    pallas_call x1, Pallas kernels, prepare(): pl.pallas_call(prepare_kernel, out_shape=outs, in_specs=vmem(4), out_spec...  3.41 us
  transfers between devices with their start and end apart: 7, of which 3 were waited for; matrix products, arithmetic and copies ran while one was open for 0% of the time, Pallas kernels for 13%

profile of v6, /device:TPU:1, one launch (start us, length us, event | category | flops | bytes accessed | tf_op | source)
XLA Modules:
  0.0 100.5 jit_solution(16850839100594292475)
XLA Ops:
  0.6 3.1 %canopy_send.1 = (f32[16,8,256]{2,1,0:T(8,128)}, f32[16,256]{1,0:T(8,128)S(1)}) custom-call(f32[8,16,256]{2,1,0:T(8,128)} %forcing.5, s32[16,256]{1,0:T(8,128)} %cover.3, f32[8,16]{1,0:T(8,128)} %bitcast.43, s32[16]{0:T(128)} %bitcast.45, s32[16,1,256]{2,1,0:T(1,128)} %bitcast.41, f32[16,16,256]{2,1,0:T(8,128)} %bitcast.37), custom_call_target="tpu_custom_call" | custom-call | tf_op jit(solution)/shard_map/canopy_send/pallas_call | solution.py:131
  3.7 7.6 %all-to-all-start = ((f32[16,8,256]{2,1,0:T(8,128)}), f32[16,8,256]{2,1,0:T(8,128)S(1)}, u32[]{:S(2)}, u32[]{:S(2)}) async-start(f32[16,8,256]{2,1,0:T(8,128)} %get-tuple-element.41.after), calls=%async_computation | async-start | bytes 262144 | tf_op jit(solution)/shard_map/all_to_all | solution.py:783
  11.3 4.0 %turn.1 = (f32[16,8,8,256]{3,2,1,0:T(8,128)S(1)}, f32[16,8,8,256]{3,2,1,0:T(8,128)S(1)}, f32[28,8,8,128]{3,2,1,0:T(8,128)S(1)}, f32[28,8,8,128]{3,2,1,0:T(8,128)...) custom-call(f32[2048,128]{1,0:T(8,128)} %bitcast.35, ...), custom_call_target="tpu_custom_call" | custom-call | tf_op jit(solution)/shard_map/turn/pallas_call | solution.py:322
  15.4 0.0 copy-start
  15.4 0.9 copy-done
  16.3 1.9 %all-to-all-done.arrived = f32[16,8,256]{2,1,0:T(8,128)S(1)} async-done(((f32[16,8,256]{2,1,0:T(8,128)}), f32[16,8,256]{2,1,0:T(8,128)S(1)}, u32[]{:S(2)}, u32[]{:S(2)}) %all-to-all-start) | async-done | bytes 131104 | tf_op jit(solution)/shard_map/all_to_all | solution.py:783
  18.2 0.1 collective-permute-start.2
  18.3 4.7 %collective-permute-start.3 = (f32[28,8,8,128]{3,2,1,0:T(8,128)S(1)}, f32[28,8,8,128]{3,2,1,0:T(8,128)S(1)}, u32[]{:S(2)}, u32[]{:S(2)}) collective-permute-start(f32[28,8,8,128]{3,2,1,0:T(8,128)S(1)} %get-tuple-element.64), channel_id=1, source_target_pairs={{8,0},{16,8},{24,16},{32,24},{40,32},{48,40},{56,48},{64,56},{72,6... | collective-permute-start | bytes 2752520 | tf_op jit(solution)/shard_map/ppermute | solution.py:755
  23.0 2.6 %canopy_source.1 = (f32[16,8,256]{2,1,0:T(8,128)S(1)}, f32[17,8,128]{2,1,0:T(8,128)S(1)}, f32[17,8,128]{2,1,0:T(8,128)S(1)}) custom-call(f32[16,8,256]{2,1,0:T(8,128)S(1)} %all-to-all-done.arrived, s32[16,1,256]{2,1,0:T(1,128)} %bitcast.42, s32[16]{0:T(128)} %bitcast.46, f32[8,16,256]{2,1,0:T(8,128)} %forcing.5, ...), custom_call_target="tpu_custom_call" | custom-call | tf_op jit(solution)/shard_map/canopy_source/pallas_call | solution.py:207
  25.5 4.0 %collective-permute-start = (f32[17,8,128]{2,1,0:T(8,128)S(1)}, f32[17,8,128]{2,1,0:T(8,128)S(1)}, u32[]{:S(2)}, u32[]{:S(2)}) collective-permute-start(f32[17,8,128]{2,1,0:T(8,128)S(1)} %get-tuple-element.52), channel_id=1, source_target_pairs={{0,1},{1,2},{2,3},{3,4},{4,5},{5,6},{6,7},{7,0},{8,9},{9,10},{10,1... | collective-permute-start | bytes 208904 | tf_op jit(solution)/shard_map/ppermute | solution.py:755
  29.6 0.0 collective-permute-start.1
  29.6 2.5 %owner_update.1.after = f32[16,16,256]{2,1,0:T(8,128)} custom-call(f32[16,8,256]{2,1,0:T(8,128)S(1)} %all-to-all-done.arrived, f32[16,16,256]{2,1,0:T(8,128)} %bitcast.38), custom_call_target="tpu_custom_call" | custom-call | tf_op jit(solution)/shard_map/owner_update/pallas_call | solution.py:238
  32.0 0.0 collective-permute-done.from_left
  32.0 1.5 %collective-permute-done.1.from_right = f32[17,8,128]{2,1,0:T(8,128)S(1)} collective-permute-done((f32[17,8,128]{2,1,0:T(8,128)S(1)}, f32[17,8,128]{2,1,0:T(8,128)S(1)}, u32[]{:S(2)}, u32[]{:S(2)}) %collective-permute-start.1) | collective-permute-done | bytes 69664 | tf_op jit(solution)/shard_map/ppermute | solution.py:755
  33.6 0.1 corners.1
  33.7 0.1 collective-permute-start.4
  33.8 4.8 %collective-permute-start.5 = (f32[29,8,128]{2,1,0:T(8,128)S(1)}, f32[29,8,128]{2,1,0:T(8,128)S(1)}, u32[]{:S(2)}, u32[]{:S(2)}) collective-permute-start(f32[29,8,128]{2,1,0:T(8,128)S(1)} %get-tuple-element.67), channel_id=1, source_target_pairs={{8,0},{16,8},{24,16},{32,24},{40,32},{48,40},{56,48},{64,56},{72,6... | collective-permute-start | bytes 356360 | tf_op jit(solution)/shard_map/ppermute | solution.py:755
  38.6 3.4 %prepare.1 = (f32[16,8,8,384]{3,2,1,0:T(8,128)S(1)}, f32[16,8,8,384]{3,2,1,0:T(8,128)S(1)}, f32[16,8,8,384]{3,2,1,0:T(8,128)S(1)}, f32[16,8,8,384]{3,2,1,0:T(8,1...) custom-call(f32[16,8,8,256]{3,2,1,0:T(8,128)S(1)} %get-tuple-element, ...), custom_call_target="tpu_custom_call" | custom-call | tf_op jit(solution)/shard_map/prepare/pallas_call | solution.py:540
  42.0 2.2 %collective-permute-done.4.corner_prev = f32[29,8,128]{2,1,0:T(8,128)S(1)} collective-permute-done((f32[29,8,128]{2,1,0:T(8,128)S(1)}, f32[29,8,128]{2,1,0:T(8,128)S(1)}, u32[]{:S(2)}, u32[]{:S(2)}) %collective-permute-start.4) | collective-permute-done | bytes 118816 | tf_op jit(solution)/shard_map/ppermute | solution.py:755
  44.2 9.2 %first_newton.1 = (f32[18,8,8,384]{3,2,1,0:T(8,128)S(1)}, f32[18,8,8,384]{3,2,1,0:T(8,128)S(1)}, f32[30,8,384]{2,1,0:T(8,128)S(1)}, f32[30,8,8,384]{3,2,1,0:T(8,...) custom-call(f32[16,8,8,384]{3,2,1,0:T(8,128)S(1)} %get-tuple-element.54.q_mid, ...), custom_call_target="tpu_custom_call" | custom-call | tf_op jit(solution)/shard_map/first_newton/pallas_call | solution.py:641
  53.4 21.2 %all_to_all.27 = f32[128,1,128]{2,1,0:T(1,128)S(1)} all-to-all(f32[128,1,128]{2,1,0:T(1,128)S(1)} %bitcast.33), channel_id=1, replica_groups=mesh['gx'=16,'gy'=8] {'gx','gy'}, dimensions={0} | all-to-all | bytes 131072 | tf_op jit(solution)/shard_map/all_to_all | solution.py:759
  74.6 9.7 %second_newton.1 = (f32[16,8,8,256]{3,2,1,0:T(8,128)S(1)}, f32[16,8,8,256]{3,2,1,0:T(8,128)S(1)}, f32[16,8,8,256]{3,2,1,0:T(8,128)S(1)}, f32[16,8,8,256]{3,2,1,0:T(8,128)S(1)}, f32[128,128]{1,0:T(8,128)S(1)}) custom-call(f32[16,8,8,384]{3,2,1,0:T(8,128)S(1)} %get-tuple-element.54.q_mid, f32[16,8,8,384]{3,2,1,0:T(8,128)S(1)} %get-tuple-element.55.k_mid, ...), custom_call_target="tpu_custom_call" | custom-call | tf_op jit(solution)/shard_map/second_newton/pallas_call | solution.py:706
  84.4 13.9 %all_to_all.28 = f32[128,1,128]{2,1,0:T(1,128)S(1)} all-to-all(f32[128,1,128]{2,1,0:T(1,128)S(1)} %bitcast.34), channel_id=1, replica_groups=mesh['gx'=16,'gy'=8] {'gx','gy'}, dimensions={0} | all-to-all | bytes 131072 | tf_op jit(solution)/shard_map/all_to_all | solution.py:759
  98.3 2.2 %final_update.1 = f32[8,256,128]{2,1,0:T(8,128)} custom-call(f32[16,8,8,256]{3,2,1,0:T(8,128)S(1)} %get-tuple-element.75.q, f32[16,8,8,256]{3,2,1,0:T(8,128)S(1)} %get-tuple-element.76.v0, f32[16,8,8,256]{3,2,1,0:T(8,128)S(1)} %get-tuple-element.77.v1, f32[16,8,8,256]{3,2,1,0:T(8,128)S(1)} %get-tuple-element.78.v2, f32[128,128]{1,0:T(8,128)S(1)} %bitcast.32), custom_call_target="tpu_custom_call" | custom-call | tf_op jit(solution)/shard_map/final_update/pallas_call | solution.py:740
  (3 shorter events, 0.0 us)
Async XLA Ops:
  3.7 14.5 %all-to-all-start = ((f32[16,8,256]{2,1,0:T(8,128)}), f32[16,8,256]{2,1,0:T(8,128)S(1)}, u32[]{:S(2)}, u32[]{:S(2)}) async-start(f32[16,8,256]{2,1,0:T(8,128)} %get-tuple-element.41.after), calls=%async_computation | async-start | bytes 262144 | tf_op jit(solution)/shard_map/all_to_all | solution.py:783
  15.4 0.9 copy-start
  18.2 26.0 %collective-permute-start.2 = (f32[28,8,8,128]{3,2,1,0:T(8,128)}, f32[28,8,8,128]{3,2,1,0:T(8,128)S(1)}, u32[]{:S(2)}, u32[]{:S(2)}) collective-permute-start(f32[28,8,8,128]{3,2,1,0:T(8,128)} %copy-done), channel_id=1, source_target_pairs={{0,8},{8,16},{16,24},{24,32},{32,40},{40,48},{48,56},{56,64},{64,7... | collective-permute-start | bytes 2752520 | tf_op jit(solution)/shard_map/ppermute | solution.py:755
  18.3 25.9 %collective-permute-start.3 = (f32[28,8,8,128]{3,2,1,0:T(8,128)S(1)}, f32[28,8,8,128]{3,2,1,0:T(8,128)S(1)}, u32[]{:S(2)}, u32[]{:S(2)}) collective-permute-start(f32[28,8,8,128]{3,2,1,0:T(8,128)S(1)} %get-tuple-element.64), channel_id=1, source_target_pairs={{8,0},{16,8},{24,16},{32,24},{40,32},{48,40},{56,48},{64,56},{72,6... | collective-permute-start | bytes 2752520 | tf_op jit(solution)/shard_map/ppermute | solution.py:755
  25.5 6.5 %collective-permute-start = (f32[17,8,128]{2,1,0:T(8,128)S(1)}, f32[17,8,128]{2,1,0:T(8,128)S(1)}, u32[]{:S(2)}, u32[]{:S(2)}) collective-permute-start(f32[17,8,128]{2,1,0:T(8,128)S(1)} %get-tuple-element.52), channel_id=1, source_target_pairs={{0,1},{1,2},{2,3},{3,4},{4,5},{5,6},{6,7},{7,0},{8,9},{9,10},{10,1... | collective-permute-start | bytes 208904 | tf_op jit(solution)/shard_map/ppermute | solution.py:755
  29.6 4.0 %collective-permute-start.1 = (f32[17,8,128]{2,1,0:T(8,128)S(1)}, f32[17,8,128]{2,1,0:T(8,128)S(1)}, u32[]{:S(2)}, u32[]{:S(2)}) collective-permute-start(f32[17,8,128]{2,1,0:T(8,128)S(1)} %get-tuple-element.53), channel_id=1, source_target_pairs={{1,0},{2,1},{3,2},{4,3},{5,4},{6,5},{7,6},{0,7},{9,8},{10,9},{11,1... | collective-permute-start | bytes 208904 | tf_op jit(solution)/shard_map/ppermute | solution.py:755
  33.7 10.5 %collective-permute-start.4 = (f32[29,8,128]{2,1,0:T(8,128)S(1)}, f32[29,8,128]{2,1,0:T(8,128)S(1)}, u32[]{:S(2)}, u32[]{:S(2)}) collective-permute-start(f32[29,8,128]{2,1,0:T(8,128)S(1)} %get-tuple-element.66), channel_id=1, source_target_pairs={{0,8},{8,16},{16,24},{24,32},{32,40},{40,48},{48,56},{56,64},{64,7... | collective-permute-start | bytes 356360 | tf_op jit(solution)/shard_map/ppermute | solution.py:755
  33.8 10.4 %collective-permute-start.5 = (f32[29,8,128]{2,1,0:T(8,128)S(1)}, f32[29,8,128]{2,1,0:T(8,128)S(1)}, u32[]{:S(2)}, u32[]{:S(2)}) collective-permute-start(f32[29,8,128]{2,1,0:T(8,128)S(1)} %get-tuple-element.67), channel_id=1, source_target_pairs={{8,0},{16,8},{24,16},{32,24},{40,32},{48,40},{56,48},{64,56},{72,6... | collective-permute-start | bytes 356360 | tf_op jit(solution)/shard_map/ppermute | solution.py:755

commit v7 on v4

--- a/solution.py
+++ b/solution.py
@@ -12,6 +12,8 @@
 COLS = 256
 L = 8
 HALO = 7
+NEAR = 4
+FAR = HALO - NEAR
 XR = ROWS + 2 * HALO
 XC = 384
 OUTSIDE = 1e37
@@ -30,6 +32,10 @@
 
 def params(mib):
     return pltpu.CompilerParams(vmem_limit_bytes=mib * 1024 * 1024)
+
+
+def work(micros):
+    return pl.CostEstimate(flops=0, transcendentals=0, bytes_accessed=int(3e6 * micros))
 
 
 def shaped(*shape):
@@ -123,7 +129,7 @@
         payload[o] = jnp.where(sub == used, live, out)
         return carry
 
-    lax.fori_loop(0, cols.shape[0], owner, 0, unroll=4)
+    lax.fori_loop(0, cols.shape[0], owner, 0, unroll=8)
 
 
 def canopy_send(forcing, cover, canopy_table, counts, cols, state):
@@ -135,6 +141,7 @@
         out_specs=tuple(vmem(2)),
         scratch_shapes=[pltpu.VMEM((15 * ROWS, COLS), BF16)],
         compiler_params=params(16),
+        cost_estimate=work(3),
         name="canopy_send",
     )(forcing, cover, canopy_table, counts, cols, state)
 
@@ -170,7 +177,7 @@
         )
         return carry
 
-    lax.fori_loop(0, cols.shape[0], owner, 0, unroll=4)
+    lax.fori_loop(0, cols.shape[0], owner, 0, unroll=8)
 
     def piece(k):
         return total[k * ROWS : (k + 1) * ROWS, :]
@@ -211,6 +218,7 @@
         out_specs=(v, v, v),
         scratch_shapes=[pltpu.VMEM((6 * ROWS, COLS), F32), pltpu.VMEM((2 * 128, 128), F32)],
         compiler_params=params(16),
+        cost_estimate=work(2.5),
         name="canopy_source",
     )(*arrays)
 
@@ -231,7 +239,7 @@
         updated[i] = jnp.where(block[5:6] > 0.5, fresh, old)
         return carry
 
-    lax.fori_loop(0, arrived.shape[0], slot, 0)
+    lax.fori_loop(0, arrived.shape[0], slot, 0, unroll=8)
 
 
 def owner_update(arrived, state):
@@ -241,6 +249,7 @@
         in_specs=vmem(2),
         out_specs=vmem()[0],
         compiler_params=params(8),
+        cost_estimate=work(2),
         name="owner_update",
     )(arrived, state)
 
@@ -257,12 +266,14 @@
     return pl.ds(32 * l + 16 * (x // 8) + 8 * t + x % 8, 8, stride=32 * L)
 
 
-RIM = 2 * HALO * 2
+def rim_shape(rows):
+    return 2 * rows * 2, L, 8, 128
 
 
 def turn_kernel(
     pressure, conductivity, forcing, cover, vegetated, root_table, after,
-    q, k, to_next, to_prev, edge_left, edge_right, uptake, surface,
+    q, k, near_next, near_prev, far_next, far_prev, edge_left, edge_right, uptake, surface,
+    near_next_rim, near_prev_rim, far_next_rim, far_prev_rim, sems,
 ):
     lane = iota((8, 128), 1)
 
@@ -274,10 +285,14 @@
                 for t in range(2):
                     part = field[chunk(x, l, t), :]
                     target[x, l, :, 128 * t : 128 * t + 128] = part
-                    if x < HALO:
-                        to_prev[2 * (f * HALO + x) + t, l] = part
-                    if x >= ROWS - HALO:
-                        to_next[2 * (f * HALO + x - ROWS + HALO) + t, l] = part
+                    if x < NEAR:
+                        near_prev_rim[2 * (f * NEAR + x) + t, l] = part
+                    elif x < HALO:
+                        far_prev_rim[2 * (f * FAR + x - NEAR) + t, l] = part
+                    if x >= ROWS - NEAR:
+                        near_next_rim[2 * (f * NEAR + x - ROWS + NEAR) + t, l] = part
+                    elif x >= ROWS - HALO:
+                        far_next_rim[2 * (f * FAR + x - ROWS + HALO) + t, l] = part
                     here = jnp.logical_and(lane >= 8 * x, lane < 8 * x + 8)
                     if t == 0:
                         first = jnp.where(here, lanes(part, 8 * x), first)
@@ -288,6 +303,14 @@
         return carry
 
     lax.fori_loop(0, L, layer, 0)
+    sends = [
+        pltpu.make_async_copy(near_next_rim, near_next, sems.at[0]),
+        pltpu.make_async_copy(near_prev_rim, near_prev, sems.at[1]),
+        pltpu.make_async_copy(far_next_rim, far_next, sems.at[2]),
+        pltpu.make_async_copy(far_prev_rim, far_prev, sems.at[3]),
+    ]
+    for send in sends:
+        send.start()
     roots = looked_up(cover[...], root_table)
     planted = vegetated[...] == 1
     for m in range(ROOT):
@@ -303,19 +326,25 @@
         if m == 0:
             evaporation = jnp.where(planted, 0.0, 0.5) * softplus(forcing[3] - forcing[2]) * moist
             surface[...] = 0.3 * softplus(forcing[4]) - evaporation
+    for send in sends:
+        send.wait()
 
 
 def turn(*arrays):
     own_shape = shaped(ROWS, L, 8, COLS)
-    rim = shaped(RIM, L, 8, 128)
+    near, far = rim_shape(NEAR), rim_shape(FAR)
+    rims = (pltpu.HBM(near, F32), pltpu.HBM(near, F32), pltpu.HBM(far, F32), pltpu.HBM(far, F32))
     edge = shaped(2 * L, 8, 128)
-    outs = (own_shape, own_shape, rim, rim, edge, edge, shaped(ROOT, ROWS, COLS), shaped(ROWS, COLS))
+    outs = (own_shape, own_shape, *rims, edge, edge, shaped(ROOT, ROWS, COLS), shaped(ROWS, COLS))
     return pl.pallas_call(
         turn_kernel,
         out_shape=outs,
         in_specs=vmem(5) + [smem(), pl.BlockSpec(memory_space=pl.ANY)],
-        out_specs=tuple(vmem(len(outs))),
+        out_specs=(*vmem(2), *[pl.BlockSpec(memory_space=pltpu.HBM)] * 4, *vmem(4)),
+        scratch_shapes=[pltpu.VMEM(shape, F32) for shape in (near, near, far, far)]
+        + [pltpu.SemaphoreType.DMA((4,))],
         compiler_params=params(24),
+        cost_estimate=work(4),
         name="turn",
     )(*arrays)
 
@@ -341,8 +370,19 @@
         in_specs=vmem(3) + [pl.BlockSpec(memory_space=pl.ANY)],
         out_specs=tuple(vmem(2)),
         compiler_params=params(16),
+        cost_estimate=work(0.4),
         name="corners",
     )(*arrays)
+
+
+def inside(axis):
+    at, count = lax.axis_index(axis), lax.axis_size(axis)
+    return jnp.where(at > 0, 1.0, 0.0), jnp.where(at < count - 1, 1.0, 0.0)
+
+
+def side_mask(lane):
+    has_left, has_right = inside("gy")
+    return jnp.where(lane < 8, has_right, jnp.where(lane >= 120, has_left, 0.0))
 
 
 def halo_tile(from_left, from_right, lane, at_left, at_right):
@@ -490,13 +530,15 @@
     q, k, resist, cx, cy, cyl, cz, diag, base,
 ):
     lane = iota((8, 128), 1)
+    keep = side_mask(lane)
 
     def fill(l, carry):
         for f, (field, target) in enumerate(((q_own, q), (k_own, k))):
             a, c = from_left[f * L + l], from_right[f * L + l]
             for x in range(ROWS):
                 target[x, l, :, :COLS] = field[x, l]
-                target[x, l, :, COLS:] = halo_tile(a, c, lane, 8 * x, 8 * x)
+                tile = halo_tile(a, c, lane, 8 * x, 8 * x)
+                target[x, l, :, COLS:] = tile * keep if f == 1 else tile
         for x in range(ROWS):
             _, resist[x, l], diag[x, l] = local_terms(q[x, l], k[x, l])
         return carry
@@ -517,12 +559,23 @@
         in_specs=vmem(4),
         out_specs=tuple(vmem(9)),
         compiler_params=params(4),
+        cost_estimate=work(3.4),
         name="prepare",
     )(*arrays)
 
 
-RSHIFT = 12
-RROWS = 18
+LSHIFT = 3
+HSHIFT = 15
+RROWS = 12
+
+
+def rim_row(parts, lane, spot, inside_flags):
+    low, high, corner = parts
+    beside = halo_tile(corner, corner, lane, spot, 64 + spot)
+    if inside_flags is not None:
+        here, keep = inside_flags
+        low, high, beside = low * here, high * here, beside * (here * keep)
+    return jnp.concatenate([low, high, beside], axis=1)
 
 
 def first_kernel(
@@ -532,23 +585,22 @@
     resist, cx, cy, cyl, cz, diag,
 ):
     lane = iota((8, 128), 1)
+    keep = side_mask(lane)
+    has_prev, has_next = inside("gx")
 
     def fill(l, carry):
         for f, target in enumerate((q, k)):
             at = 2 * BHALO + f * L + l
-            for side, corner, r, spot in (
-                (from_prev, corner_prev, 0, 8 * (8 - HALO)),
-                (from_next, corner_next, HALO + ROWS - RSHIFT, 0),
+            for side, corner, r, spot, here in (
+                (from_prev, corner_prev, 0, 8 * (8 - NEAR), has_prev),
+                (from_next, corner_next, RROWS - NEAR, 0, has_next),
             ):
-                tile = corner[at]
-                for i in range(HALO):
-                    for t in range(2):
-                        target[r + i, l, :, 128 * t : 128 * t + 128] = side[2 * (f * HALO + i) + t, l]
-                    left_at = spot + 8 * i
-                    target[r + i, l, :, COLS:] = halo_tile(tile, tile, lane, left_at, 64 + left_at)
-        for r in (*range(HALO), *range(RROWS - HALO, RROWS)):
+                for i in range(NEAR):
+                    parts = side[2 * (f * NEAR + i), l], side[2 * (f * NEAR + i) + 1, l], corner[at]
+                    target[r + i, l] = rim_row(parts, lane, spot + 8 * i, (here, keep) if f == 1 else None)
+        for r in (*range(NEAR), *range(RROWS - NEAR, RROWS)):
             _, resist[r, l], diag[r, l] = local_terms(q[r, l], k[r, l])
-        for r, x in ((7, 0), (8, 1), (9, ROWS - 2), (10, ROWS - 1)):
+        for r, x in ((4, 0), (5, 1), (6, ROWS - 2), (7, ROWS - 1)):
             q[r, l] = q_mid[x, l]
             resist[r, l] = resist_mid[x, l]
             diag[r, l] = diag_mid[x, l]
@@ -575,7 +627,7 @@
     coefs = (cx, cy, cyl, cz, diag)
     mids = (cx_mid, cy_mid, cyl_mid, cz_mid, diag_mid)
 
-    for shift, rows in ((0, (1, HALO + 1)), (RSHIFT, (RROWS - HALO - 1, RROWS - 1))):
+    for shift, rows in ((LSHIFT, (1, NEAR + 1)), (HSHIFT, (RROWS - NEAR - 1, RROWS - 1))):
 
         def emit(r, l, out, shift=shift):
             v0[r + shift, l] = source_at(b, r + shift, l, sub) - out
@@ -591,13 +643,13 @@
     blocks((low + 1, high), 2, inner, 0)
 
     sums = []
-    for v_in, v_out, deep in ((v0, v1, 5), (v1, v2, 4), (v2, None, 0)):
+    for v_in, v_out, deep in ((v0, v1, 2), (v1, v2, 1), (v2, None, 0)):
         held = apply(v_in, v_out, mids, HALO, (low + 1, high), 7, no_sums(), True)
-        held = apply(v_in, v_out, coefs, 0, (low, low + 1), 1, held, True)
-        held = apply(v_in, v_out, coefs, RSHIFT, (high, high + 1), 1, held, True)
+        held = apply(v_in, v_out, coefs, LSHIFT, (low, low + 1), 1, held, True)
+        held = apply(v_in, v_out, coefs, HSHIFT, (high, high + 1), 1, held, True)
         if deep:
-            apply(v_in, v_out, coefs, 0, (low - deep, low), deep, no_sums(), False)
-            apply(v_in, v_out, coefs, RSHIFT, (high + 1, high + 1 + deep), deep, no_sums(), False)
+            apply(v_in, v_out, coefs, LSHIFT, (low - deep, low), deep, no_sums(), False)
+            apply(v_in, v_out, coefs, HSHIFT, (high + 1, high + 1 + deep), deep, no_sums(), False)
         sums += held
     write_moments(sums, moments)
 
@@ -613,29 +665,70 @@
         out_specs=tuple(vmem(len(outs))),
         scratch_shapes=[pltpu.VMEM((RROWS, L, 8, XC), F32)] * 6,
         compiler_params=params(14),
+        cost_estimate=work(7.5),
         name="first_newton",
     )(*arrays)
 
 
 def second_kernel(
-    q_mid, k_mid, q_rim, k_rim, b, u0, u1, u2, gathered,
+    q_mid, k_mid, q_rim, k_rim, b, u0, u1, u2, far_prev, far_next, corner_prev, corner_next, gathered,
     q_own, w0, w1, w2, moments,
     q1, resist, cx, cy, cyl, cz, diag, v0, v2,
 ):
     v1 = resist
+    coefs = (cx, cy, cyl, cz, diag)
+    sub = iota((8, XC), 0)
+
+    lane = iota((8, 128), 1)
+    keep = side_mask(lane)
+    has_prev, has_next = inside("gx")
+
+    def far_rows(l, carry):
+        for side, corner, r, spot, here in (
+            (far_prev, corner_prev, 0, 8 * (8 - HALO), has_prev),
+            (far_next, corner_next, XR - FAR, 8 * NEAR, has_next),
+        ):
+            for i in range(FAR):
+                row = []
+                for f in range(2):
+                    at = 2 * (f * FAR + i)
+                    parts = side[at, l], side[at + 1, l], corner[2 * BHALO + f * L + l]
+                    row.append(rim_row(parts, lane, spot + 8 * i, (here, keep) if f == 1 else None))
+                q1[r + i, l] = row[0]
+                _, resist[r + i, l], diag[r + i, l] = local_terms(*row)
+        for r, shift in ((FAR, LSHIFT), (HALO + ROWS, HSHIFT)):
+            for i in range(NEAR):
+                old = q_rim[r + i - shift, l]
+                q1[r + i, l] = old
+                _, resist[r + i, l], diag[r + i, l] = local_terms(old, k_rim[r + i - shift, l])
+        for r in (5, 6, XR - 7, XR - 6):
+            v2[r, l] = u1[r, l]
+        return carry
+
+    lax.fori_loop(0, L, far_rows, 0)
+
+    def far_right_hand(r, l, out):
+        v0[r, l] = source_at(b, r, l, sub) - out
+
+    for rows in ((1, 6), (XR - 6, XR - 1)):
+        couplings(q1, resist, *coefs, rows, 1, far_right_hand)
+    for v_in, v_out, r in ((v0, v2, 2), (v2, q1, 3)):
+        for rows in ((r, r + 3), (XR - r - 3, XR - r)):
+            apply(v_in, v_out, coefs, 0, rows, 3, no_sums(), False)
+
     c0, c1, c2 = coefficients(gathered)
-    sub = iota((8, XC), 0)
-
-    for q, k, shift, rows in (
-        (q_rim, k_rim, 0, (3, HALO)),
-        (q_mid, k_mid, HALO, (HALO, HALO + ROWS)),
-        (q_rim, k_rim, RSHIFT, (HALO + ROWS, XR - 3)),
+    for q, k, shift, rows, block, held in (
+        (q_rim, k_rim, LSHIFT, (3, 6), 3, (v0, v2, q1)),
+        (q_rim, k_rim, LSHIFT, (6, 7), 1, (u0, u1, u2)),
+        (q_mid, k_mid, HALO, (HALO, HALO + ROWS), 2, (u0, u1, u2)),
+        (q_rim, k_rim, HSHIFT, (XR - 7, XR - 6), 1, (u0, u1, u2)),
+        (q_rim, k_rim, HSHIFT, (XR - 6, XR - 3), 3, (v0, v2, q1)),
     ):
 
-        def update(r, carry, q=q, k=k, shift=shift):
+        def update(r, carry, q=q, k=k, shift=shift, held=held):
             for l in range(L):
                 old = q[r - shift, l]
-                step = c0 * u0[r, l] + c1 * u1[r, l] + c2 * u2[r, l]
+                step = c0 * held[0][r, l] + c1 * held[1][r, l] + c2 * held[2][r, l]
                 new = old + step
                 q1[r, l] = new
                 bend, resist[r, l], diag[r, l] = local_terms(new, k[r - shift, l])
@@ -643,12 +736,11 @@
                 v0[r, l] = source_at(b, r, l, sub) - stored
             return carry
 
-        blocks(rows, 2, update, 0)
+        blocks(rows, block, update, 0)
 
     def emit(r, l, out):
         v0[r, l] = v0[r, l] - out
 
-    coefs = (cx, cy, cyl, cz, diag)
     couplings(q1, resist, *coefs, (4, XR - 4), 2, emit)
     low, high = HALO, HALO + ROWS
     sums = []
@@ -677,7 +769,8 @@
         in_specs=vmem(len(arrays)),
         out_specs=tuple(vmem(len(outs))),
         scratch_shapes=[pltpu.VMEM((XR, L, 8, XC), F32)] * 9,
-        compiler_params=params(28),
+        compiler_params=params(30),
+        cost_estimate=work(12),
         name="second_newton",
     )(*arrays)
 
@@ -692,7 +785,7 @@
             out[chunk(x, l, 1), :] = value[:, 128:]
         return carry
 
-    lax.fori_loop(0, ROWS, row, 0)
+    lax.fori_loop(0, ROWS, row, 0, unroll=2)
 
 
 def final_update(*arrays):
@@ -701,15 +794,16 @@
         out_shape=shaped(32 * LEV, 128),
         in_specs=vmem(len(arrays)),
         out_specs=vmem()[0],
-        compiler_params=params(16),
+        compiler_params=params(4),
+        cost_estimate=work(2),
         name="final_update",
     )(*arrays)
 
 
 def exchange(to_high, to_low, axis):
     count = lax.axis_size(axis)
-    up = [(i, i + 1) for i in range(count - 1)]
-    down = [(i + 1, i) for i in range(count - 1)]
+    up = [(i, (i + 1) % count) for i in range(count)]
+    down = [((i + 1) % count, i) for i in range(count)]
     return lax.ppermute(to_high, axis, up), lax.ppermute(to_low, axis, down)
 
 
@@ -739,10 +833,11 @@
 
     payload, conductance = canopy_send(forcing, cover_type, canopy_table, counts, cols, state)
     arrived = lax.all_to_all(payload, "gx", split_axis=0, concat_axis=0, tiled=True)
-    q_own, k_own, to_next, to_prev, edge_left, edge_right, uptake, surface = turn(
+    q_own, k_own, *rims, edge_left, edge_right, uptake, surface = turn(
         old, conductivity, forcing, cover_type, vegetated, root_table, payload
     )
-    from_prev, from_next = exchange(to_next, to_prev, "gx")
+    near_next, near_prev, far_next, far_prev, arrived = lax.optimization_barrier((*rims, arrived))
+    near_prev, near_next = exchange(near_next, near_prev, "gx")
     source, to_right, to_left = canopy_source(
         arrived, cols, counts, forcing, conductance, uptake, surface, edge_left, edge_right
     )
@@ -750,12 +845,18 @@
     new_state = owner_update(arrived, state)
     to_next, to_prev = corners(source, from_left, from_right, in_hbm(new_state))
     corner_prev, corner_next = exchange(to_next, to_prev, "gx")
-
+    far_next, far_prev, near_prev, near_next, corner_prev, corner_next = lax.optimization_barrier(
+        (far_next, far_prev, near_prev, near_next, corner_prev, corner_next)
+    )
     mids = prepare(q_own, k_own, from_left, from_right)
+    far_prev, far_next = exchange(far_next, far_prev, "gx")
     q, k, b, v0, v1, v2, moments = first_newton(
-        *mids, from_prev, from_next, source, corner_prev, corner_next, from_left, from_right
+        *mids, near_prev, near_next, source, corner_prev, corner_next, from_left, from_right
     )
-    q1, w0, w1, w2, moments = second_newton(mids[0], mids[1], q, k, b, v0, v1, v2, share(moments))
+    moments, far_prev, far_next = lax.optimization_barrier((moments, far_prev, far_next))
+    q1, w0, w1, w2, moments = second_newton(
+        mids[0], mids[1], q, k, b, v0, v1, v2, far_prev, far_next, corner_prev, corner_next, share(moments)
+    )
     pressure = unflat(final_update(q1, w0, w1, w2, share(moments)))
     return pressure, new_state.reshape(canopy_state.shape)
 

time: 117 us -> 103 us (0.88)
  blocking collectives: 60.3 us -> 30.4 us
  starting transfers between devices: 17.8 us -> 26.3 us
  waiting for transfers between devices: 2.15 us -> 7.82 us
  Pallas kernels: 35.7 us -> 37.4 us
    all_to_all x1 -> x0, blocking collectives: 25 us -> none  [body(): lax.all_to_all(payload, 'gx', split_axis=0, concat_axis=0, tiled=True)]
    all_to_all x0 -> x1, starting transfers between devices: none -> 7.59 us  [body(): lax.all_to_all(payload, 'gx', split_axis=0, concat_axis=0, tiled=True)]
    all_to_all x2, blocking collectives: 35.3 us -> 30.4 us  [share(): lax.all_to_all(moments, ('gx', 'gy'), split_axis=0, concat_axis=0, tiled=...]
    pallas_call x1, Pallas kernels: 9.75 us -> 13.2 us  [second_newton(): pl.pallas_call(second_kernel, out_shape=outs, in_specs=vmem(len(arrays)),...]
    ppermute x6 -> x8, waiting for transfers between devices: 2.15 us -> 5.56 us  [exchange(): return (lax.ppermute(to_high, axis, up), lax.ppermute(to_low, axis, down))]
    all_to_all x0 -> x1, waiting for transfers between devices: none -> 2.26 us  [body(): lax.all_to_all(payload, 'gx', split_axis=0, concat_axis=0, tiled=True)]
    pallas_call x1, Pallas kernels: 9.51 us -> 7.36 us  [first_newton(): pl.pallas_call(first_kernel, out_shape=outs, in_specs=vmem(len(arrays)),...]
    ppermute x6 -> x8, starting transfers between devices: 17.8 us -> 18.8 us  [exchange(): return (lax.ppermute(to_high, axis, up), lax.ppermute(to_low, axis, down))]
  transfers between devices with their start and end apart: 6 -> 9, of which waited for: 2 -> 3; matrix products, arithmetic and copies ran while one was open for 0% -> 0% of each run, Pallas kernels for 7% -> 19%
where the time goes in v7:
time: 103 us
  Pallas kernels  37.4 us (36%)
  blocking collectives  30.4 us (30%)
  starting transfers between devices  26.3 us (26%)
  waiting for transfers between devices  7.82 us (8%)
    all_to_all x2, blocking collectives, share(): lax.all_to_all(moments, ('gx', 'gy'), split_axis=0, concat_axis=0, tiled=...  30.4 us
    ppermute x8, starting transfers between devices, exchange(): return (lax.ppermute(to_high, axis, up), lax.ppermute(to_low, axis, down))  18.8 us
    pallas_call x1, Pallas kernels, second_newton(): pl.pallas_call(second_kernel, out_shape=outs, in_specs=vmem(len(arrays)),...  13.2 us
    all_to_all x1, starting transfers between devices, body(): lax.all_to_all(payload, 'gx', split_axis=0, concat_axis=0, tiled=True)  7.59 us
    pallas_call x1, Pallas kernels, first_newton(): pl.pallas_call(first_kernel, out_shape=outs, in_specs=vmem(len(arrays)),...  7.36 us
    ppermute x8, waiting for transfers between devices, exchange(): return (lax.ppermute(to_high, axis, up), lax.ppermute(to_low, axis, down))  5.56 us
    pallas_call x1, Pallas kernels, turn(): pl.pallas_call(turn_kernel, out_shape=outs, in_specs=vmem(5) + [smem(), p...  4.58 us
    pallas_call x1, Pallas kernels, prepare(): pl.pallas_call(prepare_kernel, out_shape=outs, in_specs=vmem(4), out_spec...  3.41 us
  transfers between devices with their start and end apart: 9, of which 3 were waited for; matrix products, arithmetic and copies ran while one was open for 0% of the time, Pallas kernels for 19%

profile of v7, /device:TPU:1, one launch (start us, length us, event | category | flops | bytes accessed | tf_op | source)
XLA Modules:
  0.0 102.7 jit_solution(4380623802186328258)
XLA Ops:
  0.6 2.7 %canopy_send.1 = (f32[16,8,256]{2,1,0:T(8,128)}, f32[16,256]{1,0:T(8,128)S(1)}) custom-call(f32[8,16,256]{2,1,0:T(8,128)} %forcing.5, s32[16,256]{1,0:T(8,128)} %cover.3, f32[8,16]{1,0:T(8,128)} %bitcast.43, s32[16]{0:T(128)} %bitcast.45, s32[16,1,256]{2,1,0:T(1,128)} %bitcast.41, f32[16,16,256]{2,1,0:T(8,128)} %bitcast.37), custom_call_target="tpu_custom_call" | custom-call | bytes 9000000 | tf_op jit(solution)/shard_map/canopy_send/pallas_call | solution.py:137
  3.4 7.6 %all-to-all-start = ((f32[16,8,256]{2,1,0:T(8,128)}), f32[16,8,256]{2,1,0:T(8,128)S(1)}, u32[]{:S(2)}, u32[]{:S(2)}) async-start(f32[16,8,256]{2,1,0:T(8,128)} %get-tuple-element.54.after), calls=%async_computation | async-start | bytes 262144 | tf_op jit(solution)/shard_map/all_to_all | solution.py:835
  11.0 4.6 %turn.1 = (f32[16,8,8,256]{3,2,1,0:T(8,128)S(1)}, f32[16,8,8,256]{3,2,1,0:T(8,128)S(1)}, f32[16,8,8,128]{3,2,1,0:T(8,128)}, f32[16,8,8,128]{3,2,1,0:T(8,128)}, f...) custom-call(f32[2048,128]{1,0:T(8,128)} %bitcast.35, ...), custom_call_target="tpu_custom_call" | custom-call | bytes 12000000 | tf_op jit(solution)/shard_map/turn/pallas_call | solution.py:339
  15.6 2.3 %all-to-all-done.arrived = f32[16,8,256]{2,1,0:T(8,128)S(1)} async-done(((f32[16,8,256]{2,1,0:T(8,128)}), f32[16,8,256]{2,1,0:T(8,128)S(1)}, u32[]{:S(2)}, u32[]{:S(2)}) %all-to-all-start) | async-done | bytes 131104 | tf_op jit(solution)/shard_map/all_to_all | solution.py:835
  17.8 0.1 collective-permute-start.2
  17.9 4.7 %collective-permute-start.3 = (f32[16,8,8,128]{3,2,1,0:T(8,128)}, f32[16,8,8,128]{3,2,1,0:T(8,128)S(1)}, u32[]{:S(2)}, u32[]{:S(2)}) collective-permute-start(f32[16,8,8,128]{3,2,1,0:T(8,128)} %get-tuple-element.81), channel_id=1, source_target_pairs={{8,0},{16,8},{24,16},{32,24},{40,32},{48,40},{56,48},{64,56},{72,6... | collective-permute-start | bytes 1572872 | tf_op jit(solution)/shard_map/ppermute | solution.py:807
  22.6 2.1 %canopy_source.1 = (f32[16,8,256]{2,1,0:T(8,128)S(1)}, f32[17,8,128]{2,1,0:T(8,128)S(1)}, f32[17,8,128]{2,1,0:T(8,128)S(1)}) custom-call(f32[16,8,256]{2,1,0:T(8,128)S(1)} %all-to-all-done.arrived, s32[16,1,256]{2,1,0:T(1,128)} %bitcast.42, s32[16]{0:T(128)} %bitcast.46, f32[8,16,256]{2,1,0:T(8,128)} %forcing.5, ...), custom_call_target="tpu_custom_call" | custom-call | bytes 7500000 | tf_op jit(solution)/shard_map/canopy_source/pallas_call | solution.py:214
  24.7 4.0 %collective-permute-start = (f32[17,8,128]{2,1,0:T(8,128)S(1)}, f32[17,8,128]{2,1,0:T(8,128)S(1)}, u32[]{:S(2)}, u32[]{:S(2)}) collective-permute-start(f32[17,8,128]{2,1,0:T(8,128)S(1)} %get-tuple-element.67), channel_id=1, source_target_pairs={{0,1},{1,2},{2,3},{3,4},{4,5},{5,6},{6,7},{7,0},{8,9},{9,10},{10,1... | collective-permute-start | bytes 208904 | tf_op jit(solution)/shard_map/ppermute | solution.py:807
  28.8 2.0 %owner_update.1.after = f32[16,16,256]{2,1,0:T(8,128)} custom-call(f32[16,8,256]{2,1,0:T(8,128)S(1)} %all-to-all-done.arrived, f32[16,16,256]{2,1,0:T(8,128)} %bitcast.38), custom_call_target="tpu_custom_call" | custom-call | bytes 6000000 | tf_op jit(solution)/shard_map/owner_update/pallas_call | solution.py:246
  30.7 0.0 collective-permute-done.from_left
  30.7 2.1 %collective-permute-done.1.from_right = f32[17,8,128]{2,1,0:T(8,128)S(1)} collective-permute-done((f32[17,8,128]{2,1,0:T(8,128)S(1)}, f32[17,8,128]{2,1,0:T(8,128)S(1)}, u32[]{:S(2)}, u32[]{:S(2)}) %collective-permute-start.1) | collective-permute-done | bytes 69664 | tf_op jit(solution)/shard_map/ppermute | solution.py:807
  32.8 0.1 corners.1
  32.9 0.1 collective-permute-start.4
  33.0 4.8 %collective-permute-start.5 = (f32[29,8,128]{2,1,0:T(8,128)S(1)}, f32[29,8,128]{2,1,0:T(8,128)S(1)}, u32[]{:S(2)}, u32[]{:S(2)}) collective-permute-start(f32[29,8,128]{2,1,0:T(8,128)S(1)} %get-tuple-element.84), channel_id=1, source_target_pairs={{8,0},{16,8},{24,16},{32,24},{40,32},{48,40},{56,48},{64,56},{72,6... | collective-permute-start | bytes 356360 | tf_op jit(solution)/shard_map/ppermute | solution.py:807
  37.7 3.5 %collective-permute-done.4.corner_prev = f32[29,8,128]{2,1,0:T(8,128)S(1)} collective-permute-done((f32[29,8,128]{2,1,0:T(8,128)S(1)}, f32[29,8,128]{2,1,0:T(8,128)S(1)}, u32[]{:S(2)}, u32[]{:S(2)}) %collective-permute-start.4) | collective-permute-done | bytes 118816 | tf_op jit(solution)/shard_map/ppermute | solution.py:807
  41.2 0.1 collective-permute-start.6
  41.3 5.0 %collective-permute-start.7 = (f32[12,8,8,128]{3,2,1,0:T(8,128)S(1)}, f32[12,8,8,128]{3,2,1,0:T(8,128)S(1)}, u32[]{:S(2)}, u32[]{:S(2)}) collective-permute-start(f32[12,8,8,128]{3,2,1,0:T(8,128)S(1)} %copy-done), channel_id=1, source_target_pairs={{8,0},{16,8},{24,16},{32,24},{40,32},{48,40},{56,48},{64,56},{72,6... | collective-permute-start | bytes 1179656 | tf_op jit(solution)/shard_map/ppermute | solution.py:807
  46.4 3.4 %prepare.1 = (f32[16,8,8,384]{3,2,1,0:T(8,128)S(1)}, f32[16,8,8,384]{3,2,1,0:T(8,128)S(1)}, f32[16,8,8,384]{3,2,1,0:T(8,128)S(1)}, f32[16,8,8,384]{3,2,1,0:T(8,1...) custom-call(f32[16,8,8,256]{3,2,1,0:T(8,128)S(1)} %get-tuple-element, ...), custom_call_target="tpu_custom_call" | custom-call | bytes 10200000 | tf_op jit(solution)/shard_map/prepare/pallas_call | solution.py:556
  49.8 7.4 %first_newton.1 = (f32[12,8,8,384]{3,2,1,0:T(8,128)S(1)}, f32[12,8,8,384]{3,2,1,0:T(8,128)S(1)}, f32[30,8,384]{2,1,0:T(8,128)S(1)}, f32[30,8,8,384]{3,2,1,0:T(8,...) custom-call(f32[16,8,8,384]{3,2,1,0:T(8,128)S(1)} %get-tuple-element.69.q_mid, ...), custom_call_target="tpu_custom_call" | custom-call | bytes 22500000 | tf_op jit(solution)/shard_map/first_newton/pallas_call | solution.py:661
  57.1 0.0 collective-permute-done.7.far_next
  57.1 16.4 %all_to_all.27 = f32[128,1,128]{2,1,0:T(1,128)S(1)} all-to-all(f32[128,1,128]{2,1,0:T(1,128)S(1)} %bitcast.33), channel_id=1, replica_groups=mesh['gx'=16,'gy'=8] {'gx','gy'}, dimensions={0} | all-to-all | bytes 131072 | tf_op jit(solution)/shard_map/all_to_all | solution.py:811
  73.6 13.2 %second_newton.1 = (f32[16,8,8,256]{3,2,1,0:T(8,128)S(1)}, f32[16,8,8,256]{3,2,1,0:T(8,128)S(1)}, f32[16,8,8,256]{3,2,1,0:T(8,128)S(1)}, f32[16,8,8,256]{3,2,1,0:T(8,128)S(1)}, f32[128,128]{1,0:T(8,128)S(1)}) custom-call(f32[16,8,8,384]{3,2,1,0:T(8,128)S(1)} %get-tuple-element.69.q_mid, f32[16,8,8,384]{3,2,1,0:T(8,128)S(1)} %get-tuple-element.70.k_mid, ...), custom_call_target="tpu_custom_call" | custom-call | bytes 36000000 | tf_op jit(solution)/shard_map/second_newton/pallas_call | solution.py:766
  86.8 13.9 %all_to_all.28 = f32[128,1,128]{2,1,0:T(1,128)S(1)} all-to-all(f32[128,1,128]{2,1,0:T(1,128)S(1)} %bitcast.34), channel_id=1, replica_groups=mesh['gx'=16,'gy'=8] {'gx','gy'}, dimensions={0} | all-to-all | bytes 131072 | tf_op jit(solution)/shard_map/all_to_all | solution.py:811
  100.7 1.9 %final_update.1 = f32[2048,128]{1,0:T(8,128)} custom-call(f32[16,8,8,256]{3,2,1,0:T(8,128)S(1)} %get-tuple-element.101.q, f32[16,8,8,256]{3,2,1,0:T(8,128)S(1)} %get-tuple-element.102.v0, f32[16,8,8,256]{3,2,1,0:T(8,128)S(1)} %get-tuple-element.103.v1, f32[16,8,8,256]{3,2,1,0:T(8,128)S(1)} %get-tuple-element.104.v2, f32[128,128]{1,0:T(8,128)S(1)} %bitcast.32), custom_call_target="tpu_custom_call" | custom-call | bytes 6000000 | tf_op jit(solution)/shard_map/final_update/pallas_call | solution.py:792
  (9 shorter events, 0.0 us)
Async XLA Ops:
  3.4 14.5 %all-to-all-start = ((f32[16,8,256]{2,1,0:T(8,128)}), f32[16,8,256]{2,1,0:T(8,128)S(1)}, u32[]{:S(2)}, u32[]{:S(2)}) async-start(f32[16,8,256]{2,1,0:T(8,128)} %get-tuple-element.54.after), calls=%async_computation | async-start | bytes 262144 | tf_op jit(solution)/shard_map/all_to_all | solution.py:835
  15.5 25.7 %copy-start.1 = (f32[12,8,8,128]{3,2,1,0:T(8,128)S(1)}, f32[12,8,8,128]{3,2,1,0:T(8,128)}, u32[]{:S(2)}) copy-start(f32[12,8,8,128]{3,2,1,0:T(8,128)} %get-tuple-element.96) | copy-start | bytes 1179652
  15.6 25.8 %copy-start = (f32[12,8,8,128]{3,2,1,0:T(8,128)S(1)}, f32[12,8,8,128]{3,2,1,0:T(8,128)}, u32[]{:S(2)}) copy-start(f32[12,8,8,128]{3,2,1,0:T(8,128)} %get-tuple-element.97) | copy-start | bytes 1179652
  17.8 23.4 %collective-permute-start.2 = (f32[16,8,8,128]{3,2,1,0:T(8,128)}, f32[16,8,8,128]{3,2,1,0:T(8,128)S(1)}, u32[]{:S(2)}, u32[]{:S(2)}) collective-permute-start(f32[16,8,8,128]{3,2,1,0:T(8,128)} %get-tuple-element.80), channel_id=1, source_target_pairs={{0,8},{8,16},{16,24},{24,32},{32,40},{40,48},{48,56},{56,64},{64,7... | collective-permute-start | bytes 1572872 | tf_op jit(solution)/shard_map/ppermute | solution.py:807
  17.9 23.3 %collective-permute-start.3 = (f32[16,8,8,128]{3,2,1,0:T(8,128)}, f32[16,8,8,128]{3,2,1,0:T(8,128)S(1)}, u32[]{:S(2)}, u32[]{:S(2)}) collective-permute-start(f32[16,8,8,128]{3,2,1,0:T(8,128)} %get-tuple-element.81), channel_id=1, source_target_pairs={{8,0},{16,8},{24,16},{32,24},{40,32},{48,40},{56,48},{64,56},{72,6... | collective-permute-start | bytes 1572872 | tf_op jit(solution)/shard_map/ppermute | solution.py:807
  24.7 6.0 %collective-permute-start = (f32[17,8,128]{2,1,0:T(8,128)S(1)}, f32[17,8,128]{2,1,0:T(8,128)S(1)}, u32[]{:S(2)}, u32[]{:S(2)}) collective-permute-start(f32[17,8,128]{2,1,0:T(8,128)S(1)} %get-tuple-element.67), channel_id=1, source_target_pairs={{0,1},{1,2},{2,3},{3,4},{4,5},{5,6},{6,7},{7,0},{8,9},{9,10},{10,1... | collective-permute-start | bytes 208904 | tf_op jit(solution)/shard_map/ppermute | solution.py:807
  28.7 4.0 %collective-permute-start.1 = (f32[17,8,128]{2,1,0:T(8,128)S(1)}, f32[17,8,128]{2,1,0:T(8,128)S(1)}, u32[]{:S(2)}, u32[]{:S(2)}) collective-permute-start(f32[17,8,128]{2,1,0:T(8,128)S(1)} %get-tuple-element.68), channel_id=1, source_target_pairs={{1,0},{2,1},{3,2},{4,3},{5,4},{6,5},{7,6},{0,7},{9,8},{10,9},{11,1... | collective-permute-start | bytes 208904 | tf_op jit(solution)/shard_map/ppermute | solution.py:807
  32.9 8.3 %collective-permute-start.4 = (f32[29,8,128]{2,1,0:T(8,128)S(1)}, f32[29,8,128]{2,1,0:T(8,128)S(1)}, u32[]{:S(2)}, u32[]{:S(2)}) collective-permute-start(f32[29,8,128]{2,1,0:T(8,128)S(1)} %get-tuple-element.83), channel_id=1, source_target_pairs={{0,8},{8,16},{16,24},{24,32},{32,40},{40,48},{48,56},{56,64},{64,7... | collective-permute-start | bytes 356360 | tf_op jit(solution)/shard_map/ppermute | solution.py:807
  33.0 8.3 %collective-permute-start.5 = (f32[29,8,128]{2,1,0:T(8,128)S(1)}, f32[29,8,128]{2,1,0:T(8,128)S(1)}, u32[]{:S(2)}, u32[]{:S(2)}) collective-permute-start(f32[29,8,128]{2,1,0:T(8,128)S(1)} %get-tuple-element.84), channel_id=1, source_target_pairs={{8,0},{16,8},{24,16},{32,24},{40,32},{48,40},{56,48},{64,56},{72,6... | collective-permute-start | bytes 356360 | tf_op jit(solution)/shard_map/ppermute | solution.py:807
  41.2 15.9 %collective-permute-start.6 = (f32[12,8,8,128]{3,2,1,0:T(8,128)S(1)}, f32[12,8,8,128]{3,2,1,0:T(8,128)S(1)}, u32[]{:S(2)}, u32[]{:S(2)}) collective-permute-start(f32[12,8,8,128]{3,2,1,0:T(8,128)S(1)} %copy-done.1), channel_id=1, source_target_pairs={{0,8},{8,16},{16,24},{24,32},{32,40},{40,48},{48,56},{56,64},{64,7... | collective-permute-start | bytes 1179656 | tf_op jit(solution)/shard_map/ppermute | solution.py:807
  41.3 15.8 %collective-permute-start.7 = (f32[12,8,8,128]{3,2,1,0:T(8,128)S(1)}, f32[12,8,8,128]{3,2,1,0:T(8,128)S(1)}, u32[]{:S(2)}, u32[]{:S(2)}) collective-permute-start(f32[12,8,8,128]{3,2,1,0:T(8,128)S(1)} %copy-done), channel_id=1, source_target_pairs={{8,0},{16,8},{24,16},{32,24},{40,32},{48,40},{56,48},{64,56},{72,6... | collective-permute-start | bytes 1179656 | tf_op jit(solution)/shard_map/ppermute | solution.py:807

commit v8 on v6

--- a/solution.py
+++ b/solution.py
@@ -123,7 +123,7 @@
         payload[o] = jnp.where(sub == used, live, out)
         return carry
 
-    lax.fori_loop(0, cols.shape[0], owner, 0, unroll=4)
+    lax.fori_loop(0, cols.shape[0], owner, 0, unroll=8)
 
 
 def canopy_send(forcing, cover, canopy_table, counts, cols, state):
@@ -170,7 +170,7 @@
         )
         return carry
 
-    lax.fori_loop(0, cols.shape[0], owner, 0, unroll=4)
+    lax.fori_loop(0, cols.shape[0], owner, 0, unroll=8)
 
     def piece(k):
         return total[k * ROWS : (k + 1) * ROWS, :]
@@ -231,7 +231,7 @@
         updated[i] = jnp.where(block[5:6] > 0.5, fresh, old)
         return carry
 
-    lax.fori_loop(0, arrived.shape[0], slot, 0)
+    lax.fori_loop(0, arrived.shape[0], slot, 0, unroll=8)
 
 
 def owner_update(arrived, state):
@@ -316,7 +316,7 @@
 
 def turn(*arrays):
     own_shape = shaped(ROWS, L, 8, COLS)
-    rim = shaped(RIM, L, 8, 128)
+    rim = pltpu.HBM((RIM, L, 8, 128), F32)
     edge = shaped(2 * L, 8, 128)
     outs = (own_shape, own_shape, rim, rim, edge, edge, shaped(ROOT, ROWS, COLS), shaped(ROWS, COLS))
     return pl.pallas_call(
@@ -510,8 +510,9 @@
 
 
 def prepare_kernel(
-    q_own, k_own, from_left, from_right,
-    q, k, resist, cx, cy, cyl, cz, diag, base,
+    q_own, k_own, from_left, from_right, source,
+    q, k, resist, cx, cy, cyl, cz, diag, v0, v1, v2, sums,
+    b,
 ):
     lane = iota((8, 128), 1)
     keep = side_mask(lane)
@@ -529,19 +530,32 @@
 
     lax.fori_loop(0, L, fill, 0)
 
+    a, c = from_left[2 * L], from_right[2 * L]
+    for x in range(ROWS):
+        b[x, :, :COLS] = source[x]
+        b[x, :, COLS:] = halo_tile(a, c, lane, 8 * x, 8 * x)
+    sub = iota((8, XC), 0)
+
     def emit(r, l, out):
-        base[r, l] = -out
-
-    couplings(q, resist, cx, cy, cyl, cz, diag, (1, ROWS - 1), 2, emit)
+        v0[r, l] = source_at(b, r, l, sub) - out
+
+    coefs = (cx, cy, cyl, cz, diag)
+    couplings(q, resist, *coefs, (1, ROWS - 1), 2, emit)
+    for step, (v_in, v_out, rows, block) in enumerate(
+        ((v0, v1, (2, 14), 6), (v1, v2, (3, 13), 5), (v2, None, (4, 12), 8))
+    ):
+        held = apply(v_in, v_out, coefs, 0, rows, block, no_sums(), True)
+        sums[2 * step], sums[2 * step + 1] = held
 
 
 def prepare(*arrays):
-    outs = (shaped(ROWS, L, 8, XC),) * 9
+    outs = (shaped(ROWS, L, 8, XC),) * 11 + (shaped(6, 8, COLS),)
     return pl.pallas_call(
         prepare_kernel,
         out_shape=outs,
-        in_specs=vmem(4),
-        out_specs=tuple(vmem(9)),
+        in_specs=vmem(len(arrays)),
+        out_specs=tuple(vmem(len(outs))),
+        scratch_shapes=[pltpu.VMEM((ROWS, L, XC), F32)],
         compiler_params=params(4),
         name="prepare",
     )(*arrays)
@@ -552,7 +566,7 @@
 
 
 def first_kernel(
-    q_mid, k_mid, resist_mid, cx_mid, cy_mid, cyl_mid, cz_mid, diag_mid, base,
+    q_mid, k_mid, resist_mid, cx_mid, cy_mid, cyl_mid, cz_mid, diag_mid, v0_mid, v1_mid, v2_mid, sums_mid,
     from_prev, from_next, source, corner_prev, corner_next, from_left, from_right,
     q, k, b, v0, v1, v2, moments,
     resist, cx, cy, cyl, cz, diag,
@@ -614,17 +628,17 @@
 
         couplings(q, resist, *coefs, rows, 1, emit)
 
-    def inner(r, carry):
-        for l in range(L):
-            v0[r, l] = source_at(b, r, l, sub) + base[r - HALO, l]
-        return carry
+    for mid, full, first in ((v0_mid, v0, 1), (v1_mid, v1, 2), (v2_mid, v2, 3)):
+        for x in (first, first + 1, ROWS - 2 - first, ROWS - 1 - first):
+            full[HALO + x] = mid[x]
 
     low, high = HALO, HALO + ROWS - 1
-    blocks((low + 1, high), 2, inner, 0)
-
     sums = []
-    for v_in, v_out, deep in ((v0, v1, 5), (v1, v2, 4), (v2, None, 0)):
-        held = apply(v_in, v_out, mids, HALO, (low + 1, high), 7, no_sums(), True)
+    for step, (v_in, v_out, deep) in enumerate(((v0, v1, 5), (v1, v2, 4), (v2, None, 0))):
+        held = sums_mid[2 * step], sums_mid[2 * step + 1]
+        more = step + 1
+        for rows in ((low + 1, low + 1 + more), (high - more, high)):
+            held = apply(v_in, v_out, mids, HALO, rows, more, held, True)
         held = apply(v_in, v_out, coefs, 0, (low, low + 1), 1, held, True)
         held = apply(v_in, v_out, coefs, RSHIFT, (high, high + 1), 1, held, True)
         if deep:
@@ -650,24 +664,29 @@
 
 
 def second_kernel(
-    q_mid, k_mid, q_rim, k_rim, b, u0, u1, u2, gathered,
-    q_own, w0, w1, w2, moments,
+    q_mid, k_mid, v0_mid, v1_mid, v2_mid, q_rim, k_rim, b, u0, u1, u2, gathered,
+    q_own, p0, p1, p2, moments,
     q1, resist, cx, cy, cyl, cz, diag, v0, v2,
 ):
     v1 = resist
     c0, c1, c2 = coefficients(gathered)
     sub = iota((8, XC), 0)
 
-    for q, k, shift, rows in (
-        (q_rim, k_rim, 0, (3, HALO)),
-        (q_mid, k_mid, HALO, (HALO, HALO + ROWS)),
-        (q_rim, k_rim, RSHIFT, (HALO + ROWS, XR - 3)),
+    full, mid = (u0, u1, u2), (v0_mid, v1_mid, v2_mid)
+    low, high = HALO, HALO + ROWS
+    for q, k, shift, held, back, rows, block in (
+        (q_rim, k_rim, 0, full, 0, (3, low), 2),
+        (q_mid, k_mid, low, full, 0, (low, low + 3), 3),
+        (q_mid, k_mid, low, mid, low, (low + 3, high - 3), 2),
+        (q_mid, k_mid, low, full, 0, (high - 3, high), 3),
+        (q_rim, k_rim, RSHIFT, full, 0, (high, XR - 3), 2),
     ):
 
-        def update(r, carry, q=q, k=k, shift=shift):
+        def update(r, carry, q=q, k=k, shift=shift, held=held, back=back):
             for l in range(L):
                 old = q[r - shift, l]
-                step = c0 * u0[r, l] + c1 * u1[r, l] + c2 * u2[r, l]
+                w0, w1, w2 = (w[r - back, l] for w in held)
+                step = c0 * w0 + c1 * w1 + c2 * w2
                 new = old + step
                 q1[r, l] = new
                 bend, resist[r, l], diag[r, l] = local_terms(new, k[r - shift, l])
@@ -675,14 +694,13 @@
                 v0[r, l] = source_at(b, r, l, sub) - stored
             return carry
 
-        blocks(rows, 2, update, 0)
+        blocks(rows, block, update, 0)
 
     def emit(r, l, out):
         v0[r, l] = v0[r, l] - out
 
     coefs = (cx, cy, cyl, cz, diag)
     couplings(q1, resist, *coefs, (4, XR - 4), 2, emit)
-    low, high = HALO, HALO + ROWS
     sums = []
     for v_in, v_out, deep in ((v0, v1, 2), (v1, v2, 1), (v2, None, 0)):
         sums += apply(v_in, v_out, coefs, 0, (low, high), 8, no_sums(), True)
@@ -693,7 +711,7 @@
 
     def keep(x, carry):
         for l in range(L):
-            for source, target in ((q1, q_own), (v0, w0), (v1, w1), (v2, w2)):
+            for source, target in ((q1, q_own), (v0, p0), (v1, p1), (v2, p2)):
                 target[x, l] = source[HALO + x, l, :, :COLS]
         return carry
 
@@ -714,35 +732,25 @@
     )(*arrays)
 
 
-def final_kernel(q, v0, v1, v2, gathered, out, held, sems):
+def final_kernel(q, v0, v1, v2, gathered, out):
     c0, c1, c2 = coefficients(gathered)
 
-    def send(l):
-        part = pl.ds(32 * l, 32)
-        return pltpu.make_async_copy(held.at[:, part], out.at[:, part], sems.at[l])
-
-    for l in range(L):
-
-        def row(x, carry, l=l):
+    def row(x, carry):
+        for l in range(L):
             value = q[x, l] + c0 * v0[x, l] + c1 * v1[x, l] + c2 * v2[x, l]
-            at = 32 * l + 16 * (x // 8) + x % 8
-            held[:, at, :] = value[:, :128]
-            held[:, at + 8, :] = value[:, 128:]
-            return carry
-
-        lax.fori_loop(0, ROWS, row, 0, unroll=4)
-        send(l).start()
-    for l in range(L):
-        send(l).wait()
+            out[chunk(x, l, 0), :] = value[:, :128]
+            out[chunk(x, l, 1), :] = value[:, 128:]
+        return carry
+
+    lax.fori_loop(0, ROWS, row, 0, unroll=2)
 
 
 def final_update(*arrays):
     return pl.pallas_call(
         final_kernel,
-        out_shape=shaped(8, 32 * L, 128),
+        out_shape=shaped(32 * LEV, 128),
         in_specs=vmem(len(arrays)),
-        out_specs=pl.BlockSpec(memory_space=pltpu.HBM),
-        scratch_shapes=[pltpu.VMEM((8, 32 * L, 128), F32), pltpu.SemaphoreType.DMA((L,))],
+        out_specs=vmem()[0],
         compiler_params=params(4),
         name="final_update",
     )(*arrays)
@@ -794,11 +802,13 @@
     to_next, to_prev = corners(source, from_left, from_right, in_hbm(new_state))
     corner_prev, corner_next = exchange(to_next, to_prev, "gx")
 
-    mids = prepare(q_own, k_own, from_left, from_right)
+    mids = prepare(q_own, k_own, from_left, from_right, source)
     q, k, b, v0, v1, v2, moments = first_newton(
         *mids, from_prev, from_next, source, corner_prev, corner_next, from_left, from_right
     )
-    q1, w0, w1, w2, moments = second_newton(mids[0], mids[1], q, k, b, v0, v1, v2, share(moments))
+    q1, w0, w1, w2, moments = second_newton(
+        mids[0], mids[1], *mids[8:11], q, k, b, v0, v1, v2, share(moments)
+    )
     pressure = unflat(final_update(q1, w0, w1, w2, share(moments)))
     return pressure, new_state.reshape(canopy_state.shape)
 

time: 101 us -> 97.7 us (0.967)
  waiting for transfers between devices: 5.65 us -> 4.37 us
  Pallas kernels: 36.9 us -> 35.7 us
    pallas_call x1, Pallas kernels: 9.25 us -> 6.49 us  [first_newton(): pl.pallas_call(first_kernel, out_shape=outs, in_specs=vmem(len(arrays)),...]
    pallas_call x2, Pallas kernels: 5.65 us -> 7.98 us  [the longest x1 6.04 us: prepare(): pl.pallas_call(prepare_kernel, out_shape=outs, in_specs=vmem(len(arrays))...]
    ppermute x6, waiting for transfers between devices: 3.76 us -> 2.1 us  [exchange(): return (lax.ppermute(to_high, axis, up), lax.ppermute(to_low, axis, down))]
  transfers between devices with their start and end apart: 7 -> 7, of which waited for: 3 -> 2; matrix products, arithmetic and copies ran while one was open for 0% -> 0% of each run, Pallas kernels for 13% -> 15%
where the time goes in v8:
time: 97.7 us; the launch traced here: 97.3 us
  Pallas kernels  35.7 us (37%)
  blocking collectives  35.3 us (36%)
  starting transfers between devices  21.3 us (22%)
  waiting for transfers between devices  4.37 us (4%)
    all_to_all x2, blocking collectives, share(): lax.all_to_all(moments, ('gx', 'gy'), split_axis=0, concat_axis=0, tiled=...  35.3 us
    ppermute x6, starting transfers between devices, exchange(): return (lax.ppermute(to_high, axis, up), lax.ppermute(to_low, axis, down))  13.7 us
    pallas_call x1, Pallas kernels, second_newton(): pl.pallas_call(second_kernel, out_shape=outs, in_specs=vmem(len(arrays)),...  9.74 us
    all_to_all x1, starting transfers between devices, body(): lax.all_to_all(payload, 'gx', split_axis=0, concat_axis=0, tiled=True)  7.59 us
    pallas_call x1, Pallas kernels, first_newton(): pl.pallas_call(first_kernel, out_shape=outs, in_specs=vmem(len(arrays)),...  6.49 us
    pallas_call x1, Pallas kernels, prepare(): pl.pallas_call(prepare_kernel, out_shape=outs, in_specs=vmem(len(arrays))...  6.04 us
    pallas_call x1, Pallas kernels, turn(): pl.pallas_call(turn_kernel, out_shape=outs, in_specs=vmem(5) + [smem(), p...  4.58 us
    pallas_call x1, Pallas kernels, canopy_send(): pl.pallas_call(canopy_send_kernel, out_shape=(shaped(owners, 8, COLS), sh...  2.73 us
  transfers between devices with their start and end apart: 7, of which 2 were waited for; matrix products, arithmetic and copies ran while one was open for 0% of the time, Pallas kernels for 15%

profile of v8, /device:TPU:1, one launch (start us, length us, event | category | flops | bytes accessed | tf_op | source)
XLA Modules:
  0.0 97.3 jit_solution(13652998083644857052)
XLA Ops:
  0.6 2.7 %canopy_send.1 = (f32[16,8,256]{2,1,0:T(8,128)}, f32[16,256]{1,0:T(8,128)S(1)}) custom-call(f32[8,16,256]{2,1,0:T(8,128)} %forcing.5, s32[16,256]{1,0:T(8,128)} %cover.3, f32[8,16]{1,0:T(8,128)} %bitcast.43, s32[16]{0:T(128)} %bitcast.45, s32[16,1,256]{2,1,0:T(1,128)} %bitcast.41, f32[16,16,256]{2,1,0:T(8,128)} %bitcast.37), custom_call_target="tpu_custom_call" | custom-call | tf_op jit(solution)/shard_map/canopy_send/pallas_call | solution.py:131
  3.4 7.6 %all-to-all-start = ((f32[16,8,256]{2,1,0:T(8,128)}), f32[16,8,256]{2,1,0:T(8,128)S(1)}, u32[]{:S(2)}, u32[]{:S(2)}) async-start(f32[16,8,256]{2,1,0:T(8,128)} %get-tuple-element.44.after), calls=%async_computation | async-start | bytes 262144 | tf_op jit(solution)/shard_map/all_to_all | solution.py:791
  11.0 4.6 %turn.1 = (f32[16,8,8,256]{3,2,1,0:T(8,128)S(1)}, f32[16,8,8,256]{3,2,1,0:T(8,128)S(1)}, f32[28,8,8,128]{3,2,1,0:T(8,128)}, f32[28,8,8,128]{3,2,1,0:T(8,128)}, f...) custom-call(f32[2048,128]{1,0:T(8,128)} %bitcast.35, ...), custom_call_target="tpu_custom_call" | custom-call | tf_op jit(solution)/shard_map/turn/pallas_call | solution.py:322
  15.5 2.3 %all-to-all-done.arrived = f32[16,8,256]{2,1,0:T(8,128)S(1)} async-done(((f32[16,8,256]{2,1,0:T(8,128)}), f32[16,8,256]{2,1,0:T(8,128)S(1)}, u32[]{:S(2)}, u32[]{:S(2)}) %all-to-all-start) | async-done | bytes 131104 | tf_op jit(solution)/shard_map/all_to_all | solution.py:791
  17.8 0.1 collective-permute-start.2
  17.9 4.7 %collective-permute-start.3 = (f32[28,8,8,128]{3,2,1,0:T(8,128)}, f32[28,8,8,128]{3,2,1,0:T(8,128)S(1)}, u32[]{:S(2)}, u32[]{:S(2)}) collective-permute-start(f32[28,8,8,128]{3,2,1,0:T(8,128)} %get-tuple-element.71), channel_id=1, source_target_pairs={{8,0},{16,8},{24,16},{32,24},{40,32},{48,40},{56,48},{64,56},{72,6... | collective-permute-start | bytes 2752520 | tf_op jit(solution)/shard_map/ppermute | solution.py:763
  22.6 2.1 %canopy_source.1 = (f32[16,8,256]{2,1,0:T(8,128)S(1)}, f32[17,8,128]{2,1,0:T(8,128)S(1)}, f32[17,8,128]{2,1,0:T(8,128)S(1)}) custom-call(f32[16,8,256]{2,1,0:T(8,128)S(1)} %all-to-all-done.arrived, s32[16,1,256]{2,1,0:T(1,128)} %bitcast.42, s32[16]{0:T(128)} %bitcast.46, f32[8,16,256]{2,1,0:T(8,128)} %forcing.5, ...), custom_call_target="tpu_custom_call" | custom-call | tf_op jit(solution)/shard_map/canopy_source/pallas_call | solution.py:207
  24.7 4.0 %collective-permute-start = (f32[17,8,128]{2,1,0:T(8,128)S(1)}, f32[17,8,128]{2,1,0:T(8,128)S(1)}, u32[]{:S(2)}, u32[]{:S(2)}) collective-permute-start(f32[17,8,128]{2,1,0:T(8,128)S(1)} %get-tuple-element.55), channel_id=1, source_target_pairs={{0,1},{1,2},{2,3},{3,4},{4,5},{5,6},{6,7},{7,0},{8,9},{9,10},{10,1... | collective-permute-start | bytes 208904 | tf_op jit(solution)/shard_map/ppermute | solution.py:763
  28.7 0.0 collective-permute-start.1
  28.8 2.0 %owner_update.1.after = f32[16,16,256]{2,1,0:T(8,128)} custom-call(f32[16,8,256]{2,1,0:T(8,128)S(1)} %all-to-all-done.arrived, f32[16,16,256]{2,1,0:T(8,128)} %bitcast.38), custom_call_target="tpu_custom_call" | custom-call | tf_op jit(solution)/shard_map/owner_update/pallas_call | solution.py:238
  30.7 0.0 collective-permute-done.from_left
  30.7 2.1 %collective-permute-done.1.from_right = f32[17,8,128]{2,1,0:T(8,128)S(1)} collective-permute-done((f32[17,8,128]{2,1,0:T(8,128)S(1)}, f32[17,8,128]{2,1,0:T(8,128)S(1)}, u32[]{:S(2)}, u32[]{:S(2)}) %collective-permute-start.1) | collective-permute-done | bytes 69664 | tf_op jit(solution)/shard_map/ppermute | solution.py:763
  32.8 0.1 corners.1
  32.9 0.1 collective-permute-start.4
  33.0 4.8 %collective-permute-start.5 = (f32[29,8,128]{2,1,0:T(8,128)S(1)}, f32[29,8,128]{2,1,0:T(8,128)S(1)}, u32[]{:S(2)}, u32[]{:S(2)}) collective-permute-start(f32[29,8,128]{2,1,0:T(8,128)S(1)} %get-tuple-element.73), channel_id=1, source_target_pairs={{8,0},{16,8},{24,16},{32,24},{40,32},{48,40},{56,48},{64,56},{72,6... | collective-permute-start | bytes 356360 | tf_op jit(solution)/shard_map/ppermute | solution.py:763
  37.7 6.0 %prepare.1 = (f32[16,8,8,384]{3,2,1,0:T(8,128)S(1)}, f32[16,8,8,384]{3,2,1,0:T(8,128)S(1)}, f32[16,8,8,384]{3,2,1,0:T(8,128)S(1)}, f32[16,8,8,384]{3,2,1,0:T(8,1...) custom-call(f32[16,8,8,256]{3,2,1,0:T(8,128)S(1)} %get-tuple-element, ...), custom_call_target="tpu_custom_call" | custom-call | tf_op jit(solution)/shard_map/prepare/pallas_call | solution.py:553
  43.8 0.0 collective-permute-done.4.corner_prev
  43.8 0.0 collective-permute-done.5.corner_next
  43.8 0.0 collective-permute-done.2.from_prev
  43.8 6.5 %first_newton.1 = (f32[18,8,8,384]{3,2,1,0:T(8,128)S(1)}, f32[18,8,8,384]{3,2,1,0:T(8,128)S(1)}, f32[30,8,384]{2,1,0:T(8,128)S(1)}, f32[30,8,8,384]{3,2,1,0:T(8,...) custom-call(f32[16,8,8,384]{3,2,1,0:T(8,128)S(1)} %get-tuple-element.58.q_mid, ...), custom_call_target="tpu_custom_call" | custom-call | tf_op jit(solution)/shard_map/first_newton/pallas_call | solution.py:655
  50.3 21.4 %all_to_all.27 = f32[128,1,128]{2,1,0:T(1,128)S(1)} all-to-all(f32[128,1,128]{2,1,0:T(1,128)S(1)} %bitcast.33), channel_id=1, replica_groups=mesh['gx'=16,'gy'=8] {'gx','gy'}, dimensions={0} | all-to-all | bytes 131072 | tf_op jit(solution)/shard_map/all_to_all | solution.py:767
  71.7 9.7 %second_newton.1 = (f32[16,8,8,256]{3,2,1,0:T(8,128)S(1)}, f32[16,8,8,256]{3,2,1,0:T(8,128)S(1)}, f32[16,8,8,256]{3,2,1,0:T(8,128)S(1)}, f32[16,8,8,256]{3,2,1,0:T(8,128)S(1)}, f32[128,128]{1,0:T(8,128)S(1)}) custom-call(f32[16,8,8,384]{3,2,1,0:T(8,128)S(1)} %get-tuple-element.58.q_mid, f32[16,8,8,384]{3,2,1,0:T(8,128)S(1)} %get-tuple-element.59.k_mid, ...), custom_call_target="tpu_custom_call" | custom-call | tf_op jit(solution)/shard_map/second_newton/pallas_call | solution.py:724
  81.5 13.9 %all_to_all.28 = f32[128,1,128]{2,1,0:T(1,128)S(1)} all-to-all(f32[128,1,128]{2,1,0:T(1,128)S(1)} %bitcast.34), channel_id=1, replica_groups=mesh['gx'=16,'gy'=8] {'gx','gy'}, dimensions={0} | all-to-all | bytes 131072 | tf_op jit(solution)/shard_map/all_to_all | solution.py:767
  95.4 1.9 %final_update.1 = f32[2048,128]{1,0:T(8,128)} custom-call(f32[16,8,8,256]{3,2,1,0:T(8,128)S(1)} %get-tuple-element.81.q, f32[16,8,8,256]{3,2,1,0:T(8,128)S(1)} %get-tuple-element.82.v0, f32[16,8,8,256]{3,2,1,0:T(8,128)S(1)} %get-tuple-element.83.v1, f32[16,8,8,256]{3,2,1,0:T(8,128)S(1)} %get-tuple-element.84.v2, f32[128,128]{1,0:T(8,128)S(1)} %bitcast.32), custom_call_target="tpu_custom_call" | custom-call | tf_op jit(solution)/shard_map/final_update/pallas_call | solution.py:749
  (1 shorter events, 0.0 us)
Async XLA Ops:
  3.4 14.5 %all-to-all-start = ((f32[16,8,256]{2,1,0:T(8,128)}), f32[16,8,256]{2,1,0:T(8,128)S(1)}, u32[]{:S(2)}, u32[]{:S(2)}) async-start(f32[16,8,256]{2,1,0:T(8,128)} %get-tuple-element.44.after), calls=%async_computation | async-start | bytes 262144 | tf_op jit(solution)/shard_map/all_to_all | solution.py:791
  17.8 26.0 %collective-permute-start.2 = (f32[28,8,8,128]{3,2,1,0:T(8,128)}, f32[28,8,8,128]{3,2,1,0:T(8,128)S(1)}, u32[]{:S(2)}, u32[]{:S(2)}) collective-permute-start(f32[28,8,8,128]{3,2,1,0:T(8,128)} %get-tuple-element.70), channel_id=1, source_target_pairs={{0,8},{8,16},{16,24},{24,32},{32,40},{40,48},{48,56},{56,64},{64,7... | collective-permute-start | bytes 2752520 | tf_op jit(solution)/shard_map/ppermute | solution.py:763
  17.9 25.9 %collective-permute-start.3 = (f32[28,8,8,128]{3,2,1,0:T(8,128)}, f32[28,8,8,128]{3,2,1,0:T(8,128)S(1)}, u32[]{:S(2)}, u32[]{:S(2)}) collective-permute-start(f32[28,8,8,128]{3,2,1,0:T(8,128)} %get-tuple-element.71), channel_id=1, source_target_pairs={{8,0},{16,8},{24,16},{32,24},{40,32},{48,40},{56,48},{64,56},{72,6... | collective-permute-start | bytes 2752520 | tf_op jit(solution)/shard_map/ppermute | solution.py:763
  24.7 6.0 %collective-permute-start = (f32[17,8,128]{2,1,0:T(8,128)S(1)}, f32[17,8,128]{2,1,0:T(8,128)S(1)}, u32[]{:S(2)}, u32[]{:S(2)}) collective-permute-start(f32[17,8,128]{2,1,0:T(8,128)S(1)} %get-tuple-element.55), channel_id=1, source_target_pairs={{0,1},{1,2},{2,3},{3,4},{4,5},{5,6},{6,7},{7,0},{8,9},{9,10},{10,1... | collective-permute-start | bytes 208904 | tf_op jit(solution)/shard_map/ppermute | solution.py:763
  28.7 4.0 %collective-permute-start.1 = (f32[17,8,128]{2,1,0:T(8,128)S(1)}, f32[17,8,128]{2,1,0:T(8,128)S(1)}, u32[]{:S(2)}, u32[]{:S(2)}) collective-permute-start(f32[17,8,128]{2,1,0:T(8,128)S(1)} %get-tuple-element.56), channel_id=1, source_target_pairs={{1,0},{2,1},{3,2},{4,3},{5,4},{6,5},{7,6},{0,7},{9,8},{10,9},{11,1... | collective-permute-start | bytes 208904 | tf_op jit(solution)/shard_map/ppermute | solution.py:763
  32.9 10.9 %collective-permute-start.4 = (f32[29,8,128]{2,1,0:T(8,128)S(1)}, f32[29,8,128]{2,1,0:T(8,128)S(1)}, u32[]{:S(2)}, u32[]{:S(2)}) collective-permute-start(f32[29,8,128]{2,1,0:T(8,128)S(1)} %get-tuple-element.72), channel_id=1, source_target_pairs={{0,8},{8,16},{16,24},{24,32},{32,40},{40,48},{48,56},{56,64},{64,7... | collective-permute-start | bytes 356360 | tf_op jit(solution)/shard_map/ppermute | solution.py:763
  33.0 10.8 %collective-permute-start.5 = (f32[29,8,128]{2,1,0:T(8,128)S(1)}, f32[29,8,128]{2,1,0:T(8,128)S(1)}, u32[]{:S(2)}, u32[]{:S(2)}) collective-permute-start(f32[29,8,128]{2,1,0:T(8,128)S(1)} %get-tuple-element.73), channel_id=1, source_target_pairs={{8,0},{16,8},{24,16},{32,24},{40,32},{48,40},{56,48},{64,56},{72,6... | collective-permute-start | bytes 356360 | tf_op jit(solution)/shard_map/ppermute | solution.py:763

commit v9 on v8

--- a/solution.py
+++ b/solution.py
@@ -12,6 +12,8 @@
 COLS = 256
 L = 8
 HALO = 7
+NEAR = 4
+FAR = HALO - NEAR
 XR = ROWS + 2 * HALO
 XC = 384
 OUTSIDE = 1e37
@@ -94,7 +96,7 @@
 
 
 def canopy_send_kernel(
-    forcing, cover, canopy_table, counts, cols, state, payload, conductance, split
+    forcing, cover, canopy_table, counts, cols, state, after, payload, conductance, split
 ):
     weights = looked_up(cover[...], canopy_table)
     total = weights[0] * forcing[0]
@@ -126,17 +128,17 @@
     lax.fori_loop(0, cols.shape[0], owner, 0, unroll=8)
 
 
-def canopy_send(forcing, cover, canopy_table, counts, cols, state):
+def canopy_send(forcing, cover, canopy_table, counts, cols, state, after):
     owners = cols.shape[0]
     return pl.pallas_call(
         canopy_send_kernel,
         out_shape=(shaped(owners, 8, COLS), shaped(ROWS, COLS)),
-        in_specs=vmem(2) + [smem(), smem()] + vmem(2),
+        in_specs=vmem(2) + [smem(), smem()] + vmem(2) + [pl.BlockSpec(memory_space=pl.ANY)],
         out_specs=tuple(vmem(2)),
         scratch_shapes=[pltpu.VMEM((15 * ROWS, COLS), BF16)],
         compiler_params=params(16),
         name="canopy_send",
-    )(forcing, cover, canopy_table, counts, cols, state)
+    )(forcing, cover, canopy_table, counts, cols, state, after)
 
 
 def softplus(v):
@@ -257,80 +259,120 @@
     return pl.ds(32 * l + 16 * (x // 8) + 8 * t + x % 8, 8, stride=32 * L)
 
 
-RIM = 2 * HALO * 2
+def rim_shape(rows):
+    return 2 * rows * 2, L, 8, 128
 
 
 def turn_kernel(
-    pressure, conductivity, forcing, cover, vegetated, root_table, after,
-    q, k, to_next, to_prev, edge_left, edge_right, uptake, surface,
-    next_rim, prev_rim, sems,
+    pressure, conductivity,
+    q, k, top, near_next, near_prev, far_next, far_prev,
+    held_q, held_k, near_next_rim, near_prev_rim, far_next_rim, far_prev_rim, sems,
+):
+    fetches = []
+    for l in range(L):
+        part = pl.ds(32 * l, 32)
+        for f, (field, held) in enumerate(((pressure, held_q), (conductivity, held_k))):
+            fetches.append(pltpu.make_async_copy(field.at[:, part], held.at[:, part], sems.at[f, l]))
+    for fetch in fetches:
+        fetch.start()
+    sends = []
+    for l in range(L):
+        fetches[2 * l].wait()
+        fetches[2 * l + 1].wait()
+        for f, (held, target) in enumerate(((held_q, q), (held_k, k))):
+            for x in range(ROWS):
+                for t in range(2):
+                    part = held[:, 32 * l + 16 * (x // 8) + 8 * t + x % 8, :]
+                    target[x, l, :, 128 * t : 128 * t + 128] = part
+                    if x < NEAR:
+                        near_prev_rim[2 * (f * NEAR + x) + t, l] = part
+                    elif x < HALO:
+                        far_prev_rim[2 * (f * FAR + x - NEAR) + t, l] = part
+                    if x >= ROWS - NEAR:
+                        near_next_rim[2 * (f * NEAR + x - ROWS + NEAR) + t, l] = part
+                    elif x >= ROWS - HALO:
+                        far_next_rim[2 * (f * FAR + x - ROWS + HALO) + t, l] = part
+        if l % 4 == 3:
+            part = pl.ds(l - 3, 4)
+            for i, (rim, out) in enumerate(
+                (
+                    (far_next_rim, far_next),
+                    (far_prev_rim, far_prev),
+                    (near_next_rim, near_next),
+                    (near_prev_rim, near_prev),
+                )
+            ):
+                sends.append(pltpu.make_async_copy(rim.at[:, part], out.at[:, part], sems.at[2 + i, l]))
+                sends[-1].start()
+    for m in range(ROOT):
+        for xt in range(2):
+            for t in range(2):
+                top[m, 8 * xt : 8 * xt + 8, 128 * t : 128 * t + 128] = held_q[
+                    0, pl.ds(32 * m + 16 * xt + 8 * t, 8), :
+                ]
+    for send in sends:
+        send.wait()
+
+
+def turn(*arrays):
+    own_shape = shaped(ROWS, L, 8, COLS)
+    near, far = rim_shape(NEAR), rim_shape(FAR)
+    rims = [pltpu.HBM(shape, F32) for shape in (near, near, far, far)]
+    hbm = pl.BlockSpec(memory_space=pltpu.HBM)
+    return pl.pallas_call(
+        turn_kernel,
+        out_shape=(own_shape, own_shape, shaped(ROOT, ROWS, COLS), *rims),
+        in_specs=[hbm, hbm],
+        out_specs=(*vmem(3), hbm, hbm, hbm, hbm),
+        scratch_shapes=[
+            pltpu.VMEM((8, 32 * L, 128), F32),
+            pltpu.VMEM((8, 32 * L, 128), F32),
+            *[pltpu.VMEM(shape, F32) for shape in (near, near, far, far)],
+            pltpu.SemaphoreType.DMA((6, L)),
+        ],
+        compiler_params=params(8),
+        name="turn",
+    )(*arrays)
+
+
+def sides_kernel(
+    q, k, top, forcing, cover, vegetated, root_table, edge_left, edge_right, uptake, surface
 ):
     lane = iota((8, 128), 1)
 
     def layer(l, carry):
-        for f, (field, target) in enumerate(((pressure, q), (conductivity, k))):
+        for f, field in enumerate((q, k)):
             first = jnp.zeros((8, 128), F32)
             last = jnp.zeros((8, 128), F32)
             for x in range(ROWS):
-                for t in range(2):
-                    part = field[chunk(x, l, t), :]
-                    target[x, l, :, 128 * t : 128 * t + 128] = part
-                    if x < HALO:
-                        prev_rim[2 * (f * HALO + x) + t, l] = part
-                    if x >= ROWS - HALO:
-                        next_rim[2 * (f * HALO + x - ROWS + HALO) + t, l] = part
-                    here = jnp.logical_and(lane >= 8 * x, lane < 8 * x + 8)
-                    if t == 0:
-                        first = jnp.where(here, lanes(part, 8 * x), first)
-                    else:
-                        last = jnp.where(here, lanes(part, 8 * x - 120), last)
+                here = jnp.logical_and(lane >= 8 * x, lane < 8 * x + 8)
+                first = jnp.where(here, lanes(field[x, l, :, :128], 8 * x), first)
+                last = jnp.where(here, lanes(field[x, l, :, 128:], 8 * x - 120), last)
             edge_left[f * L + l] = first
             edge_right[f * L + l] = last
         return carry
 
-    lax.fori_loop(0, L, layer, 0)
-    sends = [
-        pltpu.make_async_copy(next_rim, to_next, sems.at[0]),
-        pltpu.make_async_copy(prev_rim, to_prev, sems.at[1]),
-    ]
-    for send in sends:
-        send.start()
+    lax.fori_loop(0, L, layer, 0, unroll=4)
     roots = looked_up(cover[...], root_table)
     planted = vegetated[...] == 1
     for m in range(ROOT):
-        top = jnp.concatenate(
-            [
-                jnp.concatenate([pressure[pl.ds(32 * m + 16 * xt + 8 * t, 8), :] for t in range(2)], axis=1)
-                for xt in range(2)
-            ],
-            axis=0,
-        )
-        moist = jax.nn.sigmoid(2.0 * (top + 1.5))
+        moist = jax.nn.sigmoid(2.0 * (top[m] + 1.5))
         uptake[m] = jnp.where(planted, roots[m] * moist, 0.0)
         if m == 0:
             evaporation = jnp.where(planted, 0.0, 0.5) * softplus(forcing[3] - forcing[2]) * moist
             surface[...] = 0.3 * softplus(forcing[4]) - evaporation
-    for send in sends:
-        send.wait()
-
-
-def turn(*arrays):
-    own_shape = shaped(ROWS, L, 8, COLS)
-    rim = pltpu.HBM((RIM, L, 8, 128), F32)
+
+
+def sides(*arrays):
     edge = shaped(2 * L, 8, 128)
-    outs = (own_shape, own_shape, rim, rim, edge, edge, shaped(ROOT, ROWS, COLS), shaped(ROWS, COLS))
-    return pl.pallas_call(
-        turn_kernel,
+    outs = (edge, edge, shaped(ROOT, ROWS, COLS), shaped(ROWS, COLS))
+    return pl.pallas_call(
+        sides_kernel,
         out_shape=outs,
-        in_specs=vmem(5) + [smem(), pl.BlockSpec(memory_space=pl.ANY)],
-        out_specs=(*vmem(2), *[pl.BlockSpec(memory_space=pltpu.HBM)] * 2, *vmem(4)),
-        scratch_shapes=[
-            pltpu.VMEM((RIM, L, 8, 128), F32),
-            pltpu.VMEM((RIM, L, 8, 128), F32),
-            pltpu.SemaphoreType.DMA((2,)),
-        ],
-        compiler_params=params(24),
-        name="turn",
+        in_specs=vmem(6) + [smem()],
+        out_specs=tuple(vmem(len(outs))),
+        compiler_params=params(8),
+        name="sides",
     )(*arrays)
 
 
@@ -391,7 +433,8 @@
             held = row(rows[0] + i * block + j, held)
         return held
 
-    return lax.fori_loop(0, (rows[1] - rows[0]) // block, step, carry)
+    steps = (rows[1] - rows[0]) // block
+    return step(0, carry) if steps == 1 else lax.fori_loop(0, steps, step, carry)
 
 
 def couplings(q, resist, cx, cy, cyl, cz, diag, rows, block, emit):
@@ -540,7 +583,7 @@
         v0[r, l] = source_at(b, r, l, sub) - out
 
     coefs = (cx, cy, cyl, cz, diag)
-    couplings(q, resist, *coefs, (1, ROWS - 1), 2, emit)
+    couplings(q, resist, *coefs, (1, ROWS - 1), 7, emit)
     for step, (v_in, v_out, rows, block) in enumerate(
         ((v0, v1, (2, 14), 6), (v1, v2, (3, 13), 5), (v2, None, (4, 12), 8))
     ):
@@ -567,7 +610,7 @@
 
 def first_kernel(
     q_mid, k_mid, resist_mid, cx_mid, cy_mid, cyl_mid, cz_mid, diag_mid, v0_mid, v1_mid, v2_mid, sums_mid,
-    from_prev, from_next, source, corner_prev, corner_next, from_left, from_right,
+    near_prev, near_next, far_prev, far_next, source, corner_prev, corner_next, from_left, from_right,
     q, k, b, v0, v1, v2, moments,
     resist, cx, cy, cyl, cz, diag,
 ):
@@ -578,14 +621,16 @@
     def fill(l, carry):
         for f, target in enumerate((q, k)):
             at = 2 * BHALO + f * L + l
-            for side, corner, r, spot, here in (
-                (from_prev, corner_prev, 0, 8 * (8 - HALO), has_prev),
-                (from_next, corner_next, HALO + ROWS - RSHIFT, 0, has_next),
+            for side, rows, corner, r, spot, here in (
+                (far_prev, FAR, corner_prev, 0, 8 * (8 - HALO), has_prev),
+                (near_prev, NEAR, corner_prev, FAR, 8 * (8 - NEAR), has_prev),
+                (near_next, NEAR, corner_next, RROWS - HALO, 0, has_next),
+                (far_next, FAR, corner_next, RROWS - FAR, 8 * NEAR, has_next),
             ):
                 tile = corner[at]
-                for i in range(HALO):
+                for i in range(rows):
                     left_at = spot + 8 * i
-                    row = [side[2 * (f * HALO + i) + t, l] for t in range(2)]
+                    row = [side[2 * (f * rows + i) + t, l] for t in range(2)]
                     row.append(halo_tile(tile, tile, lane, left_at, 64 + left_at))
                     for t in range(3):
                         part = row[t]
@@ -626,7 +671,7 @@
         def emit(r, l, out, shift=shift):
             v0[r + shift, l] = source_at(b, r + shift, l, sub) - out
 
-        couplings(q, resist, *coefs, rows, 1, emit)
+        couplings(q, resist, *coefs, rows, HALO, emit)
 
     for mid, full, first in ((v0_mid, v0, 1), (v1_mid, v1, 2), (v2_mid, v2, 3)):
         for x in (first, first + 1, ROWS - 2 - first, ROWS - 1 - first):
@@ -700,7 +745,7 @@
         v0[r, l] = v0[r, l] - out
 
     coefs = (cx, cy, cyl, cz, diag)
-    couplings(q1, resist, *coefs, (4, XR - 4), 2, emit)
+    couplings(q1, resist, *coefs, (4, XR - 4), 11, emit)
     sums = []
     for v_in, v_out, deep in ((v0, v1, 2), (v1, v2, 1), (v2, None, 0)):
         sums += apply(v_in, v_out, coefs, 0, (low, high), 8, no_sums(), True)
@@ -784,16 +829,21 @@
     counts = in_hbm(pair_counts.reshape(owners))
     state = in_hbm(canopy_state.reshape(owners, 16, COLS))
     forcing, cover_type, vegetated = in_hbm(forcing), in_hbm(cover_type), in_hbm(vegetated)
-    old, conductivity = in_hbm(flat(pressure_old)), in_hbm(flat(conductivity))
+    old, conductivity = (in_hbm(flat(v).reshape(8, 32 * L, 128)) for v in (pressure_old, conductivity))
     canopy_table, root_table = in_hbm(canopy_table.T), in_hbm(root_table.T)
 
-    payload, conductance = canopy_send(forcing, cover_type, canopy_table, counts, cols, state)
+    q_own, k_own, top, near_next, near_prev, far_next, far_prev = turn(old, conductivity)
+    far_prev, far_next = exchange(far_next, far_prev, "gx")
+    payload, conductance = canopy_send(forcing, cover_type, canopy_table, counts, cols, state, top)
     arrived = lax.all_to_all(payload, "gx", split_axis=0, concat_axis=0, tiled=True)
-    q_own, k_own, to_next, to_prev, edge_left, edge_right, uptake, surface = turn(
-        old, conductivity, forcing, cover_type, vegetated, root_table, payload
+    top, payload = lax.optimization_barrier((top, payload))
+    edge_left, edge_right, uptake, surface = sides(
+        q_own, k_own, top, forcing, cover_type, vegetated, root_table
     )
-    to_next, to_prev, arrived = lax.optimization_barrier((to_next, to_prev, arrived))
-    from_prev, from_next = exchange(to_next, to_prev, "gx")
+    near_next, near_prev, arrived, far_prev, far_next, surface = lax.optimization_barrier(
+        (near_next, near_prev, arrived, far_prev, far_next, surface)
+    )
+    near_prev, near_next = exchange(near_next, near_prev, "gx")
     source, to_right, to_left = canopy_source(
         arrived, cols, counts, forcing, conductance, uptake, surface, edge_left, edge_right
     )
@@ -804,7 +854,7 @@
 
     mids = prepare(q_own, k_own, from_left, from_right, source)
     q, k, b, v0, v1, v2, moments = first_newton(
-        *mids, from_prev, from_next, source, corner_prev, corner_next, from_left, from_right
+        *mids, near_prev, near_next, far_prev, far_next, source, corner_prev, corner_next, from_left, from_right
     )
     q1, w0, w1, w2, moments = second_newton(
         mids[0], mids[1], *mids[8:11], q, k, b, v0, v1, v2, share(moments)

time: 97.7 us -> 95.7 us (0.980)
  blocking collectives: 35.3 us -> 29.1 us
  waiting for transfers between devices: 4.37 us -> 6.93 us
  starting transfers between devices: 21.3 us -> 23.6 us
    ppermute x6 -> x8, starting transfers between devices: 13.7 us -> 20.1 us  [exchange(): return (lax.ppermute(to_high, axis, up), lax.ppermute(to_low, axis, down))]
    all_to_all x2, blocking collectives: 35.3 us -> 29.1 us  [share(): lax.all_to_all(moments, ('gx', 'gy'), split_axis=0, concat_axis=0, tiled=...]
    all_to_all x1, starting transfers between devices: 7.59 us -> 3.51 us  [body(): lax.all_to_all(payload, 'gx', split_axis=0, concat_axis=0, tiled=True)]
    all_to_all x1, waiting for transfers between devices: 2.27 us -> 4.85 us  [body(): lax.all_to_all(payload, 'gx', split_axis=0, concat_axis=0, tiled=True)]
    pallas_call x1 -> x2, Pallas kernels: 4.58 us -> 5.24 us  [the longest x1 3.47 us: turn(): pl.pallas_call(turn_kernel, out_shape=(own_shape, own_shape, shaped(ROOT,...]
    ppermute x6 -> x8, waiting for transfers between devices: 2.1 us -> 2.08 us  [exchange(): return (lax.ppermute(to_high, axis, up), lax.ppermute(to_low, axis, down))]
  transfers between devices with their start and end apart: 7 -> 9, of which waited for: 2 -> 2; matrix products, arithmetic and copies ran while one was open for 0% -> 0% of each run, Pallas kernels for 15% -> 15%
where the time goes in v9:
time: 95.7 us; the launch traced here: 95.3 us
  Pallas kernels  35 us (37%)
  blocking collectives  29.1 us (30%)
  starting transfers between devices  23.6 us (25%)
  waiting for transfers between devices  6.93 us (7%)
    all_to_all x2, blocking collectives, share(): lax.all_to_all(moments, ('gx', 'gy'), split_axis=0, concat_axis=0, tiled=...  29.1 us
    ppermute x8, starting transfers between devices, exchange(): return (lax.ppermute(to_high, axis, up), lax.ppermute(to_low, axis, down))  20.1 us
    pallas_call x1, Pallas kernels, second_newton(): pl.pallas_call(second_kernel, out_shape=outs, in_specs=vmem(len(arrays)),...  9.26 us
    pallas_call x1, Pallas kernels, prepare(): pl.pallas_call(prepare_kernel, out_shape=outs, in_specs=vmem(len(arrays))...  6 us
    pallas_call x1, Pallas kernels, first_newton(): pl.pallas_call(first_kernel, out_shape=outs, in_specs=vmem(len(arrays)),...  5.64 us
    all_to_all x1, waiting for transfers between devices, body(): lax.all_to_all(payload, 'gx', split_axis=0, concat_axis=0, tiled=True)  4.85 us
    all_to_all x1, starting transfers between devices, body(): lax.all_to_all(payload, 'gx', split_axis=0, concat_axis=0, tiled=True)  3.51 us
    pallas_call x1, Pallas kernels, turn(): pl.pallas_call(turn_kernel, out_shape=(own_shape, own_shape, shaped(ROOT,...  3.47 us
  transfers between devices with their start and end apart: 9, of which 2 were waited for; matrix products, arithmetic and copies ran while one was open for 0% of the time, Pallas kernels for 15%

profile of v9, /device:TPU:1, one launch (start us, length us, event | category | flops | bytes accessed | tf_op | source)
XLA Modules:
  0.0 95.3 jit_solution(3708277026049159771)
XLA Ops:
  0.6 3.5 %turn.1 = (f32[16,8,8,256]{3,2,1,0:T(8,128)S(1)}, f32[16,8,8,256]{3,2,1,0:T(8,128)S(1)}, f32[8,16,256]{2,1,0:T(8,128)S(1)}, f32[16,8,8,128]{3,2,1,0:T(8,128)}, f...) custom-call(f32[8,256,128]{2,1,0:T(8,128)} %bitcast.37, f32[8,256,128]{2,1,0:T(8,128)} %bitcast.38), custom_call_target="tpu_custom_call" | custom-call | tf_op jit(solution)/shard_map/turn/pallas_call | solution.py:322
  4.1 2.2 %collective-permute-start = (f32[12,8,8,128]{3,2,1,0:T(8,128)}, f32[12,8,8,128]{3,2,1,0:T(8,128)S(1)}, u32[]{:S(2)}, u32[]{:S(2)}) collective-permute-start(f32[12,8,8,128]{3,2,1,0:T(8,128)} %get-tuple-element.57), channel_id=1, source_target_pairs={{0,8},{8,16},{16,24},{24,32},{32,40},{40,48},{48,56},{56,64},{64,7... | collective-permute-start | bytes 1179656 | tf_op jit(solution)/shard_map/ppermute | solution.py:808
  6.3 3.7 %collective-permute-start.1 = (f32[12,8,8,128]{3,2,1,0:T(8,128)}, f32[12,8,8,128]{3,2,1,0:T(8,128)S(1)}, u32[]{:S(2)}, u32[]{:S(2)}) collective-permute-start(f32[12,8,8,128]{3,2,1,0:T(8,128)} %get-tuple-element.58), channel_id=1, source_target_pairs={{8,0},{16,8},{24,16},{32,24},{40,32},{48,40},{56,48},{64,56},{72,6... | collective-permute-start | bytes 1179656 | tf_op jit(solution)/shard_map/ppermute | solution.py:808
  10.0 2.7 %canopy_send.1 = (f32[16,8,256]{2,1,0:T(8,128)}, f32[16,256]{1,0:T(8,128)S(1)}) custom-call(f32[8,16,256]{2,1,0:T(8,128)} %forcing.5, s32[16,256]{1,0:T(8,128)} %cover.3, f32[8,16]{1,0:T(8,128)} %bitcast.43, s32[16]{0:T(128)} %bitcast.45, s32[16,1,256]{2,1,0:T(1,128)} %bitcast.41, f32[16,16,256]{2,1,0:T(8,128)} %bitcast.35, ...), custom_call_target="tpu_custom_call" | custom-call | tf_op jit(solution)/shard_map/canopy_send/pallas_call | solution.py:133
  12.7 3.5 %all-to-all-start = ((f32[16,8,256]{2,1,0:T(8,128)}), f32[16,8,256]{2,1,0:T(8,128)S(1)}, u32[]{:S(2)}, u32[]{:S(2)}) async-start(f32[16,8,256]{2,1,0:T(8,128)} %get-tuple-element.56), calls=%async_computation | async-start | bytes 262144 | tf_op jit(solution)/shard_map/all_to_all | solution.py:838
  16.3 1.8 %sides.1 = (f32[16,8,128]{2,1,0:T(8,128)S(1)}, f32[16,8,128]{2,1,0:T(8,128)S(1)}, f32[8,16,256]{2,1,0:T(8,128)S(1)}, f32[16,256]{1,0:T(8,128)S(1)}) custom-call(f32[16,8,8,256]{3,2,1,0:T(8,128)S(1)} %get-tuple-element.51.q.q_own, f32[16,8,8,256]{3,2,1,0:T(8,128)S(1)} %get-tuple-element.52.k.k_own, f32[8,16,256]{2,1,0:T(8,128)S(1)} %get-tuple-element.59.after.top, ...), custom_call_target="tpu_custom_call" | custom-call | tf_op jit(solution)/shard_map/sides/pallas_call | solution.py:369
  18.0 4.9 %all-to-all-done.arrived = f32[16,8,256]{2,1,0:T(8,128)S(1)} async-done(((f32[16,8,256]{2,1,0:T(8,128)}), f32[16,8,256]{2,1,0:T(8,128)S(1)}, u32[]{:S(2)}, u32[]{:S(2)}) %all-to-all-start) | async-done | bytes 131104 | tf_op jit(solution)/shard_map/all_to_all | solution.py:838
  22.9 0.0 collective-permute-done.far_prev
  22.9 0.2 collective-permute-start.4
  23.1 4.6 %collective-permute-start.5 = (f32[16,8,8,128]{3,2,1,0:T(8,128)}, f32[16,8,8,128]{3,2,1,0:T(8,128)S(1)}, u32[]{:S(2)}, u32[]{:S(2)}) collective-permute-start(f32[16,8,8,128]{3,2,1,0:T(8,128)} %get-tuple-element.83), channel_id=1, source_target_pairs={{8,0},{16,8},{24,16},{32,24},{40,32},{48,40},{56,48},{64,56},{72,6... | collective-permute-start | bytes 1572872 | tf_op jit(solution)/shard_map/ppermute | solution.py:808
  27.7 2.1 %canopy_source.1 = (f32[16,8,256]{2,1,0:T(8,128)S(1)}, f32[17,8,128]{2,1,0:T(8,128)S(1)}, f32[17,8,128]{2,1,0:T(8,128)S(1)}) custom-call(f32[16,8,256]{2,1,0:T(8,128)S(1)} %all-to-all-done.arrived, s32[16,1,256]{2,1,0:T(1,128)} %bitcast.42, s32[16]{0:T(128)} %bitcast.46, f32[8,16,256]{2,1,0:T(8,128)} %forcing.5, ...), custom_call_target="tpu_custom_call" | custom-call | tf_op jit(solution)/shard_map/canopy_source/pallas_call | solution.py:209
  29.8 4.5 %collective-permute-start.2 = (f32[17,8,128]{2,1,0:T(8,128)S(1)}, f32[17,8,128]{2,1,0:T(8,128)S(1)}, u32[]{:S(2)}, u32[]{:S(2)}) collective-permute-start(f32[17,8,128]{2,1,0:T(8,128)S(1)} %get-tuple-element.67), channel_id=1, source_target_pairs={{0,1},{1,2},{2,3},{3,4},{4,5},{5,6},{6,7},{7,0},{8,9},{9,10},{10,1... | collective-permute-start | bytes 208904 | tf_op jit(solution)/shard_map/ppermute | solution.py:808
  34.3 0.0 collective-permute-start.3
  34.3 2.0 %owner_update.1.after = f32[16,16,256]{2,1,0:T(8,128)} custom-call(f32[16,8,256]{2,1,0:T(8,128)S(1)} %all-to-all-done.arrived, f32[16,16,256]{2,1,0:T(8,128)} %bitcast.36), custom_call_target="tpu_custom_call" | custom-call | tf_op jit(solution)/shard_map/owner_update/pallas_call | solution.py:240
  36.3 2.1 %collective-permute-done.3.from_right = f32[17,8,128]{2,1,0:T(8,128)S(1)} collective-permute-done((f32[17,8,128]{2,1,0:T(8,128)S(1)}, f32[17,8,128]{2,1,0:T(8,128)S(1)}, u32[]{:S(2)}, u32[]{:S(2)}) %collective-permute-start.3) | collective-permute-done | bytes 69664 | tf_op jit(solution)/shard_map/ppermute | solution.py:808
  38.4 0.1 corners.1
  38.5 0.1 collective-permute-start.6
  38.5 4.8 %collective-permute-start.7 = (f32[29,8,128]{2,1,0:T(8,128)S(1)}, f32[29,8,128]{2,1,0:T(8,128)S(1)}, u32[]{:S(2)}, u32[]{:S(2)}) collective-permute-start(f32[29,8,128]{2,1,0:T(8,128)S(1)} %get-tuple-element.87), channel_id=1, source_target_pairs={{8,0},{16,8},{24,16},{32,24},{40,32},{48,40},{56,48},{64,56},{72,6... | collective-permute-start | bytes 356360 | tf_op jit(solution)/shard_map/ppermute | solution.py:808
  43.3 6.0 %prepare.1 = (f32[16,8,8,384]{3,2,1,0:T(8,128)S(1)}, f32[16,8,8,384]{3,2,1,0:T(8,128)S(1)}, f32[16,8,8,384]{3,2,1,0:T(8,128)S(1)}, f32[16,8,8,384]{3,2,1,0:T(8,1...) custom-call(f32[16,8,8,256]{3,2,1,0:T(8,128)S(1)} %get-tuple-element, ...), custom_call_target="tpu_custom_call" | custom-call | tf_op jit(solution)/shard_map/prepare/pallas_call | solution.py:596
  49.4 5.6 %first_newton.1 = (f32[18,8,8,384]{3,2,1,0:T(8,128)S(1)}, f32[18,8,8,384]{3,2,1,0:T(8,128)S(1)}, f32[30,8,384]{2,1,0:T(8,128)S(1)}, f32[30,8,8,384]{3,2,1,0:T(8,...) custom-call(f32[16,8,8,384]{3,2,1,0:T(8,128)S(1)} %get-tuple-element.70.q_mid, ...), custom_call_target="tpu_custom_call" | custom-call | tf_op jit(solution)/shard_map/first_newton/pallas_call | solution.py:700
  55.0 15.2 %all_to_all.27 = f32[128,1,128]{2,1,0:T(1,128)S(1)} all-to-all(f32[128,1,128]{2,1,0:T(1,128)S(1)} %bitcast.33), channel_id=1, replica_groups=mesh['gx'=16,'gy'=8] {'gx','gy'}, dimensions={0} | all-to-all | bytes 131072 | tf_op jit(solution)/shard_map/all_to_all | solution.py:812
  70.2 9.3 %second_newton.1 = (f32[16,8,8,256]{3,2,1,0:T(8,128)S(1)}, f32[16,8,8,256]{3,2,1,0:T(8,128)S(1)}, f32[16,8,8,256]{3,2,1,0:T(8,128)S(1)}, f32[16,8,8,256]{3,2,1,0:T(8,128)S(1)}, f32[128,128]{1,0:T(8,128)S(1)}) custom-call(f32[16,8,8,384]{3,2,1,0:T(8,128)S(1)} %get-tuple-element.70.q_mid, f32[16,8,8,384]{3,2,1,0:T(8,128)S(1)} %get-tuple-element.71.k_mid, ...), custom_call_target="tpu_custom_call" | custom-call | tf_op jit(solution)/shard_map/second_newton/pallas_call | solution.py:769
  79.5 13.9 %all_to_all.28 = f32[128,1,128]{2,1,0:T(1,128)S(1)} all-to-all(f32[128,1,128]{2,1,0:T(1,128)S(1)} %bitcast.34), channel_id=1, replica_groups=mesh['gx'=16,'gy'=8] {'gx','gy'}, dimensions={0} | all-to-all | bytes 131072 | tf_op jit(solution)/shard_map/all_to_all | solution.py:812
  93.4 1.9 %final_update.1 = f32[2048,128]{1,0:T(8,128)} custom-call(f32[16,8,8,256]{3,2,1,0:T(8,128)S(1)} %get-tuple-element.95.q, f32[16,8,8,256]{3,2,1,0:T(8,128)S(1)} %get-tuple-element.96.v0, f32[16,8,8,256]{3,2,1,0:T(8,128)S(1)} %get-tuple-element.97.v1, f32[16,8,8,256]{3,2,1,0:T(8,128)S(1)} %get-tuple-element.98.v2, f32[128,128]{1,0:T(8,128)S(1)} %bitcast.32), custom_call_target="tpu_custom_call" | custom-call | tf_op jit(solution)/shard_map/final_update/pallas_call | solution.py:794
  (6 shorter events, 0.0 us)
Async XLA Ops:
  4.1 18.8 %collective-permute-start = (f32[12,8,8,128]{3,2,1,0:T(8,128)}, f32[12,8,8,128]{3,2,1,0:T(8,128)S(1)}, u32[]{:S(2)}, u32[]{:S(2)}) collective-permute-start(f32[12,8,8,128]{3,2,1,0:T(8,128)} %get-tuple-element.57), channel_id=1, source_target_pairs={{0,8},{8,16},{16,24},{24,32},{32,40},{40,48},{48,56},{56,64},{64,7... | collective-permute-start | bytes 1179656 | tf_op jit(solution)/shard_map/ppermute | solution.py:808
  6.3 16.6 %collective-permute-start.1 = (f32[12,8,8,128]{3,2,1,0:T(8,128)}, f32[12,8,8,128]{3,2,1,0:T(8,128)S(1)}, u32[]{:S(2)}, u32[]{:S(2)}) collective-permute-start(f32[12,8,8,128]{3,2,1,0:T(8,128)} %get-tuple-element.58), channel_id=1, source_target_pairs={{8,0},{16,8},{24,16},{32,24},{40,32},{48,40},{56,48},{64,56},{72,6... | collective-permute-start | bytes 1179656 | tf_op jit(solution)/shard_map/ppermute | solution.py:808
  12.7 10.2 %all-to-all-start = ((f32[16,8,256]{2,1,0:T(8,128)}), f32[16,8,256]{2,1,0:T(8,128)S(1)}, u32[]{:S(2)}, u32[]{:S(2)}) async-start(f32[16,8,256]{2,1,0:T(8,128)} %get-tuple-element.56), calls=%async_computation | async-start | bytes 262144 | tf_op jit(solution)/shard_map/all_to_all | solution.py:838
  22.9 26.4 %collective-permute-start.4 = (f32[16,8,8,128]{3,2,1,0:T(8,128)}, f32[16,8,8,128]{3,2,1,0:T(8,128)S(1)}, u32[]{:S(2)}, u32[]{:S(2)}) collective-permute-start(f32[16,8,8,128]{3,2,1,0:T(8,128)} %get-tuple-element.82), channel_id=1, source_target_pairs={{0,8},{8,16},{16,24},{24,32},{32,40},{40,48},{48,56},{56,64},{64,7... | collective-permute-start | bytes 1572872 | tf_op jit(solution)/shard_map/ppermute | solution.py:808
  23.1 26.2 %collective-permute-start.5 = (f32[16,8,8,128]{3,2,1,0:T(8,128)}, f32[16,8,8,128]{3,2,1,0:T(8,128)S(1)}, u32[]{:S(2)}, u32[]{:S(2)}) collective-permute-start(f32[16,8,8,128]{3,2,1,0:T(8,128)} %get-tuple-element.83), channel_id=1, source_target_pairs={{8,0},{16,8},{24,16},{32,24},{40,32},{48,40},{56,48},{64,56},{72,6... | collective-permute-start | bytes 1572872 | tf_op jit(solution)/shard_map/ppermute | solution.py:808
  29.8 6.5 %collective-permute-start.2 = (f32[17,8,128]{2,1,0:T(8,128)S(1)}, f32[17,8,128]{2,1,0:T(8,128)S(1)}, u32[]{:S(2)}, u32[]{:S(2)}) collective-permute-start(f32[17,8,128]{2,1,0:T(8,128)S(1)} %get-tuple-element.67), channel_id=1, source_target_pairs={{0,1},{1,2},{2,3},{3,4},{4,5},{5,6},{6,7},{7,0},{8,9},{9,10},{10,1... | collective-permute-start | bytes 208904 | tf_op jit(solution)/shard_map/ppermute | solution.py:808
  34.3 4.0 %collective-permute-start.3 = (f32[17,8,128]{2,1,0:T(8,128)S(1)}, f32[17,8,128]{2,1,0:T(8,128)S(1)}, u32[]{:S(2)}, u32[]{:S(2)}) collective-permute-start(f32[17,8,128]{2,1,0:T(8,128)S(1)} %get-tuple-element.68), channel_id=1, source_target_pairs={{1,0},{2,1},{3,2},{4,3},{5,4},{6,5},{7,6},{0,7},{9,8},{10,9},{11,1... | collective-permute-start | bytes 208904 | tf_op jit(solution)/shard_map/ppermute | solution.py:808
  38.5 10.9 %collective-permute-start.6 = (f32[29,8,128]{2,1,0:T(8,128)S(1)}, f32[29,8,128]{2,1,0:T(8,128)S(1)}, u32[]{:S(2)}, u32[]{:S(2)}) collective-permute-start(f32[29,8,128]{2,1,0:T(8,128)S(1)} %get-tuple-element.86), channel_id=1, source_target_pairs={{0,8},{8,16},{16,24},{24,32},{32,40},{40,48},{48,56},{56,64},{64,7... | collective-permute-start | bytes 356360 | tf_op jit(solution)/shard_map/ppermute | solution.py:808
  38.5 10.8 %collective-permute-start.7 = (f32[29,8,128]{2,1,0:T(8,128)S(1)}, f32[29,8,128]{2,1,0:T(8,128)S(1)}, u32[]{:S(2)}, u32[]{:S(2)}) collective-permute-start(f32[29,8,128]{2,1,0:T(8,128)S(1)} %get-tuple-element.87), channel_id=1, source_target_pairs={{8,0},{16,8},{24,16},{32,24},{40,32},{48,40},{56,48},{64,56},{72,6... | collective-permute-start | bytes 356360 | tf_op jit(solution)/shard_map/ppermute | solution.py:808

commit v10 on v9

--- a/solution.py
+++ b/solution.py
@@ -125,7 +125,7 @@
         payload[o] = jnp.where(sub == used, live, out)
         return carry
 
-    lax.fori_loop(0, cols.shape[0], owner, 0, unroll=8)
+    lax.fori_loop(0, cols.shape[0], owner, 0, unroll=16)
 
 
 def canopy_send(forcing, cover, canopy_table, counts, cols, state, after):
@@ -172,7 +172,7 @@
         )
         return carry
 
-    lax.fori_loop(0, cols.shape[0], owner, 0, unroll=8)
+    lax.fori_loop(0, cols.shape[0], owner, 0, unroll=16)
 
     def piece(k):
         return total[k * ROWS : (k + 1) * ROWS, :]
@@ -233,7 +233,7 @@
         updated[i] = jnp.where(block[5:6] > 0.5, fresh, old)
         return carry
 
-    lax.fori_loop(0, arrived.shape[0], slot, 0, unroll=8)
+    lax.fori_loop(0, arrived.shape[0], slot, 0, unroll=16)
 
 
 def owner_update(arrived, state):
@@ -583,9 +583,9 @@
         v0[r, l] = source_at(b, r, l, sub) - out
 
     coefs = (cx, cy, cyl, cz, diag)
-    couplings(q, resist, *coefs, (1, ROWS - 1), 7, emit)
+    couplings(q, resist, *coefs, (1, ROWS - 1), 14, emit)
     for step, (v_in, v_out, rows, block) in enumerate(
-        ((v0, v1, (2, 14), 6), (v1, v2, (3, 13), 5), (v2, None, (4, 12), 8))
+        ((v0, v1, (2, 14), 12), (v1, v2, (3, 13), 10), (v2, None, (4, 12), 8))
     ):
         held = apply(v_in, v_out, coefs, 0, rows, block, no_sums(), True)
         sums[2 * step], sums[2 * step + 1] = held
@@ -720,11 +720,11 @@
     full, mid = (u0, u1, u2), (v0_mid, v1_mid, v2_mid)
     low, high = HALO, HALO + ROWS
     for q, k, shift, held, back, rows, block in (
-        (q_rim, k_rim, 0, full, 0, (3, low), 2),
+        (q_rim, k_rim, 0, full, 0, (3, low), 4),
         (q_mid, k_mid, low, full, 0, (low, low + 3), 3),
-        (q_mid, k_mid, low, mid, low, (low + 3, high - 3), 2),
+        (q_mid, k_mid, low, mid, low, (low + 3, high - 3), 5),
         (q_mid, k_mid, low, full, 0, (high - 3, high), 3),
-        (q_rim, k_rim, RSHIFT, full, 0, (high, XR - 3), 2),
+        (q_rim, k_rim, RSHIFT, full, 0, (high, XR - 3), 4),
     ):
 
         def update(r, carry, q=q, k=k, shift=shift, held=held, back=back):
@@ -745,10 +745,10 @@
         v0[r, l] = v0[r, l] - out
 
     coefs = (cx, cy, cyl, cz, diag)
-    couplings(q1, resist, *coefs, (4, XR - 4), 11, emit)
+    couplings(q1, resist, *coefs, (4, XR - 4), 22, emit)
     sums = []
     for v_in, v_out, deep in ((v0, v1, 2), (v1, v2, 1), (v2, None, 0)):
-        sums += apply(v_in, v_out, coefs, 0, (low, high), 8, no_sums(), True)
+        sums += apply(v_in, v_out, coefs, 0, (low, high), 16, no_sums(), True)
         if deep:
             apply(v_in, v_out, coefs, 0, (low - deep, low), deep, no_sums(), False)
             apply(v_in, v_out, coefs, 0, (high, high + deep), deep, no_sums(), False)
@@ -760,7 +760,7 @@
                 target[x, l] = source[HALO + x, l, :, :COLS]
         return carry
 
-    lax.fori_loop(0, ROWS, keep, 0)
+    lax.fori_loop(0, ROWS, keep, 0, unroll=4)
 
 
 def second_newton(*arrays):
@@ -787,7 +787,7 @@
             out[chunk(x, l, 1), :] = value[:, 128:]
         return carry
 
-    lax.fori_loop(0, ROWS, row, 0, unroll=2)
+    lax.fori_loop(0, ROWS, row, 0, unroll=4)
 
 
 def final_update(*arrays):

time: 95.7 us -> 94.5 us (0.987)
  Pallas kernels: 35 us -> 33.3 us
where the time goes in v10:
time: 94.5 us; the launch traced here: 94.2 us
  Pallas kernels  33.3 us (35%)
  blocking collectives  29.6 us (31%)
  starting transfers between devices  23.6 us (25%)
  waiting for transfers between devices  6.96 us (7%)
    all_to_all x2, blocking collectives, share(): lax.all_to_all(moments, ('gx', 'gy'), split_axis=0, concat_axis=0, tiled=...  29.6 us
    ppermute x8, starting transfers between devices, exchange(): return (lax.ppermute(to_high, axis, up), lax.ppermute(to_low, axis, down))  20.1 us
    pallas_call x1, Pallas kernels, second_newton(): pl.pallas_call(second_kernel, out_shape=outs, in_specs=vmem(len(arrays)),...  8.36 us
    pallas_call x1, Pallas kernels, first_newton(): pl.pallas_call(first_kernel, out_shape=outs, in_specs=vmem(len(arrays)),...  5.64 us
    pallas_call x1, Pallas kernels, prepare(): pl.pallas_call(prepare_kernel, out_shape=outs, in_specs=vmem(len(arrays))...  5.5 us
    all_to_all x1, waiting for transfers between devices, body(): lax.all_to_all(payload, 'gx', split_axis=0, concat_axis=0, tiled=True)  4.85 us
    all_to_all x1, starting transfers between devices, body(): lax.all_to_all(payload, 'gx', split_axis=0, concat_axis=0, tiled=True)  3.51 us
    pallas_call x1, Pallas kernels, turn(): pl.pallas_call(turn_kernel, out_shape=(own_shape, own_shape, shaped(ROOT,...  3.47 us
  transfers between devices with their start and end apart: 9, of which 2 were waited for; matrix products, arithmetic and copies ran while one was open for 0% of the time, Pallas kernels for 15%

profile of v10, /device:TPU:1, one launch (start us, length us, event | category | flops | bytes accessed | tf_op | source)
XLA Modules:
  0.0 94.2 jit_solution(13328197023829958101)
XLA Ops:
  0.6 3.5 %turn.1 = (f32[16,8,8,256]{3,2,1,0:T(8,128)S(1)}, f32[16,8,8,256]{3,2,1,0:T(8,128)S(1)}, f32[8,16,256]{2,1,0:T(8,128)S(1)}, f32[16,8,8,128]{3,2,1,0:T(8,128)}, f...) custom-call(f32[8,256,128]{2,1,0:T(8,128)} %bitcast.37, f32[8,256,128]{2,1,0:T(8,128)} %bitcast.38), custom_call_target="tpu_custom_call" | custom-call | tf_op jit(solution)/shard_map/turn/pallas_call | solution.py:322
  4.1 2.2 %collective-permute-start = (f32[12,8,8,128]{3,2,1,0:T(8,128)}, f32[12,8,8,128]{3,2,1,0:T(8,128)S(1)}, u32[]{:S(2)}, u32[]{:S(2)}) collective-permute-start(f32[12,8,8,128]{3,2,1,0:T(8,128)} %get-tuple-element.57), channel_id=1, source_target_pairs={{0,8},{8,16},{16,24},{24,32},{32,40},{40,48},{48,56},{56,64},{64,7... | collective-permute-start | bytes 1179656 | tf_op jit(solution)/shard_map/ppermute | solution.py:808
  6.3 3.7 %collective-permute-start.1 = (f32[12,8,8,128]{3,2,1,0:T(8,128)}, f32[12,8,8,128]{3,2,1,0:T(8,128)S(1)}, u32[]{:S(2)}, u32[]{:S(2)}) collective-permute-start(f32[12,8,8,128]{3,2,1,0:T(8,128)} %get-tuple-element.58), channel_id=1, source_target_pairs={{8,0},{16,8},{24,16},{32,24},{40,32},{48,40},{56,48},{64,56},{72,6... | collective-permute-start | bytes 1179656 | tf_op jit(solution)/shard_map/ppermute | solution.py:808
  10.0 2.7 %canopy_send.1 = (f32[16,8,256]{2,1,0:T(8,128)}, f32[16,256]{1,0:T(8,128)S(1)}) custom-call(f32[8,16,256]{2,1,0:T(8,128)} %forcing.5, s32[16,256]{1,0:T(8,128)} %cover.3, f32[8,16]{1,0:T(8,128)} %bitcast.43, s32[16]{0:T(128)} %bitcast.45, s32[16,1,256]{2,1,0:T(1,128)} %bitcast.41, f32[16,16,256]{2,1,0:T(8,128)} %bitcast.35, ...), custom_call_target="tpu_custom_call" | custom-call | tf_op jit(solution)/shard_map/canopy_send/pallas_call | solution.py:133
  12.7 3.5 %all-to-all-start = ((f32[16,8,256]{2,1,0:T(8,128)}), f32[16,8,256]{2,1,0:T(8,128)S(1)}, u32[]{:S(2)}, u32[]{:S(2)}) async-start(f32[16,8,256]{2,1,0:T(8,128)} %get-tuple-element.56), calls=%async_computation | async-start | bytes 262144 | tf_op jit(solution)/shard_map/all_to_all | solution.py:838
  16.3 1.8 %sides.1 = (f32[16,8,128]{2,1,0:T(8,128)S(1)}, f32[16,8,128]{2,1,0:T(8,128)S(1)}, f32[8,16,256]{2,1,0:T(8,128)S(1)}, f32[16,256]{1,0:T(8,128)S(1)}) custom-call(f32[16,8,8,256]{3,2,1,0:T(8,128)S(1)} %get-tuple-element.51.q.q_own, f32[16,8,8,256]{3,2,1,0:T(8,128)S(1)} %get-tuple-element.52.k.k_own, f32[8,16,256]{2,1,0:T(8,128)S(1)} %get-tuple-element.59.after.top, ...), custom_call_target="tpu_custom_call" | custom-call | tf_op jit(solution)/shard_map/sides/pallas_call | solution.py:369
  18.0 4.9 %all-to-all-done.arrived = f32[16,8,256]{2,1,0:T(8,128)S(1)} async-done(((f32[16,8,256]{2,1,0:T(8,128)}), f32[16,8,256]{2,1,0:T(8,128)S(1)}, u32[]{:S(2)}, u32[]{:S(2)}) %all-to-all-start) | async-done | bytes 131104 | tf_op jit(solution)/shard_map/all_to_all | solution.py:838
  22.9 0.0 collective-permute-done.far_prev
  22.9 0.2 collective-permute-start.4
  23.1 4.6 %collective-permute-start.5 = (f32[16,8,8,128]{3,2,1,0:T(8,128)}, f32[16,8,8,128]{3,2,1,0:T(8,128)S(1)}, u32[]{:S(2)}, u32[]{:S(2)}) collective-permute-start(f32[16,8,8,128]{3,2,1,0:T(8,128)} %get-tuple-element.83), channel_id=1, source_target_pairs={{8,0},{16,8},{24,16},{32,24},{40,32},{48,40},{56,48},{64,56},{72,6... | collective-permute-start | bytes 1572872 | tf_op jit(solution)/shard_map/ppermute | solution.py:808
  27.7 1.9 %canopy_source.1 = (f32[16,8,256]{2,1,0:T(8,128)S(1)}, f32[17,8,128]{2,1,0:T(8,128)S(1)}, f32[17,8,128]{2,1,0:T(8,128)S(1)}) custom-call(f32[16,8,256]{2,1,0:T(8,128)S(1)} %all-to-all-done.arrived, s32[16,1,256]{2,1,0:T(1,128)} %bitcast.42, s32[16]{0:T(128)} %bitcast.46, f32[8,16,256]{2,1,0:T(8,128)} %forcing.5, ...), custom_call_target="tpu_custom_call" | custom-call | tf_op jit(solution)/shard_map/canopy_source/pallas_call | solution.py:209
  29.6 4.5 %collective-permute-start.2 = (f32[17,8,128]{2,1,0:T(8,128)S(1)}, f32[17,8,128]{2,1,0:T(8,128)S(1)}, u32[]{:S(2)}, u32[]{:S(2)}) collective-permute-start(f32[17,8,128]{2,1,0:T(8,128)S(1)} %get-tuple-element.67), channel_id=1, source_target_pairs={{0,1},{1,2},{2,3},{3,4},{4,5},{5,6},{6,7},{7,0},{8,9},{9,10},{10,1... | collective-permute-start | bytes 208904 | tf_op jit(solution)/shard_map/ppermute | solution.py:808
  34.1 0.0 collective-permute-start.3
  34.1 1.9 %owner_update.1.after = f32[16,16,256]{2,1,0:T(8,128)} custom-call(f32[16,8,256]{2,1,0:T(8,128)S(1)} %all-to-all-done.arrived, f32[16,16,256]{2,1,0:T(8,128)} %bitcast.36), custom_call_target="tpu_custom_call" | custom-call | tf_op jit(solution)/shard_map/owner_update/pallas_call | solution.py:240
  36.0 2.1 %collective-permute-done.3.from_right = f32[17,8,128]{2,1,0:T(8,128)S(1)} collective-permute-done((f32[17,8,128]{2,1,0:T(8,128)S(1)}, f32[17,8,128]{2,1,0:T(8,128)S(1)}, u32[]{:S(2)}, u32[]{:S(2)}) %collective-permute-start.3) | collective-permute-done | bytes 69664 | tf_op jit(solution)/shard_map/ppermute | solution.py:808
  38.1 0.1 corners.1
  38.2 0.1 collective-permute-start.6
  38.3 4.8 %collective-permute-start.7 = (f32[29,8,128]{2,1,0:T(8,128)S(1)}, f32[29,8,128]{2,1,0:T(8,128)S(1)}, u32[]{:S(2)}, u32[]{:S(2)}) collective-permute-start(f32[29,8,128]{2,1,0:T(8,128)S(1)} %get-tuple-element.87), channel_id=1, source_target_pairs={{8,0},{16,8},{24,16},{32,24},{40,32},{48,40},{56,48},{64,56},{72,6... | collective-permute-start | bytes 356360 | tf_op jit(solution)/shard_map/ppermute | solution.py:808
  43.1 5.5 %prepare.1 = (f32[16,8,8,384]{3,2,1,0:T(8,128)S(1)}, f32[16,8,8,384]{3,2,1,0:T(8,128)S(1)}, f32[16,8,8,384]{3,2,1,0:T(8,128)S(1)}, f32[16,8,8,384]{3,2,1,0:T(8,1...) custom-call(f32[16,8,8,256]{3,2,1,0:T(8,128)S(1)} %get-tuple-element, ...), custom_call_target="tpu_custom_call" | custom-call | tf_op jit(solution)/shard_map/prepare/pallas_call | solution.py:596
  48.6 5.6 %first_newton.1 = (f32[18,8,8,384]{3,2,1,0:T(8,128)S(1)}, f32[18,8,8,384]{3,2,1,0:T(8,128)S(1)}, f32[30,8,384]{2,1,0:T(8,128)S(1)}, f32[30,8,8,384]{3,2,1,0:T(8,...) custom-call(f32[16,8,8,384]{3,2,1,0:T(8,128)S(1)} %get-tuple-element.70.q_mid, ...), custom_call_target="tpu_custom_call" | custom-call | tf_op jit(solution)/shard_map/first_newton/pallas_call | solution.py:700
  54.3 15.7 %all_to_all.27 = f32[128,1,128]{2,1,0:T(1,128)S(1)} all-to-all(f32[128,1,128]{2,1,0:T(1,128)S(1)} %bitcast.33), channel_id=1, replica_groups=mesh['gx'=16,'gy'=8] {'gx','gy'}, dimensions={0} | all-to-all | bytes 131072 | tf_op jit(solution)/shard_map/all_to_all | solution.py:812
  70.0 8.4 %second_newton.1 = (f32[16,8,8,256]{3,2,1,0:T(8,128)S(1)}, f32[16,8,8,256]{3,2,1,0:T(8,128)S(1)}, f32[16,8,8,256]{3,2,1,0:T(8,128)S(1)}, f32[16,8,8,256]{3,2,1,0:T(8,128)S(1)}, f32[128,128]{1,0:T(8,128)S(1)}) custom-call(f32[16,8,8,384]{3,2,1,0:T(8,128)S(1)} %get-tuple-element.70.q_mid, f32[16,8,8,384]{3,2,1,0:T(8,128)S(1)} %get-tuple-element.71.k_mid, ...), custom_call_target="tpu_custom_call" | custom-call | tf_op jit(solution)/shard_map/second_newton/pallas_call | solution.py:769
  78.3 13.9 %all_to_all.28 = f32[128,1,128]{2,1,0:T(1,128)S(1)} all-to-all(f32[128,1,128]{2,1,0:T(1,128)S(1)} %bitcast.34), channel_id=1, replica_groups=mesh['gx'=16,'gy'=8] {'gx','gy'}, dimensions={0} | all-to-all | bytes 131072 | tf_op jit(solution)/shard_map/all_to_all | solution.py:812
  92.2 1.9 %final_update.1 = f32[2048,128]{1,0:T(8,128)} custom-call(f32[16,8,8,256]{3,2,1,0:T(8,128)S(1)} %get-tuple-element.95.q, f32[16,8,8,256]{3,2,1,0:T(8,128)S(1)} %get-tuple-element.96.v0, f32[16,8,8,256]{3,2,1,0:T(8,128)S(1)} %get-tuple-element.97.v1, f32[16,8,8,256]{3,2,1,0:T(8,128)S(1)} %get-tuple-element.98.v2, f32[128,128]{1,0:T(8,128)S(1)} %bitcast.32), custom_call_target="tpu_custom_call" | custom-call | tf_op jit(solution)/shard_map/final_update/pallas_call | solution.py:794
  (6 shorter events, 0.0 us)
Async XLA Ops:
  4.1 18.8 %collective-permute-start = (f32[12,8,8,128]{3,2,1,0:T(8,128)}, f32[12,8,8,128]{3,2,1,0:T(8,128)S(1)}, u32[]{:S(2)}, u32[]{:S(2)}) collective-permute-start(f32[12,8,8,128]{3,2,1,0:T(8,128)} %get-tuple-element.57), channel_id=1, source_target_pairs={{0,8},{8,16},{16,24},{24,32},{32,40},{40,48},{48,56},{56,64},{64,7... | collective-permute-start | bytes 1179656 | tf_op jit(solution)/shard_map/ppermute | solution.py:808
  6.3 16.6 %collective-permute-start.1 = (f32[12,8,8,128]{3,2,1,0:T(8,128)}, f32[12,8,8,128]{3,2,1,0:T(8,128)S(1)}, u32[]{:S(2)}, u32[]{:S(2)}) collective-permute-start(f32[12,8,8,128]{3,2,1,0:T(8,128)} %get-tuple-element.58), channel_id=1, source_target_pairs={{8,0},{16,8},{24,16},{32,24},{40,32},{48,40},{56,48},{64,56},{72,6... | collective-permute-start | bytes 1179656 | tf_op jit(solution)/shard_map/ppermute | solution.py:808
  12.7 10.2 %all-to-all-start = ((f32[16,8,256]{2,1,0:T(8,128)}), f32[16,8,256]{2,1,0:T(8,128)S(1)}, u32[]{:S(2)}, u32[]{:S(2)}) async-start(f32[16,8,256]{2,1,0:T(8,128)} %get-tuple-element.56), calls=%async_computation | async-start | bytes 262144 | tf_op jit(solution)/shard_map/all_to_all | solution.py:838
  22.9 25.7 %collective-permute-start.4 = (f32[16,8,8,128]{3,2,1,0:T(8,128)}, f32[16,8,8,128]{3,2,1,0:T(8,128)S(1)}, u32[]{:S(2)}, u32[]{:S(2)}) collective-permute-start(f32[16,8,8,128]{3,2,1,0:T(8,128)} %get-tuple-element.82), channel_id=1, source_target_pairs={{0,8},{8,16},{16,24},{24,32},{32,40},{40,48},{48,56},{56,64},{64,7... | collective-permute-start | bytes 1572872 | tf_op jit(solution)/shard_map/ppermute | solution.py:808
  23.1 25.5 %collective-permute-start.5 = (f32[16,8,8,128]{3,2,1,0:T(8,128)}, f32[16,8,8,128]{3,2,1,0:T(8,128)S(1)}, u32[]{:S(2)}, u32[]{:S(2)}) collective-permute-start(f32[16,8,8,128]{3,2,1,0:T(8,128)} %get-tuple-element.83), channel_id=1, source_target_pairs={{8,0},{16,8},{24,16},{32,24},{40,32},{48,40},{56,48},{64,56},{72,6... | collective-permute-start | bytes 1572872 | tf_op jit(solution)/shard_map/ppermute | solution.py:808
  29.6 6.4 %collective-permute-start.2 = (f32[17,8,128]{2,1,0:T(8,128)S(1)}, f32[17,8,128]{2,1,0:T(8,128)S(1)}, u32[]{:S(2)}, u32[]{:S(2)}) collective-permute-start(f32[17,8,128]{2,1,0:T(8,128)S(1)} %get-tuple-element.67), channel_id=1, source_target_pairs={{0,1},{1,2},{2,3},{3,4},{4,5},{5,6},{6,7},{7,0},{8,9},{9,10},{10,1... | collective-permute-start | bytes 208904 | tf_op jit(solution)/shard_map/ppermute | solution.py:808
  34.1 4.0 %collective-permute-start.3 = (f32[17,8,128]{2,1,0:T(8,128)S(1)}, f32[17,8,128]{2,1,0:T(8,128)S(1)}, u32[]{:S(2)}, u32[]{:S(2)}) collective-permute-start(f32[17,8,128]{2,1,0:T(8,128)S(1)} %get-tuple-element.68), channel_id=1, source_target_pairs={{1,0},{2,1},{3,2},{4,3},{5,4},{6,5},{7,6},{0,7},{9,8},{10,9},{11,1... | collective-permute-start | bytes 208904 | tf_op jit(solution)/shard_map/ppermute | solution.py:808
  38.2 10.4 %collective-permute-start.6 = (f32[29,8,128]{2,1,0:T(8,128)S(1)}, f32[29,8,128]{2,1,0:T(8,128)S(1)}, u32[]{:S(2)}, u32[]{:S(2)}) collective-permute-start(f32[29,8,128]{2,1,0:T(8,128)S(1)} %get-tuple-element.86), channel_id=1, source_target_pairs={{0,8},{8,16},{16,24},{24,32},{32,40},{40,48},{48,56},{56,64},{64,7... | collective-permute-start | bytes 356360 | tf_op jit(solution)/shard_map/ppermute | solution.py:808
  38.3 10.3 %collective-permute-start.7 = (f32[29,8,128]{2,1,0:T(8,128)S(1)}, f32[29,8,128]{2,1,0:T(8,128)S(1)}, u32[]{:S(2)}, u32[]{:S(2)}) collective-permute-start(f32[29,8,128]{2,1,0:T(8,128)S(1)} %get-tuple-element.87), channel_id=1, source_target_pairs={{8,0},{16,8},{24,16},{32,24},{40,32},{48,40},{56,48},{64,56},{72,6... | collective-permute-start | bytes 356360 | tf_op jit(solution)/shard_map/ppermute | solution.py:808

commit v11 on v10

--- a/solution.py
+++ b/solution.py
@@ -352,7 +352,7 @@
             edge_right[f * L + l] = last
         return carry
 
-    lax.fori_loop(0, L, layer, 0, unroll=4)
+    lax.fori_loop(0, L, layer, 0, unroll=8)
     roots = looked_up(cover[...], root_table)
     planted = vegetated[...] == 1
     for m in range(ROOT):
@@ -722,7 +722,7 @@
     for q, k, shift, held, back, rows, block in (
         (q_rim, k_rim, 0, full, 0, (3, low), 4),
         (q_mid, k_mid, low, full, 0, (low, low + 3), 3),
-        (q_mid, k_mid, low, mid, low, (low + 3, high - 3), 5),
+        (q_mid, k_mid, low, mid, low, (low + 3, high - 3), 10),
         (q_mid, k_mid, low, full, 0, (high - 3, high), 3),
         (q_rim, k_rim, RSHIFT, full, 0, (high, XR - 3), 4),
     ):
@@ -760,7 +760,7 @@
                 target[x, l] = source[HALO + x, l, :, :COLS]
         return carry
 
-    lax.fori_loop(0, ROWS, keep, 0, unroll=4)
+    lax.fori_loop(0, ROWS, keep, 0, unroll=8)
 
 
 def second_newton(*arrays):
@@ -777,25 +777,34 @@
     )(*arrays)
 
 
-def final_kernel(q, v0, v1, v2, gathered, out):
+def final_kernel(q, v0, v1, v2, gathered, out, held, sems):
     c0, c1, c2 = coefficients(gathered)
-
-    def row(x, carry):
-        for l in range(L):
-            value = q[x, l] + c0 * v0[x, l] + c1 * v1[x, l] + c2 * v2[x, l]
-            out[chunk(x, l, 0), :] = value[:, :128]
-            out[chunk(x, l, 1), :] = value[:, 128:]
-        return carry
-
-    lax.fori_loop(0, ROWS, row, 0, unroll=4)
+    sends = []
+    for half in range(2):
+
+        def row(i, carry, half=half):
+            x = 8 * half + i
+            for l in range(L):
+                value = q[x, l] + c0 * v0[x, l] + c1 * v1[x, l] + c2 * v2[x, l]
+                held[:, l, half, i, :] = value[:, :128]
+                held[:, l, half, 8 + i, :] = value[:, 128:]
+            return carry
+
+        lax.fori_loop(0, 8, row, 0, unroll=4)
+        sends.append(pltpu.make_async_copy(held.at[:, :, half], out.at[:, :, half], sems.at[half]))
+        sends[-1].start()
+    for send in sends:
+        send.wait()
 
 
 def final_update(*arrays):
+    shape = (8, L, 2, 16, 128)
     return pl.pallas_call(
         final_kernel,
-        out_shape=shaped(32 * LEV, 128),
+        out_shape=shaped(*shape),
         in_specs=vmem(len(arrays)),
-        out_specs=vmem()[0],
+        out_specs=pl.BlockSpec(memory_space=pltpu.HBM),
+        scratch_shapes=[pltpu.VMEM(shape, F32), pltpu.SemaphoreType.DMA((2,))],
         compiler_params=params(4),
         name="final_update",
     )(*arrays)

time: 94.5 us -> 94.4 us (level)
  no operation moved by 1% of the time
where the time goes in v11:
time: 94.4 us; the launch traced here: 94.1 us
  Pallas kernels  32.8 us (35%)
  blocking collectives  29.6 us (31%)
  starting transfers between devices  23.6 us (25%)
  waiting for transfers between devices  7.13 us (8%)
    all_to_all x2, blocking collectives, share(): lax.all_to_all(moments, ('gx', 'gy'), split_axis=0, concat_axis=0, tiled=...  29.6 us
    ppermute x8, starting transfers between devices, exchange(): return (lax.ppermute(to_high, axis, up), lax.ppermute(to_low, axis, down))  20.1 us
    pallas_call x1, Pallas kernels, second_newton(): pl.pallas_call(second_kernel, out_shape=outs, in_specs=vmem(len(arrays)),...  8.23 us
    pallas_call x1, Pallas kernels, first_newton(): pl.pallas_call(first_kernel, out_shape=outs, in_specs=vmem(len(arrays)),...  5.64 us
    pallas_call x1, Pallas kernels, prepare(): pl.pallas_call(prepare_kernel, out_shape=outs, in_specs=vmem(len(arrays))...  5.5 us
    all_to_all x1, waiting for transfers between devices, body(): lax.all_to_all(payload, 'gx', split_axis=0, concat_axis=0, tiled=True)  5.03 us
    all_to_all x1, starting transfers between devices, body(): lax.all_to_all(payload, 'gx', split_axis=0, concat_axis=0, tiled=True)  3.51 us
    pallas_call x1, Pallas kernels, turn(): pl.pallas_call(turn_kernel, out_shape=(own_shape, own_shape, shaped(ROOT,...  3.47 us
  transfers between devices with their start and end apart: 9, of which 2 were waited for; matrix products, arithmetic and copies ran while one was open for 0% of the time, Pallas kernels for 15%

profile of v11, /device:TPU:1, one launch (start us, length us, event | category | flops | bytes accessed | tf_op | source)
XLA Modules:
  0.0 94.1 jit_solution(13977304806468002954)
XLA Ops:
  0.6 3.5 %turn.1 = (f32[16,8,8,256]{3,2,1,0:T(8,128)S(1)}, f32[16,8,8,256]{3,2,1,0:T(8,128)S(1)}, f32[8,16,256]{2,1,0:T(8,128)S(1)}, f32[16,8,8,128]{3,2,1,0:T(8,128)}, f...) custom-call(f32[8,256,128]{2,1,0:T(8,128)} %bitcast.37, f32[8,256,128]{2,1,0:T(8,128)} %bitcast.38), custom_call_target="tpu_custom_call" | custom-call | tf_op jit(solution)/shard_map/turn/pallas_call | solution.py:322
  4.1 2.2 %collective-permute-start = (f32[12,8,8,128]{3,2,1,0:T(8,128)}, f32[12,8,8,128]{3,2,1,0:T(8,128)S(1)}, u32[]{:S(2)}, u32[]{:S(2)}) collective-permute-start(f32[12,8,8,128]{3,2,1,0:T(8,128)} %get-tuple-element.57), channel_id=1, source_target_pairs={{0,8},{8,16},{16,24},{24,32},{32,40},{40,48},{48,56},{56,64},{64,7... | collective-permute-start | bytes 1179656 | tf_op jit(solution)/shard_map/ppermute | solution.py:817
  6.3 3.7 %collective-permute-start.1 = (f32[12,8,8,128]{3,2,1,0:T(8,128)}, f32[12,8,8,128]{3,2,1,0:T(8,128)S(1)}, u32[]{:S(2)}, u32[]{:S(2)}) collective-permute-start(f32[12,8,8,128]{3,2,1,0:T(8,128)} %get-tuple-element.58), channel_id=1, source_target_pairs={{8,0},{16,8},{24,16},{32,24},{40,32},{48,40},{56,48},{64,56},{72,6... | collective-permute-start | bytes 1179656 | tf_op jit(solution)/shard_map/ppermute | solution.py:817
  10.0 2.7 %canopy_send.1 = (f32[16,8,256]{2,1,0:T(8,128)}, f32[16,256]{1,0:T(8,128)S(1)}) custom-call(f32[8,16,256]{2,1,0:T(8,128)} %forcing.5, s32[16,256]{1,0:T(8,128)} %cover.3, f32[8,16]{1,0:T(8,128)} %bitcast.43, s32[16]{0:T(128)} %bitcast.45, s32[16,1,256]{2,1,0:T(1,128)} %bitcast.41, f32[16,16,256]{2,1,0:T(8,128)} %bitcast.35, ...), custom_call_target="tpu_custom_call" | custom-call | tf_op jit(solution)/shard_map/canopy_send/pallas_call | solution.py:133
  12.7 3.5 %all-to-all-start = ((f32[16,8,256]{2,1,0:T(8,128)}), f32[16,8,256]{2,1,0:T(8,128)S(1)}, u32[]{:S(2)}, u32[]{:S(2)}) async-start(f32[16,8,256]{2,1,0:T(8,128)} %get-tuple-element.56), calls=%async_computation | async-start | bytes 262144 | tf_op jit(solution)/shard_map/all_to_all | solution.py:847
  16.3 1.6 %sides.1 = (f32[16,8,128]{2,1,0:T(8,128)S(1)}, f32[16,8,128]{2,1,0:T(8,128)S(1)}, f32[8,16,256]{2,1,0:T(8,128)S(1)}, f32[16,256]{1,0:T(8,128)S(1)}) custom-call(f32[16,8,8,256]{3,2,1,0:T(8,128)S(1)} %get-tuple-element.51.q.q_own, f32[16,8,8,256]{3,2,1,0:T(8,128)S(1)} %get-tuple-element.52.k.k_own, f32[8,16,256]{2,1,0:T(8,128)S(1)} %get-tuple-element.59.after.top, ...), custom_call_target="tpu_custom_call" | custom-call | tf_op jit(solution)/shard_map/sides/pallas_call | solution.py:369
  17.9 5.0 %all-to-all-done.arrived = f32[16,8,256]{2,1,0:T(8,128)S(1)} async-done(((f32[16,8,256]{2,1,0:T(8,128)}), f32[16,8,256]{2,1,0:T(8,128)S(1)}, u32[]{:S(2)}, u32[]{:S(2)}) %all-to-all-start) | async-done | bytes 131104 | tf_op jit(solution)/shard_map/all_to_all | solution.py:847
  22.9 0.2 collective-permute-start.4
  23.1 4.6 %collective-permute-start.5 = (f32[16,8,8,128]{3,2,1,0:T(8,128)}, f32[16,8,8,128]{3,2,1,0:T(8,128)S(1)}, u32[]{:S(2)}, u32[]{:S(2)}) collective-permute-start(f32[16,8,8,128]{3,2,1,0:T(8,128)} %get-tuple-element.83), channel_id=1, source_target_pairs={{8,0},{16,8},{24,16},{32,24},{40,32},{48,40},{56,48},{64,56},{72,6... | collective-permute-start | bytes 1572872 | tf_op jit(solution)/shard_map/ppermute | solution.py:817
  27.7 1.9 %canopy_source.1 = (f32[16,8,256]{2,1,0:T(8,128)S(1)}, f32[17,8,128]{2,1,0:T(8,128)S(1)}, f32[17,8,128]{2,1,0:T(8,128)S(1)}) custom-call(f32[16,8,256]{2,1,0:T(8,128)S(1)} %all-to-all-done.arrived, s32[16,1,256]{2,1,0:T(1,128)} %bitcast.42, s32[16]{0:T(128)} %bitcast.46, f32[8,16,256]{2,1,0:T(8,128)} %forcing.5, ...), custom_call_target="tpu_custom_call" | custom-call | tf_op jit(solution)/shard_map/canopy_source/pallas_call | solution.py:209
  29.6 4.5 %collective-permute-start.2 = (f32[17,8,128]{2,1,0:T(8,128)S(1)}, f32[17,8,128]{2,1,0:T(8,128)S(1)}, u32[]{:S(2)}, u32[]{:S(2)}) collective-permute-start(f32[17,8,128]{2,1,0:T(8,128)S(1)} %get-tuple-element.67), channel_id=1, source_target_pairs={{0,1},{1,2},{2,3},{3,4},{4,5},{5,6},{6,7},{7,0},{8,9},{9,10},{10,1... | collective-permute-start | bytes 208904 | tf_op jit(solution)/shard_map/ppermute | solution.py:817
  34.1 0.0 collective-permute-start.3
  34.1 1.9 %owner_update.1.after = f32[16,16,256]{2,1,0:T(8,128)} custom-call(f32[16,8,256]{2,1,0:T(8,128)S(1)} %all-to-all-done.arrived, f32[16,16,256]{2,1,0:T(8,128)} %bitcast.36), custom_call_target="tpu_custom_call" | custom-call | tf_op jit(solution)/shard_map/owner_update/pallas_call | solution.py:240
  36.0 0.0 collective-permute-done.2.from_left
  36.0 2.1 %collective-permute-done.3.from_right = f32[17,8,128]{2,1,0:T(8,128)S(1)} collective-permute-done((f32[17,8,128]{2,1,0:T(8,128)S(1)}, f32[17,8,128]{2,1,0:T(8,128)S(1)}, u32[]{:S(2)}, u32[]{:S(2)}) %collective-permute-start.3) | collective-permute-done | bytes 69664 | tf_op jit(solution)/shard_map/ppermute | solution.py:817
  38.1 0.1 corners.1
  38.2 0.1 collective-permute-start.6
  38.3 4.8 %collective-permute-start.7 = (f32[29,8,128]{2,1,0:T(8,128)S(1)}, f32[29,8,128]{2,1,0:T(8,128)S(1)}, u32[]{:S(2)}, u32[]{:S(2)}) collective-permute-start(f32[29,8,128]{2,1,0:T(8,128)S(1)} %get-tuple-element.87), channel_id=1, source_target_pairs={{8,0},{16,8},{24,16},{32,24},{40,32},{48,40},{56,48},{64,56},{72,6... | collective-permute-start | bytes 356360 | tf_op jit(solution)/shard_map/ppermute | solution.py:817
  43.1 5.5 %prepare.1 = (f32[16,8,8,384]{3,2,1,0:T(8,128)S(1)}, f32[16,8,8,384]{3,2,1,0:T(8,128)S(1)}, f32[16,8,8,384]{3,2,1,0:T(8,128)S(1)}, f32[16,8,8,384]{3,2,1,0:T(8,1...) custom-call(f32[16,8,8,256]{3,2,1,0:T(8,128)S(1)} %get-tuple-element, ...), custom_call_target="tpu_custom_call" | custom-call | tf_op jit(solution)/shard_map/prepare/pallas_call | solution.py:596
  48.6 5.6 %first_newton.1 = (f32[18,8,8,384]{3,2,1,0:T(8,128)S(1)}, f32[18,8,8,384]{3,2,1,0:T(8,128)S(1)}, f32[30,8,384]{2,1,0:T(8,128)S(1)}, f32[30,8,8,384]{3,2,1,0:T(8,...) custom-call(f32[16,8,8,384]{3,2,1,0:T(8,128)S(1)} %get-tuple-element.70.q_mid, ...), custom_call_target="tpu_custom_call" | custom-call | tf_op jit(solution)/shard_map/first_newton/pallas_call | solution.py:700
  54.3 15.7 %all_to_all.27 = f32[128,1,128]{2,1,0:T(1,128)S(1)} all-to-all(f32[128,1,128]{2,1,0:T(1,128)S(1)} %bitcast.33), channel_id=1, replica_groups=mesh['gx'=16,'gy'=8] {'gx','gy'}, dimensions={0} | all-to-all | bytes 131072 | tf_op jit(solution)/shard_map/all_to_all | solution.py:821
  70.0 8.2 %second_newton.1 = (f32[16,8,8,256]{3,2,1,0:T(8,128)S(1)}, f32[16,8,8,256]{3,2,1,0:T(8,128)S(1)}, f32[16,8,8,256]{3,2,1,0:T(8,128)S(1)}, f32[16,8,8,256]{3,2,1,0:T(8,128)S(1)}, f32[128,128]{1,0:T(8,128)S(1)}) custom-call(f32[16,8,8,384]{3,2,1,0:T(8,128)S(1)} %get-tuple-element.70.q_mid, f32[16,8,8,384]{3,2,1,0:T(8,128)S(1)} %get-tuple-element.71.k_mid, ...), custom_call_target="tpu_custom_call" | custom-call | tf_op jit(solution)/shard_map/second_newton/pallas_call | solution.py:769
  78.2 13.9 %all_to_all.28 = f32[128,1,128]{2,1,0:T(1,128)S(1)} all-to-all(f32[128,1,128]{2,1,0:T(1,128)S(1)} %bitcast.34), channel_id=1, replica_groups=mesh['gx'=16,'gy'=8] {'gx','gy'}, dimensions={0} | all-to-all | bytes 131072 | tf_op jit(solution)/shard_map/all_to_all | solution.py:821
  92.1 1.8 %final_update.1 = f32[8,8,2,16,128]{4,3,2,1,0:T(8,128)} custom-call(f32[16,8,8,256]{3,2,1,0:T(8,128)S(1)} %get-tuple-element.95.q, f32[16,8,8,256]{3,2,1,0:T(8,128)S(1)} %get-tuple-element.96.v0, f32[16,8,8,256]{3,2,1,0:T(8,128)S(1)} %get-tuple-element.97.v1, f32[16,8,8,256]{3,2,1,0:T(8,128)S(1)} %get-tuple-element.98.v2, f32[128,128]{1,0:T(8,128)S(1)} %bitcast.32), custom_call_target="tpu_custom_call" | custom-call | tf_op jit(solution)/shard_map/final_update/pallas_call | solution.py:802
  (6 shorter events, 0.0 us)
Async XLA Ops:
  4.1 18.8 %collective-permute-start = (f32[12,8,8,128]{3,2,1,0:T(8,128)}, f32[12,8,8,128]{3,2,1,0:T(8,128)S(1)}, u32[]{:S(2)}, u32[]{:S(2)}) collective-permute-start(f32[12,8,8,128]{3,2,1,0:T(8,128)} %get-tuple-element.57), channel_id=1, source_target_pairs={{0,8},{8,16},{16,24},{24,32},{32,40},{40,48},{48,56},{56,64},{64,7... | collective-permute-start | bytes 1179656 | tf_op jit(solution)/shard_map/ppermute | solution.py:817
  6.3 16.6 %collective-permute-start.1 = (f32[12,8,8,128]{3,2,1,0:T(8,128)}, f32[12,8,8,128]{3,2,1,0:T(8,128)S(1)}, u32[]{:S(2)}, u32[]{:S(2)}) collective-permute-start(f32[12,8,8,128]{3,2,1,0:T(8,128)} %get-tuple-element.58), channel_id=1, source_target_pairs={{8,0},{16,8},{24,16},{32,24},{40,32},{48,40},{56,48},{64,56},{72,6... | collective-permute-start | bytes 1179656 | tf_op jit(solution)/shard_map/ppermute | solution.py:817
  12.7 10.2 %all-to-all-start = ((f32[16,8,256]{2,1,0:T(8,128)}), f32[16,8,256]{2,1,0:T(8,128)S(1)}, u32[]{:S(2)}, u32[]{:S(2)}) async-start(f32[16,8,256]{2,1,0:T(8,128)} %get-tuple-element.56), calls=%async_computation | async-start | bytes 262144 | tf_op jit(solution)/shard_map/all_to_all | solution.py:847
  22.9 25.7 %collective-permute-start.4 = (f32[16,8,8,128]{3,2,1,0:T(8,128)}, f32[16,8,8,128]{3,2,1,0:T(8,128)S(1)}, u32[]{:S(2)}, u32[]{:S(2)}) collective-permute-start(f32[16,8,8,128]{3,2,1,0:T(8,128)} %get-tuple-element.82), channel_id=1, source_target_pairs={{0,8},{8,16},{16,24},{24,32},{32,40},{40,48},{48,56},{56,64},{64,7... | collective-permute-start | bytes 1572872 | tf_op jit(solution)/shard_map/ppermute | solution.py:817
  23.1 25.5 %collective-permute-start.5 = (f32[16,8,8,128]{3,2,1,0:T(8,128)}, f32[16,8,8,128]{3,2,1,0:T(8,128)S(1)}, u32[]{:S(2)}, u32[]{:S(2)}) collective-permute-start(f32[16,8,8,128]{3,2,1,0:T(8,128)} %get-tuple-element.83), channel_id=1, source_target_pairs={{8,0},{16,8},{24,16},{32,24},{40,32},{48,40},{56,48},{64,56},{72,6... | collective-permute-start | bytes 1572872 | tf_op jit(solution)/shard_map/ppermute | solution.py:817
  29.6 6.4 %collective-permute-start.2 = (f32[17,8,128]{2,1,0:T(8,128)S(1)}, f32[17,8,128]{2,1,0:T(8,128)S(1)}, u32[]{:S(2)}, u32[]{:S(2)}) collective-permute-start(f32[17,8,128]{2,1,0:T(8,128)S(1)} %get-tuple-element.67), channel_id=1, source_target_pairs={{0,1},{1,2},{2,3},{3,4},{4,5},{5,6},{6,7},{7,0},{8,9},{9,10},{10,1... | collective-permute-start | bytes 208904 | tf_op jit(solution)/shard_map/ppermute | solution.py:817
  34.1 4.0 %collective-permute-start.3 = (f32[17,8,128]{2,1,0:T(8,128)S(1)}, f32[17,8,128]{2,1,0:T(8,128)S(1)}, u32[]{:S(2)}, u32[]{:S(2)}) collective-permute-start(f32[17,8,128]{2,1,0:T(8,128)S(1)} %get-tuple-element.68), channel_id=1, source_target_pairs={{1,0},{2,1},{3,2},{4,3},{5,4},{6,5},{7,6},{0,7},{9,8},{10,9},{11,1... | collective-permute-start | bytes 208904 | tf_op jit(solution)/shard_map/ppermute | solution.py:817
  38.2 10.4 %collective-permute-start.6 = (f32[29,8,128]{2,1,0:T(8,128)S(1)}, f32[29,8,128]{2,1,0:T(8,128)S(1)}, u32[]{:S(2)}, u32[]{:S(2)}) collective-permute-start(f32[29,8,128]{2,1,0:T(8,128)S(1)} %get-tuple-element.86), channel_id=1, source_target_pairs={{0,8},{8,16},{16,24},{24,32},{32,40},{40,48},{48,56},{56,64},{64,7... | collective-permute-start | bytes 356360 | tf_op jit(solution)/shard_map/ppermute | solution.py:817
  38.3 10.3 %collective-permute-start.7 = (f32[29,8,128]{2,1,0:T(8,128)S(1)}, f32[29,8,128]{2,1,0:T(8,128)S(1)}, u32[]{:S(2)}, u32[]{:S(2)}) collective-permute-start(f32[29,8,128]{2,1,0:T(8,128)S(1)} %get-tuple-element.87), channel_id=1, source_target_pairs={{8,0},{16,8},{24,16},{32,24},{40,32},{48,40},{56,48},{64,56},{72,6... | collective-permute-start | bytes 356360 | tf_op jit(solution)/shard_map/ppermute | solution.py:817
